TPU v7x, 128 devices: a whole 4x4x4 slice. The times are simulated.
128 devices in a mesh: seq: 8 (over y, core), head: 16 (over z, x).
Axes of the slice: x: 4, y: 4, z: 4, core: 2. Of those that a mesh axis runs over, the one named last changes fastest.
Arguments:
- inputs: bfloat16 [8192, 6144], P('seq', 'head'), may hold values from -6 to 6
- frozen: bfloat16 [3, 8192, 8192], P(None, 'seq', 'head'), may hold values from -6 to 6
- adapter_down: bfloat16 [3, 6144, 64], P(None, 'head'), may hold values from -0.078125 to 0.078125
- adapter_up: bfloat16 [3, 64, 8192], P(None, None, 'head'), may hold values from -0.75 to 0.75
- out_grad: bfloat16 [8192, 8192], P('seq', 'head'), may hold values from -0.29882812 to 0.29882812
- log_decay: bfloat16 [64, 8192], P('head', 'seq'), may hold values from -2.5 to 0, as said below
- doc_start: int32 [8192], P('seq'), may hold values from 0 to 1, as said below
- lengths: int32 [8], replicated, may hold values from 0 to 1024, as said below
Outputs:
- attn_out: bfloat16 [8192, 8192], P('seq', 'head')
- projection_grad: bfloat16 [3, 8192, 8192], P(None, 'seq', 'head')
- down_grad: float32 [3, 6144, 64], P(None, 'head')
- up_grad: float32 [3, 64, 8192], P(None, None, 'head')
Inputs may be any that keep to these rules, and one draw needn't show every extreme that they name: lengths[i] live slots stand at the front of the 1024 slots of the i-th index of seq; they add up to 4096; the sum of the first i of them lies between i * 512 and (i + 1) * 512; one of them equals 1024. `doc_start`: values at slots that are not live are not read. `log_decay`: values at slots that are not live are not read.
All inputs are finite; a program needn't handle non-finite values.
Results may differ from a plain program's by a relative error of at most 0.028.
Values may be sent and summed in bfloat16 or wider, within the bound.
No kernel may reach another device: no remote copies, remote signals or barrier semaphores. Data moves between devices by JAX's collectives and lax.ppermute only.
A program may use at most 128 MiB of HBM per device.

v0:
```python
import jax
import jax.numpy as jnp
from jax import lax
from jax.sharding import PartitionSpec as P

HIGHEST = lax.Precision.HIGHEST


def entering_2(array, axis, join, neutral, backward):
    count = lax.axis_size(axis)
    place = lax.axis_index(axis)
    ahead = count - 1 - place if backward else place
    gathered = jax.tree.map(
        lambda a, kind: lax.all_gather(a.astype(kind), axis),
        array,
        jax.tree.map(lambda a: jnp.bfloat16 if a.dtype == jnp.float32 else a.dtype, array),
    )
    state = jax.tree.map(lambda a, e: jnp.zeros_like(a) + jnp.asarray(e, a.dtype), array, neutral)

    def one(turn, state):
        source = count - 1 - turn if backward else turn
        return join(
            state,
            jax.tree.map(
                lambda a, own: lax.dynamic_index_in_dim(a, source, 0, False).astype(own.dtype),
                gathered,
                array,
            ),
        )

    return lax.fori_loop(0, ahead, one, state)


def combine(earlier, later):
    return (earlier[0] * later[0], later[0][:, None, None] * earlier[1] + later[1])


def edges(decay, starts):
    cumulative = jnp.cumsum(decay, axis=1)
    segment = jnp.cumsum(starts)
    entering = jnp.where((segment == 0)[None, :], jnp.exp(cumulative), 0.0)
    leaving = jnp.where(
        (segment == segment[-1])[None, :], jnp.exp(cumulative[:, -1:] - cumulative), 0.0
    )
    passing = jnp.where(segment[-1] == 0, jnp.exp(cumulative[:, -1]), 0.0)
    return (cumulative, segment, entering, leaving, passing)


def weights_of(cumulative, segment):
    row_count = segment.shape[0]
    causal = lax.broadcasted_iota(jnp.int32, (row_count, row_count), 0) >= lax.broadcasted_iota(
        jnp.int32, (row_count, row_count), 1
    )
    allowed = (causal & (segment[:, None] == segment[None, :]))[None]
    spread = jnp.where(allowed, cumulative[:, :, None] - cumulative[:, None, :], 0.0)
    return jnp.where(allowed, jnp.exp(spread), 0.0)


def attend(moving, decay, starts):
    streams, row_count, feature_count = moving.shape
    head_count = decay.shape[0]
    head_size = feature_count // head_count
    inverse = 1.0 / head_size
    block_rows = min(1024, row_count)
    block_count = row_count // block_rows
    number = 0
    block_data = moving.reshape(streams, block_rows, head_count, head_size)
    pieces = [(block_data, edges(decay, starts))]
    identity = (
        jnp.ones((head_count,), jnp.float32),
        jnp.zeros((head_count, head_size, head_size), jnp.float32),
    )
    block_data, bounds = pieces[0]
    keyed = block_data[1].astype(jnp.float32) * bounds[3].T[:, :, None]
    local_states = [
        jnp.einsum("shd,she->hde", keyed, block_data[2].astype(jnp.float32), precision=HIGHEST)
    ]
    summary = identity
    for (block_data, bounds), own_state in zip(pieces, local_states):
        summary = combine(summary, (bounds[4], own_state))
    incoming = entering_2(summary, "seq", combine, identity, False)[1]
    outputs = []
    before_list = []
    carried = incoming
    for (block_data, bounds), own_state in zip(pieces, local_states):
        before_list.append(carried)
        weights = weights_of(bounds[0], bounds[1])
        scores = jnp.einsum(
            "thd,shd->hts", block_data[0], block_data[1], preferred_element_type=jnp.float32
        )
        weighted = (scores * weights * inverse).astype(jnp.bfloat16)
        inside = jnp.einsum(
            "hts,she->the", weighted, block_data[2], preferred_element_type=jnp.float32
        )
        outside = (
            jnp.einsum(
                "thd,hde->the", block_data[0].astype(jnp.float32), carried, precision=HIGHEST
            )
            * (bounds[2].T * inverse)[:, :, None]
        )
        outputs.append((inside + outside).astype(jnp.bfloat16).reshape(block_rows, feature_count))
        carried = bounds[4][:, None, None] * carried + own_state
    block_data, bounds = pieces[0]
    scaled_query = block_data[0].astype(jnp.float32) * (bounds[2].T * inverse)[:, :, None]
    returning = [
        jnp.einsum(
            "thd,the->hde", scaled_query, block_data[3].astype(jnp.float32), precision=HIGHEST
        )
    ]
    summary_back = identity
    for number in reversed(range(block_count)):
        summary_back = combine(summary_back, (pieces[number][1][4], returning[number]))
    later_state = entering_2(summary_back, "seq", combine, identity, True)[1]
    grad_blocks = [None] * block_count
    for number in reversed(range(block_count)):
        block_data, bounds = pieces[number]
        weights = weights_of(bounds[0], bounds[1])
        scores = jnp.einsum(
            "thd,shd->hts", block_data[0], block_data[1], preferred_element_type=jnp.float32
        )
        weighted = (scores * weights * inverse).astype(jnp.bfloat16)
        grad_weighted = (
            jnp.einsum(
                "the,she->hts", block_data[3], block_data[2], preferred_element_type=jnp.float32
            )
            * weights
            * inverse
        ).astype(jnp.bfloat16)
        key_wide = block_data[1].astype(jnp.float32)
        value_wide = block_data[2].astype(jnp.float32)
        grad_wide = block_data[3].astype(jnp.float32)
        query_grad = (
            jnp.einsum(
                "hts,shd->thd", grad_weighted, block_data[1], preferred_element_type=jnp.float32
            )
            + jnp.einsum("the,hde->thd", grad_wide, before_list[number], precision=HIGHEST)
            * (bounds[2].T * inverse)[:, :, None]
        )
        key_grad = (
            jnp.einsum(
                "hts,thd->shd", grad_weighted, block_data[0], preferred_element_type=jnp.float32
            )
            + jnp.einsum("she,hde->shd", value_wide, later_state, precision=HIGHEST)
            * bounds[3].T[:, :, None]
        )
        value_grad = (
            jnp.einsum("hts,the->she", weighted, block_data[3], preferred_element_type=jnp.float32)
            + jnp.einsum("shd,hde->she", key_wide, later_state, precision=HIGHEST)
            * bounds[3].T[:, :, None]
        )
        grad_blocks[number] = (
            jnp.stack([query_grad, key_grad, value_grad])
            .astype(jnp.bfloat16)
            .reshape(3, block_rows, feature_count)
        )
        later_state = bounds[4][:, None, None] * later_state + returning[number]
    first_part = outputs[0][None]
    grad_part = grad_blocks[0]
    return jnp.concatenate([first_part, grad_part], axis=0)


def local(inputs, frozen, adapter_down, adapter_up, out_grad, log_decay, doc_start, lengths):
    slot_count = inputs.shape[0]
    device = lax.axis_index("seq")
    live_count = lengths[device]
    live = jnp.arange(slot_count, dtype=jnp.int32) < live_count
    whole_input, whole_down = (
        lax.all_gather(inputs, "head", axis=1, tiled=True),
        lax.all_gather(adapter_down, "head", axis=1, tiled=True),
    )
    low = jnp.einsum(
        "td,kdr->tkr", whole_input, whole_down, preferred_element_type=jnp.float32
    ).astype(jnp.bfloat16)
    lifted = jnp.einsum("tkr,krf->ktf", low, adapter_up, preferred_element_type=jnp.float32)
    projected = (frozen.astype(jnp.float32) + lifted).astype(jnp.bfloat16)
    moving = jnp.concatenate([projected, out_grad[None]], axis=0)
    moving = jnp.where(live[None, :, None], moving, jnp.zeros((), jnp.bfloat16))
    decay = jnp.where(live[None, :], log_decay, jnp.zeros((), jnp.bfloat16))
    starts = jnp.where(live, doc_start, 0).astype(jnp.bfloat16)
    placed = attend(moving, decay.astype(jnp.float32), starts.astype(jnp.float32))
    attn_out = placed[0]
    projection_grad = placed[1:]
    up_grad = jnp.einsum("tkr,ktf->krf", low, projection_grad, preferred_element_type=jnp.float32)
    low_grad_part = jnp.einsum(
        "ktf,krf->tkr", projection_grad, adapter_up, preferred_element_type=jnp.float32
    )
    low_grad = lax.psum(low_grad_part.astype(jnp.bfloat16), "head")
    down_grad = jnp.einsum("td,tkr->kdr", inputs, low_grad, preferred_element_type=jnp.float32)
    down_total, up_total = (
        lax.psum(down_grad.astype(jnp.bfloat16), "seq").astype(jnp.float32),
        lax.psum(up_grad.astype(jnp.bfloat16), "seq").astype(jnp.float32),
    )
    return (attn_out, projection_grad, down_total, up_total)


def solution(mesh):
    in_specs = (
        P("seq", "head"),
        P(None, "seq", "head"),
        P(None, "head", None),
        P(None, None, "head"),
        P("seq", "head"),
        P("head", "seq"),
        P("seq"),
        P(),
    )
    out_specs = (
        P("seq", "head"),
        P(None, "seq", "head"),
        P(None, "head", None),
        P(None, None, "head"),
    )
    return jax.shard_map(local, mesh=mesh, in_specs=in_specs, out_specs=out_specs, check_vma=False)
```

profile of v0, /device:TPU:1, one launch (start us, length us, event | category | flops | bytes accessed | tf_op | source)
XLA Modules:
  0.0 410.2 jit_solution(15280296816318429638)
XLA Ops:
  8.0 0.7 all-gather.8.cloned.1.call-update
  8.7 1.2 dynamic_slice.29
  10.6 0.7 convert_bitcast_fusion
  11.3 1.1 reduce-window.19
  12.9 1.3 fusion.35
  14.6 3.2 copy.50
  17.8 2.3 copy.51
  23.2 13.4 %all-reduce = bf16[32]{0:T(256)(128)(2,1)S(1)} all-reduce(bf16[32]{0:T(256)(128)(2,1)S(1)} %dynamic-update-slice), channel_id=2, replica_groups=mesh['seq'=8,'head'=16] {'seq'}, use_global_device_ids=true, to_apply=%add | all-reduce | flops 32 | bytes 128
  37.5 1.6 fusion
  39.1 22.4 %all-gather.10.cloned.1.call-done = bf16[3,6144,64]{1,2,0:T(8,128)(2,1)} async-done(((bf16[3,384,64]{1,2,0:T(8,128)(2,1)}), bf16[3,6144,64]{1,2,0:T(8,128)(2,1)}) %all-gather.10.cloned.1.call-update) | async-done | bytes 2359312 | tf_op jit(solution)/shard_map/all_gather | solution.py:169
  61.5 101.2 %all-gather.8.cloned.1.call-done = bf16[1024,6144]{1,0:T(8,128)(2,1)} async-done(((bf16[1024,384]{1,0:T(8,128)(2,1)}), bf16[1024,6144]{1,0:T(8,128)(2,1)}) %all-gather.8.cloned.1.call-update) | async-done | bytes 12582928 | tf_op jit(solution)/shard_map/all_gather | solution.py:168
  162.7 7.9 %fusion.40 = f32[1024,192]{0,1:S(1)} fusion(bf16[1024,6144]{1,0:T(8,128)(2,1)} %all-gather.8.cloned.1.call-done, bf16[6144,192]{0,1:T(8,128)(2,1)} %bitcast.168), kind=kOutput, calls=%fused_computation.65 | convolution fusion | flops 2415919104 | bytes 15728640
  170.7 1.0 add_convert_fusion
  173.2 0.7 copy-done.10
  173.9 6.0 %multiply_convert_fusion = bf16[4,1024,1024]{2,1,0:T(8,128)(2,1)S(1)} fusion(bf16[1024,4,128]{0,2,1:T(8,128)(2,1)S(1)} %bitcast.149, bf16[1024,4,128]{0,2,1:T(8,128)(2,1)S(1)} %bitcast.141, f32[4,1024]{1,0:T(4,128)S(1)} %bitcast.164, pred[1024,1024]{1,0:T(8,128)(4,1)S(1)} %copy-done.10), kind=kOutput, calls=%fused_computation.4 | convolution fusion | flops 1098907648 | bytes 11550720 | tf_op jit(solution)/shard_map/the,she->hts/dot_general | solution.py:123
  179.9 4.2 %fusion.42 = f32[4,128,1024]{2,1,0:T(8,128)} fusion(bf16[1024,4,128]{0,2,1:T(8,128)(2,1)S(1)} %bitcast.145, bf16[4,1024,1024]{2,1,0:T(8,128)(2,1)S(1)} %multiply_convert_fusion), kind=kOutput, calls=%fused_computation.67 | convolution fusion | flops 1073741824 | bytes 11534336 | tf_op jit(solution)/shard_map/hts,shd->thd/dot_general | solution.py:133
  184.2 1.9 fusion.25
  186.3 3.1 fusion.22
  189.4 6.1 %fusion.43 = f32[4,128,1024]{2,1,0:T(8,128)} fusion(bf16[1024,4,128]{0,2,1:T(8,128)(2,1)S(1)} %bitcast.138, bf16[4,1024,1024]{2,1,0:T(8,128)(2,1)} %copy-done.1), kind=kOutput, calls=%fused_computation.68 | convolution fusion | flops 1073741824 | bytes 11534336 | tf_op jit(solution)/shard_map/hts,thd->shd/dot_general | solution.py:140
  195.5 8.0 %multiply_convert_fusion.1 = bf16[4,1024,1024]{2,1,0:T(8,128)(2,1)} fusion(bf16[1024,4,128]{0,2,1:T(8,128)(2,1)S(1)} %bitcast.139, bf16[1024,4,128]{0,2,1:T(8,128)(2,1)S(1)} %bitcast.147, f32[4,1024]{1,0:T(4,128)S(1)} %bitcast.165, pred[1024,1024]{1,0:T(8,128)(4,1)S(1)} %copy-done.11), kind=kOutput, calls=%fused_computation.5 | convolution fusion | flops 1098907648 | bytes 11550720 | tf_op jit(solution)/shard_map/thd,shd->hts/dot_general | solution.py:88
  203.6 6.4 %fusion.44 = f32[4,128,1024]{2,1,0:T(8,128)} fusion(bf16[1024,4,128]{0,2,1:T(8,128)(2,1)} %bitcast.151, bf16[4,1024,1024]{2,1,0:T(8,128)(2,1)} %multiply_convert_fusion.1), kind=kOutput, calls=%fused_computation.69 | convolution fusion | flops 1073741824 | bytes 11534336 | tf_op jit(solution)/shard_map/hts,the->she/dot_general | solution.py:147
  210.2 1.1 while.26
  210.2 1.0 convert_add_fusion.4
  211.3 4.0 fusion.6
  215.3 2.3 copy.65
  217.5 18.0 %all-gather.14.cloned.1.call-done = bf16[32,128,128]{2,1,0:T(8,128)(2,1)} async-done(((bf16[4,128,128]{2,1,0:T(8,128)(2,1)}), bf16[32,128,128]{2,1,0:T(8,128)(2,1)}) %all-gather.14.cloned.1.call-update) | async-done | bytes 1048592 | tf_op jit(solution)/shard_map/all_gather | solution.py:14
  235.6 6.4 %while.27 = (s32[]{:T(128)}, f32[4,128,128]{2,1,0:T(8,128)S(1)}, s32[]{:T(128)}, bf16[8,4]{1,0:T(8,128)(2,1)S(1)}, bf16[8,4,128,128]{3,2,1,0:T(8,128)(2,1)}, /*index=5*/s32[]{:T(128)}, s32[]{:T(128)}, s32[]{:T(128)}, s32[]{:T(128)}) while((s32[]{:T(128)}, f32[4,128,128]{2,1,0:T(8,128)S(1)}, s32[]{:T(128)}, bf16[8,4]{1,0:T(8,128)(2,1)S(1)}, ...), condition=%wide.region_7.8_spmd, body=%wide.region_6.7_spmd.sunk | while | flops 196618 | bytes 655547 | solution.py:31
  235.6 1.0 convert_add_fusion.5
  236.7 1.0 convert_add_fusion.5
  237.8 1.0 convert_add_fusion.5
  238.8 1.0 convert_add_fusion.5
  239.9 1.0 convert_add_fusion.5
  240.9 1.0 convert_add_fusion.5
  242.0 3.6 fusion.4
  245.6 2.3 copy.66
  247.9 2.7 fusion.2
  250.6 1.3 copy.67
  251.9 2.2 pad_maximum_fusion
  254.2 1.8 fusion.15
  256.3 8.1 %fusion.41 = f32[4,128,1024]{2,1,0:T(8,128)} fusion(bf16[1024,4,128]{0,2,1:T(8,128)(2,1)} %bitcast.144, bf16[4,1024,1024]{2,1,0:T(8,128)(2,1)} %multiply_convert_fusion.1), kind=kOutput, calls=%fused_computation.66 | convolution fusion | flops 1073741824 | bytes 11534336 | tf_op jit(solution)/shard_map/hts,she->the/dot_general | solution.py:92
  264.3 1.3 convolution_convert_fusion.1
  265.7 73.0 %all-reduce.5.cloned.1.call-done = bf16[1024,3,64]{0,2,1:T(8,128)(2,1)} async-done(((bf16[1024,3,64]{0,2,1:T(8,128)(2,1)}), bf16[1024,3,64]{0,2,1:T(8,128)(2,1)}) %all-reduce.5.cloned.1.call-update) | async-done | bytes 393232 | tf_op jit(solution)/shard_map/psum | solution.py:187
  338.6 2.3 fusion.28
  341.0 3.1 fusion.8
  344.1 1.3 copy.68
  345.4 54.7 %all-reduce.7.cloned.1.call-done = (bf16[3,384,64]{1,2,0:T(8,128)(2,1)}, bf16[3,64,512]{2,1,0:T(8,128)(2,1)}) async-done(((bf16[3,384,64]{1,2,0:T(8,128)(2,1)}, bf16[3,64,512]{2,1,0:T(8,128)(2,1)}), (bf16[3,384,64]{1,2,0:T(8,128)(2,1)}, bf16[3,64,512]{2,1,0:T(8,128)(2,1)})) %all-reduce.7.cloned.1.call-update) | async-done | bytes 344080 | tf_op jit(solution)/shard_map/psum | solution.py:190
  400.0 1.7 convert_element_type.140
  401.7 1.6 convert_element_type.138
  (70 shorter events, 7.2 us)
Async XLA Ops:
  7.2 163.5 %copy-start = (bf16[3,64,512]{2,1,0:T(8,128)(2,1)S(1)}, bf16[3,64,512]{2,1,0:T(8,128)(2,1)}, u32[]{:S(2)}) copy-start(bf16[3,64,512]{2,1,0:T(8,128)(2,1)} %param.15) | copy-start | bytes 589828
  7.2 54.3 %all-gather.10.cloned.1.call-start = ((), (), s32[]{:S(2)}) async-start(), calls=%async_computation.1 | async-start | bytes 2506752 | tf_op jit(solution)/shard_map/all_gather | solution.py:169
  7.9 154.8 %all-gather.8.cloned.1.call-start = ((), (), s32[]{:S(2)}) async-start(), calls=%async_computation | async-start | bytes 13369344 | tf_op jit(solution)/shard_map/all_gather | solution.py:168
  8.7 201.5 %all-gather.12.cloned.1.call-start = ((), (), s32[]{:S(2)}) async-start(), calls=%async_computation.3 | async-start | bytes 1179648 | tf_op jit(solution)/shard_map/all_gather | solution.py:14
  14.6 7.1 %copy-start.12 = (u32[128]{0:T(128)S(1)}, u32[128]{0:T(128)}, u32[]{:S(2)}) copy-start(u32[128]{0:T(128)} %constant.78) | copy-start | bytes 1540
  170.7 1.1 copy-start.8
  170.7 1.5 copy-start.7
  172.7 1.2 copy-start.10
  173.1 6.8 %copy-start.6 = (bf16[1,1024,512]{1,2,0:T(8,128)(2,1)}, bf16[1,1024,512]{1,2,0:T(8,128)(2,1)S(1)}, u32[]{:S(2)}) copy-start(bf16[1,1024,512]{1,2,0:T(8,128)(2,1)S(1)} %get-tuple-element.170) | copy-start | bytes 3145732
  173.2 22.4 %copy-start.4 = (bf16[1,1024,512]{1,2,0:T(8,128)(2,1)}, bf16[1,1024,512]{1,2,0:T(8,128)(2,1)S(1)}, u32[]{:S(2)}) copy-start(bf16[1,1024,512]{1,2,0:T(8,128)(2,1)S(1)} %get-tuple-element.172) | copy-start | bytes 3145732
  173.2 68.8 %copy-start.5 = (bf16[1,1024,512]{1,2,0:T(8,128)(2,1)}, bf16[1,1024,512]{1,2,0:T(8,128)(2,1)S(1)}, u32[]{:S(2)}) copy-start(bf16[1,1024,512]{1,2,0:T(8,128)(2,1)S(1)} %get-tuple-element.173) | copy-start | bytes 3145732
  179.9 4.3 %copy-start.1 = (bf16[4,1024,1024]{2,1,0:T(8,128)(2,1)}, bf16[4,1024,1024]{2,1,0:T(8,128)(2,1)S(1)}, u32[]{:S(2)}) copy-start(bf16[4,1024,1024]{2,1,0:T(8,128)(2,1)S(1)} %multiply_convert_fusion) | copy-start | bytes 25165828
  186.1 49.5 %all-gather.14.cloned.1.call-start = ((), (), s32[]{:S(2)}) async-start(), calls=%async_computation.4 | async-start | bytes 1179648 | tf_op jit(solution)/shard_map/all_gather | solution.py:14
  189.4 6.1 %copy-start.11 = (pred[1024,1024]{1,0:T(8,128)(4,1)S(1)}, pred[1024,1024]{1,0:T(8,128)(4,1)}, u32[]{:S(2)}) copy-start(pred[1024,1024]{1,0:T(8,128)(4,1)} %fusion) | copy-start | bytes 3145732
  203.5 135.1 %all-reduce.5.cloned.1.call-start = ((), (), s32[]{:S(2)}) async-start(), calls=%async_computation.2 | async-start | bytes 786432 | tf_op jit(solution)/shard_map/psum | solution.py:187
  211.3 6.3 %copy-start.3 = (f32[4,128,128]{2,1,0:T(8,128)}, f32[4,128,128]{2,1,0:T(8,128)S(1)}, u32[]{:S(2)}) copy-start(f32[4,128,128]{2,1,0:T(8,128)S(1)} %get-tuple-element.132) | copy-start | bytes 786436
  254.1 10.2 %copy-start.2 = (bf16[3,1024,512]{2,1,0:T(8,128)(2,1)}, bf16[3,1024,512]{2,1,0:T(8,128)(2,1)S(1)}, u32[]{:S(2)}) copy-start(bf16[3,1024,512]{2,1,0:T(8,128)(2,1)S(1)} %pad_maximum_fusion) | copy-start | bytes 9437188
  256.0 144.0 %all-reduce.7.cloned.1.call-start = ((), (), s32[]{:S(2)}) async-start(), calls=%async_computation.5 | async-start | bytes 688128 | tf_op jit(solution)/shard_map/psum | solution.py:190
  256.3 8.1 %copy-start.9 = (f32[1024,192]{0,1:S(1)}, f32[1024,192]{0,1}, u32[]{:S(2)}) copy-start(f32[1024,192]{0,1} %copy-done.8) | copy-start | bytes 2359300
Sparse Core Ops, SparseCore 0:
  10.1 51.3 all-gather.9
  63.6 99.0 all-gather.7
  186.2 23.9 all-gather.11
  212.3 23.2 all-gather.13
  256.1 82.4 all-reduce.4
  341.5 58.5 all-reduce.6
where the time goes:
time: 411 us; the launch traced here: 410 us
  waiting for transfers between devices  271 us (66%)
  matrix products  71.5 us (17%)
  other arithmetic  20 us (5%)
  local copies, waits for them, and re-layouts  17.7 us (4%)
  between operations  15.7 us (4%)
  blocking collectives  13.4 us (3%)
    all_gather x1, waiting for transfers between devices, local(): lax.all_gather(inputs, 'head', axis=1, tiled=True)  101 us
    psum x1, waiting for transfers between devices, local(): low_grad = lax.psum(low_grad_part.astype(jnp.bfloat16), 'head')  73 us
    psum x1, waiting for transfers between devices, local(): lax.psum(down_grad.astype(jnp.bfloat16), 'seq').astype(jnp.float32)  54.7 us
    all_gather x1, waiting for transfers between devices, local(): lax.all_gather(adapter_down, 'head', axis=1, tiled=True)  22.4 us
    all_gather x2, waiting for transfers between devices, entering_2(): lax.all_gather(a.astype(kind), axis)  18.2 us
    unnamed x1, blocking collectives  13.4 us
    unnamed x35, local copies, waits for them, and re-layouts  8.98 us
  transfers between devices with their start and end apart: 6, of which 6 were waited for; matrix products, arithmetic and copies ran while one was open for 15% of the time, Pallas kernels for 0%

commit v1 on v0

v1 whole, which is shorter than its diff:
```python
import functools

import jax
import jax.numpy as jnp
from jax import lax
from jax.experimental import pallas as pl
from jax.experimental.pallas import tpu as pltpu
from jax.sharding import PartitionSpec as P

F32 = jnp.float32
BF16 = jnp.bfloat16
CHUNK = 256
VMEM_BYTES = 48 * 1024 * 1024
NEGATIVE = -1e30

CUM, SEG, ENTER, LEAVE, ENTER_ALL, LEAVE_ALL = 0, 4, 8, 12, 16, 20


def dot_nn(a, b):
    return lax.dot_general(a, b, (((1,), (0,)), ((), ())), preferred_element_type=F32)


def dot_nt(a, b):
    return lax.dot_general(a, b, (((1,), (1,)), ((), ())), preferred_element_type=F32)


def dot_tn(a, b):
    return lax.dot_general(a, b, (((0,), (0,)), ((), ())), preferred_element_type=F32)


def params(**more):
    return pltpu.CompilerParams(vmem_limit_bytes=VMEM_BYTES, **more)


def cost(flops, moved):
    return pl.CostEstimate(flops=int(flops), bytes_accessed=int(moved), transcendentals=0)


VMEM = pl.BlockSpec(memory_space=pltpu.VMEM)
SMEM = pl.BlockSpec(memory_space=pltpu.SMEM)


def low_kernel(x_ref, down_ref, out_ref):
    rank = down_ref.shape[2]
    x = x_ref[...]
    for c in range(3):
        out_ref[:, c * rank : (c + 1) * rank] = dot_nn(x, down_ref[c]).astype(BF16)


def partial_low(x, down):
    rows, width = x.shape
    rank = down.shape[2]
    block = min(512, rows)
    return pl.pallas_call(
        low_kernel,
        out_shape=jax.ShapeDtypeStruct((rows, 3 * rank), BF16),
        grid=(rows // block,),
        in_specs=[
            pl.BlockSpec((block, width), lambda i: (i, 0)),
            pl.BlockSpec(down.shape, lambda i: (0, 0, 0)),
        ],
        out_specs=pl.BlockSpec((block, 3 * rank), lambda i: (i, 0)),
        compiler_params=params(),
        name="partial_low",
    )(x, down)


def sum_spread_kernel(in_ref, out_ref):
    count = in_ref.shape[0]
    total = in_ref[0].astype(F32)
    for i in range(1, count):
        total = total + in_ref[i].astype(F32)
    total = total.astype(BF16)
    for i in range(count):
        out_ref[i] = total


def sum_over_head(part):
    count = lax.axis_size("head")
    rows, width = part.shape
    pieces = part.reshape(count, rows // count, width)
    pieces = lax.all_to_all(pieces, "head", 0, 0)
    spread = pl.pallas_call(
        sum_spread_kernel,
        out_shape=jax.ShapeDtypeStruct(pieces.shape, BF16),
        in_specs=[VMEM],
        out_specs=VMEM,
        compiler_params=params(),
        name="sum_spread",
    )(pieces)
    return lax.all_to_all(spread, "head", 0, 0).reshape(rows, width)


def decay_kernel(meta_ref, decay_ref, start_ref, row_ref, col_ref, pass_ref):
    heads, rows = decay_ref.shape
    live = meta_ref[0]
    slot = lax.broadcasted_iota(jnp.int32, (1, rows), 1)
    keep = slot < live
    decay = jnp.where(keep, decay_ref[...].astype(F32), 0.0)
    starts = jnp.where(keep, start_ref[...].astype(F32), 0.0)
    both = jnp.concatenate([decay, starts, jnp.zeros((8 - heads - 1, rows), F32)], axis=0)
    both = both.astype(BF16)
    row_i = lax.broadcasted_iota(jnp.int32, (CHUNK, CHUNK), 0)
    col_i = lax.broadcasted_iota(jnp.int32, (CHUNK, CHUNK), 1)
    upper = jnp.where(row_i <= col_i, 1.0, 0.0).astype(BF16)
    lower = jnp.where(row_i >= col_i, 1.0, 0.0).astype(BF16)
    count = rows // CHUNK
    enters, leaves, passes = [], [], []
    for c in range(count):
        span = slice(c * CHUNK, (c + 1) * CHUNK)
        piece = both[:, span]
        by_row = dot_nn(piece, upper)
        by_col = dot_nt(lower, piece)
        row_ref[:, span] = by_row
        col_ref[span, 0:8] = by_col
        cum = by_col[:, :heads]
        seg = by_col[:, heads : heads + 1]
        cum_end = by_col[CHUNK - 1 : CHUNK, :heads]
        seg_end = by_col[CHUNK - 1 : CHUNK, heads : heads + 1]
        enter = jnp.where(seg == 0.0, jnp.exp(cum), 0.0)
        leave = jnp.where(seg == seg_end, jnp.exp(cum_end - cum), 0.0)
        col_ref[span, ENTER : ENTER + heads] = enter
        col_ref[span, LEAVE : LEAVE + heads] = leave
        enters.append(enter)
        leaves.append(leave)
        passes.append(jnp.where(seg_end == 0.0, jnp.exp(cum_end), 0.0))
        end_row = by_row[:, CHUNK - 1 : CHUNK]
        passing_col = jnp.where(end_row[heads : heads + 1] == 0.0, jnp.exp(end_row[:heads]), 0.0)
        pass_ref[c * heads : (c + 1) * heads, :] = jnp.broadcast_to(passing_col, (heads, 128))
    before = jnp.ones((1, heads), F32)
    for c in range(count):
        span = slice(c * CHUNK, (c + 1) * CHUNK)
        col_ref[span, ENTER_ALL : ENTER_ALL + heads] = enters[c] * before
        before = before * passes[c]
    after = jnp.ones((1, heads), F32)
    for c in reversed(range(count)):
        span = slice(c * CHUNK, (c + 1) * CHUNK)
        col_ref[span, LEAVE_ALL : LEAVE_ALL + heads] = leaves[c] * after
        after = after * passes[c]


def decay_tables(meta, decay, starts):
    heads, rows = decay.shape
    count = rows // CHUNK
    return pl.pallas_call(
        decay_kernel,
        out_shape=(
            jax.ShapeDtypeStruct((8, rows), F32),
            jax.ShapeDtypeStruct((rows, 128), F32),
            jax.ShapeDtypeStruct((count * heads, 128), F32),
        ),
        in_specs=[SMEM, VMEM, VMEM],
        out_specs=(VMEM, VMEM, VMEM),
        compiler_params=params(),
        cost_estimate=cost(4e9, 1e6),
        name="decay_tables",
    )(meta, decay, starts.reshape(1, rows))


def project_kernel(
    meta_ref, frozen_ref, low_ref, up_ref, grad_ref, col_ref, pass_ref,
    moving_ref, before_ref, after_ref, summary_ref,
    own, returning, running,
):
    step = pl.program_id(0)
    count = pl.num_programs(0)
    rank = up_ref.shape[1]
    features = frozen_ref.shape[2]
    heads = features // 128
    live = meta_ref[0]

    @pl.when(step == 0)
    def _():
        own[...] = jnp.zeros_like(own)
        running[...] = jnp.ones_like(running)
        summary_ref[...] = jnp.zeros_like(summary_ref)

    slot = step * CHUNK + lax.broadcasted_iota(jnp.int32, (CHUNK, 1), 0)
    keep = slot < live
    low = low_ref[...]
    for c in range(3):
        lifted = dot_nn(low[:, c * rank : (c + 1) * rank], up_ref[c])
        summed = frozen_ref[c].astype(F32) + lifted
        moving_ref[c] = jnp.where(keep, summed, 0.0).astype(BF16)
    moving_ref[3] = jnp.where(keep, grad_ref[...].astype(F32), 0.0).astype(BF16)
    col = col_ref[...]
    for h in range(heads):
        span = slice(h * 128, (h + 1) * 128)
        passing = pass_ref[pl.ds(step * heads + h, 1), :]
        leave = col[:, LEAVE + h : LEAVE + h + 1]
        enter = col[:, ENTER + h : ENTER + h + 1]
        keyed = (moving_ref[1, :, span].astype(F32) * leave).astype(BF16)
        scaled = (moving_ref[0, :, span].astype(F32) * enter).astype(BF16)
        state = own[h]
        before_ref[0, h] = state.astype(BF16)
        own[h] = passing * state + dot_tn(keyed, moving_ref[2, :, span])
        returning[step, h] = dot_tn(scaled, moving_ref[3, :, span])

    @pl.when(step == count - 1)
    def _():
        chunks = returning.shape[0]
        size = heads * 128
        for h in range(heads):
            back = jnp.zeros((128, 128), F32)
            whole = jnp.ones((1, 128), F32)
            for c in reversed(range(chunks)):
                passing = pass_ref[c * heads + h : c * heads + h + 1, :]
                after_ref[c, h] = back.astype(BF16)
                back = passing * back + returning[c, h]
                whole = whole * passing
            summary_ref[h * 128 : (h + 1) * 128, :] = own[h].astype(BF16)
            summary_ref[size + h * 128 : size + (h + 1) * 128, :] = back.astype(BF16)
            first = whole.astype(BF16)
            rest = whole - first.astype(F32)
            second = rest.astype(BF16)
            third = (rest - second.astype(F32)).astype(BF16)
            tail = jnp.concatenate(
                [first.astype(F32), second.astype(F32), third.astype(F32), jnp.zeros((13, 128), F32)],
                axis=0,
            )
            base = 2 * size + 16 * h
            summary_ref[base : base + 16, :] = tail.astype(BF16)


def project(meta, frozen, low, up, grad, col, passes):
    _, rows, features = frozen.shape
    heads = features // 128
    count = rows // CHUNK
    summary_rows = 2 * features + 16 * heads
    return pl.pallas_call(
        project_kernel,
        out_shape=(
            jax.ShapeDtypeStruct((4, rows, features), BF16),
            jax.ShapeDtypeStruct((count, heads, 128, 128), BF16),
            jax.ShapeDtypeStruct((count, heads, 128, 128), BF16),
            jax.ShapeDtypeStruct((summary_rows, 128), BF16),
        ),
        grid=(count,),
        in_specs=[
            SMEM,
            pl.BlockSpec((3, CHUNK, features), lambda i: (0, i, 0)),
            pl.BlockSpec((CHUNK, low.shape[1]), lambda i: (i, 0)),
            pl.BlockSpec(up.shape, lambda i: (0, 0, 0)),
            pl.BlockSpec((CHUNK, features), lambda i: (i, 0)),
            pl.BlockSpec((CHUNK, 128), lambda i: (i, 0)),
            pl.BlockSpec(passes.shape, lambda i: (0, 0)),
        ],
        out_specs=(
            pl.BlockSpec((4, CHUNK, features), lambda i: (0, i, 0)),
            pl.BlockSpec((1, heads, 128, 128), lambda i: (i, 0, 0, 0)),
            pl.BlockSpec((count, heads, 128, 128), lambda i: (0, 0, 0, 0)),
            pl.BlockSpec((summary_rows, 128), lambda i: (0, 0)),
        ),
        scratch_shapes=[
            pltpu.VMEM((heads, 128, 128), F32),
            pltpu.VMEM((count, heads, 128, 128), F32),
            pltpu.VMEM((heads, 128), F32),
        ],
        compiler_params=params(dimension_semantics=("arbitrary",)),
        cost_estimate=cost(4e9, 10e6),
        name="project",
    )(meta, frozen, low, up, grad, col, passes)


def passing_of(ref, base):
    return (
        ref[base : base + 1, :].astype(F32)
        + ref[base + 1 : base + 2, :].astype(F32)
        + ref[base + 2 : base + 3, :].astype(F32)
    )


def join_kernel(meta_ref, own_ref, mate_ref, *out_refs):
    y = meta_ref[1]
    core = meta_ref[2]
    total = own_ref.shape[0]
    heads = (total - 0) // (2 * 128 + 16)
    size = heads * 128
    chips = len(out_refs) + 1
    second = core == 1
    for h in range(heads):
        rows = slice(h * 128, (h + 1) * 128)
        back_rows = slice(size + h * 128, size + (h + 1) * 128)
        base = 2 * size + 16 * h
        own_pass = passing_of(own_ref, base)
        mate_pass = passing_of(mate_ref, base)
        own_state = own_ref[rows, :].astype(F32)
        mate_state = mate_ref[rows, :].astype(F32)
        own_back = own_ref[back_rows, :].astype(F32)
        mate_back = mate_ref[back_rows, :].astype(F32)
        one = jnp.ones_like(own_pass)
        state = jnp.where(second, own_pass, one) * mate_state + jnp.where(second, one, mate_pass) * own_state
        back = jnp.where(second, one, own_pass) * mate_back + jnp.where(second, mate_pass, one) * own_back
        whole = own_pass * mate_pass
        first = whole.astype(BF16).astype(F32)
        rest = whole - first
        middle = rest.astype(BF16).astype(F32)
        third = (rest - middle).astype(BF16).astype(F32)
        tail = jnp.concatenate([first, middle, third, jnp.zeros((13, 128), F32)], axis=0).astype(BF16)
        for k, out_ref in enumerate(out_refs):
            later = y + (k + 1) < chips
            out_ref[rows, :] = jnp.where(later, state, back).astype(BF16)
            out_ref[size + 16 * h : size + 16 * h + 16, :] = tail


def join(meta, own, mate, chips):
    heads = own.shape[0] // (2 * 128 + 16)
    message = jax.ShapeDtypeStruct((heads * (128 + 16), 128), BF16)
    return pl.pallas_call(
        join_kernel,
        out_shape=(message,) * (chips - 1),
        in_specs=[SMEM, VMEM, VMEM],
        out_specs=(VMEM,) * (chips - 1),
        compiler_params=params(),
        name="join",
    )(meta, own, mate)


def inside_kernel(moving_ref, row_ref, col_ref, before_ref, after_ref, part_ref):
    features = moving_ref.shape[2]
    heads = features // 128
    row_i = lax.broadcasted_iota(jnp.int32, (CHUNK, CHUNK), 0)
    col_i = lax.broadcasted_iota(jnp.int32, (CHUNK, CHUNK), 1)
    col = col_ref[...]
    allowed = (row_i >= col_i) & (col[:, SEG : SEG + 1] == row_ref[SEG : SEG + 1, :])
    shut = jnp.where(allowed, 0.0, NEGATIVE)
    for h in range(heads):
        span = slice(h * 128, (h + 1) * 128)
        q = moving_ref[0, :, span]
        k = moving_ref[1, :, span]
        v = moving_ref[2, :, span]
        g = moving_ref[3, :, span]
        weights = jnp.exp((col[:, h : h + 1] - row_ref[h : h + 1, :]) + shut)
        a = (dot_nt(q, k) * weights).astype(BF16)
        b = (dot_nt(g, v) * weights).astype(BF16)
        enter = col[:, ENTER + h : ENTER + h + 1]
        leave = col[:, LEAVE + h : LEAVE + h + 1]
        before = before_ref[0, h]
        after = after_ref[0, h]
        part_ref[0, :, span] = dot_nn(a, v) + enter * dot_nn(q, before)
        part_ref[1, :, span] = dot_nn(b, k) + enter * dot_nt(g, before)
        part_ref[2, :, span] = dot_tn(b, q) + leave * dot_nt(v, after)
        part_ref[3, :, span] = dot_tn(a, g) + leave * dot_nn(k, after)


def inside(moving, row, col, before, after):
    _, rows, features = moving.shape
    heads = features // 128
    count = rows // CHUNK
    return pl.pallas_call(
        inside_kernel,
        out_shape=jax.ShapeDtypeStruct((4, rows, features), F32),
        grid=(count,),
        in_specs=[
            pl.BlockSpec((4, CHUNK, features), lambda i: (0, i, 0)),
            pl.BlockSpec((8, CHUNK), lambda i: (0, i)),
            pl.BlockSpec((CHUNK, 128), lambda i: (i, 0)),
            pl.BlockSpec((1, heads, 128, 128), lambda i: (i, 0, 0, 0)),
            pl.BlockSpec((1, heads, 128, 128), lambda i: (i, 0, 0, 0)),
        ],
        out_specs=pl.BlockSpec((4, CHUNK, features), lambda i: (0, i, 0)),
        compiler_params=params(dimension_semantics=("arbitrary",)),
        cost_estimate=cost(14e9, 14e6),
        name="inside",
    )(moving, row, col, before, after)


def finish_kernel(chips, meta_ref, moving_ref, part_ref, col_ref, low_ref, up_ref, mate_ref, *refs):
    message_refs = refs[: chips - 1]
    attn_ref, grad_ref, low_grad_ref, up_grad_ref, state_in, back_in, up_sum = refs[chips - 1 :]
    step = pl.program_id(0)
    count = pl.num_programs(0)
    features = moving_ref.shape[2]
    heads = features // 128
    size = heads * 128
    rank = up_ref.shape[1]
    inverse = 1.0 / 128.0

    @pl.when(step == 0)
    def _():
        y = meta_ref[1]
        second = meta_ref[2] == 1
        up_sum[...] = jnp.zeros_like(up_sum)
        for h in range(heads):
            rows = slice(h * 128, (h + 1) * 128)
            factor = jnp.ones((1, 128), F32)
            state = jnp.zeros((128, 128), F32)
            for k in range(1, chips):
                ref = message_refs[k - 1]
                state = state + jnp.where(k <= y, factor, 0.0) * ref[rows, :].astype(F32)
                factor = factor * passing_of(ref, size + 16 * h)
            factor = jnp.ones((1, 128), F32)
            back = jnp.zeros((128, 128), F32)
            for k in reversed(range(1, chips)):
                ref = message_refs[k - 1]
                back = back + jnp.where(k > y, factor, 0.0) * ref[rows, :].astype(F32)
                factor = factor * passing_of(ref, size + 16 * h)
            mate_pass = passing_of(mate_ref, 2 * size + 16 * h)
            mate_state = mate_ref[rows, :].astype(F32)
            mate_back = mate_ref[size + h * 128 : size + (h + 1) * 128, :].astype(F32)
            state_in[h] = jnp.where(second, mate_pass * state + mate_state, state).astype(BF16)
            back_in[h] = jnp.where(second, back, mate_pass * back + mate_back).astype(BF16)

    col = col_ref[...]
    for h in range(heads):
        span = slice(h * 128, (h + 1) * 128)
        q = moving_ref[0, :, span]
        k = moving_ref[1, :, span]
        v = moving_ref[2, :, span]
        g = moving_ref[3, :, span]
        enter = col[:, ENTER_ALL + h : ENTER_ALL + h + 1]
        leave = col[:, LEAVE_ALL + h : LEAVE_ALL + h + 1]
        state = state_in[h]
        back = back_in[h]
        attn_ref[:, span] = ((part_ref[0, :, span] + enter * dot_nn(q, state)) * inverse).astype(BF16)
        grad_ref[0, :, span] = ((part_ref[1, :, span] + enter * dot_nt(g, state)) * inverse).astype(BF16)
        grad_ref[1, :, span] = ((part_ref[2, :, span] + leave * dot_nt(v, back)) * inverse).astype(BF16)
        grad_ref[2, :, span] = ((part_ref[3, :, span] + leave * dot_nn(k, back)) * inverse).astype(BF16)
    low = low_ref[...]
    for c in range(3):
        lanes = slice(c * rank, (c + 1) * rank)
        low_grad_ref[:, lanes] = dot_nt(grad_ref[c], up_ref[c]).astype(BF16)
        up_sum[c] += dot_tn(low[:, lanes], grad_ref[c])

    @pl.when(step == count - 1)
    def _():
        up_grad_ref[...] = up_sum[...].astype(BF16)


def finish(meta, moving, part, col, low, up, mate, messages):
    _, rows, features = moving.shape
    heads = features // 128
    count = rows // CHUNK
    chips = len(messages) + 1
    return pl.pallas_call(
        functools.partial(finish_kernel, chips),
        out_shape=(
            jax.ShapeDtypeStruct((rows, features), BF16),
            jax.ShapeDtypeStruct((3, rows, features), BF16),
            jax.ShapeDtypeStruct(low.shape, BF16),
            jax.ShapeDtypeStruct(up.shape, BF16),
        ),
        grid=(count,),
        in_specs=[
            SMEM,
            pl.BlockSpec((4, CHUNK, features), lambda i: (0, i, 0)),
            pl.BlockSpec((4, CHUNK, features), lambda i: (0, i, 0)),
            pl.BlockSpec((CHUNK, 128), lambda i: (i, 0)),
            pl.BlockSpec((CHUNK, low.shape[1]), lambda i: (i, 0)),
            pl.BlockSpec(up.shape, lambda i: (0, 0, 0)),
            pl.BlockSpec(mate.shape, lambda i: (0, 0)),
        ]
        + [pl.BlockSpec(m.shape, lambda i: (0, 0)) for m in messages],
        out_specs=(
            pl.BlockSpec((CHUNK, features), lambda i: (i, 0)),
            pl.BlockSpec((3, CHUNK, features), lambda i: (0, i, 0)),
            pl.BlockSpec((CHUNK, low.shape[1]), lambda i: (i, 0)),
            pl.BlockSpec(up.shape, lambda i: (0, 0, 0)),
        ),
        scratch_shapes=[
            pltpu.VMEM((heads, 128, 128), BF16),
            pltpu.VMEM((heads, 128, 128), BF16),
            pltpu.VMEM(up.shape, F32),
        ],
        compiler_params=params(dimension_semantics=("arbitrary",)),
        cost_estimate=cost(4e9, 18e6),
        name="finish",
    )(meta, moving, part, col, low, up, mate, *messages)


def down_kernel(x_ref, grad_ref, out_ref):
    out_ref[...] = dot_tn(x_ref[...], grad_ref[...]).astype(BF16)


def partial_down(x, low_grad):
    return pl.pallas_call(
        down_kernel,
        out_shape=jax.ShapeDtypeStruct((x.shape[1], low_grad.shape[1]), BF16),
        in_specs=[VMEM, VMEM],
        out_specs=VMEM,
        compiler_params=params(),
        name="partial_down",
    )(x, low_grad)


def add_kernel(*refs):
    total = refs[0][...].astype(F32)
    for ref in refs[1:-1]:
        total = total + ref[...].astype(F32)
    refs[-1][...] = total.astype(refs[-1].dtype)


def add_all(arrays, dtype):
    return pl.pallas_call(
        add_kernel,
        out_shape=jax.ShapeDtypeStruct(arrays[0].shape, dtype),
        in_specs=[VMEM] * len(arrays),
        out_specs=VMEM,
        compiler_params=params(),
        name="add_all",
    )(*arrays)


def split_kernel(*refs):
    total = refs[0][...].astype(F32)
    for ref in refs[1:-1]:
        total = total + ref[...].astype(F32)
    out_ref = refs[-1]
    rank = out_ref.shape[2]
    for c in range(out_ref.shape[0]):
        out_ref[c] = total[:, c * rank : (c + 1) * rank]


def add_split(arrays, count):
    rows, width = arrays[0].shape
    return pl.pallas_call(
        split_kernel,
        out_shape=jax.ShapeDtypeStruct((count, rows, width // count), F32),
        in_specs=[VMEM] * len(arrays),
        out_specs=VMEM,
        compiler_params=params(),
        name="add_split",
    )(*arrays)


def to_mate(a):
    return lax.ppermute(a, "seq", [(i, i ^ 1) for i in range(lax.axis_size("seq"))])


def along_y(a, k):
    count = lax.axis_size("seq")
    return lax.ppermute(a, "seq", [(i, (i + 2 * k) % count) for i in range(count)])


def local(inputs, frozen, adapter_down, adapter_up, out_grad, log_decay, doc_start, lengths):
    device = lax.axis_index("seq")
    chips = lax.axis_size("seq") // 2
    meta = jnp.stack([lengths[device], device // 2, device % 2]).astype(jnp.int32)
    row, col, passes = decay_tables(meta, log_decay, doc_start)
    low = sum_over_head(partial_low(inputs, adapter_down))
    moving, before, after, summary = project(meta, frozen, low, adapter_up, out_grad, col, passes)
    mate = to_mate(summary)
    outgoing = join(meta, summary, mate, chips)
    messages = [along_y(m, k + 1) for k, m in enumerate(outgoing)]
    part = inside(moving, row, col, before, after)
    attn, grads, low_grad_part, up_part = finish(
        meta, moving, part, col, low, adapter_up, mate, messages
    )
    up_chip = add_all([up_part, to_mate(up_part)], BF16)
    up_total = add_all([up_chip] + [along_y(up_chip, k) for k in range(1, chips)], F32)
    low_grad = sum_over_head(low_grad_part)
    down_part = partial_down(inputs, low_grad)
    down_chip = add_all([down_part, to_mate(down_part)], BF16)
    down_total = add_split([down_chip] + [along_y(down_chip, k) for k in range(1, chips)], 3)
    return (attn, grads, down_total, up_total)


def solution(mesh):
    in_specs = (
        P("seq", "head"),
        P(None, "seq", "head"),
        P(None, "head", None),
        P(None, None, "head"),
        P("seq", "head"),
        P("head", "seq"),
        P("seq"),
        P(),
    )
    out_specs = (
        P("seq", "head"),
        P(None, "seq", "head"),
        P(None, "head", None),
        P(None, None, "head"),
    )
    return jax.shard_map(local, mesh=mesh, in_specs=in_specs, out_specs=out_specs, check_vma=False)
```

time: 411 us -> 126 us (0.31)
  waiting for transfers between devices: 271 us -> 39.7 us
  matrix products: 71.5 us -> 0 us
  starting transfers between devices: 0.64 us -> 34 us
  Pallas kernels: 0 us -> 30.2 us
  other arithmetic: 20 us -> 0.72 us
  between operations: 15.7 us -> 0.78 us
  local copies, waits for them, and re-layouts: 17.7 us -> 6.66 us
    all_gather x4 -> x0, waiting for transfers between devices: 142 us -> none  [the longest x1 101 us: local(): lax.all_gather(inputs, 'head', axis=1, tiled=True)]
    psum x2 -> x0, waiting for transfers between devices: 128 us -> none  [the longest x1 73 us: local(): low_grad = lax.psum(low_grad_part.astype(jnp.bfloat16), 'head')]
    dot_general x16 -> x0, matrix products: 63.6 us -> none  [the longest x1 8.06 us: attend(): jnp.einsum('hts,she->the', weighted, block_data[2], preferred_element_typ...]
    pallas_call x0 -> x13, Pallas kernels: none -> 30.2 us  [the longest x1 8.69 us: finish(): pl.pallas_call(functools.partial(finish_kernel, chips), out_shape=(jax.Sh...]
    all_to_all x0 -> x3, waiting for transfers between devices: none -> 22.1 us  [the longest x2 13.6 us: sum_over_head(): return lax.all_to_all(spread, 'head', 0, 0).reshape(rows, width)]
    ppermute x0 -> x12, starting transfers between devices: none -> 18.5 us  [the longest x9 9.92 us: along_y(): lax.ppermute(a, 'seq', [(i, (i + 2 * k) % count) for i in range(count)])]
    ppermute x0 -> x12, waiting for transfers between devices: none -> 17.6 us  [the longest x9 15.2 us: along_y(): lax.ppermute(a, 'seq', [(i, (i + 2 * k) % count) for i in range(count)])]
    all_to_all x0 -> x3, starting transfers between devices: none -> 15.6 us  [the longest x1 8.43 us: sum_over_head(): pieces = lax.all_to_all(pieces, 'head', 0, 0)]
  transfers between devices with their start and end apart: 6 -> 15, of which waited for: 6 -> 10; matrix products, arithmetic and copies ran while one was open for 15% -> 2% of each run, Pallas kernels for 0% -> 9%
where the time goes in v1:
time: 126 us; the launch traced here: 125 us
  waiting for transfers between devices  39.7 us (32%)
  starting transfers between devices  34 us (27%)
  Pallas kernels  30.2 us (24%)
  blocking collectives  12.9 us (10%)
  local copies, waits for them, and re-layouts  6.66 us (5%)
    ppermute x9, waiting for transfers between devices, along_y(): lax.ppermute(a, 'seq', [(i, (i + 2 * k) % count) for i in range(count)])  15.2 us
    all_to_all x2, waiting for transfers between devices, sum_over_head(): return lax.all_to_all(spread, 'head', 0, 0).reshape(rows, width)  13.6 us
    all_to_all x1, blocking collectives, sum_over_head(): pieces = lax.all_to_all(pieces, 'head', 0, 0)  12.9 us
    ppermute x9, starting transfers between devices, along_y(): lax.ppermute(a, 'seq', [(i, (i + 2 * k) % count) for i in range(count)])  9.92 us
    pallas_call x1, Pallas kernels, finish(): pl.pallas_call(functools.partial(finish_kernel, chips), out_shape=(jax.Sh...  8.69 us
    ppermute x3, starting transfers between devices, to_mate(): lax.ppermute(a, 'seq', [(i, i ^ 1) for i in range(lax.axis_size('seq'))])  8.53 us
    all_to_all x1, waiting for transfers between devices, sum_over_head(): pieces = lax.all_to_all(pieces, 'head', 0, 0)  8.52 us
    all_to_all x1, starting transfers between devices, sum_over_head(): pieces = lax.all_to_all(pieces, 'head', 0, 0)  8.43 us
  transfers between devices with their start and end apart: 15, of which 10 were waited for; matrix products, arithmetic and copies ran while one was open for 2% of the time, Pallas kernels for 9%

profile of v1, /device:TPU:1, one launch (start us, length us, event | category | flops | bytes accessed | tf_op | source)
XLA Modules:
  0.0 124.9 jit_solution(8499075667196189627)
XLA Ops:
  0.7 1.1 copy.12.down_ref
  1.8 0.0 copy-start
  1.8 1.1 copy-done
  2.9 1.6 %partial_low.1 = bf16[1024,192]{1,0:T(8,128)(2,1)} custom-call(bf16[1024,384]{1,0:T(8,128)(2,1)S(1)} %copy-done, bf16[3,384,64]{2,1,0:T(8,128)(2,1)S(1)} %copy.12.down_ref), custom_call_target="tpu_custom_call" | custom-call | tf_op jit(solution)/shard_map/partial_low/pallas_call | solution.py:54
  4.6 8.4 %all-to-all-start = ((bf16[16,64,192]{2,1,0:T(8,128)(2,1)}), bf16[16,64,192]{2,1,0:T(8,128)(2,1)S(1)}, u32[]{:S(2)}, u32[]{:S(2)}) async-start(bf16[16,64,192]{2,1,0:T(8,128)(2,1)} %bitcast.2), calls=%async_computation | async-start | bytes 1048576 | tf_op jit(solution)/shard_map/all_to_all | solution.py:82
  13.0 1.2 dynamic_slice.3
  14.3 0.7 pad_add_fusion.meta_ref
  15.0 8.5 %all-to-all-done.in_ref = bf16[16,64,192]{2,1,0:T(8,128)(2,1)S(1)} async-done(((bf16[16,64,192]{2,1,0:T(8,128)(2,1)}), bf16[16,64,192]{2,1,0:T(8,128)(2,1)S(1)}, u32[]{:S(2)}, u32[]{:S(2)}) %all-to-all-start) | async-done | bytes 393248 | tf_op jit(solution)/shard_map/all_to_all | solution.py:82
  23.5 0.9 sum_spread.2
  24.4 3.6 %all-to-all-start.1 = ((bf16[16,64,192]{2,1,0:T(8,128)(2,1)}), bf16[16,64,192]{2,1,0:T(8,128)(2,1)S(1)}, u32[]{:S(2)}, u32[]{:S(2)}) async-start(bf16[16,64,192]{2,1,0:T(8,128)(2,1)} %sum_spread.2), calls=%async_computation.1 | async-start | bytes 1048576 | tf_op jit(solution)/shard_map/all_to_all | solution.py:91
  28.0 0.0 copy-start.2
  28.0 0.0 copy-start.3
  28.0 1.6 %decay_tables.1 = (f32[8,1024]{1,0:T(8,128)S(1)}, f32[1024,128]{1,0:T(8,128)S(1)}, f32[16,128]{1,0:T(8,128)S(1)}) custom-call(s32[3]{0:T(128)S(1)} %pad_add_fusion.meta_ref, bf16[4,1024]{1,0:T(4,128)(2,1)S(1)} %copy-done.4, s32[1,1024]{1,0:T(1,128)S(1)} %bitcast.11), custom_call_target="tpu_custom_call" | custom-call | flops 4000000000 | bytes 1000000 | tf_op jit(solution)/shard_map/decay_tables/pallas_call | solution.py:145
  29.7 8.0 %all-to-all-done.1 = bf16[16,64,192]{2,1,0:T(8,128)(2,1)S(1)} async-done(((bf16[16,64,192]{2,1,0:T(8,128)(2,1)}), bf16[16,64,192]{2,1,0:T(8,128)(2,1)S(1)}, u32[]{:S(2)}, u32[]{:S(2)}) %all-to-all-start.1) | async-done | bytes 393248 | tf_op jit(solution)/shard_map/all_to_all | solution.py:91
  37.6 6.5 %project.1 = (bf16[4,1024,512]{2,1,0:T(8,128)(2,1)}, bf16[4,4,128,128]{3,2,1,0:T(8,128)(2,1)S(1)}, bf16[4,4,128,128]{3,2,1,0:T(8,128)(2,1)S(1)}, bf16[1088,128]{1,0:T(8,128)(2,1)S(1)}) custom-call(s32[3]{0:T(128)S(1)} %pad_add_fusion.meta_ref, bf16[3,1024,512]{2,1,0:T(8,128)(2,1)} %frozen_ref.1, bf16[1024,192]{1,0:T(8,128)(2,1)S(1)} %bitcast.8, ...), custom_call_target="tpu_custom_call" | custom-call | flops 4000000000 | bytes 10000000 | tf_op jit(solution)/shard_map/project/pallas_call | solution.py:230
  44.1 2.8 %collective-permute-start = (bf16[1088,128]{1,0:T(8,128)(2,1)S(1)}, bf16[1088,128]{1,0:T(8,128)(2,1)S(1)}, u32[]{:S(2)}, u32[]{:S(2)}) collective-permute-start(bf16[1088,128]{1,0:T(8,128)(2,1)S(1)} %get-tuple-element.24.own_ref), channel_id=1, source_target_pairs={{0,16},{16,0},{32,48},{48,32},{64,80},{80,64},{96,112},{112,96},{1... | collective-permute-start | bytes 835592 | tf_op jit(solution)/shard_map/ppermute | solution.py:527
  47.0 1.2 collective-permute-done.mate_ref
  48.1 0.7 join.1
  48.8 1.4 %collective-permute-start.1 = (bf16[576,128]{1,0:T(8,128)(2,1)S(1)}, bf16[576,128]{1,0:T(8,128)(2,1)S(1)}, u32[]{:S(2)}, u32[]{:S(2)}) collective-permute-start(bf16[576,128]{1,0:T(8,128)(2,1)S(1)} %get-tuple-element.25), channel_id=1, source_target_pairs={{0,32},{16,48},{32,64},{48,80},{64,96},{80,112},{96,0},{112,16},{1... | collective-permute-start | bytes 442376 | tf_op jit(solution)/shard_map/ppermute | solution.py:532
  50.2 2.6 %collective-permute-start.2 = (bf16[576,128]{1,0:T(8,128)(2,1)S(1)}, bf16[576,128]{1,0:T(8,128)(2,1)S(1)}, u32[]{:S(2)}, u32[]{:S(2)}) collective-permute-start(bf16[576,128]{1,0:T(8,128)(2,1)S(1)} %get-tuple-element.26), channel_id=1, source_target_pairs={{0,64},{16,80},{32,96},{48,112},{64,0},{80,16},{96,32},{112,48},{1... | collective-permute-start | bytes 442376 | tf_op jit(solution)/shard_map/ppermute | solution.py:532
  52.8 1.1 collective-permute-start.3
  53.9 2.2 %copy-done.6 = bf16[4,1024,512]{2,1,0:T(8,128)(2,1)S(1)} copy-done((bf16[4,1024,512]{2,1,0:T(8,128)(2,1)S(1)}, bf16[4,1024,512]{2,1,0:T(8,128)(2,1)}, u32[]{:S(2)}) %copy-start.6) | copy-done | bytes 4194328
  56.1 7.7 %inside.1.part_ref = f32[4,1024,512]{2,1,0:T(8,128)} custom-call(bf16[4,1024,512]{2,1,0:T(8,128)(2,1)S(1)} %copy-done.6, f32[8,1024]{1,0:T(8,128)S(1)} %get-tuple-element.21.row_ref, f32[1024,128]{1,0:T(8,128)S(1)} %get-tuple-element.18.col_ref, bf16[4,4,128,128]{3,2,1,0:T(8,128)(2,1)S(1)} %get-tuple-element.22.before_ref, ...), custom_call_target="tpu_custom_call" | custom-call | flops 14000000000 | bytes 14000000 | tf_op jit(solution)/shard_map/inside/pallas_call | solution.py:350
  63.8 0.0 collective-permute-done.1.refs_0_
  63.8 0.0 collective-permute-done.2.refs_1_
  63.8 8.7 %finish.1 = (bf16[1024,512]{1,0:T(8,128)(2,1)}, bf16[3,1024,512]{2,1,0:T(8,128)(2,1)}, bf16[1024,192]{1,0:T(8,128)(2,1)S(1)}, bf16[3,64,512]{2,1,0:T(8,128)(2,1)S(1)}) custom-call(s32[3]{0:T(128)S(1)} %pad_add_fusion.meta_ref, bf16[4,1024,512]{2,1,0:T(8,128)(2,1)} %get-tuple-element.20.moving_ref, f32[4,1024,512]{2,1,0:T(8,128)} %inside.1.part_ref, ...), custom_call_target="tpu_custom_call" | custom-call | flops 4000000000 | bytes 18000000 | tf_op jit(solution)/shard_map/finish/pallas_call | solution.py:435
  72.5 12.9 %all_to_all.20.in_ref = bf16[16,64,192]{2,1,0:T(8,128)(2,1)S(1)} all-to-all(bf16[16,64,192]{2,1,0:T(8,128)(2,1)S(1)} %bitcast.10), channel_id=1, replica_groups=mesh['seq'=8,'head'=16] {'head'}, dimensions={0} | all-to-all | bytes 786432 | tf_op jit(solution)/shard_map/all_to_all | solution.py:82
  85.4 0.9 sum_spread.3
  86.3 3.6 %all-to-all-start.3 = ((bf16[16,64,192]{2,1,0:T(8,128)(2,1)}), bf16[16,64,192]{2,1,0:T(8,128)(2,1)S(1)}, u32[]{:S(2)}, u32[]{:S(2)}) async-start(bf16[16,64,192]{2,1,0:T(8,128)(2,1)} %sum_spread.3), calls=%async_computation.3 | async-start | bytes 1048576 | tf_op jit(solution)/shard_map/all_to_all | solution.py:91
  89.9 2.4 %collective-permute-start.8 = (bf16[3,64,512]{2,1,0:T(8,128)(2,1)S(1)}, bf16[3,64,512]{2,1,0:T(8,128)(2,1)S(1)}, u32[]{:S(2)}, u32[]{:S(2)}) collective-permute-start(bf16[3,64,512]{2,1,0:T(8,128)(2,1)S(1)} %get-tuple-element.31.refs_0_), channel_id=1, source_target_pairs={{0,16},{16,0},{32,48},{48,32},{64,80},{80,64},{96,112},{112,96},{1... | collective-permute-start | bytes 589832 | tf_op jit(solution)/shard_map/ppermute | solution.py:527
  92.3 1.1 collective-permute-done.8.refs_1_
  93.4 0.1 collective-permute-start.11
  93.5 5.6 %all-to-all-done.3 = bf16[16,64,192]{2,1,0:T(8,128)(2,1)S(1)} async-done(((bf16[16,64,192]{2,1,0:T(8,128)(2,1)}), bf16[16,64,192]{2,1,0:T(8,128)(2,1)S(1)}, u32[]{:S(2)}, u32[]{:S(2)}) %all-to-all-start.3) | async-done | bytes 393248 | tf_op jit(solution)/shard_map/all_to_all | solution.py:91
  99.2 0.4 partial_down.1.refs_0_
  99.6 3.2 %collective-permute-start.4 = (bf16[384,192]{1,0:T(8,128)(2,1)S(1)}, bf16[384,192]{1,0:T(8,128)(2,1)S(1)}, u32[]{:S(2)}, u32[]{:S(2)}) collective-permute-start(bf16[384,192]{1,0:T(8,128)(2,1)S(1)} %partial_down.1.refs_0_), channel_id=1, source_target_pairs={{0,16},{16,0},{32,48},{48,32},{64,80},{80,64},{96,112},{112,96},{1... | collective-permute-start | bytes 442376 | tf_op jit(solution)/shard_map/ppermute | solution.py:527
  102.8 0.4 collective-permute-start.10
  103.3 0.5 collective-permute-start.9
  103.7 0.1 collective-permute-done.4.refs_1_
  103.9 2.1 %collective-permute-start.7 = (bf16[384,192]{1,0:T(8,128)(2,1)S(1)}, bf16[384,192]{1,0:T(8,128)(2,1)S(1)}, u32[]{:S(2)}, u32[]{:S(2)}) collective-permute-start(bf16[384,192]{1,0:T(8,128)(2,1)S(1)} %add_all.3.refs_0_), channel_id=1, source_target_pairs={{0,96},{16,112},{32,0},{48,16},{64,32},{80,48},{96,64},{112,80},{1... | collective-permute-start | bytes 442376 | tf_op jit(solution)/shard_map/ppermute | solution.py:532
  106.1 1.3 %collective-permute-start.6 = (bf16[384,192]{1,0:T(8,128)(2,1)S(1)}, bf16[384,192]{1,0:T(8,128)(2,1)S(1)}, u32[]{:S(2)}, u32[]{:S(2)}) collective-permute-start(bf16[384,192]{1,0:T(8,128)(2,1)S(1)} %add_all.3.refs_0_), channel_id=1, source_target_pairs={{0,64},{16,80},{32,96},{48,112},{64,0},{80,16},{96,32},{112,48},{1... | collective-permute-start | bytes 442376 | tf_op jit(solution)/shard_map/ppermute | solution.py:532
  107.4 0.4 collective-permute-start.5
  107.8 3.0 %collective-permute-done.10.refs_2_ = bf16[3,64,512]{2,1,0:T(8,128)(2,1)S(1)} collective-permute-done((bf16[3,64,512]{2,1,0:T(8,128)(2,1)S(1)}, bf16[3,64,512]{2,1,0:T(8,128)(2,1)S(1)}, u32[]{:S(2)}, u32[]{:S(2)}) %collective-permute-start.10) | collective-permute-done | bytes 196640 | tf_op jit(solution)/shard_map/ppermute | solution.py:532
  110.8 4.9 %collective-permute-done.9.refs_1_ = bf16[3,64,512]{2,1,0:T(8,128)(2,1)S(1)} collective-permute-done((bf16[3,64,512]{2,1,0:T(8,128)(2,1)S(1)}, bf16[3,64,512]{2,1,0:T(8,128)(2,1)S(1)}, u32[]{:S(2)}, u32[]{:S(2)}) %collective-permute-start.9) | collective-permute-done | bytes 196640 | tf_op jit(solution)/shard_map/ppermute | solution.py:532
  115.8 0.8 add_all.5
  116.6 2.7 %collective-permute-done.6.refs_2_ = bf16[384,192]{1,0:T(8,128)(2,1)S(1)} collective-permute-done((bf16[384,192]{1,0:T(8,128)(2,1)S(1)}, bf16[384,192]{1,0:T(8,128)(2,1)S(1)}, u32[]{:S(2)}, u32[]{:S(2)}) %collective-permute-start.6) | collective-permute-done | bytes 147488 | tf_op jit(solution)/shard_map/ppermute | solution.py:532
  119.3 4.5 %collective-permute-done.5.refs_1_ = bf16[384,192]{1,0:T(8,128)(2,1)S(1)} collective-permute-done((bf16[384,192]{1,0:T(8,128)(2,1)S(1)}, bf16[384,192]{1,0:T(8,128)(2,1)S(1)}, u32[]{:S(2)}, u32[]{:S(2)}) %collective-permute-start.5) | collective-permute-done | bytes 147488 | tf_op jit(solution)/shard_map/ppermute | solution.py:532
  123.8 0.2 add_split.1
  124.0 0.9 copy.13
  (14 shorter events, 0.1 us)
Async XLA Ops:
  0.6 27.4 %copy-start.5 = (s32[1024]{0:T(1024)S(1)}, s32[1024]{0:T(1024)}, u32[]{:S(2)}) copy-start(s32[1024]{0:T(1024)} %param.14) | copy-start | bytes 12292
  0.6 27.4 %copy-start.4 = (bf16[4,1024]{1,0:T(4,128)(2,1)S(1)}, bf16[4,1024]{1,0:T(4,128)(2,1)}, u32[]{:S(2)}) copy-start(bf16[4,1024]{1,0:T(4,128)(2,1)} %decay_ref.1) | copy-start | bytes 24580
  1.8 1.1 copy-start
  4.6 18.9 %all-to-all-start = ((bf16[16,64,192]{2,1,0:T(8,128)(2,1)}), bf16[16,64,192]{2,1,0:T(8,128)(2,1)S(1)}, u32[]{:S(2)}, u32[]{:S(2)}) async-start(bf16[16,64,192]{2,1,0:T(8,128)(2,1)} %bitcast.2), calls=%async_computation | async-start | bytes 1048576 | tf_op jit(solution)/shard_map/all_to_all | solution.py:82
  24.4 13.2 %all-to-all-start.1 = ((bf16[16,64,192]{2,1,0:T(8,128)(2,1)}), bf16[16,64,192]{2,1,0:T(8,128)(2,1)S(1)}, u32[]{:S(2)}, u32[]{:S(2)}) async-start(bf16[16,64,192]{2,1,0:T(8,128)(2,1)} %sum_spread.2), calls=%async_computation.1 | async-start | bytes 1048576 | tf_op jit(solution)/shard_map/all_to_all | solution.py:91
  28.0 9.6 %copy-start.2 = (bf16[1024,512]{1,0:T(8,128)(2,1)S(1)}, bf16[1024,512]{1,0:T(8,128)(2,1)}, u32[]{:S(2)}) copy-start(bf16[1024,512]{1,0:T(8,128)(2,1)} %grad_ref.1) | copy-start | bytes 3145732
  28.0 9.6 %copy-start.3 = (bf16[3,64,512]{2,1,0:T(8,128)(2,1)S(1)}, bf16[3,64,512]{2,1,0:T(8,128)(2,1)}, u32[]{:S(2)}) copy-start(bf16[3,64,512]{2,1,0:T(8,128)(2,1)} %up_ref.3) | copy-start | bytes 589828
  44.1 4.0 %collective-permute-start = (bf16[1088,128]{1,0:T(8,128)(2,1)S(1)}, bf16[1088,128]{1,0:T(8,128)(2,1)S(1)}, u32[]{:S(2)}, u32[]{:S(2)}) collective-permute-start(bf16[1088,128]{1,0:T(8,128)(2,1)S(1)} %get-tuple-element.24.own_ref), channel_id=1, source_target_pairs={{0,16},{16,0},{32,48},{48,32},{64,80},{80,64},{96,112},{112,96},{1... | collective-permute-start | bytes 835592 | tf_op jit(solution)/shard_map/ppermute | solution.py:527
  48.8 15.0 %collective-permute-start.1 = (bf16[576,128]{1,0:T(8,128)(2,1)S(1)}, bf16[576,128]{1,0:T(8,128)(2,1)S(1)}, u32[]{:S(2)}, u32[]{:S(2)}) collective-permute-start(bf16[576,128]{1,0:T(8,128)(2,1)S(1)} %get-tuple-element.25), channel_id=1, source_target_pairs={{0,32},{16,48},{32,64},{48,80},{64,96},{80,112},{96,0},{112,16},{1... | collective-permute-start | bytes 442376 | tf_op jit(solution)/shard_map/ppermute | solution.py:532
  50.2 13.6 %collective-permute-start.2 = (bf16[576,128]{1,0:T(8,128)(2,1)S(1)}, bf16[576,128]{1,0:T(8,128)(2,1)S(1)}, u32[]{:S(2)}, u32[]{:S(2)}) collective-permute-start(bf16[576,128]{1,0:T(8,128)(2,1)S(1)} %get-tuple-element.26), channel_id=1, source_target_pairs={{0,64},{16,80},{32,96},{48,112},{64,0},{80,16},{96,32},{112,48},{1... | collective-permute-start | bytes 442376 | tf_op jit(solution)/shard_map/ppermute | solution.py:532
  52.8 11.0 %collective-permute-start.3 = (bf16[576,128]{1,0:T(8,128)(2,1)S(1)}, bf16[576,128]{1,0:T(8,128)(2,1)S(1)}, u32[]{:S(2)}, u32[]{:S(2)}) collective-permute-start(bf16[576,128]{1,0:T(8,128)(2,1)S(1)} %get-tuple-element.27), channel_id=1, source_target_pairs={{0,96},{16,112},{32,0},{48,16},{64,32},{80,48},{96,64},{112,80},{1... | collective-permute-start | bytes 442376 | tf_op jit(solution)/shard_map/ppermute | solution.py:532
  53.9 2.2 %copy-start.6 = (bf16[4,1024,512]{2,1,0:T(8,128)(2,1)S(1)}, bf16[4,1024,512]{2,1,0:T(8,128)(2,1)}, u32[]{:S(2)}) copy-start(bf16[4,1024,512]{2,1,0:T(8,128)(2,1)} %get-tuple-element.20.moving_ref) | copy-start | bytes 12582916
  72.5 26.6 %copy-start.1 = (bf16[1024,384]{1,0:T(8,128)(2,1)S(1)}, bf16[1024,384]{1,0:T(8,128)(2,1)}, u32[]{:S(2)}) copy-start(bf16[1024,384]{1,0:T(8,128)(2,1)} %x_ref.3) | copy-start | bytes 2359300
  86.3 12.9 %all-to-all-start.3 = ((bf16[16,64,192]{2,1,0:T(8,128)(2,1)}), bf16[16,64,192]{2,1,0:T(8,128)(2,1)S(1)}, u32[]{:S(2)}, u32[]{:S(2)}) async-start(bf16[16,64,192]{2,1,0:T(8,128)(2,1)} %sum_spread.3), calls=%async_computation.3 | async-start | bytes 1048576 | tf_op jit(solution)/shard_map/all_to_all | solution.py:91
  89.9 3.5 %collective-permute-start.8 = (bf16[3,64,512]{2,1,0:T(8,128)(2,1)S(1)}, bf16[3,64,512]{2,1,0:T(8,128)(2,1)S(1)}, u32[]{:S(2)}, u32[]{:S(2)}) collective-permute-start(bf16[3,64,512]{2,1,0:T(8,128)(2,1)S(1)} %get-tuple-element.31.refs_0_), channel_id=1, source_target_pairs={{0,16},{16,0},{32,48},{48,32},{64,80},{80,64},{96,112},{112,96},{1... | collective-permute-start | bytes 589832 | tf_op jit(solution)/shard_map/ppermute | solution.py:527
  93.4 14.0 %collective-permute-start.11 = (bf16[3,64,512]{2,1,0:T(8,128)(2,1)S(1)}, bf16[3,64,512]{2,1,0:T(8,128)(2,1)S(1)}, u32[]{:S(2)}, u32[]{:S(2)}) collective-permute-start(bf16[3,64,512]{2,1,0:T(8,128)(2,1)S(1)} %add_all.4.refs_0_), channel_id=1, source_target_pairs={{0,96},{16,112},{32,0},{48,16},{64,32},{80,48},{96,64},{112,80},{1... | collective-permute-start | bytes 589832 | tf_op jit(solution)/shard_map/ppermute | solution.py:532
  99.6 4.3 %collective-permute-start.4 = (bf16[384,192]{1,0:T(8,128)(2,1)S(1)}, bf16[384,192]{1,0:T(8,128)(2,1)S(1)}, u32[]{:S(2)}, u32[]{:S(2)}) collective-permute-start(bf16[384,192]{1,0:T(8,128)(2,1)S(1)} %partial_down.1.refs_0_), channel_id=1, source_target_pairs={{0,16},{16,0},{32,48},{48,32},{64,80},{80,64},{96,112},{112,96},{1... | collective-permute-start | bytes 442376 | tf_op jit(solution)/shard_map/ppermute | solution.py:527
  102.8 8.0 %collective-permute-start.10 = (bf16[3,64,512]{2,1,0:T(8,128)(2,1)S(1)}, bf16[3,64,512]{2,1,0:T(8,128)(2,1)S(1)}, u32[]{:S(2)}, u32[]{:S(2)}) collective-permute-start(bf16[3,64,512]{2,1,0:T(8,128)(2,1)S(1)} %add_all.4.refs_0_), channel_id=1, source_target_pairs={{0,64},{16,80},{32,96},{48,112},{64,0},{80,16},{96,32},{112,48},{1... | collective-permute-start | bytes 589832 | tf_op jit(solution)/shard_map/ppermute | solution.py:532
  103.3 12.5 %collective-permute-start.9 = (bf16[3,64,512]{2,1,0:T(8,128)(2,1)S(1)}, bf16[3,64,512]{2,1,0:T(8,128)(2,1)S(1)}, u32[]{:S(2)}, u32[]{:S(2)}) collective-permute-start(bf16[3,64,512]{2,1,0:T(8,128)(2,1)S(1)} %add_all.4.refs_0_), channel_id=1, source_target_pairs={{0,32},{16,48},{32,64},{48,80},{64,96},{80,112},{96,0},{112,16},{1... | collective-permute-start | bytes 589832 | tf_op jit(solution)/shard_map/ppermute | solution.py:532
  103.9 12.6 %collective-permute-start.7 = (bf16[384,192]{1,0:T(8,128)(2,1)S(1)}, bf16[384,192]{1,0:T(8,128)(2,1)S(1)}, u32[]{:S(2)}, u32[]{:S(2)}) collective-permute-start(bf16[384,192]{1,0:T(8,128)(2,1)S(1)} %add_all.3.refs_0_), channel_id=1, source_target_pairs={{0,96},{16,112},{32,0},{48,16},{64,32},{80,48},{96,64},{112,80},{1... | collective-permute-start | bytes 442376 | tf_op jit(solution)/shard_map/ppermute | solution.py:532
  106.1 13.2 %collective-permute-start.6 = (bf16[384,192]{1,0:T(8,128)(2,1)S(1)}, bf16[384,192]{1,0:T(8,128)(2,1)S(1)}, u32[]{:S(2)}, u32[]{:S(2)}) collective-permute-start(bf16[384,192]{1,0:T(8,128)(2,1)S(1)} %add_all.3.refs_0_), channel_id=1, source_target_pairs={{0,64},{16,80},{32,96},{48,112},{64,0},{80,16},{96,32},{112,48},{1... | collective-permute-start | bytes 442376 | tf_op jit(solution)/shard_map/ppermute | solution.py:532
  107.4 16.4 %collective-permute-start.5 = (bf16[384,192]{1,0:T(8,128)(2,1)S(1)}, bf16[384,192]{1,0:T(8,128)(2,1)S(1)}, u32[]{:S(2)}, u32[]{:S(2)}) collective-permute-start(bf16[384,192]{1,0:T(8,128)(2,1)S(1)} %add_all.3.refs_0_), channel_id=1, source_target_pairs={{0,32},{16,48},{32,64},{48,80},{64,96},{80,112},{96,0},{112,16},{1... | collective-permute-start | bytes 442376 | tf_op jit(solution)/shard_map/ppermute | solution.py:532

commit v2 on v1

--- a/solution.py
+++ b/solution.py
@@ -10,7 +10,7 @@
 F32 = jnp.float32
 BF16 = jnp.bfloat16
 CHUNK = 256
-VMEM_BYTES = 48 * 1024 * 1024
+VMEM_BYTES = 20 * 1024 * 1024
 NEGATIVE = -1e30
 
 CUM, SEG, ENTER, LEAVE, ENTER_ALL, LEAVE_ALL = 0, 4, 8, 12, 16, 20
@@ -41,15 +41,15 @@
 
 
 def low_kernel(x_ref, down_ref, out_ref):
-    rank = down_ref.shape[2]
+    rank = down_ref.shape[1]
     x = x_ref[...]
     for c in range(3):
-        out_ref[:, c * rank : (c + 1) * rank] = dot_nn(x, down_ref[c]).astype(BF16)
+        out_ref[:, c * rank : (c + 1) * rank] = dot_nt(x, down_ref[c]).astype(BF16)
 
 
 def partial_low(x, down):
     rows, width = x.shape
-    rank = down.shape[2]
+    rank = down.shape[1]
     block = min(512, rows)
     return pl.pallas_call(
         low_kernel,
@@ -75,12 +75,15 @@
         out_ref[i] = total
 
 
-def sum_over_head(part):
+def to_pieces(part):
     count = lax.axis_size("head")
     rows, width = part.shape
-    pieces = part.reshape(count, rows // count, width)
-    pieces = lax.all_to_all(pieces, "head", 0, 0)
-    spread = pl.pallas_call(
+    return lax.all_to_all(part.reshape(count, rows // count, width), "head", 0, 0)
+
+
+def sum_spread(pieces):
+    count, rows, width = pieces.shape
+    return pl.pallas_call(
         sum_spread_kernel,
         out_shape=jax.ShapeDtypeStruct(pieces.shape, BF16),
         in_specs=[VMEM],
@@ -88,7 +91,6 @@
         compiler_params=params(),
         name="sum_spread",
     )(pieces)
-    return lax.all_to_all(spread, "head", 0, 0).reshape(rows, width)
 
 
 def decay_kernel(meta_ref, decay_ref, start_ref, row_ref, col_ref, pass_ref):
@@ -322,7 +324,7 @@
     row_i = lax.broadcasted_iota(jnp.int32, (CHUNK, CHUNK), 0)
     col_i = lax.broadcasted_iota(jnp.int32, (CHUNK, CHUNK), 1)
     col = col_ref[...]
-    allowed = (row_i >= col_i) & (col[:, SEG : SEG + 1] == row_ref[SEG : SEG + 1, :])
+    allowed = (row_i <= col_i) & (col[:, SEG : SEG + 1] == row_ref[SEG : SEG + 1, :])
     shut = jnp.where(allowed, 0.0, NEGATIVE)
     for h in range(heads):
         span = slice(h * 128, (h + 1) * 128)
@@ -330,17 +332,16 @@
         k = moving_ref[1, :, span]
         v = moving_ref[2, :, span]
         g = moving_ref[3, :, span]
-        weights = jnp.exp((col[:, h : h + 1] - row_ref[h : h + 1, :]) + shut)
-        a = (dot_nt(q, k) * weights).astype(BF16)
-        b = (dot_nt(g, v) * weights).astype(BF16)
+        weights = jnp.exp((row_ref[h : h + 1, :] - col[:, h : h + 1]) + shut)
+        a = (dot_nt(k, q) * weights).astype(BF16)
+        b = (dot_nt(v, g) * weights).astype(BF16)
         enter = col[:, ENTER + h : ENTER + h + 1]
         leave = col[:, LEAVE + h : LEAVE + h + 1]
         before = before_ref[0, h]
         after = after_ref[0, h]
-        part_ref[0, :, span] = dot_nn(a, v) + enter * dot_nn(q, before)
-        part_ref[1, :, span] = dot_nn(b, k) + enter * dot_nt(g, before)
-        part_ref[2, :, span] = dot_tn(b, q) + leave * dot_nt(v, after)
-        part_ref[3, :, span] = dot_tn(a, g) + leave * dot_nn(k, after)
+        part_ref[0, :, span] = dot_tn(b, k) + enter * dot_nt(g, before)
+        part_ref[1, :, span] = dot_nn(b, q) + leave * dot_nt(v, after)
+        part_ref[2, :, span] = dot_nn(a, g) + leave * dot_nn(k, after)
 
 
 def inside(moving, row, col, before, after):
@@ -349,7 +350,7 @@
     count = rows // CHUNK
     return pl.pallas_call(
         inside_kernel,
-        out_shape=jax.ShapeDtypeStruct((4, rows, features), F32),
+        out_shape=jax.ShapeDtypeStruct((3, rows, features), F32),
         grid=(count,),
         in_specs=[
             pl.BlockSpec((4, CHUNK, features), lambda i: (0, i, 0)),
@@ -358,18 +359,86 @@
             pl.BlockSpec((1, heads, 128, 128), lambda i: (i, 0, 0, 0)),
             pl.BlockSpec((1, heads, 128, 128), lambda i: (i, 0, 0, 0)),
         ],
-        out_specs=pl.BlockSpec((4, CHUNK, features), lambda i: (0, i, 0)),
+        out_specs=pl.BlockSpec((3, CHUNK, features), lambda i: (0, i, 0)),
         compiler_params=params(dimension_semantics=("arbitrary",)),
-        cost_estimate=cost(14e9, 14e6),
+        cost_estimate=cost(12e9, 12e6),
         name="inside",
     )(moving, row, col, before, after)
 
 
-def finish_kernel(chips, meta_ref, moving_ref, part_ref, col_ref, low_ref, up_ref, mate_ref, *refs):
-    message_refs = refs[: chips - 1]
-    attn_ref, grad_ref, low_grad_ref, up_grad_ref, state_in, back_in, up_sum = refs[chips - 1 :]
+def late_kernel(
+    moving_ref, row_ref, col_ref, before_ref, state_ref, low_ref, grad_ref, attn_ref, up_grad_ref, up_sum
+):
     step = pl.program_id(0)
     count = pl.num_programs(0)
+    features = moving_ref.shape[2]
+    heads = features // 128
+    rank = up_sum.shape[1]
+    inverse = 1.0 / 128.0
+
+    @pl.when(step == 0)
+    def _():
+        up_sum[...] = jnp.zeros_like(up_sum)
+
+    row_i = lax.broadcasted_iota(jnp.int32, (CHUNK, CHUNK), 0)
+    col_i = lax.broadcasted_iota(jnp.int32, (CHUNK, CHUNK), 1)
+    col = col_ref[...]
+    allowed = (row_i >= col_i) & (col[:, SEG : SEG + 1] == row_ref[SEG : SEG + 1, :])
+    shut = jnp.where(allowed, 0.0, NEGATIVE)
+    for h in range(heads):
+        span = slice(h * 128, (h + 1) * 128)
+        q = moving_ref[0, :, span]
+        weights = jnp.exp((col[:, h : h + 1] - row_ref[h : h + 1, :]) + shut)
+        a = (dot_nt(q, moving_ref[1, :, span]) * weights).astype(BF16)
+        enter = col[:, ENTER + h : ENTER + h + 1]
+        enter_all = col[:, ENTER_ALL + h : ENTER_ALL + h + 1]
+        out = dot_nn(a, moving_ref[2, :, span])
+        out = out + enter * dot_nn(q, before_ref[0, h]) + enter_all * dot_nn(q, state_ref[h])
+        attn_ref[:, span] = (out * inverse).astype(BF16)
+    low = low_ref[...]
+    for c in range(3):
+        up_sum[c] += dot_tn(low[:, c * rank : (c + 1) * rank], grad_ref[c])
+
+    @pl.when(step == count - 1)
+    def _():
+        up_grad_ref[...] = up_sum[...].astype(BF16)
+
+
+def late(moving, row, col, before, state, low, grads, up_shape):
+    _, rows, features = moving.shape
+    heads = features // 128
+    count = rows // CHUNK
+    return pl.pallas_call(
+        late_kernel,
+        out_shape=(
+            jax.ShapeDtypeStruct((rows, features), BF16),
+            jax.ShapeDtypeStruct(up_shape, BF16),
+        ),
+        grid=(count,),
+        in_specs=[
+            pl.BlockSpec((3, CHUNK, features), lambda i: (0, i, 0)),
+            pl.BlockSpec((8, CHUNK), lambda i: (0, i)),
+            pl.BlockSpec((CHUNK, 128), lambda i: (i, 0)),
+            pl.BlockSpec((1, heads, 128, 128), lambda i: (i, 0, 0, 0)),
+            pl.BlockSpec(state.shape, lambda i: (0, 0, 0)),
+            pl.BlockSpec((CHUNK, low.shape[1]), lambda i: (i, 0)),
+            pl.BlockSpec((3, CHUNK, features), lambda i: (0, i, 0)),
+        ],
+        out_specs=(
+            pl.BlockSpec((CHUNK, features), lambda i: (i, 0)),
+            pl.BlockSpec(up_shape, lambda i: (0, 0, 0)),
+        ),
+        scratch_shapes=[pltpu.VMEM(up_shape, F32)],
+        compiler_params=params(dimension_semantics=("arbitrary",)),
+        cost_estimate=cost(6e9, 10e6),
+        name="late",
+    )(moving, row, col, before, state, low, grads)
+
+
+def finish_kernel(chips, meta_ref, moving_ref, part_ref, col_ref, up_ref, mate_ref, *refs):
+    message_refs = refs[: chips - 1]
+    grad_ref, low_grad_ref, state_in, back_in = refs[chips - 1 :]
+    step = pl.program_id(0)
     features = moving_ref.shape[2]
     heads = features // 128
     size = heads * 128
@@ -380,7 +449,6 @@
     def _():
         y = meta_ref[1]
         second = meta_ref[2] == 1
-        up_sum[...] = jnp.zeros_like(up_sum)
         for h in range(heads):
             rows = slice(h * 128, (h + 1) * 128)
             factor = jnp.ones((1, 128), F32)
@@ -404,7 +472,6 @@
     col = col_ref[...]
     for h in range(heads):
         span = slice(h * 128, (h + 1) * 128)
-        q = moving_ref[0, :, span]
         k = moving_ref[1, :, span]
         v = moving_ref[2, :, span]
         g = moving_ref[3, :, span]
@@ -412,70 +479,57 @@
         leave = col[:, LEAVE_ALL + h : LEAVE_ALL + h + 1]
         state = state_in[h]
         back = back_in[h]
-        attn_ref[:, span] = ((part_ref[0, :, span] + enter * dot_nn(q, state)) * inverse).astype(BF16)
-        grad_ref[0, :, span] = ((part_ref[1, :, span] + enter * dot_nt(g, state)) * inverse).astype(BF16)
-        grad_ref[1, :, span] = ((part_ref[2, :, span] + leave * dot_nt(v, back)) * inverse).astype(BF16)
-        grad_ref[2, :, span] = ((part_ref[3, :, span] + leave * dot_nn(k, back)) * inverse).astype(BF16)
-    low = low_ref[...]
+        grad_ref[0, :, span] = ((part_ref[0, :, span] + enter * dot_nt(g, state)) * inverse).astype(BF16)
+        grad_ref[1, :, span] = ((part_ref[1, :, span] + leave * dot_nt(v, back)) * inverse).astype(BF16)
+        grad_ref[2, :, span] = ((part_ref[2, :, span] + leave * dot_nn(k, back)) * inverse).astype(BF16)
     for c in range(3):
         lanes = slice(c * rank, (c + 1) * rank)
         low_grad_ref[:, lanes] = dot_nt(grad_ref[c], up_ref[c]).astype(BF16)
-        up_sum[c] += dot_tn(low[:, lanes], grad_ref[c])
-
-    @pl.when(step == count - 1)
-    def _():
-        up_grad_ref[...] = up_sum[...].astype(BF16)
-
-
-def finish(meta, moving, part, col, low, up, mate, messages):
+
+
+def finish(meta, moving, part, col, up, mate, messages):
     _, rows, features = moving.shape
     heads = features // 128
     count = rows // CHUNK
     chips = len(messages) + 1
+    width = up.shape[0] * up.shape[1]
     return pl.pallas_call(
         functools.partial(finish_kernel, chips),
         out_shape=(
-            jax.ShapeDtypeStruct((rows, features), BF16),
             jax.ShapeDtypeStruct((3, rows, features), BF16),
-            jax.ShapeDtypeStruct(low.shape, BF16),
-            jax.ShapeDtypeStruct(up.shape, BF16),
+            jax.ShapeDtypeStruct((rows, width), BF16),
+            jax.ShapeDtypeStruct((heads, 128, 128), BF16),
         ),
         grid=(count,),
         in_specs=[
             SMEM,
             pl.BlockSpec((4, CHUNK, features), lambda i: (0, i, 0)),
-            pl.BlockSpec((4, CHUNK, features), lambda i: (0, i, 0)),
+            pl.BlockSpec((3, CHUNK, features), lambda i: (0, i, 0)),
             pl.BlockSpec((CHUNK, 128), lambda i: (i, 0)),
-            pl.BlockSpec((CHUNK, low.shape[1]), lambda i: (i, 0)),
             pl.BlockSpec(up.shape, lambda i: (0, 0, 0)),
             pl.BlockSpec(mate.shape, lambda i: (0, 0)),
         ]
         + [pl.BlockSpec(m.shape, lambda i: (0, 0)) for m in messages],
         out_specs=(
-            pl.BlockSpec((CHUNK, features), lambda i: (i, 0)),
             pl.BlockSpec((3, CHUNK, features), lambda i: (0, i, 0)),
-            pl.BlockSpec((CHUNK, low.shape[1]), lambda i: (i, 0)),
-            pl.BlockSpec(up.shape, lambda i: (0, 0, 0)),
+            pl.BlockSpec((CHUNK, width), lambda i: (i, 0)),
+            pl.BlockSpec((heads, 128, 128), lambda i: (0, 0, 0)),
         ),
-        scratch_shapes=[
-            pltpu.VMEM((heads, 128, 128), BF16),
-            pltpu.VMEM((heads, 128, 128), BF16),
-            pltpu.VMEM(up.shape, F32),
-        ],
+        scratch_shapes=[pltpu.VMEM((heads, 128, 128), BF16)],
         compiler_params=params(dimension_semantics=("arbitrary",)),
-        cost_estimate=cost(4e9, 18e6),
+        cost_estimate=cost(4e9, 14e6),
         name="finish",
-    )(meta, moving, part, col, low, up, mate, *messages)
+    )(meta, moving, part, col, up, mate, *messages)
 
 
 def down_kernel(x_ref, grad_ref, out_ref):
-    out_ref[...] = dot_tn(x_ref[...], grad_ref[...]).astype(BF16)
+    out_ref[...] = dot_tn(grad_ref[...], x_ref[...]).astype(BF16)
 
 
 def partial_down(x, low_grad):
     return pl.pallas_call(
         down_kernel,
-        out_shape=jax.ShapeDtypeStruct((x.shape[1], low_grad.shape[1]), BF16),
+        out_shape=jax.ShapeDtypeStruct((low_grad.shape[1], x.shape[1]), BF16),
         in_specs=[VMEM, VMEM],
         out_specs=VMEM,
         compiler_params=params(),
@@ -501,28 +555,6 @@
     )(*arrays)
 
 
-def split_kernel(*refs):
-    total = refs[0][...].astype(F32)
-    for ref in refs[1:-1]:
-        total = total + ref[...].astype(F32)
-    out_ref = refs[-1]
-    rank = out_ref.shape[2]
-    for c in range(out_ref.shape[0]):
-        out_ref[c] = total[:, c * rank : (c + 1) * rank]
-
-
-def add_split(arrays, count):
-    rows, width = arrays[0].shape
-    return pl.pallas_call(
-        split_kernel,
-        out_shape=jax.ShapeDtypeStruct((count, rows, width // count), F32),
-        in_specs=[VMEM] * len(arrays),
-        out_specs=VMEM,
-        compiler_params=params(),
-        name="add_split",
-    )(*arrays)
-
-
 def to_mate(a):
     return lax.ppermute(a, "seq", [(i, i ^ 1) for i in range(lax.axis_size("seq"))])
 
@@ -535,23 +567,30 @@
 def local(inputs, frozen, adapter_down, adapter_up, out_grad, log_decay, doc_start, lengths):
     device = lax.axis_index("seq")
     chips = lax.axis_size("seq") // 2
+    rank = adapter_up.shape[1]
     meta = jnp.stack([lengths[device], device // 2, device % 2]).astype(jnp.int32)
     row, col, passes = decay_tables(meta, log_decay, doc_start)
-    low = sum_over_head(partial_low(inputs, adapter_down))
+    spread = sum_spread(to_pieces(partial_low(inputs, jnp.swapaxes(adapter_down, 1, 2))))
+    low = lax.all_to_all(spread, "head", 0, 0).reshape(inputs.shape[0], 3 * rank)
     moving, before, after, summary = project(meta, frozen, low, adapter_up, out_grad, col, passes)
     mate = to_mate(summary)
     outgoing = join(meta, summary, mate, chips)
     messages = [along_y(m, k + 1) for k, m in enumerate(outgoing)]
     part = inside(moving, row, col, before, after)
-    attn, grads, low_grad_part, up_part = finish(
-        meta, moving, part, col, low, adapter_up, mate, messages
+    grads, low_grad_part, state = finish(meta, moving, part, col, adapter_up, mate, messages)
+    attn, up_part = late(moving, row, col, before, state, low, grads, adapter_up.shape)
+    pieces, up_mate = lax.optimization_barrier((to_pieces(low_grad_part), to_mate(up_part)))
+    spread = sum_spread(pieces)
+    up_chip = add_all([up_part, up_mate], BF16)
+    low_grad, *up_others = lax.optimization_barrier(
+        [lax.all_to_all(spread, "head", 0, 0)] + [along_y(up_chip, k) for k in range(1, chips)]
     )
-    up_chip = add_all([up_part, to_mate(up_part)], BF16)
-    up_total = add_all([up_chip] + [along_y(up_chip, k) for k in range(1, chips)], F32)
-    low_grad = sum_over_head(low_grad_part)
+    low_grad = low_grad.reshape(inputs.shape[0], 3 * rank)
+    up_total = add_all([up_chip] + up_others, F32)
     down_part = partial_down(inputs, low_grad)
     down_chip = add_all([down_part, to_mate(down_part)], BF16)
-    down_total = add_split([down_chip] + [along_y(down_chip, k) for k in range(1, chips)], 3)
+    down_total = add_all([down_chip] + [along_y(down_chip, k) for k in range(1, chips)], F32)
+    down_total = jnp.swapaxes(down_total.reshape(3, rank, inputs.shape[1]), 1, 2)
     return (attn, grads, down_total, up_total)
 
 

time: 126 us -> 117 us (0.929)
  blocking collectives: 12.9 us -> 0 us
  starting transfers between devices: 34 us -> 37.1 us
  local copies, waits for them, and re-layouts: 6.66 us -> 9.28 us
  waiting for transfers between devices: 39.7 us -> 37.9 us
    all_to_all x1 -> x0, blocking collectives: 12.9 us -> none  [sum_over_head(): pieces = lax.all_to_all(pieces, 'head', 0, 0)]
    all_to_all x3 -> x4, starting transfers between devices: 15.6 us -> 22.4 us  [the longest x2 12 us: to_pieces(): lax.all_to_all(part.reshape(count, rows // count, width), 'head', 0, 0)]
    all_to_all x3 -> x4, waiting for transfers between devices: 22.1 us -> 16.5 us  [the longest x2 8.53 us: to_pieces(): lax.all_to_all(part.reshape(count, rows // count, width), 'head', 0, 0)]
    pallas_call x5, Pallas kernels: 10.1 us -> 15 us  [the longest x1 8.02 us: inside(): pl.pallas_call(inside_kernel, out_shape=jax.ShapeDtypeStruct((3, rows, fe...]
    ppermute x3, starting transfers between devices: 8.53 us -> 4.81 us  [to_mate(): lax.ppermute(a, 'seq', [(i, i ^ 1) for i in range(lax.axis_size('seq'))])]
    pallas_call x1, Pallas kernels: 8.69 us -> 5.13 us  [finish(): pl.pallas_call(functools.partial(finish_kernel, chips), out_shape=(jax.Sh...]
    ppermute x9, waiting for transfers between devices: 15.2 us -> 18.1 us  [along_y(): lax.ppermute(a, 'seq', [(i, (i + 2 * k) % count) for i in range(count)])]
    unnamed x16 -> x26, local copies, waits for them, and re-layouts: 5.41 us -> 8.04 us
  transfers between devices with their start and end apart: 15 -> 16, of which waited for: 10 -> 11; matrix products, arithmetic and copies ran while one was open for 2% -> 2% of each run, Pallas kernels for 9% -> 13%
where the time goes in v2:
time: 117 us; the launch traced here: 116 us
  waiting for transfers between devices  37.9 us (32%)
  starting transfers between devices  37.1 us (32%)
  Pallas kernels  30.4 us (26%)
  local copies, waits for them, and re-layouts  9.28 us (8%)
    ppermute x9, waiting for transfers between devices, along_y(): lax.ppermute(a, 'seq', [(i, (i + 2 * k) % count) for i in range(count)])  18.1 us
    all_to_all x2, starting transfers between devices, to_pieces(): lax.all_to_all(part.reshape(count, rows // count, width), 'head', 0, 0)  12 us
    ppermute x9, starting transfers between devices, along_y(): lax.ppermute(a, 'seq', [(i, (i + 2 * k) % count) for i in range(count)])  9.8 us
    all_to_all x2, waiting for transfers between devices, to_pieces(): lax.all_to_all(part.reshape(count, rows // count, width), 'head', 0, 0)  8.53 us
    unnamed x26, local copies, waits for them, and re-layouts  8.04 us
    pallas_call x1, Pallas kernels, inside(): pl.pallas_call(inside_kernel, out_shape=jax.ShapeDtypeStruct((3, rows, fe...  8.02 us
    all_to_all x1, waiting for transfers between devices, local(): lax.all_to_all(spread, 'head', 0, 0).reshape(inputs.shape[0], 3 * rank)  7.98 us
    all_to_all x1, starting transfers between devices, local(): lax.all_to_all(spread, 'head', 0, 0)  6.87 us
  transfers between devices with their start and end apart: 16, of which 11 were waited for; matrix products, arithmetic and copies ran while one was open for 2% of the time, Pallas kernels for 13%

profile of v2, /device:TPU:1, one launch (start us, length us, event | category | flops | bytes accessed | tf_op | source)
XLA Modules:
  0.0 116.2 jit_solution(10080725860558660898)
XLA Ops:
  0.6 1.1 copy-done
  1.8 0.9 copy-done.2
  2.7 1.6 %partial_low.1 = bf16[1024,192]{1,0:T(8,128)(2,1)} custom-call(bf16[1024,384]{1,0:T(8,128)(2,1)S(1)} %copy-done, bf16[3,64,384]{2,1,0:T(8,128)(2,1)S(1)} %bitcast.14), custom_call_target="tpu_custom_call" | custom-call | tf_op jit(solution)/shard_map/partial_low/pallas_call | solution.py:54
  4.3 8.4 %all-to-all-start = ((bf16[16,64,192]{2,1,0:T(8,128)(2,1)}), bf16[16,64,192]{2,1,0:T(8,128)(2,1)S(1)}, u32[]{:S(2)}, u32[]{:S(2)}) async-start(bf16[16,64,192]{2,1,0:T(8,128)(2,1)} %bitcast.3), calls=%async_computation | async-start | bytes 1048576 | tf_op jit(solution)/shard_map/all_to_all | solution.py:81
  12.8 1.2 %dynamic_slice.3 = s32[1]{0:T(128)} dynamic-slice(s32[8]{0:T(128)} %param.15, s32[]{:T(128)S(6)} %select_n.14), dynamic_slice_sizes={1} | dynamic-slice | bytes 12 | tf_op jit(solution)/shard_map/dynamic_slice | solution.py:571
  14.0 0.7 pad_add_fusion.meta_ref
  14.7 8.5 %all-to-all-done.in_ref = bf16[16,64,192]{2,1,0:T(8,128)(2,1)S(1)} async-done(((bf16[16,64,192]{2,1,0:T(8,128)(2,1)}), bf16[16,64,192]{2,1,0:T(8,128)(2,1)S(1)}, u32[]{:S(2)}, u32[]{:S(2)}) %all-to-all-start) | async-done | bytes 393248 | tf_op jit(solution)/shard_map/all_to_all | solution.py:81
  23.2 0.9 sum_spread.2
  24.1 3.6 %all-to-all-start.1 = ((bf16[16,64,192]{2,1,0:T(8,128)(2,1)}), bf16[16,64,192]{2,1,0:T(8,128)(2,1)S(1)}, u32[]{:S(2)}, u32[]{:S(2)}) async-start(bf16[16,64,192]{2,1,0:T(8,128)(2,1)} %sum_spread.2), calls=%async_computation.1 | async-start | bytes 1048576 | tf_op jit(solution)/shard_map/all_to_all | solution.py:574
  27.7 0.0 copy-start.4
  27.7 0.0 copy-start.5
  27.8 1.6 %decay_tables.1 = (f32[8,1024]{1,0:T(8,128)S(1)}, f32[1024,128]{1,0:T(8,128)S(1)}, f32[16,128]{1,0:T(8,128)S(1)}) custom-call(s32[3]{0:T(128)S(1)} %pad_add_fusion.meta_ref, bf16[4,1024]{1,0:T(4,128)(2,1)S(1)} %copy-done.6, s32[1,1024]{1,0:T(1,128)S(1)} %bitcast.15), custom_call_target="tpu_custom_call" | custom-call | flops 4000000000 | bytes 1000000 | tf_op jit(solution)/shard_map/decay_tables/pallas_call | solution.py:147
  29.4 8.0 %all-to-all-done.1 = bf16[16,64,192]{2,1,0:T(8,128)(2,1)S(1)} async-done(((bf16[16,64,192]{2,1,0:T(8,128)(2,1)}), bf16[16,64,192]{2,1,0:T(8,128)(2,1)S(1)}, u32[]{:S(2)}, u32[]{:S(2)}) %all-to-all-start.1) | async-done | bytes 393248 | tf_op jit(solution)/shard_map/all_to_all | solution.py:574
  37.4 1.9 %copy-done.3 = bf16[3,1024,512]{2,1,0:T(8,128)(2,1)S(1)} copy-done((bf16[3,1024,512]{2,1,0:T(8,128)(2,1)S(1)}, bf16[3,1024,512]{2,1,0:T(8,128)(2,1)}, u32[]{:S(2)}) %copy-start.3) | copy-done | bytes 3145752
  39.3 4.6 %project.1 = (bf16[4,1024,512]{2,1,0:T(8,128)(2,1)S(1)}, bf16[4,4,128,128]{3,2,1,0:T(8,128)(2,1)S(1)}, bf16[4,4,128,128]{3,2,1,0:T(8,128)(2,1)S(1)}, bf16[1088,128]{1,0:T(8,128)(2,1)S(1)}) custom-call(s32[3]{0:T(128)S(1)} %pad_add_fusion.meta_ref, bf16[3,1024,512]{2,1,0:T(8,128)(2,1)S(1)} %copy-done.3, bf16[1024,192]{1,0:T(8,128)(2,1)S(1)} %bitcast.12, ...), custom_call_target="tpu_custom_call" | custom-call | flops 4000000000 | bytes 10000000 | tf_op jit(solution)/shard_map/project/pallas_call | solution.py:232
  43.9 0.0 copy-start.11
  43.9 2.9 %collective-permute-start = (bf16[1088,128]{1,0:T(8,128)(2,1)S(1)}, bf16[1088,128]{1,0:T(8,128)(2,1)S(1)}, u32[]{:S(2)}, u32[]{:S(2)}) collective-permute-start(bf16[1088,128]{1,0:T(8,128)(2,1)S(1)} %get-tuple-element.31.own_ref), channel_id=1, source_target_pairs={{0,16},{16,0},{32,48},{48,32},{64,80},{80,64},{96,112},{112,96},{1... | collective-permute-start | bytes 835592 | tf_op jit(solution)/shard_map/ppermute | solution.py:559
  46.9 1.2 %collective-permute-done.mate_ref = bf16[1088,128]{1,0:T(8,128)(2,1)S(1)} collective-permute-done((bf16[1088,128]{1,0:T(8,128)(2,1)S(1)}, bf16[1088,128]{1,0:T(8,128)(2,1)S(1)}, u32[]{:S(2)}, u32[]{:S(2)}) %collective-permute-start) | collective-permute-done | bytes 278560 | tf_op jit(solution)/shard_map/ppermute | solution.py:559
  48.0 0.7 join.1
  48.7 1.4 %collective-permute-start.1 = (bf16[576,128]{1,0:T(8,128)(2,1)S(1)}, bf16[576,128]{1,0:T(8,128)(2,1)S(1)}, u32[]{:S(2)}, u32[]{:S(2)}) collective-permute-start(bf16[576,128]{1,0:T(8,128)(2,1)S(1)} %get-tuple-element.32), channel_id=1, source_target_pairs={{0,32},{16,48},{32,64},{48,80},{64,96},{80,112},{96,0},{112,16},{1... | collective-permute-start | bytes 442376 | tf_op jit(solution)/shard_map/ppermute | solution.py:564
  50.1 2.6 %collective-permute-start.2 = (bf16[576,128]{1,0:T(8,128)(2,1)S(1)}, bf16[576,128]{1,0:T(8,128)(2,1)S(1)}, u32[]{:S(2)}, u32[]{:S(2)}) collective-permute-start(bf16[576,128]{1,0:T(8,128)(2,1)S(1)} %get-tuple-element.33), channel_id=1, source_target_pairs={{0,64},{16,80},{32,96},{48,112},{64,0},{80,16},{96,32},{112,48},{1... | collective-permute-start | bytes 442376 | tf_op jit(solution)/shard_map/ppermute | solution.py:564
  52.7 1.1 collective-permute-start.3
  53.8 8.0 %inside.1.part_ref = f32[3,1024,512]{2,1,0:T(8,128)S(1)} custom-call(bf16[4,1024,512]{2,1,0:T(8,128)(2,1)S(1)} %get-tuple-element.27.moving_ref, f32[8,1024]{1,0:T(8,128)S(1)} %get-tuple-element.28.row_ref, f32[1024,128]{1,0:T(8,128)S(1)} %get-tuple-element.25.col_ref, bf16[4,4,128,128]{3,2,1,0:T(8,128)(2,1)S(1)} %get-tuple-element.29.before_ref, ...), custom_call_target="tpu_custom_call" | custom-call | flops 12000000000 | bytes 12000000 | tf_op jit(solution)/shard_map/inside/pallas_call | solution.py:351
  61.9 5.1 %finish.1 = (bf16[3,1024,512]{2,1,0:T(8,128)(2,1)}, bf16[1024,192]{1,0:T(8,128)(2,1)}, bf16[4,128,128]{2,1,0:T(8,128)(2,1)S(1)}) custom-call(s32[3]{0:T(128)S(1)} %pad_add_fusion.meta_ref, bf16[4,1024,512]{2,1,0:T(8,128)(2,1)S(1)} %get-tuple-element.27.moving_ref, f32[3,1024,512]{2,1,0:T(8,128)S(1)} %inside.1.part_ref, ...), custom_call_target="tpu_custom_call" | custom-call | flops 4000000000 | bytes 14000000 | tf_op jit(solution)/shard_map/finish/pallas_call | solution.py:496
  67.0 3.6 %all-to-all-start.2 = ((bf16[16,64,192]{2,1,0:T(8,128)(2,1)}), bf16[16,64,192]{2,1,0:T(8,128)(2,1)S(1)}, u32[]{:S(2)}, u32[]{:S(2)}) async-start(bf16[16,64,192]{2,1,0:T(8,128)(2,1)} %bitcast.6), calls=%async_computation.2 | async-start | bytes 1048576 | tf_op jit(solution)/shard_map/all_to_all | solution.py:81
  70.6 0.0 copy-start.8
  70.6 1.9 %copy-done.8 = bf16[3,1024,512]{2,1,0:T(8,128)(2,1)S(1)} copy-done((bf16[3,1024,512]{2,1,0:T(8,128)(2,1)S(1)}, bf16[3,1024,512]{2,1,0:T(8,128)(2,1)}, u32[]{:S(2)}) %copy-start.8) | copy-done | bytes 3145752
  72.5 2.2 %copy-done.10 = bf16[4,1024,512]{2,1,0:T(8,128)(2,1)S(1)} copy-done((bf16[4,1024,512]{2,1,0:T(8,128)(2,1)S(1)}, bf16[4,1024,512]{2,1,0:T(8,128)(2,1)}, u32[]{:S(2)}) %copy-start.10) | copy-done | bytes 4194328
  74.7 4.8 %late.1 = (bf16[1024,512]{1,0:T(8,128)(2,1)}, bf16[3,64,512]{2,1,0:T(8,128)(2,1)S(1)}) custom-call(bf16[4,1024,512]{2,1,0:T(8,128)(2,1)S(1)} %copy-done.10, f32[8,1024]{1,0:T(8,128)S(1)} %get-tuple-element.28.row_ref, f32[1024,128]{1,0:T(8,128)S(1)} %get-tuple-element.25.col_ref, bf16[4,4,128,128]{3,2,1,0:T(8,128)(2,1)S(1)} %copy-done.12, ...), custom_call_target="tpu_custom_call" | custom-call | flops 6000000000 | bytes 10000000 | tf_op jit(solution)/shard_map/late/pallas_call | solution.py:411
  79.5 1.2 %collective-permute-start.4 = (bf16[3,64,512]{2,1,0:T(8,128)(2,1)S(1)}, bf16[3,64,512]{2,1,0:T(8,128)(2,1)S(1)}, u32[]{:S(2)}, u32[]{:S(2)}) collective-permute-start(bf16[3,64,512]{2,1,0:T(8,128)(2,1)S(1)} %get-tuple-element.39.refs_0_), channel_id=1, source_target_pairs={{0,16},{16,0},{32,48},{48,32},{64,80},{80,64},{96,112},{112,96},{1... | collective-permute-start | bytes 589832 | tf_op jit(solution)/shard_map/ppermute | solution.py:559
  80.7 1.1 collective-permute-done.4.refs_1_
  81.8 0.9 sum_spread.3
  82.6 6.9 %all-to-all-start.3 = ((bf16[16,64,192]{2,1,0:T(8,128)(2,1)}), bf16[16,64,192]{2,1,0:T(8,128)(2,1)S(1)}, u32[]{:S(2)}, u32[]{:S(2)}) async-start(bf16[16,64,192]{2,1,0:T(8,128)(2,1)} %sum_spread.3), calls=%async_computation.3 | async-start | bytes 1048576 | tf_op jit(solution)/shard_map/all_to_all | solution.py:586
  89.6 0.1 collective-permute-start.7
  89.7 2.2 %collective-permute-start.6 = (bf16[3,64,512]{2,1,0:T(8,128)(2,1)S(1)}, bf16[3,64,512]{2,1,0:T(8,128)(2,1)S(1)}, u32[]{:S(2)}, u32[]{:S(2)}) collective-permute-start(bf16[3,64,512]{2,1,0:T(8,128)(2,1)S(1)} %add_all.4.refs_0_), channel_id=1, source_target_pairs={{0,64},{16,80},{32,96},{48,112},{64,0},{80,16},{96,32},{112,48},{1... | collective-permute-start | bytes 589832 | tf_op jit(solution)/shard_map/ppermute | solution.py:564
  91.8 3.6 %collective-permute-done.7.refs_3_ = bf16[3,64,512]{2,1,0:T(8,128)(2,1)S(1)} collective-permute-done((bf16[3,64,512]{2,1,0:T(8,128)(2,1)S(1)}, bf16[3,64,512]{2,1,0:T(8,128)(2,1)S(1)}, u32[]{:S(2)}, u32[]{:S(2)}) %collective-permute-start.7) | collective-permute-done | bytes 196640 | tf_op jit(solution)/shard_map/ppermute | solution.py:564
  95.4 1.6 %collective-permute-done.6.refs_2_ = bf16[3,64,512]{2,1,0:T(8,128)(2,1)S(1)} collective-permute-done((bf16[3,64,512]{2,1,0:T(8,128)(2,1)S(1)}, bf16[3,64,512]{2,1,0:T(8,128)(2,1)S(1)}, u32[]{:S(2)}, u32[]{:S(2)}) %collective-permute-start.6) | collective-permute-done | bytes 196640 | tf_op jit(solution)/shard_map/ppermute | solution.py:564
  97.0 5.1 %collective-permute-done.5.refs_1_ = bf16[3,64,512]{2,1,0:T(8,128)(2,1)S(1)} collective-permute-done((bf16[3,64,512]{2,1,0:T(8,128)(2,1)S(1)}, bf16[3,64,512]{2,1,0:T(8,128)(2,1)S(1)}, u32[]{:S(2)}, u32[]{:S(2)}) %collective-permute-start.5) | collective-permute-done | bytes 196640 | tf_op jit(solution)/shard_map/ppermute | solution.py:564
  102.2 0.4 partial_down.1.refs_0_
  102.6 0.7 collective-permute-start.8
  103.3 1.0 collective-permute-done.8.refs_1_
  104.3 0.9 collective-permute-start.11
  105.2 1.6 %collective-permute-start.10 = (bf16[192,384]{1,0:T(8,128)(2,1)S(1)}, bf16[192,384]{1,0:T(8,128)(2,1)S(1)}, u32[]{:S(2)}, u32[]{:S(2)}) collective-permute-start(bf16[192,384]{1,0:T(8,128)(2,1)S(1)} %add_all.5.refs_0_), channel_id=1, source_target_pairs={{0,64},{16,80},{32,96},{48,112},{64,0},{80,16},{96,32},{112,48},{1... | collective-permute-start | bytes 442376 | tf_op jit(solution)/shard_map/ppermute | solution.py:564
  106.8 0.8 add_all.7
  107.6 1.8 %collective-permute-done.11.refs_3_ = bf16[192,384]{1,0:T(8,128)(2,1)S(1)} collective-permute-done((bf16[192,384]{1,0:T(8,128)(2,1)S(1)}, bf16[192,384]{1,0:T(8,128)(2,1)S(1)}, u32[]{:S(2)}, u32[]{:S(2)}) %collective-permute-start.11) | collective-permute-done | bytes 147488 | tf_op jit(solution)/shard_map/ppermute | solution.py:564
  109.5 2.0 %collective-permute-done.10.refs_2_ = bf16[192,384]{1,0:T(8,128)(2,1)S(1)} collective-permute-done((bf16[192,384]{1,0:T(8,128)(2,1)S(1)}, bf16[192,384]{1,0:T(8,128)(2,1)S(1)}, u32[]{:S(2)}, u32[]{:S(2)}) %collective-permute-start.10) | collective-permute-done | bytes 147488 | tf_op jit(solution)/shard_map/ppermute | solution.py:564
  111.4 3.9 %collective-permute-done.9.refs_1_ = bf16[192,384]{1,0:T(8,128)(2,1)S(1)} collective-permute-done((bf16[192,384]{1,0:T(8,128)(2,1)S(1)}, bf16[192,384]{1,0:T(8,128)(2,1)S(1)}, u32[]{:S(2)}, u32[]{:S(2)}) %collective-permute-start.9) | collective-permute-done | bytes 147488 | tf_op jit(solution)/shard_map/ppermute | solution.py:564
  115.4 0.8 add_all.6
  (26 shorter events, 0.1 us)
Async XLA Ops:
  0.6 1.1 copy-start
  1.8 0.9 copy-start.2
  2.7 25.0 %copy-start.6 = (bf16[4,1024]{1,0:T(4,128)(2,1)S(1)}, bf16[4,1024]{1,0:T(4,128)(2,1)}, u32[]{:S(2)}) copy-start(bf16[4,1024]{1,0:T(4,128)(2,1)} %decay_ref.1) | copy-start | bytes 24580
  2.7 25.0 %copy-start.7 = (s32[1024]{0:T(1024)S(1)}, s32[1024]{0:T(1024)}, u32[]{:S(2)}) copy-start(s32[1024]{0:T(1024)} %param.14) | copy-start | bytes 12292
  4.3 18.9 %all-to-all-start = ((bf16[16,64,192]{2,1,0:T(8,128)(2,1)}), bf16[16,64,192]{2,1,0:T(8,128)(2,1)S(1)}, u32[]{:S(2)}, u32[]{:S(2)}) async-start(bf16[16,64,192]{2,1,0:T(8,128)(2,1)} %bitcast.3), calls=%async_computation | async-start | bytes 1048576 | tf_op jit(solution)/shard_map/all_to_all | solution.py:81
  24.1 13.2 %all-to-all-start.1 = ((bf16[16,64,192]{2,1,0:T(8,128)(2,1)}), bf16[16,64,192]{2,1,0:T(8,128)(2,1)S(1)}, u32[]{:S(2)}, u32[]{:S(2)}) async-start(bf16[16,64,192]{2,1,0:T(8,128)(2,1)} %sum_spread.2), calls=%async_computation.1 | async-start | bytes 1048576 | tf_op jit(solution)/shard_map/all_to_all | solution.py:574
  27.7 9.6 %copy-start.4 = (bf16[1024,512]{1,0:T(8,128)(2,1)S(1)}, bf16[1024,512]{1,0:T(8,128)(2,1)}, u32[]{:S(2)}) copy-start(bf16[1024,512]{1,0:T(8,128)(2,1)} %grad_ref.1) | copy-start | bytes 3145732
  27.7 9.6 %copy-start.5 = (bf16[3,64,512]{2,1,0:T(8,128)(2,1)S(1)}, bf16[3,64,512]{2,1,0:T(8,128)(2,1)}, u32[]{:S(2)}) copy-start(bf16[3,64,512]{2,1,0:T(8,128)(2,1)} %up_ref.3) | copy-start | bytes 589828
  37.4 1.9 %copy-start.3 = (bf16[3,1024,512]{2,1,0:T(8,128)(2,1)S(1)}, bf16[3,1024,512]{2,1,0:T(8,128)(2,1)}, u32[]{:S(2)}) copy-start(bf16[3,1024,512]{2,1,0:T(8,128)(2,1)} %frozen_ref.1) | copy-start | bytes 9437188
  43.9 17.9 %copy-start.11 = (bf16[4,4,128,128]{3,2,1,0:T(8,128)(2,1)}, bf16[4,4,128,128]{3,2,1,0:T(8,128)(2,1)S(1)}, u32[]{:S(2)}) copy-start(bf16[4,4,128,128]{3,2,1,0:T(8,128)(2,1)S(1)} %get-tuple-element.29.before_ref) | copy-start | bytes 1572868
  43.9 17.9 %copy-start.9 = (bf16[4,1024,512]{2,1,0:T(8,128)(2,1)}, bf16[4,1024,512]{2,1,0:T(8,128)(2,1)S(1)}, u32[]{:S(2)}) copy-start(bf16[4,1024,512]{2,1,0:T(8,128)(2,1)S(1)} %get-tuple-element.27.moving_ref) | copy-start | bytes 12582916
  43.9 4.1 %collective-permute-start = (bf16[1088,128]{1,0:T(8,128)(2,1)S(1)}, bf16[1088,128]{1,0:T(8,128)(2,1)S(1)}, u32[]{:S(2)}, u32[]{:S(2)}) collective-permute-start(bf16[1088,128]{1,0:T(8,128)(2,1)S(1)} %get-tuple-element.31.own_ref), channel_id=1, source_target_pairs={{0,16},{16,0},{32,48},{48,32},{64,80},{80,64},{96,112},{112,96},{1... | collective-permute-start | bytes 835592 | tf_op jit(solution)/shard_map/ppermute | solution.py:559
  48.7 13.1 %collective-permute-start.1 = (bf16[576,128]{1,0:T(8,128)(2,1)S(1)}, bf16[576,128]{1,0:T(8,128)(2,1)S(1)}, u32[]{:S(2)}, u32[]{:S(2)}) collective-permute-start(bf16[576,128]{1,0:T(8,128)(2,1)S(1)} %get-tuple-element.32), channel_id=1, source_target_pairs={{0,32},{16,48},{32,64},{48,80},{64,96},{80,112},{96,0},{112,16},{1... | collective-permute-start | bytes 442376 | tf_op jit(solution)/shard_map/ppermute | solution.py:564
  50.1 11.8 %collective-permute-start.2 = (bf16[576,128]{1,0:T(8,128)(2,1)S(1)}, bf16[576,128]{1,0:T(8,128)(2,1)S(1)}, u32[]{:S(2)}, u32[]{:S(2)}) collective-permute-start(bf16[576,128]{1,0:T(8,128)(2,1)S(1)} %get-tuple-element.33), channel_id=1, source_target_pairs={{0,64},{16,80},{32,96},{48,112},{64,0},{80,16},{96,32},{112,48},{1... | collective-permute-start | bytes 442376 | tf_op jit(solution)/shard_map/ppermute | solution.py:564
  52.7 9.1 %collective-permute-start.3 = (bf16[576,128]{1,0:T(8,128)(2,1)S(1)}, bf16[576,128]{1,0:T(8,128)(2,1)S(1)}, u32[]{:S(2)}, u32[]{:S(2)}) collective-permute-start(bf16[576,128]{1,0:T(8,128)(2,1)S(1)} %get-tuple-element.34), channel_id=1, source_target_pairs={{0,96},{16,112},{32,0},{48,16},{64,32},{80,48},{96,64},{112,80},{1... | collective-permute-start | bytes 442376 | tf_op jit(solution)/shard_map/ppermute | solution.py:564
  61.8 8.8 %copy-start.12 = (bf16[4,4,128,128]{3,2,1,0:T(8,128)(2,1)S(1)}, bf16[4,4,128,128]{3,2,1,0:T(8,128)(2,1)}, u32[]{:S(2)}) copy-start(bf16[4,4,128,128]{3,2,1,0:T(8,128)(2,1)} %copy-done.11) | copy-start | bytes 1572868
  67.0 14.7 %all-to-all-start.2 = ((bf16[16,64,192]{2,1,0:T(8,128)(2,1)}), bf16[16,64,192]{2,1,0:T(8,128)(2,1)S(1)}, u32[]{:S(2)}, u32[]{:S(2)}) async-start(bf16[16,64,192]{2,1,0:T(8,128)(2,1)} %bitcast.6), calls=%async_computation.2 | async-start | bytes 1048576 | tf_op jit(solution)/shard_map/all_to_all | solution.py:81
  70.6 1.9 %copy-start.8 = (bf16[3,1024,512]{2,1,0:T(8,128)(2,1)S(1)}, bf16[3,1024,512]{2,1,0:T(8,128)(2,1)}, u32[]{:S(2)}) copy-start(bf16[3,1024,512]{2,1,0:T(8,128)(2,1)} %get-tuple-element.22.grad_ref) | copy-start | bytes 9437188
  72.5 2.2 %copy-start.10 = (bf16[4,1024,512]{2,1,0:T(8,128)(2,1)S(1)}, bf16[4,1024,512]{2,1,0:T(8,128)(2,1)}, u32[]{:S(2)}) copy-start(bf16[4,1024,512]{2,1,0:T(8,128)(2,1)} %copy-done.9) | copy-start | bytes 12582916
  74.7 27.5 %copy-start.1 = (bf16[1024,384]{1,0:T(8,128)(2,1)S(1)}, bf16[1024,384]{1,0:T(8,128)(2,1)}, u32[]{:S(2)}) copy-start(bf16[1024,384]{1,0:T(8,128)(2,1)} %x_ref.3) | copy-start | bytes 2359300
  79.5 2.3 %collective-permute-start.4 = (bf16[3,64,512]{2,1,0:T(8,128)(2,1)S(1)}, bf16[3,64,512]{2,1,0:T(8,128)(2,1)S(1)}, u32[]{:S(2)}, u32[]{:S(2)}) collective-permute-start(bf16[3,64,512]{2,1,0:T(8,128)(2,1)S(1)} %get-tuple-element.39.refs_0_), channel_id=1, source_target_pairs={{0,16},{16,0},{32,48},{48,32},{64,80},{80,64},{96,112},{112,96},{1... | collective-permute-start | bytes 589832 | tf_op jit(solution)/shard_map/ppermute | solution.py:559
  82.6 19.5 %all-to-all-start.3 = ((bf16[16,64,192]{2,1,0:T(8,128)(2,1)}), bf16[16,64,192]{2,1,0:T(8,128)(2,1)S(1)}, u32[]{:S(2)}, u32[]{:S(2)}) async-start(bf16[16,64,192]{2,1,0:T(8,128)(2,1)} %sum_spread.3), calls=%async_computation.3 | async-start | bytes 1048576 | tf_op jit(solution)/shard_map/all_to_all | solution.py:586
  89.6 5.9 %collective-permute-start.7 = (bf16[3,64,512]{2,1,0:T(8,128)(2,1)S(1)}, bf16[3,64,512]{2,1,0:T(8,128)(2,1)S(1)}, u32[]{:S(2)}, u32[]{:S(2)}) collective-permute-start(bf16[3,64,512]{2,1,0:T(8,128)(2,1)S(1)} %add_all.4.refs_0_), channel_id=1, source_target_pairs={{0,96},{16,112},{32,0},{48,16},{64,32},{80,48},{96,64},{112,80},{1... | collective-permute-start | bytes 589832 | tf_op jit(solution)/shard_map/ppermute | solution.py:564
  89.7 7.4 %collective-permute-start.6 = (bf16[3,64,512]{2,1,0:T(8,128)(2,1)S(1)}, bf16[3,64,512]{2,1,0:T(8,128)(2,1)S(1)}, u32[]{:S(2)}, u32[]{:S(2)}) collective-permute-start(bf16[3,64,512]{2,1,0:T(8,128)(2,1)S(1)} %add_all.4.refs_0_), channel_id=1, source_target_pairs={{0,64},{16,80},{32,96},{48,112},{64,0},{80,16},{96,32},{112,48},{1... | collective-permute-start | bytes 589832 | tf_op jit(solution)/shard_map/ppermute | solution.py:564
  91.8 10.4 %collective-permute-start.5 = (bf16[3,64,512]{2,1,0:T(8,128)(2,1)S(1)}, bf16[3,64,512]{2,1,0:T(8,128)(2,1)S(1)}, u32[]{:S(2)}, u32[]{:S(2)}) collective-permute-start(bf16[3,64,512]{2,1,0:T(8,128)(2,1)S(1)} %add_all.4.refs_0_), channel_id=1, source_target_pairs={{0,32},{16,48},{32,64},{48,80},{64,96},{80,112},{96,0},{112,16},{1... | collective-permute-start | bytes 589832 | tf_op jit(solution)/shard_map/ppermute | solution.py:564
  102.6 1.7 %collective-permute-start.8 = (bf16[192,384]{1,0:T(8,128)(2,1)S(1)}, bf16[192,384]{1,0:T(8,128)(2,1)S(1)}, u32[]{:S(2)}, u32[]{:S(2)}) collective-permute-start(bf16[192,384]{1,0:T(8,128)(2,1)S(1)} %partial_down.1.refs_0_), channel_id=1, source_target_pairs={{0,16},{16,0},{32,48},{48,32},{64,80},{80,64},{96,112},{112,96},{1... | collective-permute-start | bytes 442376 | tf_op jit(solution)/shard_map/ppermute | solution.py:559
  104.3 5.1 %collective-permute-start.11 = (bf16[192,384]{1,0:T(8,128)(2,1)S(1)}, bf16[192,384]{1,0:T(8,128)(2,1)S(1)}, u32[]{:S(2)}, u32[]{:S(2)}) collective-permute-start(bf16[192,384]{1,0:T(8,128)(2,1)S(1)} %add_all.5.refs_0_), channel_id=1, source_target_pairs={{0,96},{16,112},{32,0},{48,16},{64,32},{80,48},{96,64},{112,80},{1... | collective-permute-start | bytes 442376 | tf_op jit(solution)/shard_map/ppermute | solution.py:564
  105.2 6.3 %collective-permute-start.10 = (bf16[192,384]{1,0:T(8,128)(2,1)S(1)}, bf16[192,384]{1,0:T(8,128)(2,1)S(1)}, u32[]{:S(2)}, u32[]{:S(2)}) collective-permute-start(bf16[192,384]{1,0:T(8,128)(2,1)S(1)} %add_all.5.refs_0_), channel_id=1, source_target_pairs={{0,64},{16,80},{32,96},{48,112},{64,0},{80,16},{96,32},{112,48},{1... | collective-permute-start | bytes 442376 | tf_op jit(solution)/shard_map/ppermute | solution.py:564
  106.8 8.6 %collective-permute-start.9 = (bf16[192,384]{1,0:T(8,128)(2,1)S(1)}, bf16[192,384]{1,0:T(8,128)(2,1)S(1)}, u32[]{:S(2)}, u32[]{:S(2)}) collective-permute-start(bf16[192,384]{1,0:T(8,128)(2,1)S(1)} %add_all.5.refs_0_), channel_id=1, source_target_pairs={{0,32},{16,48},{32,64},{48,80},{64,96},{80,112},{96,0},{112,16},{1... | collective-permute-start | bytes 442376 | tf_op jit(solution)/shard_map/ppermute | solution.py:564

commit v3 on v2

v3 whole, which is shorter than its diff:
```python
import functools

import jax
import jax.numpy as jnp
from jax import lax
from jax.experimental import pallas as pl
from jax.experimental.pallas import tpu as pltpu
from jax.sharding import PartitionSpec as P

F32 = jnp.float32
BF16 = jnp.bfloat16
CHUNK = 256
VMEM_BYTES = 20 * 1024 * 1024
NEGATIVE = -1e30

CUM, SEG, ENTER, LEAVE, ENTER_ALL, LEAVE_ALL = 0, 4, 8, 12, 16, 20


def dot_nn(a, b):
    return lax.dot_general(a, b, (((1,), (0,)), ((), ())), preferred_element_type=F32)


def dot_nt(a, b):
    return lax.dot_general(a, b, (((1,), (1,)), ((), ())), preferred_element_type=F32)


def dot_tn(a, b):
    return lax.dot_general(a, b, (((0,), (0,)), ((), ())), preferred_element_type=F32)


def params(limit=VMEM_BYTES, **more):
    return pltpu.CompilerParams(vmem_limit_bytes=limit, **more)


def chunk_rows(c):
    return pl.ds(pl.multiple_of(c * CHUNK, CHUNK), CHUNK)


def cost(flops, moved):
    return pl.CostEstimate(flops=int(flops), bytes_accessed=int(moved), transcendentals=0)


VMEM = pl.BlockSpec(memory_space=pltpu.VMEM)
SMEM = pl.BlockSpec(memory_space=pltpu.SMEM)


def store_pieces(out_ref, value):
    half = value.shape[0] // 2
    for r in range(2):
        for l in range(2):
            out_ref[2 * r + l] = value[r * half : (r + 1) * half, l * 128 : (l + 1) * 128]


def load_pieces(ref):
    rows = [jnp.concatenate([ref[2 * r], ref[2 * r + 1]], axis=1) for r in range(2)]
    return jnp.concatenate(rows, axis=0)


def piece_shape(rows, width):
    return (rows // CHUNK * 4, width // 2, CHUNK // 2)


def piece_spec(width):
    return pl.BlockSpec((4, width // 2, CHUNK // 2), lambda i: (i, 0, 0))


def low_kernel(x_ref, down_ref, out_ref, x_held, down_held, sems):
    count = x_ref.shape[0] // CHUNK
    first = pltpu.make_async_copy(down_ref, down_held, sems.at[count])
    first.start()
    copies = []
    for c in range(count):
        rows = pl.ds(c * CHUNK, CHUNK)
        copies.append(pltpu.make_async_copy(x_ref.at[rows], x_held.at[rows], sems.at[c]))
        copies[c].start()
    first.wait()
    for c in range(count):
        copies[c].wait()
        part = dot_nt(down_held[...], x_held[c * CHUNK : (c + 1) * CHUNK, :])
        store_pieces(out_ref.at[pl.ds(4 * c, 4)], part.astype(BF16))


def partial_low(x, down):
    rows, _ = x.shape
    far = pl.BlockSpec(memory_space=pltpu.HBM)
    return pl.pallas_call(
        low_kernel,
        out_shape=jax.ShapeDtypeStruct(piece_shape(rows, down.shape[0]), BF16),
        in_specs=[far, far],
        out_specs=VMEM,
        scratch_shapes=[
            pltpu.VMEM(x.shape, BF16),
            pltpu.VMEM(down.shape, BF16),
            pltpu.SemaphoreType.DMA((rows // CHUNK + 1,)),
        ],
        compiler_params=params(),
        name="partial_low",
    )(*(pltpu.with_memory_space_constraint(a, pltpu.HBM) for a in (x, down)))


def sum_spread_kernel(in_ref, out_ref):
    count = in_ref.shape[0]
    total = in_ref[0].astype(F32)
    for i in range(1, count):
        total = total + in_ref[i].astype(F32)
    total = total.astype(BF16)
    for i in range(count):
        out_ref[i] = total


def exchange(pieces):
    return lax.all_to_all(pieces, "head", 0, 0)


def sum_spread(pieces):
    count, rows, width = pieces.shape
    return pl.pallas_call(
        sum_spread_kernel,
        out_shape=jax.ShapeDtypeStruct(pieces.shape, BF16),
        in_specs=[VMEM],
        out_specs=VMEM,
        compiler_params=params(),
        name="sum_spread",
    )(pieces)


def decay_kernel(meta_ref, decay_ref, start_ref, row_ref, col_ref, pass_ref):
    heads, rows = decay_ref.shape
    live = meta_ref[0]
    slot = lax.broadcasted_iota(jnp.int32, (1, rows), 1)
    keep = slot < live
    decay = jnp.where(keep, decay_ref[...].astype(F32), 0.0)
    starts = jnp.where(keep, start_ref[...].astype(F32), 0.0)
    both = jnp.concatenate([decay, starts, jnp.zeros((8 - heads - 1, rows), F32)], axis=0)
    both = both.astype(BF16)
    row_i = lax.broadcasted_iota(jnp.int32, (CHUNK, CHUNK), 0)
    col_i = lax.broadcasted_iota(jnp.int32, (CHUNK, CHUNK), 1)
    upper = jnp.where(row_i <= col_i, 1.0, 0.0).astype(BF16)
    lower = jnp.where(row_i >= col_i, 1.0, 0.0).astype(BF16)
    count = rows // CHUNK
    enters, leaves, passes = [], [], []
    for c in range(count):
        span = slice(c * CHUNK, (c + 1) * CHUNK)
        piece = both[:, span]
        by_row = dot_nn(piece, upper)
        by_col = dot_nt(lower, piece)
        here = keep[:, span]
        here_col = c * CHUNK + lax.broadcasted_iota(jnp.int32, (CHUNK, 1), 0) < live
        head_row = lax.broadcasted_iota(jnp.int32, (8, CHUNK), 0)
        head_lane = lax.broadcasted_iota(jnp.int32, (CHUNK, 8), 1)
        row_ref[:, span] = jnp.where(here | (head_row != heads), by_row, -1.0)
        col_ref[span, 0:8] = jnp.where(here_col | (head_lane != heads), by_col, -2.0)
        cum = by_col[:, :heads]
        seg = by_col[:, heads : heads + 1]
        cum_end = by_col[CHUNK - 1 : CHUNK, :heads]
        seg_end = by_col[CHUNK - 1 : CHUNK, heads : heads + 1]
        enter = jnp.where((seg == 0.0) & here_col, jnp.exp(cum), 0.0)
        leave = jnp.where((seg == seg_end) & here_col, jnp.exp(cum_end - cum), 0.0)
        col_ref[span, ENTER : ENTER + heads] = enter
        col_ref[span, LEAVE : LEAVE + heads] = leave
        enters.append(enter)
        leaves.append(leave)
        passes.append(jnp.where(seg_end == 0.0, jnp.exp(cum_end), 0.0))
        end_row = by_row[:, CHUNK - 1 : CHUNK]
        passing_col = jnp.where(end_row[heads : heads + 1] == 0.0, jnp.exp(end_row[:heads]), 0.0)
        pass_ref[c * heads : (c + 1) * heads, :] = jnp.broadcast_to(passing_col, (heads, 128))
    before = jnp.ones((1, heads), F32)
    for c in range(count):
        span = slice(c * CHUNK, (c + 1) * CHUNK)
        col_ref[span, ENTER_ALL : ENTER_ALL + heads] = enters[c] * before
        before = before * passes[c]
    after = jnp.ones((1, heads), F32)
    for c in reversed(range(count)):
        span = slice(c * CHUNK, (c + 1) * CHUNK)
        col_ref[span, LEAVE_ALL : LEAVE_ALL + heads] = leaves[c] * after
        after = after * passes[c]


def decay_tables(meta, decay, starts):
    heads, rows = decay.shape
    count = rows // CHUNK
    return pl.pallas_call(
        decay_kernel,
        out_shape=(
            jax.ShapeDtypeStruct((8, rows), F32),
            jax.ShapeDtypeStruct((rows, 128), F32),
            jax.ShapeDtypeStruct((count * heads, 128), F32),
        ),
        in_specs=[SMEM, VMEM, VMEM],
        out_specs=(VMEM, VMEM, VMEM),
        compiler_params=params(),
        cost_estimate=cost(4e9, 1e6),
        name="decay_tables",
    )(meta, decay, starts.reshape(1, rows))


def project_kernel(
    frozen_ref, low_ref, up_ref, grad_ref, col_ref, pass_ref,
    moving_ref, before_ref, after_ref, summary_ref, returning, held, sems,
):
    chunks = returning.shape[0]
    rank = up_ref.shape[1]
    features = frozen_ref.shape[2]
    heads = features // 128
    size = heads * 128
    copies = []
    for c in range(chunks):
        rows = pl.ds(c * CHUNK, CHUNK)
        copies.append(pltpu.make_async_copy(frozen_ref.at[:, rows], held.at[:, rows], sems.at[c]))
        copies[c].start()
    states = [jnp.zeros((128, 128), F32)] * heads
    for c in range(chunks):
        rows = pl.ds(c * CHUNK, CHUNK)
        low = load_pieces(low_ref.at[pl.ds(4 * c, 4)])
        copies[c].wait()
        for i in range(3):
            lifted = dot_tn(low[i * rank : (i + 1) * rank, :], up_ref[i])
            moving_ref[i, rows, :] = (held[i, rows, :].astype(F32) + lifted).astype(BF16)
        col = col_ref[rows, :]
        for h in range(heads):
            span = slice(h * 128, (h + 1) * 128)
            passing = pass_ref[c * heads + h : c * heads + h + 1, :]
            leave = col[:, LEAVE + h : LEAVE + h + 1]
            enter = col[:, ENTER + h : ENTER + h + 1]
            keyed = (moving_ref[1, rows, span].astype(F32) * leave).astype(BF16)
            scaled = (moving_ref[0, rows, span].astype(F32) * enter).astype(BF16)
            before_ref[c, h] = states[h].astype(BF16)
            states[h] = passing * states[h] + dot_tn(keyed, moving_ref[2, rows, span])
            returning[c, h] = dot_tn(scaled, grad_ref[rows, span])
    for h in range(heads):
        back = jnp.zeros((128, 128), F32)
        whole = jnp.ones((1, 128), F32)
        for c in reversed(range(chunks)):
            passing = pass_ref[c * heads + h : c * heads + h + 1, :]
            after_ref[c, h] = back.astype(BF16)
            back = passing * back + returning[c, h]
            whole = whole * passing
        summary_ref[h * 128 : (h + 1) * 128, :] = states[h].astype(BF16)
        summary_ref[size + h * 128 : size + (h + 1) * 128, :] = back.astype(BF16)
        summary_ref[2 * size + 16 * h : 2 * size + 16 * h + 16, :] = passing_rows(whole)


def passing_rows(row):
    first = row.astype(BF16).astype(F32)
    rest = row - first
    second = rest.astype(BF16).astype(F32)
    third = (rest - second).astype(BF16).astype(F32)
    return jnp.concatenate([first, second, third, jnp.zeros((13, 128), F32)], axis=0).astype(BF16)


def project(frozen, low, up, grad, col, passes):
    _, rows, features = frozen.shape
    heads = features // 128
    count = rows // CHUNK
    summary_rows = 2 * features + 16 * heads
    states = jax.ShapeDtypeStruct((count, heads, 128, 128), BF16)
    return pl.pallas_call(
        project_kernel,
        out_shape=(
            jax.ShapeDtypeStruct((3, rows, features), BF16),
            states,
            states,
            jax.ShapeDtypeStruct((summary_rows, 128), BF16),
        ),
        in_specs=[pl.BlockSpec(memory_space=pltpu.HBM)] + [VMEM] * 5,
        out_specs=(VMEM,) * 4,
        scratch_shapes=[
            pltpu.VMEM(states.shape, F32),
            pltpu.VMEM(frozen.shape, BF16),
            pltpu.SemaphoreType.DMA((count,)),
        ],
        compiler_params=params(),
        cost_estimate=cost(4e9, 10e6),
        name="project",
    )(pltpu.with_memory_space_constraint(frozen, pltpu.HBM), low, up, grad, col, passes)


def passing_of(ref, base):
    return (
        ref[base : base + 1, :].astype(F32)
        + ref[base + 1 : base + 2, :].astype(F32)
        + ref[base + 2 : base + 3, :].astype(F32)
    )


def join_kernel(meta_ref, own_ref, mate_ref, *out_refs):
    y = meta_ref[1]
    core = meta_ref[2]
    total = own_ref.shape[0]
    heads = total // (2 * 128 + 16)
    size = heads * 128
    chips = len(out_refs) + 1
    second = core == 1
    for h in range(heads):
        rows = slice(h * 128, (h + 1) * 128)
        back_rows = slice(size + h * 128, size + (h + 1) * 128)
        base = 2 * size + 16 * h
        own_pass = passing_of(own_ref, base)
        mate_pass = passing_of(mate_ref, base)
        own_state = own_ref[rows, :].astype(F32)
        mate_state = mate_ref[rows, :].astype(F32)
        own_back = own_ref[back_rows, :].astype(F32)
        mate_back = mate_ref[back_rows, :].astype(F32)
        one = jnp.ones_like(own_pass)
        state = jnp.where(second, own_pass, one) * mate_state + jnp.where(second, one, mate_pass) * own_state
        back = jnp.where(second, one, own_pass) * mate_back + jnp.where(second, mate_pass, one) * own_back
        tail = passing_rows(own_pass * mate_pass)
        for k, out_ref in enumerate(out_refs):
            later = y + (k + 1) < chips
            out_ref[rows, :] = jnp.where(later, state, back).astype(BF16)
            out_ref[size + 16 * h : size + 16 * h + 16, :] = tail


def join(meta, own, mate, chips):
    heads = own.shape[0] // (2 * 128 + 16)
    message = jax.ShapeDtypeStruct((heads * (128 + 16), 128), BF16)
    return pl.pallas_call(
        join_kernel,
        out_shape=(message,) * (chips - 1),
        in_specs=[SMEM, VMEM, VMEM],
        out_specs=(VMEM,) * (chips - 1),
        compiler_params=params(),
        name="join",
    )(meta, own, mate)


def inside_kernel(moving_ref, grad_ref, row_ref, col_ref, before_ref, after_ref, part_ref):
    features = moving_ref.shape[2]
    heads = features // 128
    row_i = lax.broadcasted_iota(jnp.int32, (CHUNK, CHUNK), 0)
    col_i = lax.broadcasted_iota(jnp.int32, (CHUNK, CHUNK), 1)

    @pl.loop(0, moving_ref.shape[1] // CHUNK)
    def _(c):
        rows = chunk_rows(c)
        col = col_ref[rows, :]
        row = row_ref[:, rows]
        allowed = (row_i <= col_i) & (col[:, SEG : SEG + 1] == row[SEG : SEG + 1, :])
        shut = jnp.where(allowed, 0.0, NEGATIVE)
        for h in range(heads):
            span = slice(h * 128, (h + 1) * 128)
            q = moving_ref[0, rows, span]
            k = moving_ref[1, rows, span]
            v = moving_ref[2, rows, span]
            g = grad_ref[rows, span]
            weights = jnp.exp((row[h : h + 1, :] - col[:, h : h + 1]) + shut)
            a = (dot_nt(k, q) * weights).astype(BF16)
            b = (dot_nt(v, g) * weights).astype(BF16)
            enter = col[:, ENTER + h : ENTER + h + 1]
            leave = col[:, LEAVE + h : LEAVE + h + 1]
            before = before_ref[c, h]
            after = after_ref[c, h]
            part_ref[0, rows, span] = dot_tn(b, k) + enter * dot_nt(g, before)
            part_ref[1, rows, span] = dot_nn(b, q) + leave * dot_nt(v, after)
            part_ref[2, rows, span] = dot_nn(a, g) + leave * dot_nn(k, after)


def inside(moving, grad, row, col, before, after):
    return pl.pallas_call(
        inside_kernel,
        out_shape=jax.ShapeDtypeStruct(moving.shape, F32),
        in_specs=[VMEM] * 6,
        out_specs=VMEM,
        compiler_params=params(),
        cost_estimate=cost(12e9, 12e6),
        name="inside",
    )(moving, grad, row, col, before, after)


def late_kernel(moving_ref, row_ref, col_ref, before_ref, state_ref, attn_ref):
    features = moving_ref.shape[2]
    heads = features // 128
    inverse = 1.0 / 128.0
    row_i = lax.broadcasted_iota(jnp.int32, (CHUNK, CHUNK), 0)
    col_i = lax.broadcasted_iota(jnp.int32, (CHUNK, CHUNK), 1)
    col = col_ref[...]
    allowed = (row_i >= col_i) & (col[:, SEG : SEG + 1] == row_ref[SEG : SEG + 1, :])
    shut = jnp.where(allowed, 0.0, NEGATIVE)
    for h in range(heads):
        span = slice(h * 128, (h + 1) * 128)
        q = moving_ref[0, :, span]
        weights = jnp.exp((col[:, h : h + 1] - row_ref[h : h + 1, :]) + shut)
        a = (dot_nt(q, moving_ref[1, :, span]) * weights).astype(BF16)
        enter = col[:, ENTER + h : ENTER + h + 1]
        enter_all = col[:, ENTER_ALL + h : ENTER_ALL + h + 1]
        out = dot_nn(a, moving_ref[2, :, span])
        out = out + enter * dot_nn(q, before_ref[0, h]) + enter_all * dot_nn(q, state_ref[h])
        attn_ref[:, span] = (out * inverse).astype(BF16)


def late(moving, row, col, before, state):
    _, rows, features = moving.shape
    heads = features // 128
    count = rows // CHUNK
    return pl.pallas_call(
        late_kernel,
        out_shape=jax.ShapeDtypeStruct((rows, features), BF16),
        grid=(count,),
        in_specs=[
            pl.BlockSpec((3, CHUNK, features), lambda i: (0, i, 0)),
            pl.BlockSpec((8, CHUNK), lambda i: (0, i)),
            pl.BlockSpec((CHUNK, 128), lambda i: (i, 0)),
            pl.BlockSpec((1, heads, 128, 128), lambda i: (i, 0, 0, 0)),
            pl.BlockSpec(state.shape, lambda i: (0, 0, 0)),
        ],
        out_specs=pl.BlockSpec((CHUNK, features), lambda i: (i, 0)),
        compiler_params=params(dimension_semantics=("arbitrary",)),
        cost_estimate=cost(6e9, 6e6),
        name="late",
    )(moving, row, col, before, state)


def store_halves(core, total, keep_ref, send_ref):
    half = total.shape[0] // 2
    keep_ref[...] = total[pl.ds(pl.multiple_of(core * half, 16), half), :].astype(BF16)
    send_ref[...] = total[pl.ds(pl.multiple_of((1 - core) * half, 16), half), :].astype(BF16)


def up_kernel(meta_ref, low_ref, grad_ref, keep_ref, send_ref, total):
    step = pl.program_id(0)
    rank = total.shape[0] // 3

    @pl.when(step == 0)
    def _():
        total[...] = jnp.zeros_like(total)

    low = load_pieces(low_ref)
    for c in range(3):
        rows = slice(c * rank, (c + 1) * rank)
        total[rows, :] += dot_nn(low[rows, :], grad_ref[c])

    @pl.when(step == pl.num_programs(0) - 1)
    def _():
        store_halves(meta_ref[2], total, keep_ref, send_ref)


def partial_up(meta, low, grads):
    _, rows, features = grads.shape
    width = 2 * low.shape[1]
    half = jax.ShapeDtypeStruct((width // 2, features), BF16)
    return pl.pallas_call(
        up_kernel,
        out_shape=(half, half),
        grid=(rows // CHUNK,),
        in_specs=[
            SMEM,
            piece_spec(width),
            pl.BlockSpec((3, CHUNK, features), lambda i: (0, i, 0)),
        ],
        out_specs=(pl.BlockSpec(half.shape, lambda i: (0, 0)),) * 2,
        scratch_shapes=[pltpu.VMEM((width, features), F32)],
        compiler_params=params(dimension_semantics=("arbitrary",)),
        cost_estimate=cost(2e9, 4e6),
        name="partial_up",
    )(meta, low, grads)


def finish_kernel(chips, meta_ref, moving_ref, g_ref, part_ref, col_ref, up_ref, mate_ref, *refs):
    message_refs = refs[: chips - 1]
    out_ref, low_grad_ref, state_in, back_in, grad_ref, sems = refs[chips - 1 :]
    features = moving_ref.shape[2]
    heads = features // 128
    size = heads * 128
    count = moving_ref.shape[1] // CHUNK
    inverse = 1.0 / 128.0
    y = meta_ref[1]
    second = meta_ref[2] == 1
    for h in range(heads):
        rows = slice(h * 128, (h + 1) * 128)
        factor = jnp.ones((1, 128), F32)
        state = jnp.zeros((128, 128), F32)
        for k in range(1, chips):
            ref = message_refs[k - 1]
            state = state + jnp.where(k <= y, factor, 0.0) * ref[rows, :].astype(F32)
            factor = factor * passing_of(ref, size + 16 * h)
        factor = jnp.ones((1, 128), F32)
        back = jnp.zeros((128, 128), F32)
        for k in reversed(range(1, chips)):
            ref = message_refs[k - 1]
            back = back + jnp.where(k > y, factor, 0.0) * ref[rows, :].astype(F32)
            factor = factor * passing_of(ref, size + 16 * h)
        mate_pass = passing_of(mate_ref, 2 * size + 16 * h)
        mate_state = mate_ref[rows, :].astype(F32)
        mate_back = mate_ref[size + h * 128 : size + (h + 1) * 128, :].astype(F32)
        state_in[h] = jnp.where(second, mate_pass * state + mate_state, state).astype(BF16)
        back_in[h] = jnp.where(second, back, mate_pass * back + mate_back).astype(BF16)
    copies = []
    for c in range(count):
        rows = pl.ds(c * CHUNK, CHUNK)
        col = col_ref[rows, :]
        for h in range(heads):
            span = slice(h * 128, (h + 1) * 128)
            k = moving_ref[1, rows, span]
            v = moving_ref[2, rows, span]
            g = g_ref[rows, span]
            enter = col[:, ENTER_ALL + h : ENTER_ALL + h + 1]
            leave = col[:, LEAVE_ALL + h : LEAVE_ALL + h + 1]
            state = state_in[h]
            back = back_in[h]
            query = part_ref[0, rows, span] + enter * dot_nt(g, state)
            key = part_ref[1, rows, span] + leave * dot_nt(v, back)
            value = part_ref[2, rows, span] + leave * dot_nn(k, back)
            for i, result in enumerate((query, key, value)):
                grad_ref[i, rows, span] = (result * inverse).astype(BF16)
        copies.append(pltpu.make_async_copy(grad_ref.at[:, rows], out_ref.at[:, rows], sems.at[c]))
        copies[c].start()
        low_grad = [dot_nt(up_ref[i], grad_ref[i, rows, :]).astype(BF16) for i in range(3)]
        store_pieces(low_grad_ref.at[pl.ds(4 * c, 4)], jnp.concatenate(low_grad, axis=0))
    for copy in copies:
        copy.wait()


def finish(meta, moving, grad, part, col, up, mate, messages):
    _, rows, features = moving.shape
    heads = features // 128
    chips = len(messages) + 1
    width = up.shape[0] * up.shape[1]
    return pl.pallas_call(
        functools.partial(finish_kernel, chips),
        out_shape=(
            jax.ShapeDtypeStruct(moving.shape, BF16),
            jax.ShapeDtypeStruct(piece_shape(rows, width), BF16),
            jax.ShapeDtypeStruct((heads, 128, 128), BF16),
        ),
        in_specs=[SMEM] + [VMEM] * (6 + len(messages)),
        out_specs=(pl.BlockSpec(memory_space=pltpu.HBM), VMEM, VMEM),
        scratch_shapes=[
            pltpu.VMEM((heads, 128, 128), BF16),
            pltpu.VMEM(moving.shape, BF16),
            pltpu.SemaphoreType.DMA((rows // CHUNK,)),
        ],
        compiler_params=params(),
        cost_estimate=cost(4e9, 14e6),
        name="finish",
    )(meta, moving, grad, part, col, up, mate, *messages)


def down_kernel(meta_ref, x_ref, grad_ref, keep_ref, send_ref, total):
    value = jnp.zeros(total.shape, F32)
    for c in range(x_ref.shape[0] // CHUNK):
        low_grad = load_pieces(grad_ref.at[pl.ds(4 * c, 4)])
        value = value + dot_nn(low_grad, x_ref[c * CHUNK : (c + 1) * CHUNK, :])
    total[...] = value
    store_halves(meta_ref[2], total, keep_ref, send_ref)


def partial_down(meta, x, low_grad):
    width = 2 * low_grad.shape[1]
    half = jax.ShapeDtypeStruct((width // 2, x.shape[1]), BF16)
    return pl.pallas_call(
        down_kernel,
        out_shape=(half, half),
        in_specs=[SMEM, VMEM, VMEM],
        out_specs=(VMEM, VMEM),
        scratch_shapes=[pltpu.VMEM((width, x.shape[1]), F32)],
        compiler_params=params(),
        name="partial_down",
    )(meta, x, low_grad)


def halves_kernel(meta_ref, own_ref, mate_ref, out_ref):
    core = meta_ref[2]
    half = own_ref.shape[0]
    out_ref[pl.ds(pl.multiple_of(core * half, 8), half), :] = own_ref[...]
    out_ref[pl.ds(pl.multiple_of((1 - core) * half, 8), half), :] = mate_ref[...]


def join_halves(meta, own, mate):
    return pl.pallas_call(
        halves_kernel,
        out_shape=jax.ShapeDtypeStruct((2 * own.shape[0], own.shape[1]), F32),
        in_specs=[SMEM, VMEM, VMEM],
        out_specs=VMEM,
        compiler_params=params(),
        name="join_halves",
    )(meta, own, mate)


def add_kernel(*refs):
    total = refs[0][...].astype(F32)
    for ref in refs[1:-1]:
        total = total + ref[...].astype(F32)
    refs[-1][...] = total.astype(refs[-1].dtype)


def add_all(arrays, dtype):
    return pl.pallas_call(
        add_kernel,
        out_shape=jax.ShapeDtypeStruct(arrays[0].shape, dtype),
        in_specs=[VMEM] * len(arrays),
        out_specs=VMEM,
        compiler_params=params(),
        name="add_all",
    )(*arrays)


def to_mate(a):
    return lax.ppermute(a, "seq", [(i, i ^ 1) for i in range(lax.axis_size("seq"))])


def along_y(a, k):
    count = lax.axis_size("seq")
    return lax.ppermute(a, "seq", [(i, (i + 2 * k) % count) for i in range(count)])


def local(inputs, frozen, adapter_down, adapter_up, out_grad, log_decay, doc_start, lengths):
    device = lax.axis_index("seq")
    chips = lax.axis_size("seq") // 2
    rank = adapter_up.shape[1]
    meta = jnp.stack([lengths[device], device // 2, device % 2]).astype(jnp.int32)
    down = jnp.swapaxes(adapter_down, 1, 2).reshape(3 * rank, inputs.shape[1])
    row, col, passes = decay_tables(meta, log_decay, doc_start)
    low = exchange(sum_spread(exchange(partial_low(inputs, down))))
    moving, before, after, summary = project(frozen, low, adapter_up, out_grad, col, passes)
    mate = to_mate(summary)
    outgoing = join(meta, summary, mate, chips)
    messages = [along_y(m, k + 1) for k, m in enumerate(outgoing)]
    part = inside(moving, out_grad, row, col, before, after)
    grads, low_grad_part, state = finish(meta, moving, out_grad, part, col, adapter_up, mate, messages)
    up_keep, up_send = partial_up(meta, low, grads)
    attn = late(moving, row, col, before, state)
    up_chip = add_all([up_keep, to_mate(up_send)], BF16)
    pieces, up_chip, attn = lax.optimization_barrier((exchange(low_grad_part), up_chip, attn))
    up_parts = [up_chip] + [along_y(up_chip, k) for k in range(1, chips)]
    low_grad, *up_parts = lax.optimization_barrier([exchange(sum_spread(pieces))] + up_parts)
    down_keep, down_send = partial_down(meta, inputs, low_grad)
    down_chip = add_all([down_keep, to_mate(down_send)], BF16)
    down_chip, *up_parts = lax.optimization_barrier([down_chip] + up_parts)
    down_parts = [down_chip] + [along_y(down_chip, k) for k in range(1, chips)]
    up_half = add_all(up_parts, F32)
    up_total = join_halves(meta, up_half, to_mate(up_half))
    up_total, *down_parts = lax.optimization_barrier([up_total] + down_parts)
    down_half = add_all(down_parts, F32)
    down_total = join_halves(meta, down_half, to_mate(down_half))
    down_total = jnp.swapaxes(down_total.reshape(3, rank, inputs.shape[1]), 1, 2)
    return (attn, grads, down_total, up_total.reshape(adapter_up.shape))


def solution(mesh):
    in_specs = (
        P("seq", "head"),
        P(None, "seq", "head"),
        P(None, "head", None),
        P(None, None, "head"),
        P("seq", "head"),
        P("head", "seq"),
        P("seq"),
        P(),
    )
    out_specs = (
        P("seq", "head"),
        P(None, "seq", "head"),
        P(None, "head", None),
        P(None, None, "head"),
    )
    return jax.shard_map(local, mesh=mesh, in_specs=in_specs, out_specs=out_specs, check_vma=False)
```

time: 117 us -> 107 us (0.915)
  waiting for transfers between devices: 37.9 us -> 27.3 us
  local copies, waits for them, and re-layouts: 9.28 us -> 3.16 us
  Pallas kernels: 30.4 us -> 33.7 us
  starting transfers between devices: 37.1 us -> 40.4 us
    ppermute x9, waiting for transfers between devices: 18.1 us -> 8.42 us  [along_y(): lax.ppermute(a, 'seq', [(i, (i + 2 * k) % count) for i in range(count)])]
    unnamed x26 -> x16, local copies, waits for them, and re-layouts: 8.04 us -> 1.92 us
    pallas_call x5 -> x8, Pallas kernels: 19.4 us -> 25.1 us  [the longest x1 7.39 us: inside(): pl.pallas_call(inside_kernel, out_shape=jax.ShapeDtypeStruct(moving.shape...]
    ppermute x3 -> x5, starting transfers between devices: 4.81 us -> 8.44 us  [to_mate(): lax.ppermute(a, 'seq', [(i, i ^ 1) for i in range(lax.axis_size('seq'))])]
    pallas_call x4, Pallas kernels: 1.71 us -> 0.14 us  [add_all(): pl.pallas_call(add_kernel, out_shape=jax.ShapeDtypeStruct(arrays[0].shape...]
    ppermute x3 -> x5, waiting for transfers between devices: 3.26 us -> 3.11 us  [to_mate(): lax.ppermute(a, 'seq', [(i, i ^ 1) for i in range(lax.axis_size('seq'))])]
  transfers between devices with their start and end apart: 16 -> 18, of which waited for: 11 -> 12; matrix products, arithmetic and copies ran while one was open for 2% -> 2% of each run, Pallas kernels for 13% -> 15%
where the time goes in v3:
time: 107 us; the launch traced here: 106 us
  starting transfers between devices  40.4 us (38%)
  Pallas kernels  33.7 us (31%)
  waiting for transfers between devices  27.3 us (26%)
  local copies, waits for them, and re-layouts  3.16 us (3%)
    all_to_all x4, starting transfers between devices, exchange(): return lax.all_to_all(pieces, 'head', 0, 0)  22.4 us
    all_to_all x4, waiting for transfers between devices, exchange(): return lax.all_to_all(pieces, 'head', 0, 0)  15.8 us
    ppermute x9, starting transfers between devices, along_y(): lax.ppermute(a, 'seq', [(i, (i + 2 * k) % count) for i in range(count)])  9.5 us
    ppermute x5, starting transfers between devices, to_mate(): lax.ppermute(a, 'seq', [(i, i ^ 1) for i in range(lax.axis_size('seq'))])  8.44 us
    ppermute x9, waiting for transfers between devices, along_y(): lax.ppermute(a, 'seq', [(i, (i + 2 * k) % count) for i in range(count)])  8.42 us
    pallas_call x1, Pallas kernels, inside(): pl.pallas_call(inside_kernel, out_shape=jax.ShapeDtypeStruct(moving.shape...  7.39 us
    pallas_call x1, Pallas kernels, project(): pl.pallas_call(project_kernel, out_shape=(jax.ShapeDtypeStruct((3, rows,...  5.25 us
    pallas_call x1, Pallas kernels, finish(): pl.pallas_call(functools.partial(finish_kernel, chips), out_shape=(jax.Sh...  4.57 us
  transfers between devices with their start and end apart: 18, of which 12 were waited for; matrix products, arithmetic and copies ran while one was open for 2% of the time, Pallas kernels for 15%

profile of v3, /device:TPU:1, one launch (start us, length us, event | category | flops | bytes accessed | tf_op | source)
XLA Modules:
  0.0 106.2 jit_solution(8878667784894122555)
XLA Ops:
  0.7 2.9 %partial_low.1 = bf16[16,96,128]{2,1,0:T(8,128)(2,1)} custom-call(bf16[1024,384]{1,0:T(8,128)(2,1)} %x_ref.3, bf16[192,384]{1,0:T(8,128)(2,1)} %bitcast.13), custom_call_target="tpu_custom_call" | custom-call | tf_op jit(solution)/shard_map/partial_low/pallas_call | solution.py:86
  3.6 8.4 %all-to-all-start = ((bf16[16,96,128]{2,1,0:T(8,128)(2,1)}), bf16[16,96,128]{2,1,0:T(8,128)(2,1)S(1)}, u32[]{:S(2)}, u32[]{:S(2)}) async-start(bf16[16,96,128]{2,1,0:T(8,128)(2,1)} %partial_low.1), calls=%async_computation | async-start | bytes 786432 | tf_op jit(solution)/shard_map/all_to_all | solution.py:112
  12.1 1.2 %dynamic_slice.3 = s32[1]{0:T(128)} dynamic-slice(s32[8]{0:T(128)} %param.15, s32[]{:T(128)S(6)} %select_n.14), dynamic_slice_sizes={1} | dynamic-slice | bytes 12 | tf_op jit(solution)/shard_map/dynamic_slice | solution.py:610
  13.3 0.7 pad_add_fusion.meta_ref
  14.0 7.2 %all-to-all-done.in_ref = bf16[16,96,128]{2,1,0:T(8,128)(2,1)S(1)} async-done(((bf16[16,96,128]{2,1,0:T(8,128)(2,1)}), bf16[16,96,128]{2,1,0:T(8,128)(2,1)S(1)}, u32[]{:S(2)}, u32[]{:S(2)}) %all-to-all-start) | async-done | bytes 393248 | tf_op jit(solution)/shard_map/all_to_all | solution.py:112
  21.2 0.8 sum_spread.2
  22.0 3.6 %all-to-all-start.1 = ((bf16[16,96,128]{2,1,0:T(8,128)(2,1)}), bf16[16,96,128]{2,1,0:T(8,128)(2,1)S(1)}, u32[]{:S(2)}, u32[]{:S(2)}) async-start(bf16[16,96,128]{2,1,0:T(8,128)(2,1)} %sum_spread.2), calls=%async_computation.1 | async-start | bytes 786432 | tf_op jit(solution)/shard_map/all_to_all | solution.py:112
  25.6 0.0 copy-start.1
  25.6 0.0 copy-start.2
  25.6 1.6 %decay_tables.1 = (f32[8,1024]{1,0:T(8,128)S(1)}, f32[1024,128]{1,0:T(8,128)S(1)}, f32[16,128]{1,0:T(8,128)S(1)}) custom-call(s32[3]{0:T(128)S(1)} %pad_add_fusion.meta_ref, bf16[4,1024]{1,0:T(4,128)(2,1)S(1)} %copy-done.3, s32[1,1024]{1,0:T(1,128)S(1)} %bitcast.10), custom_call_target="tpu_custom_call" | custom-call | flops 4000000000 | bytes 1000000 | tf_op jit(solution)/shard_map/decay_tables/pallas_call | solution.py:182
  27.3 6.5 %all-to-all-done.1.low_ref = bf16[16,96,128]{2,1,0:T(8,128)(2,1)S(1)} async-done(((bf16[16,96,128]{2,1,0:T(8,128)(2,1)}), bf16[16,96,128]{2,1,0:T(8,128)(2,1)S(1)}, u32[]{:S(2)}, u32[]{:S(2)}) %all-to-all-start.1) | async-done | bytes 393248 | tf_op jit(solution)/shard_map/all_to_all | solution.py:112
  33.8 5.3 %project.1 = (bf16[3,1024,512]{2,1,0:T(8,128)(2,1)S(1)}, bf16[4,4,128,128]{3,2,1,0:T(8,128)(2,1)S(1)}, bf16[4,4,128,128]{3,2,1,0:T(8,128)(2,1)S(1)}, bf16[1088,128]{1,0:T(8,128)(2,1)S(1)}) custom-call(bf16[3,1024,512]{2,1,0:T(8,128)(2,1)} %frozen_ref.1, bf16[16,96,128]{2,1,0:T(8,128)(2,1)S(1)} %all-to-all-done.1.low_ref, bf16[3,64,512]{2,1,0:T(8,128)(2,1)S(1)} %copy-done.2, ...), custom_call_target="tpu_custom_call" | custom-call | flops 4000000000 | bytes 10000000 | tf_op jit(solution)/shard_map/project/pallas_call | solution.py:257
  39.1 3.1 %collective-permute-start = (bf16[1088,128]{1,0:T(8,128)(2,1)S(1)}, bf16[1088,128]{1,0:T(8,128)(2,1)S(1)}, u32[]{:S(2)}, u32[]{:S(2)}) collective-permute-start(bf16[1088,128]{1,0:T(8,128)(2,1)S(1)} %get-tuple-element.45.own_ref), channel_id=1, source_target_pairs={{0,16},{16,0},{32,48},{48,32},{64,80},{80,64},{96,112},{112,96},{1... | collective-permute-start | bytes 835592 | tf_op jit(solution)/shard_map/ppermute | solution.py:598
  42.2 1.2 %collective-permute-done.mate_ref = bf16[1088,128]{1,0:T(8,128)(2,1)S(1)} collective-permute-done((bf16[1088,128]{1,0:T(8,128)(2,1)S(1)}, bf16[1088,128]{1,0:T(8,128)(2,1)S(1)}, u32[]{:S(2)}, u32[]{:S(2)}) %collective-permute-start) | collective-permute-done | bytes 278560 | tf_op jit(solution)/shard_map/ppermute | solution.py:598
  43.3 0.7 join.1
  44.0 1.4 %collective-permute-start.1 = (bf16[576,128]{1,0:T(8,128)(2,1)S(1)}, bf16[576,128]{1,0:T(8,128)(2,1)S(1)}, u32[]{:S(2)}, u32[]{:S(2)}) collective-permute-start(bf16[576,128]{1,0:T(8,128)(2,1)S(1)} %get-tuple-element.46), channel_id=1, source_target_pairs={{0,32},{16,48},{32,64},{48,80},{64,96},{80,112},{96,0},{112,16},{1... | collective-permute-start | bytes 442376 | tf_op jit(solution)/shard_map/ppermute | solution.py:603
  45.4 2.6 %collective-permute-start.2 = (bf16[576,128]{1,0:T(8,128)(2,1)S(1)}, bf16[576,128]{1,0:T(8,128)(2,1)S(1)}, u32[]{:S(2)}, u32[]{:S(2)}) collective-permute-start(bf16[576,128]{1,0:T(8,128)(2,1)S(1)} %get-tuple-element.47), channel_id=1, source_target_pairs={{0,64},{16,80},{32,96},{48,112},{64,0},{80,16},{96,32},{112,48},{1... | collective-permute-start | bytes 442376 | tf_op jit(solution)/shard_map/ppermute | solution.py:603
  48.0 1.1 %collective-permute-start.3 = (bf16[576,128]{1,0:T(8,128)(2,1)S(1)}, bf16[576,128]{1,0:T(8,128)(2,1)S(1)}, u32[]{:S(2)}, u32[]{:S(2)}) collective-permute-start(bf16[576,128]{1,0:T(8,128)(2,1)S(1)} %get-tuple-element.48), channel_id=1, source_target_pairs={{0,96},{16,112},{32,0},{48,16},{64,32},{80,48},{96,64},{112,80},{1... | collective-permute-start | bytes 442376 | tf_op jit(solution)/shard_map/ppermute | solution.py:603
  49.1 7.4 %inside.1.part_ref = f32[3,1024,512]{2,1,0:T(8,128)S(1)} custom-call(bf16[3,1024,512]{2,1,0:T(8,128)(2,1)S(1)} %get-tuple-element.41.moving_ref, bf16[1024,512]{1,0:T(8,128)(2,1)S(1)} %copy-done.1, f32[8,1024]{1,0:T(8,128)S(1)} %get-tuple-element.42.row_ref, f32[1024,128]{1,0:T(8,128)S(1)} %get-tuple-element.39.col_ref, ...), custom_call_target="tpu_custom_call" | custom-call | flops 12000000000 | bytes 12000000 | tf_op jit(solution)/shard_map/inside/pallas_call | solution.py:359
  56.5 4.6 %finish.1 = (bf16[3,1024,512]{2,1,0:T(8,128)(2,1)}, bf16[16,96,128]{2,1,0:T(8,128)(2,1)}, bf16[4,128,128]{2,1,0:T(8,128)(2,1)S(1)}) custom-call(s32[3]{0:T(128)S(1)} %pad_add_fusion.meta_ref, bf16[3,1024,512]{2,1,0:T(8,128)(2,1)S(1)} %get-tuple-element.41.moving_ref, bf16[1024,512]{1,0:T(8,128)(2,1)S(1)} %copy-done.1, f32[3,1024,512]{2,1,0:T(8,128)S(1)} %inside.1.part_ref, ...), custom_call_target="tpu_custom_call" | custom-call | flops 4000000000 | bytes 14000000 | tf_op jit(solution)/shard_map/finish/pallas_call | solution.py:518
  61.1 3.6 %all-to-all-start.2 = ((bf16[16,96,128]{2,1,0:T(8,128)(2,1)}), bf16[16,96,128]{2,1,0:T(8,128)(2,1)S(1)}, u32[]{:S(2)}, u32[]{:S(2)}) async-start(bf16[16,96,128]{2,1,0:T(8,128)(2,1)} %get-tuple-element.49), calls=%async_computation.2 | async-start | bytes 786432 | tf_op jit(solution)/shard_map/all_to_all | solution.py:112
  64.7 0.0 copy-start.5
  64.7 1.9 %copy-done.5 = bf16[3,1024,512]{2,1,0:T(8,128)(2,1)S(1)} copy-done((bf16[3,1024,512]{2,1,0:T(8,128)(2,1)S(1)}, bf16[3,1024,512]{2,1,0:T(8,128)(2,1)}, u32[]{:S(2)}) %copy-start.5) | copy-done | bytes 3145752
  66.6 1.9 %partial_up.1 = (bf16[96,512]{1,0:T(8,128)(2,1)S(1)}, bf16[96,512]{1,0:T(8,128)(2,1)S(1)}) custom-call(s32[3]{0:T(128)S(1)} %pad_add_fusion.meta_ref, bf16[16,96,128]{2,1,0:T(8,128)(2,1)S(1)} %all-to-all-done.1.low_ref, bf16[3,1024,512]{2,1,0:T(8,128)(2,1)S(1)} %copy-done.5), custom_call_target="tpu_custom_call" | custom-call | flops 2000000000 | bytes 4000000 | tf_op jit(solution)/shard_map/partial_up/pallas_call | solution.py:441
  68.5 1.5 %collective-permute-start.4 = (bf16[96,512]{1,0:T(8,128)(2,1)S(1)}, bf16[96,512]{1,0:T(8,128)(2,1)S(1)}, u32[]{:S(2)}, u32[]{:S(2)}) collective-permute-start(bf16[96,512]{1,0:T(8,128)(2,1)S(1)} %get-tuple-element.52), channel_id=1, source_target_pairs={{0,16},{16,0},{32,48},{48,32},{64,80},{80,64},{96,112},{112,96},{1... | collective-permute-start | bytes 294920 | tf_op jit(solution)/shard_map/ppermute | solution.py:598
  69.9 4.1 %late.1 = bf16[1024,512]{1,0:T(8,128)(2,1)} custom-call(bf16[3,1024,512]{2,1,0:T(8,128)(2,1)S(1)} %copy-done.7, f32[8,1024]{1,0:T(8,128)S(1)} %get-tuple-element.42.row_ref, f32[1024,128]{1,0:T(8,128)S(1)} %get-tuple-element.39.col_ref, bf16[4,4,128,128]{3,2,1,0:T(8,128)(2,1)S(1)} %get-tuple-element.43.before_ref, ...), custom_call_target="tpu_custom_call" | custom-call | flops 6000000000 | bytes 6000000 | tf_op jit(solution)/shard_map/late/pallas_call | solution.py:395
  74.1 0.8 sum_spread.3
  74.9 6.9 %all-to-all-start.3 = ((bf16[16,96,128]{2,1,0:T(8,128)(2,1)}), bf16[16,96,128]{2,1,0:T(8,128)(2,1)S(1)}, u32[]{:S(2)}, u32[]{:S(2)}) async-start(bf16[16,96,128]{2,1,0:T(8,128)(2,1)} %sum_spread.3), calls=%async_computation.3 | async-start | bytes 786432 | tf_op jit(solution)/shard_map/all_to_all | solution.py:112
  81.8 0.2 collective-permute-start.7
  82.0 2.1 %collective-permute-start.6 = (bf16[96,512]{1,0:T(8,128)(2,1)S(1)}, bf16[96,512]{1,0:T(8,128)(2,1)S(1)}, u32[]{:S(2)}, u32[]{:S(2)}) collective-permute-start(bf16[96,512]{1,0:T(8,128)(2,1)S(1)} %add_all.4.refs_0_), channel_id=1, source_target_pairs={{0,64},{16,80},{32,96},{48,112},{64,0},{80,16},{96,32},{112,48},{1... | collective-permute-start | bytes 294920 | tf_op jit(solution)/shard_map/ppermute | solution.py:603
  84.1 1.9 %collective-permute-done.7.refs_3_ = bf16[96,512]{1,0:T(8,128)(2,1)S(1)} collective-permute-done((bf16[96,512]{1,0:T(8,128)(2,1)S(1)}, bf16[96,512]{1,0:T(8,128)(2,1)S(1)}, u32[]{:S(2)}, u32[]{:S(2)}) %collective-permute-start.7) | collective-permute-done | bytes 98336 | tf_op jit(solution)/shard_map/ppermute | solution.py:603
  85.9 1.3 %collective-permute-done.6.refs_2_ = bf16[96,512]{1,0:T(8,128)(2,1)S(1)} collective-permute-done((bf16[96,512]{1,0:T(8,128)(2,1)S(1)}, bf16[96,512]{1,0:T(8,128)(2,1)S(1)}, u32[]{:S(2)}, u32[]{:S(2)}) %collective-permute-start.6) | collective-permute-done | bytes 98336 | tf_op jit(solution)/shard_map/ppermute | solution.py:603
  87.2 2.1 %collective-permute-done.5.refs_1_ = bf16[96,512]{1,0:T(8,128)(2,1)S(1)} collective-permute-done((bf16[96,512]{1,0:T(8,128)(2,1)S(1)}, bf16[96,512]{1,0:T(8,128)(2,1)S(1)}, u32[]{:S(2)}, u32[]{:S(2)}) %collective-permute-start.5) | collective-permute-done | bytes 98336 | tf_op jit(solution)/shard_map/ppermute | solution.py:603
  89.4 2.0 %all-to-all-done.3.grad_ref = bf16[16,96,128]{2,1,0:T(8,128)(2,1)S(1)} async-done(((bf16[16,96,128]{2,1,0:T(8,128)(2,1)}), bf16[16,96,128]{2,1,0:T(8,128)(2,1)S(1)}, u32[]{:S(2)}, u32[]{:S(2)}) %all-to-all-start.3) | async-done | bytes 393248 | tf_op jit(solution)/shard_map/all_to_all | solution.py:112
  91.4 0.9 partial_down.1
  92.3 1.5 %collective-permute-start.8 = (bf16[96,384]{1,0:T(8,128)(2,1)S(1)}, bf16[96,384]{1,0:T(8,128)(2,1)S(1)}, u32[]{:S(2)}, u32[]{:S(2)}) collective-permute-start(bf16[96,384]{1,0:T(8,128)(2,1)S(1)} %get-tuple-element.59), channel_id=1, source_target_pairs={{0,16},{16,0},{32,48},{48,32},{64,80},{80,64},{96,112},{112,96},{1... | collective-permute-start | bytes 221192 | tf_op jit(solution)/shard_map/ppermute | solution.py:598
  93.9 0.9 collective-permute-done.8.refs_1_
  94.8 0.1 add_all.6.own_ref
  94.9 0.4 collective-permute-start.9
  95.3 0.1 collective-permute-start.12
  95.4 2.1 %collective-permute-start.11 = (bf16[96,384]{1,0:T(8,128)(2,1)S(1)}, bf16[96,384]{1,0:T(8,128)(2,1)S(1)}, u32[]{:S(2)}, u32[]{:S(2)}) collective-permute-start(bf16[96,384]{1,0:T(8,128)(2,1)S(1)} %add_all.5.refs_0_), channel_id=1, source_target_pairs={{0,64},{16,80},{32,96},{48,112},{64,0},{80,16},{96,32},{112,48},{1... | collective-permute-start | bytes 221192 | tf_op jit(solution)/shard_map/ppermute | solution.py:603
  97.5 1.3 %join_halves.2 = f32[192,512]{1,0:T(8,128)} custom-call(s32[3]{0:T(128)S(1)} %pad_add_fusion.meta_ref, f32[96,512]{1,0:T(8,128)S(1)} %add_all.6.own_ref, f32[96,512]{1,0:T(8,128)S(1)} %collective-permute-done.9.mate_ref), custom_call_target="tpu_custom_call" | custom-call | tf_op jit(solution)/shard_map/join_halves/pallas_call | solution.py:569
  98.8 0.2 collective-permute-done.12.refs_3_
  99.0 1.1 %collective-permute-done.11.refs_2_ = bf16[96,384]{1,0:T(8,128)(2,1)S(1)} collective-permute-done((bf16[96,384]{1,0:T(8,128)(2,1)S(1)}, bf16[96,384]{1,0:T(8,128)(2,1)S(1)}, u32[]{:S(2)}, u32[]{:S(2)}) %collective-permute-start.11) | collective-permute-done | bytes 73760 | tf_op jit(solution)/shard_map/ppermute | solution.py:603
  100.1 1.8 %collective-permute-done.10.refs_1_ = bf16[96,384]{1,0:T(8,128)(2,1)S(1)} collective-permute-done((bf16[96,384]{1,0:T(8,128)(2,1)S(1)}, bf16[96,384]{1,0:T(8,128)(2,1)S(1)}, u32[]{:S(2)}, u32[]{:S(2)}) %collective-permute-start.10) | collective-permute-done | bytes 73760 | tf_op jit(solution)/shard_map/ppermute | solution.py:603
  101.9 1.9 %collective-permute-start.13 = (f32[96,384]{1,0:T(8,128)S(1)}, f32[96,384]{1,0:T(8,128)S(1)}, u32[]{:S(2)}, u32[]{:S(2)}) collective-permute-start(f32[96,384]{1,0:T(8,128)S(1)} %add_all.7.own_ref), channel_id=1, source_target_pairs={{0,16},{16,0},{32,48},{48,32},{64,80},{80,64},{96,112},{112,96},{1... | collective-permute-start | bytes 442376 | tf_op jit(solution)/shard_map/ppermute | solution.py:598
  103.9 1.0 collective-permute-done.13.mate_ref
  104.9 1.3 %join_halves.3 = f32[192,384]{1,0:T(8,128)} custom-call(s32[3]{0:T(128)S(1)} %pad_add_fusion.meta_ref, f32[96,384]{1,0:T(8,128)S(1)} %add_all.7.own_ref, f32[96,384]{1,0:T(8,128)S(1)} %collective-permute-done.13.mate_ref), custom_call_target="tpu_custom_call" | custom-call | tf_op jit(solution)/shard_map/join_halves/pallas_call | solution.py:569
  (23 shorter events, 0.1 us)
Async XLA Ops:
  0.6 25.0 %copy-start.4 = (s32[1024]{0:T(1024)S(1)}, s32[1024]{0:T(1024)}, u32[]{:S(2)}) copy-start(s32[1024]{0:T(1024)} %param.14) | copy-start | bytes 12292
  0.6 25.0 %copy-start.3 = (bf16[4,1024]{1,0:T(4,128)(2,1)S(1)}, bf16[4,1024]{1,0:T(4,128)(2,1)}, u32[]{:S(2)}) copy-start(bf16[4,1024]{1,0:T(4,128)(2,1)} %decay_ref.1) | copy-start | bytes 24580
  3.6 17.6 %all-to-all-start = ((bf16[16,96,128]{2,1,0:T(8,128)(2,1)}), bf16[16,96,128]{2,1,0:T(8,128)(2,1)S(1)}, u32[]{:S(2)}, u32[]{:S(2)}) async-start(bf16[16,96,128]{2,1,0:T(8,128)(2,1)} %partial_low.1), calls=%async_computation | async-start | bytes 786432 | tf_op jit(solution)/shard_map/all_to_all | solution.py:112
  22.0 11.8 %all-to-all-start.1 = ((bf16[16,96,128]{2,1,0:T(8,128)(2,1)}), bf16[16,96,128]{2,1,0:T(8,128)(2,1)S(1)}, u32[]{:S(2)}, u32[]{:S(2)}) async-start(bf16[16,96,128]{2,1,0:T(8,128)(2,1)} %sum_spread.2), calls=%async_computation.1 | async-start | bytes 786432 | tf_op jit(solution)/shard_map/all_to_all | solution.py:112
  25.6 8.2 %copy-start.1 = (bf16[1024,512]{1,0:T(8,128)(2,1)S(1)}, bf16[1024,512]{1,0:T(8,128)(2,1)}, u32[]{:S(2)}) copy-start(bf16[1024,512]{1,0:T(8,128)(2,1)} %g_ref.1) | copy-start | bytes 3145732
  25.6 8.2 %copy-start.2 = (bf16[3,64,512]{2,1,0:T(8,128)(2,1)S(1)}, bf16[3,64,512]{2,1,0:T(8,128)(2,1)}, u32[]{:S(2)}) copy-start(bf16[3,64,512]{2,1,0:T(8,128)(2,1)} %up_ref.3) | copy-start | bytes 589828
  39.1 17.5 %copy-start.6 = (bf16[3,1024,512]{2,1,0:T(8,128)(2,1)}, bf16[3,1024,512]{2,1,0:T(8,128)(2,1)S(1)}, u32[]{:S(2)}) copy-start(bf16[3,1024,512]{2,1,0:T(8,128)(2,1)S(1)} %get-tuple-element.41.moving_ref) | copy-start | bytes 9437188
  39.1 4.2 %collective-permute-start = (bf16[1088,128]{1,0:T(8,128)(2,1)S(1)}, bf16[1088,128]{1,0:T(8,128)(2,1)S(1)}, u32[]{:S(2)}, u32[]{:S(2)}) collective-permute-start(bf16[1088,128]{1,0:T(8,128)(2,1)S(1)} %get-tuple-element.45.own_ref), channel_id=1, source_target_pairs={{0,16},{16,0},{32,48},{48,32},{64,80},{80,64},{96,112},{112,96},{1... | collective-permute-start | bytes 835592 | tf_op jit(solution)/shard_map/ppermute | solution.py:598
  44.0 12.5 %collective-permute-start.1 = (bf16[576,128]{1,0:T(8,128)(2,1)S(1)}, bf16[576,128]{1,0:T(8,128)(2,1)S(1)}, u32[]{:S(2)}, u32[]{:S(2)}) collective-permute-start(bf16[576,128]{1,0:T(8,128)(2,1)S(1)} %get-tuple-element.46), channel_id=1, source_target_pairs={{0,32},{16,48},{32,64},{48,80},{64,96},{80,112},{96,0},{112,16},{1... | collective-permute-start | bytes 442376 | tf_op jit(solution)/shard_map/ppermute | solution.py:603
  45.4 11.1 %collective-permute-start.2 = (bf16[576,128]{1,0:T(8,128)(2,1)S(1)}, bf16[576,128]{1,0:T(8,128)(2,1)S(1)}, u32[]{:S(2)}, u32[]{:S(2)}) collective-permute-start(bf16[576,128]{1,0:T(8,128)(2,1)S(1)} %get-tuple-element.47), channel_id=1, source_target_pairs={{0,64},{16,80},{32,96},{48,112},{64,0},{80,16},{96,32},{112,48},{1... | collective-permute-start | bytes 442376 | tf_op jit(solution)/shard_map/ppermute | solution.py:603
  48.0 8.5 %collective-permute-start.3 = (bf16[576,128]{1,0:T(8,128)(2,1)S(1)}, bf16[576,128]{1,0:T(8,128)(2,1)S(1)}, u32[]{:S(2)}, u32[]{:S(2)}) collective-permute-start(bf16[576,128]{1,0:T(8,128)(2,1)S(1)} %get-tuple-element.48), channel_id=1, source_target_pairs={{0,96},{16,112},{32,0},{48,16},{64,32},{80,48},{96,64},{112,80},{1... | collective-permute-start | bytes 442376 | tf_op jit(solution)/shard_map/ppermute | solution.py:603
  61.1 13.0 %all-to-all-start.2 = ((bf16[16,96,128]{2,1,0:T(8,128)(2,1)}), bf16[16,96,128]{2,1,0:T(8,128)(2,1)S(1)}, u32[]{:S(2)}, u32[]{:S(2)}) async-start(bf16[16,96,128]{2,1,0:T(8,128)(2,1)} %get-tuple-element.49), calls=%async_computation.2 | async-start | bytes 786432 | tf_op jit(solution)/shard_map/all_to_all | solution.py:112
  64.7 1.9 %copy-start.5 = (bf16[3,1024,512]{2,1,0:T(8,128)(2,1)S(1)}, bf16[3,1024,512]{2,1,0:T(8,128)(2,1)}, u32[]{:S(2)}) copy-start(bf16[3,1024,512]{2,1,0:T(8,128)(2,1)} %get-tuple-element.36.grad_ref) | copy-start | bytes 9437188
  66.6 3.4 %copy-start.7 = (bf16[3,1024,512]{2,1,0:T(8,128)(2,1)S(1)}, bf16[3,1024,512]{2,1,0:T(8,128)(2,1)}, u32[]{:S(2)}) copy-start(bf16[3,1024,512]{2,1,0:T(8,128)(2,1)} %copy-done.6) | copy-start | bytes 9437188
  68.5 5.6 %collective-permute-start.4 = (bf16[96,512]{1,0:T(8,128)(2,1)S(1)}, bf16[96,512]{1,0:T(8,128)(2,1)S(1)}, u32[]{:S(2)}, u32[]{:S(2)}) collective-permute-start(bf16[96,512]{1,0:T(8,128)(2,1)S(1)} %get-tuple-element.52), channel_id=1, source_target_pairs={{0,16},{16,0},{32,48},{48,32},{64,80},{80,64},{96,112},{112,96},{1... | collective-permute-start | bytes 294920 | tf_op jit(solution)/shard_map/ppermute | solution.py:598
  69.9 21.5 %copy-start = (bf16[1024,384]{1,0:T(8,128)(2,1)S(1)}, bf16[1024,384]{1,0:T(8,128)(2,1)}, u32[]{:S(2)}) copy-start(bf16[1024,384]{1,0:T(8,128)(2,1)} %x_ref.3) | copy-start | bytes 2359300
  74.9 16.5 %all-to-all-start.3 = ((bf16[16,96,128]{2,1,0:T(8,128)(2,1)}), bf16[16,96,128]{2,1,0:T(8,128)(2,1)S(1)}, u32[]{:S(2)}, u32[]{:S(2)}) async-start(bf16[16,96,128]{2,1,0:T(8,128)(2,1)} %sum_spread.3), calls=%async_computation.3 | async-start | bytes 786432 | tf_op jit(solution)/shard_map/all_to_all | solution.py:112
  81.8 4.1 %collective-permute-start.7 = (bf16[96,512]{1,0:T(8,128)(2,1)S(1)}, bf16[96,512]{1,0:T(8,128)(2,1)S(1)}, u32[]{:S(2)}, u32[]{:S(2)}) collective-permute-start(bf16[96,512]{1,0:T(8,128)(2,1)S(1)} %add_all.4.refs_0_), channel_id=1, source_target_pairs={{0,96},{16,112},{32,0},{48,16},{64,32},{80,48},{96,64},{112,80},{1... | collective-permute-start | bytes 294920 | tf_op jit(solution)/shard_map/ppermute | solution.py:603
  82.0 5.3 %collective-permute-start.6 = (bf16[96,512]{1,0:T(8,128)(2,1)S(1)}, bf16[96,512]{1,0:T(8,128)(2,1)S(1)}, u32[]{:S(2)}, u32[]{:S(2)}) collective-permute-start(bf16[96,512]{1,0:T(8,128)(2,1)S(1)} %add_all.4.refs_0_), channel_id=1, source_target_pairs={{0,64},{16,80},{32,96},{48,112},{64,0},{80,16},{96,32},{112,48},{1... | collective-permute-start | bytes 294920 | tf_op jit(solution)/shard_map/ppermute | solution.py:603
  84.0 5.3 %collective-permute-start.5 = (bf16[96,512]{1,0:T(8,128)(2,1)S(1)}, bf16[96,512]{1,0:T(8,128)(2,1)S(1)}, u32[]{:S(2)}, u32[]{:S(2)}) collective-permute-start(bf16[96,512]{1,0:T(8,128)(2,1)S(1)} %add_all.4.refs_0_), channel_id=1, source_target_pairs={{0,32},{16,48},{32,64},{48,80},{64,96},{80,112},{96,0},{112,16},{1... | collective-permute-start | bytes 294920 | tf_op jit(solution)/shard_map/ppermute | solution.py:603
  92.3 2.4 %collective-permute-start.8 = (bf16[96,384]{1,0:T(8,128)(2,1)S(1)}, bf16[96,384]{1,0:T(8,128)(2,1)S(1)}, u32[]{:S(2)}, u32[]{:S(2)}) collective-permute-start(bf16[96,384]{1,0:T(8,128)(2,1)S(1)} %get-tuple-element.59), channel_id=1, source_target_pairs={{0,16},{16,0},{32,48},{48,32},{64,80},{80,64},{96,112},{112,96},{1... | collective-permute-start | bytes 221192 | tf_op jit(solution)/shard_map/ppermute | solution.py:598
  94.9 2.6 %collective-permute-start.9 = (f32[96,512]{1,0:T(8,128)S(1)}, f32[96,512]{1,0:T(8,128)S(1)}, u32[]{:S(2)}, u32[]{:S(2)}) collective-permute-start(f32[96,512]{1,0:T(8,128)S(1)} %add_all.6.own_ref), channel_id=1, source_target_pairs={{0,16},{16,0},{32,48},{48,32},{64,80},{80,64},{96,112},{112,96},{1... | collective-permute-start | bytes 589832 | tf_op jit(solution)/shard_map/ppermute | solution.py:598
  95.3 3.7 %collective-permute-start.12 = (bf16[96,384]{1,0:T(8,128)(2,1)S(1)}, bf16[96,384]{1,0:T(8,128)(2,1)S(1)}, u32[]{:S(2)}, u32[]{:S(2)}) collective-permute-start(bf16[96,384]{1,0:T(8,128)(2,1)S(1)} %add_all.5.refs_0_), channel_id=1, source_target_pairs={{0,96},{16,112},{32,0},{48,16},{64,32},{80,48},{96,64},{112,80},{1... | collective-permute-start | bytes 221192 | tf_op jit(solution)/shard_map/ppermute | solution.py:603
  95.4 4.7 %collective-permute-start.11 = (bf16[96,384]{1,0:T(8,128)(2,1)S(1)}, bf16[96,384]{1,0:T(8,128)(2,1)S(1)}, u32[]{:S(2)}, u32[]{:S(2)}) collective-permute-start(bf16[96,384]{1,0:T(8,128)(2,1)S(1)} %add_all.5.refs_0_), channel_id=1, source_target_pairs={{0,64},{16,80},{32,96},{48,112},{64,0},{80,16},{96,32},{112,48},{1... | collective-permute-start | bytes 221192 | tf_op jit(solution)/shard_map/ppermute | solution.py:603
  97.5 4.4 %collective-permute-start.10 = (bf16[96,384]{1,0:T(8,128)(2,1)S(1)}, bf16[96,384]{1,0:T(8,128)(2,1)S(1)}, u32[]{:S(2)}, u32[]{:S(2)}) collective-permute-start(bf16[96,384]{1,0:T(8,128)(2,1)S(1)} %add_all.5.refs_0_), channel_id=1, source_target_pairs={{0,32},{16,48},{32,64},{48,80},{64,96},{80,112},{96,0},{112,16},{1... | collective-permute-start | bytes 221192 | tf_op jit(solution)/shard_map/ppermute | solution.py:603
  101.9 3.0 %collective-permute-start.13 = (f32[96,384]{1,0:T(8,128)S(1)}, f32[96,384]{1,0:T(8,128)S(1)}, u32[]{:S(2)}, u32[]{:S(2)}) collective-permute-start(f32[96,384]{1,0:T(8,128)S(1)} %add_all.7.own_ref), channel_id=1, source_target_pairs={{0,16},{16,0},{32,48},{48,32},{64,80},{80,64},{96,112},{112,96},{1... | collective-permute-start | bytes 442376 | tf_op jit(solution)/shard_map/ppermute | solution.py:598

commit v4 on v3

--- a/solution.py
+++ b/solution.py
@@ -9,7 +9,8 @@
 
 F32 = jnp.float32
 BF16 = jnp.bfloat16
-CHUNK = 256
+CHUNK = 128
+BLOCK = 256
 VMEM_BYTES = 20 * 1024 * 1024
 NEGATIVE = -1e30
 
@@ -34,6 +35,24 @@
 
 def chunk_rows(c):
     return pl.ds(pl.multiple_of(c * CHUNK, CHUNK), CHUNK)
+
+
+def diagonal(a, b):
+    zero = jnp.zeros_like(a)
+    return jnp.concatenate(
+        [jnp.concatenate([a, zero], axis=1), jnp.concatenate([zero, b], axis=1)], axis=0
+    )
+
+
+def diagonal_of(pair):
+    return diagonal(pair[:, :128], pair[:, 128:])
+
+
+def widen(table, lane):
+    shape = (table.shape[0], 128)
+    return jnp.concatenate(
+        [jnp.broadcast_to(table[:, i : i + 1], shape) for i in (lane, lane + 1)], axis=1
+    )
 
 
 def cost(flops, moved):
@@ -57,26 +76,26 @@
 
 
 def piece_shape(rows, width):
-    return (rows // CHUNK * 4, width // 2, CHUNK // 2)
+    return (rows // BLOCK * 4, width // 2, BLOCK // 2)
 
 
 def piece_spec(width):
-    return pl.BlockSpec((4, width // 2, CHUNK // 2), lambda i: (i, 0, 0))
+    return pl.BlockSpec((4, width // 2, BLOCK // 2), lambda i: (i, 0, 0))
 
 
 def low_kernel(x_ref, down_ref, out_ref, x_held, down_held, sems):
-    count = x_ref.shape[0] // CHUNK
+    count = x_ref.shape[0] // BLOCK
     first = pltpu.make_async_copy(down_ref, down_held, sems.at[count])
     first.start()
     copies = []
     for c in range(count):
-        rows = pl.ds(c * CHUNK, CHUNK)
+        rows = pl.ds(c * BLOCK, BLOCK)
         copies.append(pltpu.make_async_copy(x_ref.at[rows], x_held.at[rows], sems.at[c]))
         copies[c].start()
     first.wait()
     for c in range(count):
         copies[c].wait()
-        part = dot_nt(down_held[...], x_held[c * CHUNK : (c + 1) * CHUNK, :])
+        part = dot_nt(down_held[...], x_held[c * BLOCK : (c + 1) * BLOCK, :])
         store_pieces(out_ref.at[pl.ds(4 * c, 4)], part.astype(BF16))
 
 
@@ -91,7 +110,7 @@
         scratch_shapes=[
             pltpu.VMEM(x.shape, BF16),
             pltpu.VMEM(down.shape, BF16),
-            pltpu.SemaphoreType.DMA((rows // CHUNK + 1,)),
+            pltpu.SemaphoreType.DMA((rows // BLOCK + 1,)),
         ],
         compiler_params=params(),
         name="partial_low",
@@ -109,7 +128,7 @@
 
 
 def exchange(pieces):
-    return lax.all_to_all(pieces, "head", 0, 0)
+    return lax.all_to_all(pieces, ("z", "x"), 0, 0)
 
 
 def sum_spread(pieces):
@@ -139,6 +158,7 @@
     lower = jnp.where(row_i >= col_i, 1.0, 0.0).astype(BF16)
     count = rows // CHUNK
     enters, leaves, passes = [], [], []
+    prefix = jnp.ones((heads, 128), F32)
     for c in range(count):
         span = slice(c * CHUNK, (c + 1) * CHUNK)
         piece = both[:, span]
@@ -163,7 +183,11 @@
         passes.append(jnp.where(seg_end == 0.0, jnp.exp(cum_end), 0.0))
         end_row = by_row[:, CHUNK - 1 : CHUNK]
         passing_col = jnp.where(end_row[heads : heads + 1] == 0.0, jnp.exp(end_row[:heads]), 0.0)
-        pass_ref[c * heads : (c + 1) * heads, :] = jnp.broadcast_to(passing_col, (heads, 128))
+        passing_rows_here = jnp.broadcast_to(passing_col, (heads, 128))
+        pass_ref[c * heads : (c + 1) * heads, :] = passing_rows_here
+        first = (count + c) * heads
+        pass_ref[first : first + heads, :] = prefix
+        prefix = prefix * passing_rows_here
     before = jnp.ones((1, heads), F32)
     for c in range(count):
         span = slice(c * CHUNK, (c + 1) * CHUNK)
@@ -184,7 +208,7 @@
         out_shape=(
             jax.ShapeDtypeStruct((8, rows), F32),
             jax.ShapeDtypeStruct((rows, 128), F32),
-            jax.ShapeDtypeStruct((count * heads, 128), F32),
+            jax.ShapeDtypeStruct((2 * count * heads, 128), F32),
         ),
         in_specs=[SMEM, VMEM, VMEM],
         out_specs=(VMEM, VMEM, VMEM),
@@ -204,29 +228,31 @@
     heads = features // 128
     size = heads * 128
     copies = []
-    for c in range(chunks):
-        rows = pl.ds(c * CHUNK, CHUNK)
-        copies.append(pltpu.make_async_copy(frozen_ref.at[:, rows], held.at[:, rows], sems.at[c]))
-        copies[c].start()
+    for n in range(frozen_ref.shape[1] // BLOCK):
+        rows = pl.ds(n * BLOCK, BLOCK)
+        copies.append(pltpu.make_async_copy(frozen_ref.at[:, rows], held.at[:, rows], sems.at[n]))
+        copies[n].start()
     states = [jnp.zeros((128, 128), F32)] * heads
-    for c in range(chunks):
-        rows = pl.ds(c * CHUNK, CHUNK)
-        low = load_pieces(low_ref.at[pl.ds(4 * c, 4)])
-        copies[c].wait()
+    for n, copy in enumerate(copies):
+        low = load_pieces(low_ref.at[pl.ds(4 * n, 4)])
+        copy.wait()
+        rows = pl.ds(n * BLOCK, BLOCK)
         for i in range(3):
             lifted = dot_tn(low[i * rank : (i + 1) * rank, :], up_ref[i])
             moving_ref[i, rows, :] = (held[i, rows, :].astype(F32) + lifted).astype(BF16)
-        col = col_ref[rows, :]
-        for h in range(heads):
-            span = slice(h * 128, (h + 1) * 128)
-            passing = pass_ref[c * heads + h : c * heads + h + 1, :]
-            leave = col[:, LEAVE + h : LEAVE + h + 1]
-            enter = col[:, ENTER + h : ENTER + h + 1]
-            keyed = (moving_ref[1, rows, span].astype(F32) * leave).astype(BF16)
-            scaled = (moving_ref[0, rows, span].astype(F32) * enter).astype(BF16)
-            before_ref[c, h] = states[h].astype(BF16)
-            states[h] = passing * states[h] + dot_tn(keyed, moving_ref[2, rows, span])
-            returning[c, h] = dot_tn(scaled, grad_ref[rows, span])
+        for c in range(n * BLOCK // CHUNK, (n + 1) * BLOCK // CHUNK):
+            rows = pl.ds(c * CHUNK, CHUNK)
+            col = col_ref[rows, :]
+            for h in range(heads):
+                span = slice(h * 128, (h + 1) * 128)
+                passing = pass_ref[c * heads + h : c * heads + h + 1, :]
+                leave = col[:, LEAVE + h : LEAVE + h + 1]
+                enter = col[:, ENTER + h : ENTER + h + 1]
+                keyed = (moving_ref[1, rows, span].astype(F32) * leave).astype(BF16)
+                scaled = (moving_ref[0, rows, span].astype(F32) * enter).astype(BF16)
+                before_ref[c, h] = states[h].astype(BF16)
+                states[h] = passing * states[h] + dot_tn(keyed, moving_ref[2, rows, span])
+                returning[c, h] = dot_tn(scaled, grad_ref[rows, span])
     for h in range(heads):
         back = jnp.zeros((128, 128), F32)
         whole = jnp.ones((1, 128), F32)
@@ -267,7 +293,7 @@
         scratch_shapes=[
             pltpu.VMEM(states.shape, F32),
             pltpu.VMEM(frozen.shape, BF16),
-            pltpu.SemaphoreType.DMA((count,)),
+            pltpu.SemaphoreType.DMA((rows // BLOCK,)),
         ],
         compiler_params=params(),
         cost_estimate=cost(4e9, 10e6),
@@ -330,29 +356,36 @@
     row_i = lax.broadcasted_iota(jnp.int32, (CHUNK, CHUNK), 0)
     col_i = lax.broadcasted_iota(jnp.int32, (CHUNK, CHUNK), 1)
 
-    @pl.loop(0, moving_ref.shape[1] // CHUNK)
+    @pl.loop(0, moving_ref.shape[1] // CHUNK, unroll=4)
     def _(c):
         rows = chunk_rows(c)
         col = col_ref[rows, :]
         row = row_ref[:, rows]
         allowed = (row_i <= col_i) & (col[:, SEG : SEG + 1] == row[SEG : SEG + 1, :])
         shut = jnp.where(allowed, 0.0, NEGATIVE)
-        for h in range(heads):
-            span = slice(h * 128, (h + 1) * 128)
+        for h in range(0, heads, 2):
+            span = slice(h * 128, (h + 2) * 128)
             q = moving_ref[0, rows, span]
             k = moving_ref[1, rows, span]
             v = moving_ref[2, rows, span]
             g = grad_ref[rows, span]
-            weights = jnp.exp((row[h : h + 1, :] - col[:, h : h + 1]) + shut)
-            a = (dot_nt(k, q) * weights).astype(BF16)
-            b = (dot_nt(v, g) * weights).astype(BF16)
-            enter = col[:, ENTER + h : ENTER + h + 1]
-            leave = col[:, LEAVE + h : LEAVE + h + 1]
-            before = before_ref[c, h]
-            after = after_ref[c, h]
-            part_ref[0, rows, span] = dot_tn(b, k) + enter * dot_nt(g, before)
-            part_ref[1, rows, span] = dot_nn(b, q) + leave * dot_nt(v, after)
-            part_ref[2, rows, span] = dot_nn(a, g) + leave * dot_nn(k, after)
+            weights = jnp.exp(
+                jnp.concatenate(
+                    [(row[i : i + 1, :] - col[:, i : i + 1]) + shut for i in (h, h + 1)], axis=1
+                )
+            )
+            queries = diagonal_of(q)
+            cotangents = diagonal_of(g)
+            before = diagonal(before_ref[c, h], before_ref[c, h + 1])
+            after = diagonal(after_ref[c, h], after_ref[c, h + 1])
+            enter = widen(col, ENTER + h)
+            leave = widen(col, LEAVE + h)
+            a = (dot_nt(k, queries) * weights).astype(BF16)
+            b = (dot_nt(v, cotangents) * weights).astype(BF16)
+            turned = jnp.concatenate([b[:, :128].T, b[:, 128:].T], axis=1)
+            part_ref[0, rows, span] = dot_nn(turned, diagonal_of(k)) + enter * dot_nt(g, before)
+            part_ref[1, rows, span] = dot_nn(b, queries) + leave * dot_nt(v, after)
+            part_ref[2, rows, span] = dot_nn(a, cotangents) + leave * dot_nn(k, after)
 
 
 def inside(moving, grad, row, col, before, after):
@@ -367,47 +400,70 @@
     )(moving, grad, row, col, before, after)
 
 
-def late_kernel(moving_ref, row_ref, col_ref, before_ref, state_ref, attn_ref):
+def late_kernel(first_block, moving_ref, row_ref, col_ref, pass_ref, before_ref, state_ref, *refs):
+    attn_ref = refs[-1]
     features = moving_ref.shape[2]
     heads = features // 128
     inverse = 1.0 / 128.0
+    step = first_block + pl.program_id(0)
+    prefix_base = pass_ref.shape[0] // 2
     row_i = lax.broadcasted_iota(jnp.int32, (CHUNK, CHUNK), 0)
     col_i = lax.broadcasted_iota(jnp.int32, (CHUNK, CHUNK), 1)
-    col = col_ref[...]
-    allowed = (row_i >= col_i) & (col[:, SEG : SEG + 1] == row_ref[SEG : SEG + 1, :])
-    shut = jnp.where(allowed, 0.0, NEGATIVE)
-    for h in range(heads):
-        span = slice(h * 128, (h + 1) * 128)
-        q = moving_ref[0, :, span]
-        weights = jnp.exp((col[:, h : h + 1] - row_ref[h : h + 1, :]) + shut)
-        a = (dot_nt(q, moving_ref[1, :, span]) * weights).astype(BF16)
-        enter = col[:, ENTER + h : ENTER + h + 1]
-        enter_all = col[:, ENTER_ALL + h : ENTER_ALL + h + 1]
-        out = dot_nn(a, moving_ref[2, :, span])
-        out = out + enter * dot_nn(q, before_ref[0, h]) + enter_all * dot_nn(q, state_ref[h])
-        attn_ref[:, span] = (out * inverse).astype(BF16)
-
-
-def late(moving, row, col, before, state):
+    for n in range(BLOCK // CHUNK):
+        rows = pl.ds(n * CHUNK, CHUNK)
+        col = col_ref[rows, :]
+        row = row_ref[:, rows]
+        allowed = (row_i >= col_i) & (col[:, SEG : SEG + 1] == row[SEG : SEG + 1, :])
+        shut = jnp.where(allowed, 0.0, NEGATIVE)
+        first = prefix_base + (step * (BLOCK // CHUNK) + n) * heads
+        states = []
+        for h in range(heads):
+            prefix = pass_ref[pl.ds(first + h, 1), :]
+            state = before_ref[n, h].astype(F32) + prefix * state_ref[h].astype(F32)
+            states.append(state.astype(BF16))
+        for h in range(0, heads, 2):
+            span = slice(h * 128, (h + 2) * 128)
+            q = moving_ref[0, rows, span]
+            weights = jnp.exp(
+                jnp.concatenate(
+                    [(col[:, i : i + 1] - row[i : i + 1, :]) + shut for i in (h, h + 1)], axis=1
+                )
+            )
+            a = (dot_nt(q, diagonal_of(moving_ref[1, rows, span])) * weights).astype(BF16)
+            out = dot_nn(a, diagonal_of(moving_ref[2, rows, span]))
+            out = out + widen(col, ENTER + h) * dot_nn(q, diagonal(states[h], states[h + 1]))
+            attn_ref[rows, span] = (out * inverse).astype(BF16)
+
+
+def late(moving, row, col, passes, before, state, first_block, block_count, earlier=None):
     _, rows, features = moving.shape
     heads = features // 128
-    count = rows // CHUNK
-    return pl.pallas_call(
-        late_kernel,
+    far = pl.BlockSpec(memory_space=pltpu.HBM)
+    return pl.pallas_call(
+        functools.partial(late_kernel, first_block),
         out_shape=jax.ShapeDtypeStruct((rows, features), BF16),
-        grid=(count,),
+        grid=(block_count,),
         in_specs=[
-            pl.BlockSpec((3, CHUNK, features), lambda i: (0, i, 0)),
-            pl.BlockSpec((8, CHUNK), lambda i: (0, i)),
-            pl.BlockSpec((CHUNK, 128), lambda i: (i, 0)),
-            pl.BlockSpec((1, heads, 128, 128), lambda i: (i, 0, 0, 0)),
+            pl.BlockSpec((3, BLOCK, features), lambda i: (0, first_block + i, 0)),
+            pl.BlockSpec((8, BLOCK), lambda i: (0, first_block + i)),
+            pl.BlockSpec((BLOCK, 128), lambda i: (first_block + i, 0)),
+            pl.BlockSpec(passes.shape, lambda i: (0, 0)),
+            pl.BlockSpec((BLOCK // CHUNK, heads, 128, 128), lambda i: (first_block + i, 0, 0, 0)),
             pl.BlockSpec(state.shape, lambda i: (0, 0, 0)),
-        ],
-        out_specs=pl.BlockSpec((CHUNK, features), lambda i: (i, 0)),
+        ]
+        + ([] if earlier is None else [far]),
+        out_specs=pl.BlockSpec((BLOCK, features), lambda i: (first_block + i, 0)),
+        input_output_aliases={} if earlier is None else {6: 0},
         compiler_params=params(dimension_semantics=("arbitrary",)),
         cost_estimate=cost(6e9, 6e6),
         name="late",
-    )(moving, row, col, before, state)
+    )(
+        pltpu.with_memory_space_constraint(moving, pltpu.HBM),
+        row, col, passes,
+        pltpu.with_memory_space_constraint(before, pltpu.HBM),
+        state,
+        *([] if earlier is None else [earlier]),
+    )
 
 
 def store_halves(core, total, keep_ref, send_ref):
@@ -416,52 +472,17 @@
     send_ref[...] = total[pl.ds(pl.multiple_of((1 - core) * half, 16), half), :].astype(BF16)
 
 
-def up_kernel(meta_ref, low_ref, grad_ref, keep_ref, send_ref, total):
-    step = pl.program_id(0)
-    rank = total.shape[0] // 3
-
-    @pl.when(step == 0)
-    def _():
-        total[...] = jnp.zeros_like(total)
-
-    low = load_pieces(low_ref)
-    for c in range(3):
-        rows = slice(c * rank, (c + 1) * rank)
-        total[rows, :] += dot_nn(low[rows, :], grad_ref[c])
-
-    @pl.when(step == pl.num_programs(0) - 1)
-    def _():
-        store_halves(meta_ref[2], total, keep_ref, send_ref)
-
-
-def partial_up(meta, low, grads):
-    _, rows, features = grads.shape
-    width = 2 * low.shape[1]
-    half = jax.ShapeDtypeStruct((width // 2, features), BF16)
-    return pl.pallas_call(
-        up_kernel,
-        out_shape=(half, half),
-        grid=(rows // CHUNK,),
-        in_specs=[
-            SMEM,
-            piece_spec(width),
-            pl.BlockSpec((3, CHUNK, features), lambda i: (0, i, 0)),
-        ],
-        out_specs=(pl.BlockSpec(half.shape, lambda i: (0, 0)),) * 2,
-        scratch_shapes=[pltpu.VMEM((width, features), F32)],
-        compiler_params=params(dimension_semantics=("arbitrary",)),
-        cost_estimate=cost(2e9, 4e6),
-        name="partial_up",
-    )(meta, low, grads)
-
-
-def finish_kernel(chips, meta_ref, moving_ref, g_ref, part_ref, col_ref, up_ref, mate_ref, *refs):
+def finish_kernel(
+    chips, meta_ref, moving_ref, g_ref, part_ref, col_ref, low_ref, up_ref, mate_ref, *refs
+):
     message_refs = refs[: chips - 1]
-    out_ref, low_grad_ref, state_in, back_in, grad_ref, sems = refs[chips - 1 :]
+    out_ref, low_grad_ref, state_in, keep_ref, send_ref = refs[chips - 1 : chips + 4]
+    back_in, grad_ref, total, sems = refs[chips + 4 :]
+    rank = up_ref.shape[1]
     features = moving_ref.shape[2]
     heads = features // 128
     size = heads * 128
-    count = moving_ref.shape[1] // CHUNK
+    count = moving_ref.shape[1] // BLOCK
     inverse = 1.0 / 128.0
     y = meta_ref[1]
     second = meta_ref[2] == 1
@@ -485,61 +506,68 @@
         state_in[h] = jnp.where(second, mate_pass * state + mate_state, state).astype(BF16)
         back_in[h] = jnp.where(second, back, mate_pass * back + mate_back).astype(BF16)
     copies = []
-    for c in range(count):
-        rows = pl.ds(c * CHUNK, CHUNK)
+    for n in range(count):
+        rows = pl.ds(n * BLOCK, BLOCK)
         col = col_ref[rows, :]
-        for h in range(heads):
-            span = slice(h * 128, (h + 1) * 128)
-            k = moving_ref[1, rows, span]
-            v = moving_ref[2, rows, span]
-            g = g_ref[rows, span]
-            enter = col[:, ENTER_ALL + h : ENTER_ALL + h + 1]
-            leave = col[:, LEAVE_ALL + h : LEAVE_ALL + h + 1]
-            state = state_in[h]
-            back = back_in[h]
-            query = part_ref[0, rows, span] + enter * dot_nt(g, state)
-            key = part_ref[1, rows, span] + leave * dot_nt(v, back)
-            value = part_ref[2, rows, span] + leave * dot_nn(k, back)
+        for h in range(0, heads, 2):
+            span = slice(h * 128, (h + 2) * 128)
+            enter = widen(col, ENTER_ALL + h)
+            leave = widen(col, LEAVE_ALL + h)
+            state = diagonal(state_in[h], state_in[h + 1])
+            back = diagonal(back_in[h], back_in[h + 1])
+            query = part_ref[0, rows, span] + enter * dot_nt(g_ref[rows, span], state)
+            key = part_ref[1, rows, span] + leave * dot_nt(moving_ref[2, rows, span], back)
+            value = part_ref[2, rows, span] + leave * dot_nn(moving_ref[1, rows, span], back)
             for i, result in enumerate((query, key, value)):
                 grad_ref[i, rows, span] = (result * inverse).astype(BF16)
-        copies.append(pltpu.make_async_copy(grad_ref.at[:, rows], out_ref.at[:, rows], sems.at[c]))
-        copies[c].start()
+        copies.append(pltpu.make_async_copy(grad_ref.at[:, rows], out_ref.at[:, rows], sems.at[n]))
+        copies[n].start()
         low_grad = [dot_nt(up_ref[i], grad_ref[i, rows, :]).astype(BF16) for i in range(3)]
-        store_pieces(low_grad_ref.at[pl.ds(4 * c, 4)], jnp.concatenate(low_grad, axis=0))
+        store_pieces(low_grad_ref.at[pl.ds(4 * n, 4)], jnp.concatenate(low_grad, axis=0))
+        low = load_pieces(low_ref.at[pl.ds(4 * n, 4)])
+        for i in range(3):
+            lanes = slice(i * rank, (i + 1) * rank)
+            term = dot_nn(low[lanes, :], grad_ref[i, rows, :])
+            total[lanes, :] = term if n == 0 else total[lanes, :] + term
+    store_halves(meta_ref[2], total, keep_ref, send_ref)
     for copy in copies:
         copy.wait()
 
 
-def finish(meta, moving, grad, part, col, up, mate, messages):
+def finish(meta, moving, grad, part, col, low, up, mate, messages):
     _, rows, features = moving.shape
     heads = features // 128
+    width = up.shape[0] * up.shape[1]
+    half = jax.ShapeDtypeStruct((width // 2, features), BF16)
     chips = len(messages) + 1
-    width = up.shape[0] * up.shape[1]
     return pl.pallas_call(
         functools.partial(finish_kernel, chips),
         out_shape=(
             jax.ShapeDtypeStruct(moving.shape, BF16),
             jax.ShapeDtypeStruct(piece_shape(rows, width), BF16),
             jax.ShapeDtypeStruct((heads, 128, 128), BF16),
+            half,
+            half,
         ),
-        in_specs=[SMEM] + [VMEM] * (6 + len(messages)),
-        out_specs=(pl.BlockSpec(memory_space=pltpu.HBM), VMEM, VMEM),
+        in_specs=[SMEM] + [VMEM] * (7 + len(messages)),
+        out_specs=(pl.BlockSpec(memory_space=pltpu.HBM),) + (VMEM,) * 4,
         scratch_shapes=[
             pltpu.VMEM((heads, 128, 128), BF16),
             pltpu.VMEM(moving.shape, BF16),
-            pltpu.SemaphoreType.DMA((rows // CHUNK,)),
+            pltpu.VMEM((width, features), F32),
+            pltpu.SemaphoreType.DMA((rows // BLOCK,)),
         ],
         compiler_params=params(),
         cost_estimate=cost(4e9, 14e6),
         name="finish",
-    )(meta, moving, grad, part, col, up, mate, *messages)
+    )(meta, moving, grad, part, col, low, up, mate, *messages)
 
 
 def down_kernel(meta_ref, x_ref, grad_ref, keep_ref, send_ref, total):
     value = jnp.zeros(total.shape, F32)
-    for c in range(x_ref.shape[0] // CHUNK):
+    for c in range(x_ref.shape[0] // BLOCK):
         low_grad = load_pieces(grad_ref.at[pl.ds(4 * c, 4)])
-        value = value + dot_nn(low_grad, x_ref[c * CHUNK : (c + 1) * CHUNK, :])
+        value = value + dot_nn(low_grad, x_ref[c * BLOCK : (c + 1) * BLOCK, :])
     total[...] = value
     store_halves(meta_ref[2], total, keep_ref, send_ref)
 
@@ -595,41 +623,45 @@
 
 
 def to_mate(a):
-    return lax.ppermute(a, "seq", [(i, i ^ 1) for i in range(lax.axis_size("seq"))])
+    return lax.ppermute(a, "core", [(0, 1), (1, 0)])
 
 
 def along_y(a, k):
-    count = lax.axis_size("seq")
-    return lax.ppermute(a, "seq", [(i, (i + 2 * k) % count) for i in range(count)])
+    count = lax.axis_size("y")
+    return lax.ppermute(a, "y", [(i, (i + k) % count) for i in range(count)])
 
 
 def local(inputs, frozen, adapter_down, adapter_up, out_grad, log_decay, doc_start, lengths):
-    device = lax.axis_index("seq")
-    chips = lax.axis_size("seq") // 2
+    y, core = lax.axis_index("y"), lax.axis_index("core")
+    chips = lax.axis_size("y")
     rank = adapter_up.shape[1]
-    meta = jnp.stack([lengths[device], device // 2, device % 2]).astype(jnp.int32)
+    meta = jnp.stack([lengths[2 * y + core], y, core]).astype(jnp.int32)
     down = jnp.swapaxes(adapter_down, 1, 2).reshape(3 * rank, inputs.shape[1])
     row, col, passes = decay_tables(meta, log_decay, doc_start)
     low = exchange(sum_spread(exchange(partial_low(inputs, down))))
     moving, before, after, summary = project(frozen, low, adapter_up, out_grad, col, passes)
     mate = to_mate(summary)
-    outgoing = join(meta, summary, mate, chips)
-    messages = [along_y(m, k + 1) for k, m in enumerate(outgoing)]
+    messages = [along_y(m, k + 1) for k, m in enumerate(join(meta, summary, mate, chips))]
     part = inside(moving, out_grad, row, col, before, after)
-    grads, low_grad_part, state = finish(meta, moving, out_grad, part, col, adapter_up, mate, messages)
-    up_keep, up_send = partial_up(meta, low, grads)
-    attn = late(moving, row, col, before, state)
+    grads, low_grad_part, state, up_keep, up_send = finish(
+        meta, moving, out_grad, part, col, low, adapter_up, mate, messages
+    )
     up_chip = add_all([up_keep, to_mate(up_send)], BF16)
-    pieces, up_chip, attn = lax.optimization_barrier((exchange(low_grad_part), up_chip, attn))
     up_parts = [up_chip] + [along_y(up_chip, k) for k in range(1, chips)]
-    low_grad, *up_parts = lax.optimization_barrier([exchange(sum_spread(pieces))] + up_parts)
+    pieces, up_chip = lax.optimization_barrier((exchange(low_grad_part), up_chip))
+    half = inputs.shape[0] // BLOCK // 2
+    first_half = late(moving, row, col, passes, before, state, 0, half)
+    low_grad, first_half, *up_parts = lax.optimization_barrier(
+        [exchange(sum_spread(pieces)), first_half] + up_parts
+    )
     down_keep, down_send = partial_down(meta, inputs, low_grad)
     down_chip = add_all([down_keep, to_mate(down_send)], BF16)
-    down_chip, *up_parts = lax.optimization_barrier([down_chip] + up_parts)
+    down_chip, state, *up_parts = lax.optimization_barrier([down_chip, state] + up_parts)
     down_parts = [down_chip] + [along_y(down_chip, k) for k in range(1, chips)]
     up_half = add_all(up_parts, F32)
     up_total = join_halves(meta, up_half, to_mate(up_half))
-    up_total, *down_parts = lax.optimization_barrier([up_total] + down_parts)
+    attn = late(moving, row, col, passes, before, state, half, half, first_half)
+    up_total, attn, *down_parts = lax.optimization_barrier([up_total, attn] + down_parts)
     down_half = add_all(down_parts, F32)
     down_total = join_halves(meta, down_half, to_mate(down_half))
     down_total = jnp.swapaxes(down_total.reshape(3, rank, inputs.shape[1]), 1, 2)
@@ -637,20 +669,28 @@
 
 
 def solution(mesh):
+    seq, head = mesh.shape["seq"], mesh.shape["head"]
+    side = 1
+    while side * side < head:
+        side *= 2
+    mesh = jax.sharding.Mesh(
+        mesh.devices.reshape(seq // 2, 2, head // side, side), ("y", "core", "z", "x")
+    )
+    seq, head = ("y", "core"), ("z", "x")
     in_specs = (
-        P("seq", "head"),
-        P(None, "seq", "head"),
-        P(None, "head", None),
-        P(None, None, "head"),
-        P("seq", "head"),
-        P("head", "seq"),
-        P("seq"),
+        P(seq, head),
+        P(None, seq, head),
+        P(None, head, None),
+        P(None, None, head),
+        P(seq, head),
+        P(head, seq),
+        P(seq),
         P(),
     )
     out_specs = (
-        P("seq", "head"),
-        P(None, "seq", "head"),
-        P(None, "head", None),
-        P(None, None, "head"),
+        P(seq, head),
+        P(None, seq, head),
+        P(None, head, None),
+        P(None, None, head),
     )
     return jax.shard_map(local, mesh=mesh, in_specs=in_specs, out_specs=out_specs, check_vma=False)

time: 107 us -> 103 us (0.963)
  local copies, waits for them, and re-layouts: 3.16 us -> 1.28 us
  starting transfers between devices: 40.4 us -> 38.6 us
    ppermute x14, waiting for transfers between devices: 11.5 us -> 4.08 us  [the longest x5 4.05 us: to_mate(): return lax.ppermute(a, 'core', [(0, 1), (1, 0)])]
    all_to_all x4, waiting for transfers between devices: 15.8 us -> 23.2 us  [exchange(): return lax.all_to_all(pieces, ('z', 'x'), 0, 0)]
    all_to_all x4, starting transfers between devices: 22.4 us -> 19.1 us  [exchange(): return lax.all_to_all(pieces, ('z', 'x'), 0, 0)]
    unnamed x16 -> x14, local copies, waits for them, and re-layouts: 1.92 us -> 0.04 us
    ppermute x14, starting transfers between devices: 17.9 us -> 19.4 us  [the longest x5 9.88 us: to_mate(): return lax.ppermute(a, 'core', [(0, 1), (1, 0)])]
  transfers between devices with their start and end apart: 18 -> 18, of which waited for: 12 -> 8; matrix products, arithmetic and copies ran while one was open for 2% -> 2% of each run, Pallas kernels for 15% -> 16%
where the time goes in v4:
time: 103 us
  starting transfers between devices  38.6 us (37%)
  Pallas kernels  34 us (33%)
  waiting for transfers between devices  27.2 us (26%)
  local copies, waits for them, and re-layouts  1.28 us (1%)
    all_to_all x4, waiting for transfers between devices, exchange(): return lax.all_to_all(pieces, ('z', 'x'), 0, 0)  23.2 us
    all_to_all x4, starting transfers between devices, exchange(): return lax.all_to_all(pieces, ('z', 'x'), 0, 0)  19.1 us
    ppermute x5, starting transfers between devices, to_mate(): return lax.ppermute(a, 'core', [(0, 1), (1, 0)])  9.88 us
    ppermute x9, starting transfers between devices, along_y(): return lax.ppermute(a, 'y', [(i, (i + k) % count) for i in range(count)])  9.56 us
    pallas_call x1, Pallas kernels, inside(): pl.pallas_call(inside_kernel, out_shape=jax.ShapeDtypeStruct(moving.shape...  6.71 us
    pallas_call x2, Pallas kernels, late(): pl.pallas_call(functools.partial(late_kernel, first_block), out_shape=jax...  6.21 us
    pallas_call x1, Pallas kernels, project(): pl.pallas_call(project_kernel, out_shape=(jax.ShapeDtypeStruct((3, rows,...  5.73 us
    pallas_call x1, Pallas kernels, finish(): pl.pallas_call(functools.partial(finish_kernel, chips), out_shape=(jax.Sh...  4.64 us
  transfers between devices with their start and end apart: 18, of which 8 were waited for; matrix products, arithmetic and copies ran while one was open for 2% of the time, Pallas kernels for 16%

profile of v4, /device:TPU:1, one launch (start us, length us, event | category | flops | bytes accessed | tf_op | source)
XLA Modules:
  0.0 102.7 jit_solution(4772011236539689955)
XLA Ops:
  0.7 2.9 %partial_low.1 = bf16[16,96,128]{2,1,0:T(8,128)(2,1)} custom-call(bf16[1024,384]{1,0:T(8,128)(2,1)} %x_ref.3, bf16[192,384]{1,0:T(8,128)(2,1)} %bitcast.13), custom_call_target="tpu_custom_call" | custom-call | tf_op jit(solution)/shard_map/partial_low/pallas_call | solution.py:105
  3.6 8.4 %all-to-all-start = ((bf16[16,96,128]{2,1,0:T(8,128)(2,1)}), bf16[16,96,128]{2,1,0:T(8,128)(2,1)S(1)}, u32[]{:S(2)}, u32[]{:S(2)}) async-start(bf16[16,96,128]{2,1,0:T(8,128)(2,1)} %partial_low.1), calls=%async_computation | async-start | bytes 786432 | tf_op jit(solution)/shard_map/all_to_all | solution.py:131
  12.0 1.2 %dynamic_slice.3 = s32[1]{0:T(128)} dynamic-slice(s32[8]{0:T(128)} %param.15, s32[]{:T(128)S(6)} %select_n.3), dynamic_slice_sizes={1} | dynamic-slice | bytes 12 | tf_op jit(solution)/shard_map/dynamic_slice | solution.py:638
  13.3 0.7 pad_add_fusion.meta_ref
  14.0 7.2 %all-to-all-done.in_ref = bf16[16,96,128]{2,1,0:T(8,128)(2,1)S(1)} async-done(((bf16[16,96,128]{2,1,0:T(8,128)(2,1)}), bf16[16,96,128]{2,1,0:T(8,128)(2,1)S(1)}, u32[]{:S(2)}, u32[]{:S(2)}) %all-to-all-start) | async-done | bytes 393248 | tf_op jit(solution)/shard_map/all_to_all | solution.py:131
  21.2 0.8 sum_spread.2
  22.0 3.6 %all-to-all-start.1 = ((bf16[16,96,128]{2,1,0:T(8,128)(2,1)}), bf16[16,96,128]{2,1,0:T(8,128)(2,1)S(1)}, u32[]{:S(2)}, u32[]{:S(2)}) async-start(bf16[16,96,128]{2,1,0:T(8,128)(2,1)} %sum_spread.2), calls=%async_computation.1 | async-start | bytes 786432 | tf_op jit(solution)/shard_map/all_to_all | solution.py:131
  25.6 0.0 copy-start.1
  25.6 0.0 copy-start.2
  25.6 1.8 %decay_tables.1 = (f32[8,1024]{1,0:T(8,128)S(1)}, f32[1024,128]{1,0:T(8,128)S(1)}, f32[64,128]{1,0:T(8,128)S(1)}) custom-call(s32[3]{0:T(128)S(1)} %pad_add_fusion.meta_ref, bf16[4,1024]{1,0:T(4,128)(2,1)S(1)} %copy-done.3, s32[1,1024]{1,0:T(1,128)S(1)} %bitcast.10), custom_call_target="tpu_custom_call" | custom-call | flops 4000000000 | bytes 1000000 | tf_op jit(solution)/shard_map/decay_tables/pallas_call | solution.py:206
  27.4 6.4 %all-to-all-done.1.low_ref = bf16[16,96,128]{2,1,0:T(8,128)(2,1)S(1)} async-done(((bf16[16,96,128]{2,1,0:T(8,128)(2,1)}), bf16[16,96,128]{2,1,0:T(8,128)(2,1)S(1)}, u32[]{:S(2)}, u32[]{:S(2)}) %all-to-all-start.1) | async-done | bytes 393248 | tf_op jit(solution)/shard_map/all_to_all | solution.py:131
  33.8 5.7 %project.1 = (bf16[3,1024,512]{2,1,0:T(8,128)(2,1)S(1)}, bf16[8,4,128,128]{3,2,1,0:T(8,128)(2,1)S(1)}, bf16[8,4,128,128]{3,2,1,0:T(8,128)(2,1)S(1)}, bf16[1088,128]{1,0:T(8,128)(2,1)S(1)}) custom-call(bf16[3,1024,512]{2,1,0:T(8,128)(2,1)} %frozen_ref.1, bf16[16,96,128]{2,1,0:T(8,128)(2,1)S(1)} %all-to-all-done.1.low_ref, bf16[3,64,512]{2,1,0:T(8,128)(2,1)S(1)} %copy-done.2, ...), custom_call_target="tpu_custom_call" | custom-call | flops 4000000000 | bytes 10000000 | tf_op jit(solution)/shard_map/project/pallas_call | solution.py:283
  39.6 3.1 %collective-permute-start = (bf16[1088,128]{1,0:T(8,128)(2,1)S(1)}, bf16[1088,128]{1,0:T(8,128)(2,1)S(1)}, u32[]{:S(2)}, u32[]{:S(2)}) collective-permute-start(bf16[1088,128]{1,0:T(8,128)(2,1)S(1)} %get-tuple-element.46.own_ref), channel_id=1, source_target_pairs={{0,16},{16,0},{1,17},{17,1},{2,18},{18,2},{3,19},{19,3},{4,20},{20... | collective-permute-start | bytes 835592 | tf_op jit(solution)/shard_map/ppermute | solution.py:626
  42.7 1.2 %collective-permute-done.mate_ref = bf16[1088,128]{1,0:T(8,128)(2,1)S(1)} collective-permute-done((bf16[1088,128]{1,0:T(8,128)(2,1)S(1)}, bf16[1088,128]{1,0:T(8,128)(2,1)S(1)}, u32[]{:S(2)}, u32[]{:S(2)}) %collective-permute-start) | collective-permute-done | bytes 278560 | tf_op jit(solution)/shard_map/ppermute | solution.py:626
  43.8 0.7 join.1
  44.5 1.4 %collective-permute-start.1 = (bf16[576,128]{1,0:T(8,128)(2,1)S(1)}, bf16[576,128]{1,0:T(8,128)(2,1)S(1)}, u32[]{:S(2)}, u32[]{:S(2)}) collective-permute-start(bf16[576,128]{1,0:T(8,128)(2,1)S(1)} %get-tuple-element.47), channel_id=1, source_target_pairs={{0,32},{32,64},{64,96},{96,0},{1,33},{33,65},{65,97},{97,1},{2,34}... | collective-permute-start | bytes 442376 | tf_op jit(solution)/shard_map/ppermute | solution.py:631
  45.9 2.6 %collective-permute-start.2 = (bf16[576,128]{1,0:T(8,128)(2,1)S(1)}, bf16[576,128]{1,0:T(8,128)(2,1)S(1)}, u32[]{:S(2)}, u32[]{:S(2)}) collective-permute-start(bf16[576,128]{1,0:T(8,128)(2,1)S(1)} %get-tuple-element.48), channel_id=1, source_target_pairs={{0,64},{32,96},{64,0},{96,32},{1,65},{33,97},{65,1},{97,33},{2,66}... | collective-permute-start | bytes 442376 | tf_op jit(solution)/shard_map/ppermute | solution.py:631
  48.5 1.1 %collective-permute-start.3 = (bf16[576,128]{1,0:T(8,128)(2,1)S(1)}, bf16[576,128]{1,0:T(8,128)(2,1)S(1)}, u32[]{:S(2)}, u32[]{:S(2)}) collective-permute-start(bf16[576,128]{1,0:T(8,128)(2,1)S(1)} %get-tuple-element.49), channel_id=1, source_target_pairs={{0,96},{32,0},{64,32},{96,64},{1,97},{33,1},{65,33},{97,65},{2,98}... | collective-permute-start | bytes 442376 | tf_op jit(solution)/shard_map/ppermute | solution.py:631
  49.6 6.7 %inside.1.part_ref = f32[3,1024,512]{2,1,0:T(8,128)S(1)} custom-call(bf16[3,1024,512]{2,1,0:T(8,128)(2,1)S(1)} %get-tuple-element.42.moving_ref, bf16[1024,512]{1,0:T(8,128)(2,1)S(1)} %copy-done.1, f32[8,1024]{1,0:T(8,128)S(1)} %get-tuple-element.43.row_ref, f32[1024,128]{1,0:T(8,128)S(1)} %get-tuple-element.40.col_ref, ...), custom_call_target="tpu_custom_call" | custom-call | flops 12000000000 | bytes 12000000 | tf_op jit(solution)/shard_map/inside/pallas_call | solution.py:392
  56.3 0.0 collective-permute-done.1.refs_0_
  56.3 4.6 %finish.1 = (bf16[3,1024,512]{2,1,0:T(8,128)(2,1)}, bf16[16,96,128]{2,1,0:T(8,128)(2,1)}, bf16[4,128,128]{2,1,0:T(8,128)(2,1)S(1)}, bf16[96,512]{1,0:T(8,128)(2,1)S(1)}, bf16[96,512]{1,0:T(8,128)(2,1)S(1)}) custom-call(s32[3]{0:T(128)S(1)} %pad_add_fusion.meta_ref, bf16[3,1024,512]{2,1,0:T(8,128)(2,1)S(1)} %get-tuple-element.42.moving_ref, ...), custom_call_target="tpu_custom_call" | custom-call | flops 4000000000 | bytes 14000000 | tf_op jit(solution)/shard_map/finish/pallas_call | solution.py:543
  61.0 3.6 %all-to-all-start.2 = ((bf16[16,96,128]{2,1,0:T(8,128)(2,1)}), bf16[16,96,128]{2,1,0:T(8,128)(2,1)S(1)}, u32[]{:S(2)}, u32[]{:S(2)}) async-start(bf16[16,96,128]{2,1,0:T(8,128)(2,1)} %get-tuple-element.50), calls=%async_computation.2 | async-start | bytes 786432 | tf_op jit(solution)/shard_map/all_to_all | solution.py:131
  64.6 1.3 %collective-permute-start.4 = (bf16[96,512]{1,0:T(8,128)(2,1)S(1)}, bf16[96,512]{1,0:T(8,128)(2,1)S(1)}, u32[]{:S(2)}, u32[]{:S(2)}) collective-permute-start(bf16[96,512]{1,0:T(8,128)(2,1)S(1)} %get-tuple-element.52), channel_id=1, source_target_pairs={{0,16},{16,0},{1,17},{17,1},{2,18},{18,2},{3,19},{19,3},{4,20},{20... | collective-permute-start | bytes 294920 | tf_op jit(solution)/shard_map/ppermute | solution.py:626
  65.9 0.9 collective-permute-done.4.refs_1_
  66.8 0.9 collective-permute-start.7
  67.7 1.4 %collective-permute-start.6 = (bf16[96,512]{1,0:T(8,128)(2,1)S(1)}, bf16[96,512]{1,0:T(8,128)(2,1)S(1)}, u32[]{:S(2)}, u32[]{:S(2)}) collective-permute-start(bf16[96,512]{1,0:T(8,128)(2,1)S(1)} %add_all.4.refs_0_), channel_id=1, source_target_pairs={{0,64},{32,96},{64,0},{96,32},{1,65},{33,97},{65,1},{97,33},{2,66}... | collective-permute-start | bytes 294920 | tf_op jit(solution)/shard_map/ppermute | solution.py:631
  69.1 0.0 collective-permute-start.5
  69.1 4.3 %all-to-all-done.2.in_ref = bf16[16,96,128]{2,1,0:T(8,128)(2,1)S(1)} async-done(((bf16[16,96,128]{2,1,0:T(8,128)(2,1)}), bf16[16,96,128]{2,1,0:T(8,128)(2,1)S(1)}, u32[]{:S(2)}, u32[]{:S(2)}) %all-to-all-start.2) | async-done | bytes 393248 | tf_op jit(solution)/shard_map/all_to_all | solution.py:131
  73.4 0.8 sum_spread.3
  74.2 3.6 %all-to-all-start.3 = ((bf16[16,96,128]{2,1,0:T(8,128)(2,1)}), bf16[16,96,128]{2,1,0:T(8,128)(2,1)S(1)}, u32[]{:S(2)}, u32[]{:S(2)}) async-start(bf16[16,96,128]{2,1,0:T(8,128)(2,1)} %sum_spread.3), calls=%async_computation.3 | async-start | bytes 786432 | tf_op jit(solution)/shard_map/all_to_all | solution.py:131
  77.8 0.0 copy-start
  77.8 3.2 %late.2.refs_0_ = bf16[1024,512]{1,0:T(8,128)(2,1)} custom-call(bf16[3,1024,512]{2,1,0:T(8,128)(2,1)} %copy-done.5, f32[8,1024]{1,0:T(8,128)S(1)} %get-tuple-element.43.row_ref, f32[1024,128]{1,0:T(8,128)S(1)} %get-tuple-element.40.col_ref, f32[64,128]{1,0:T(8,128)S(1)} %get-tuple-element.41.pass_ref, bf16[8,4,128,128]{3,2,1,0:T(8,128)(2,1)} %copy-done.6, ...), custom_call_target="tpu_custom_call" | custom-call | flops 6000000000 | bytes 6000000 | tf_op jit(solution)/shard_map/late/pallas_call | solution.py:442
  81.0 0.0 collective-permute-done.7.refs_3_
  81.0 0.0 collective-permute-done.6.refs_2_
  81.0 5.2 %all-to-all-done.3.grad_ref = bf16[16,96,128]{2,1,0:T(8,128)(2,1)S(1)} async-done(((bf16[16,96,128]{2,1,0:T(8,128)(2,1)}), bf16[16,96,128]{2,1,0:T(8,128)(2,1)S(1)}, u32[]{:S(2)}, u32[]{:S(2)}) %all-to-all-start.3) | async-done | bytes 393248 | tf_op jit(solution)/shard_map/all_to_all | solution.py:131
  86.2 0.9 partial_down.1
  87.2 3.1 %collective-permute-start.8 = (bf16[96,384]{1,0:T(8,128)(2,1)S(1)}, bf16[96,384]{1,0:T(8,128)(2,1)S(1)}, u32[]{:S(2)}, u32[]{:S(2)}) collective-permute-start(bf16[96,384]{1,0:T(8,128)(2,1)S(1)} %get-tuple-element.57), channel_id=1, source_target_pairs={{0,16},{16,0},{1,17},{17,1},{2,18},{18,2},{3,19},{19,3},{4,20},{20... | collective-permute-start | bytes 221192 | tf_op jit(solution)/shard_map/ppermute | solution.py:626
  90.3 0.9 collective-permute-done.8.refs_1_
  91.2 1.2 %collective-permute-start.12 = (bf16[96,384]{1,0:T(8,128)(2,1)S(1)}, bf16[96,384]{1,0:T(8,128)(2,1)S(1)}, u32[]{:S(2)}, u32[]{:S(2)}) collective-permute-start(bf16[96,384]{1,0:T(8,128)(2,1)S(1)} %add_all.5.refs_0_), channel_id=1, source_target_pairs={{0,96},{32,0},{64,32},{96,64},{1,97},{33,1},{65,33},{97,65},{2,98}... | collective-permute-start | bytes 221192 | tf_op jit(solution)/shard_map/ppermute | solution.py:631
  92.4 1.1 %collective-permute-start.11 = (bf16[96,384]{1,0:T(8,128)(2,1)S(1)}, bf16[96,384]{1,0:T(8,128)(2,1)S(1)}, u32[]{:S(2)}, u32[]{:S(2)}) collective-permute-start(bf16[96,384]{1,0:T(8,128)(2,1)S(1)} %add_all.5.refs_0_), channel_id=1, source_target_pairs={{0,64},{32,96},{64,0},{96,32},{1,65},{33,97},{65,1},{97,33},{2,66}... | collective-permute-start | bytes 221192 | tf_op jit(solution)/shard_map/ppermute | solution.py:631
  93.5 0.0 collective-permute-start.10
  93.6 1.3 %collective-permute-start.9 = (f32[96,512]{1,0:T(8,128)S(1)}, f32[96,512]{1,0:T(8,128)S(1)}, u32[]{:S(2)}, u32[]{:S(2)}) collective-permute-start(f32[96,512]{1,0:T(8,128)S(1)} %add_all.6.own_ref), channel_id=1, source_target_pairs={{0,16},{16,0},{1,17},{17,1},{2,18},{18,2},{3,19},{19,3},{4,20},{20... | collective-permute-start | bytes 589832 | tf_op jit(solution)/shard_map/ppermute | solution.py:626
  94.8 3.1 %late.3 = bf16[1024,512]{1,0:T(8,128)(2,1)} custom-call(bf16[3,1024,512]{2,1,0:T(8,128)(2,1)} %copy-done.5, f32[8,1024]{1,0:T(8,128)S(1)} %get-tuple-element.43.row_ref, f32[1024,128]{1,0:T(8,128)S(1)} %get-tuple-element.40.col_ref, f32[64,128]{1,0:T(8,128)S(1)} %get-tuple-element.41.pass_ref, ...), custom_call_target="tpu_custom_call", output_to_operand_aliasing={{}: (6, {})} | custom-call | flops 6000000000 | bytes 6000000 | tf_op jit(solution)/shard_map/late/pallas_call | solution.py:442
  97.9 1.3 %join_halves.2 = f32[192,512]{1,0:T(8,128)} custom-call(s32[3]{0:T(128)S(1)} %pad_add_fusion.meta_ref, f32[96,512]{1,0:T(8,128)S(1)} %add_all.6.own_ref, f32[96,512]{1,0:T(8,128)S(1)} %collective-permute-done.9.mate_ref), custom_call_target="tpu_custom_call" | custom-call | tf_op jit(solution)/shard_map/join_halves/pallas_call | solution.py:597
  99.2 0.0 collective-permute-done.12.refs_3_
  99.2 1.1 %collective-permute-start.13 = (f32[96,384]{1,0:T(8,128)S(1)}, f32[96,384]{1,0:T(8,128)S(1)}, u32[]{:S(2)}, u32[]{:S(2)}) collective-permute-start(f32[96,384]{1,0:T(8,128)S(1)} %add_all.7.own_ref), channel_id=1, source_target_pairs={{0,16},{16,0},{1,17},{17,1},{2,18},{18,2},{3,19},{19,3},{4,20},{20... | collective-permute-start | bytes 442376 | tf_op jit(solution)/shard_map/ppermute | solution.py:626
  100.4 1.0 collective-permute-done.13.mate_ref
  101.4 1.3 %join_halves.3 = f32[192,384]{1,0:T(8,128)} custom-call(s32[3]{0:T(128)S(1)} %pad_add_fusion.meta_ref, f32[96,384]{1,0:T(8,128)S(1)} %add_all.7.own_ref, f32[96,384]{1,0:T(8,128)S(1)} %collective-permute-done.13.mate_ref), custom_call_target="tpu_custom_call" | custom-call | tf_op jit(solution)/shard_map/join_halves/pallas_call | solution.py:597
  (21 shorter events, 0.2 us)
Async XLA Ops:
  0.6 25.0 %copy-start.4 = (s32[1024]{0:T(1024)S(1)}, s32[1024]{0:T(1024)}, u32[]{:S(2)}) copy-start(s32[1024]{0:T(1024)} %param.14) | copy-start | bytes 12292
  0.6 25.0 %copy-start.3 = (bf16[4,1024]{1,0:T(4,128)(2,1)S(1)}, bf16[4,1024]{1,0:T(4,128)(2,1)}, u32[]{:S(2)}) copy-start(bf16[4,1024]{1,0:T(4,128)(2,1)} %decay_ref.1) | copy-start | bytes 24580
  3.6 17.6 %all-to-all-start = ((bf16[16,96,128]{2,1,0:T(8,128)(2,1)}), bf16[16,96,128]{2,1,0:T(8,128)(2,1)S(1)}, u32[]{:S(2)}, u32[]{:S(2)}) async-start(bf16[16,96,128]{2,1,0:T(8,128)(2,1)} %partial_low.1), calls=%async_computation | async-start | bytes 786432 | tf_op jit(solution)/shard_map/all_to_all | solution.py:131
  22.0 11.8 %all-to-all-start.1 = ((bf16[16,96,128]{2,1,0:T(8,128)(2,1)}), bf16[16,96,128]{2,1,0:T(8,128)(2,1)S(1)}, u32[]{:S(2)}, u32[]{:S(2)}) async-start(bf16[16,96,128]{2,1,0:T(8,128)(2,1)} %sum_spread.2), calls=%async_computation.1 | async-start | bytes 786432 | tf_op jit(solution)/shard_map/all_to_all | solution.py:131
  25.6 8.2 %copy-start.1 = (bf16[1024,512]{1,0:T(8,128)(2,1)S(1)}, bf16[1024,512]{1,0:T(8,128)(2,1)}, u32[]{:S(2)}) copy-start(bf16[1024,512]{1,0:T(8,128)(2,1)} %g_ref.1) | copy-start | bytes 3145732
  25.6 8.2 %copy-start.2 = (bf16[3,64,512]{2,1,0:T(8,128)(2,1)S(1)}, bf16[3,64,512]{2,1,0:T(8,128)(2,1)}, u32[]{:S(2)}) copy-start(bf16[3,64,512]{2,1,0:T(8,128)(2,1)} %up_ref.3) | copy-start | bytes 589828
  39.6 16.7 %copy-start.6 = (bf16[8,4,128,128]{3,2,1,0:T(8,128)(2,1)}, bf16[8,4,128,128]{3,2,1,0:T(8,128)(2,1)S(1)}, u32[]{:S(2)}) copy-start(bf16[8,4,128,128]{3,2,1,0:T(8,128)(2,1)S(1)} %get-tuple-element.44.before_ref) | copy-start | bytes 3145732
  39.6 16.8 %copy-start.5 = (bf16[3,1024,512]{2,1,0:T(8,128)(2,1)}, bf16[3,1024,512]{2,1,0:T(8,128)(2,1)S(1)}, u32[]{:S(2)}) copy-start(bf16[3,1024,512]{2,1,0:T(8,128)(2,1)S(1)} %get-tuple-element.42.moving_ref) | copy-start | bytes 9437188
  39.6 4.3 %collective-permute-start = (bf16[1088,128]{1,0:T(8,128)(2,1)S(1)}, bf16[1088,128]{1,0:T(8,128)(2,1)S(1)}, u32[]{:S(2)}, u32[]{:S(2)}) collective-permute-start(bf16[1088,128]{1,0:T(8,128)(2,1)S(1)} %get-tuple-element.46.own_ref), channel_id=1, source_target_pairs={{0,16},{16,0},{1,17},{17,1},{2,18},{18,2},{3,19},{19,3},{4,20},{20... | collective-permute-start | bytes 835592 | tf_op jit(solution)/shard_map/ppermute | solution.py:626
  44.5 11.8 %collective-permute-start.1 = (bf16[576,128]{1,0:T(8,128)(2,1)S(1)}, bf16[576,128]{1,0:T(8,128)(2,1)S(1)}, u32[]{:S(2)}, u32[]{:S(2)}) collective-permute-start(bf16[576,128]{1,0:T(8,128)(2,1)S(1)} %get-tuple-element.47), channel_id=1, source_target_pairs={{0,32},{32,64},{64,96},{96,0},{1,33},{33,65},{65,97},{97,1},{2,34}... | collective-permute-start | bytes 442376 | tf_op jit(solution)/shard_map/ppermute | solution.py:631
  45.9 10.4 %collective-permute-start.2 = (bf16[576,128]{1,0:T(8,128)(2,1)S(1)}, bf16[576,128]{1,0:T(8,128)(2,1)S(1)}, u32[]{:S(2)}, u32[]{:S(2)}) collective-permute-start(bf16[576,128]{1,0:T(8,128)(2,1)S(1)} %get-tuple-element.48), channel_id=1, source_target_pairs={{0,64},{32,96},{64,0},{96,32},{1,65},{33,97},{65,1},{97,33},{2,66}... | collective-permute-start | bytes 442376 | tf_op jit(solution)/shard_map/ppermute | solution.py:631
  48.5 7.8 %collective-permute-start.3 = (bf16[576,128]{1,0:T(8,128)(2,1)S(1)}, bf16[576,128]{1,0:T(8,128)(2,1)S(1)}, u32[]{:S(2)}, u32[]{:S(2)}) collective-permute-start(bf16[576,128]{1,0:T(8,128)(2,1)S(1)} %get-tuple-element.49), channel_id=1, source_target_pairs={{0,96},{32,0},{64,32},{96,64},{1,97},{33,1},{65,33},{97,65},{2,98}... | collective-permute-start | bytes 442376 | tf_op jit(solution)/shard_map/ppermute | solution.py:631
  61.0 12.4 %all-to-all-start.2 = ((bf16[16,96,128]{2,1,0:T(8,128)(2,1)}), bf16[16,96,128]{2,1,0:T(8,128)(2,1)S(1)}, u32[]{:S(2)}, u32[]{:S(2)}) async-start(bf16[16,96,128]{2,1,0:T(8,128)(2,1)} %get-tuple-element.50), calls=%async_computation.2 | async-start | bytes 786432 | tf_op jit(solution)/shard_map/all_to_all | solution.py:131
  64.6 2.2 %collective-permute-start.4 = (bf16[96,512]{1,0:T(8,128)(2,1)S(1)}, bf16[96,512]{1,0:T(8,128)(2,1)S(1)}, u32[]{:S(2)}, u32[]{:S(2)}) collective-permute-start(bf16[96,512]{1,0:T(8,128)(2,1)S(1)} %get-tuple-element.52), channel_id=1, source_target_pairs={{0,16},{16,0},{1,17},{17,1},{2,18},{18,2},{3,19},{19,3},{4,20},{20... | collective-permute-start | bytes 294920 | tf_op jit(solution)/shard_map/ppermute | solution.py:626
  66.8 14.1 %collective-permute-start.7 = (bf16[96,512]{1,0:T(8,128)(2,1)S(1)}, bf16[96,512]{1,0:T(8,128)(2,1)S(1)}, u32[]{:S(2)}, u32[]{:S(2)}) collective-permute-start(bf16[96,512]{1,0:T(8,128)(2,1)S(1)} %add_all.4.refs_0_), channel_id=1, source_target_pairs={{0,96},{32,0},{64,32},{96,64},{1,97},{33,1},{65,33},{97,65},{2,98}... | collective-permute-start | bytes 294920 | tf_op jit(solution)/shard_map/ppermute | solution.py:631
  67.7 13.3 %collective-permute-start.6 = (bf16[96,512]{1,0:T(8,128)(2,1)S(1)}, bf16[96,512]{1,0:T(8,128)(2,1)S(1)}, u32[]{:S(2)}, u32[]{:S(2)}) collective-permute-start(bf16[96,512]{1,0:T(8,128)(2,1)S(1)} %add_all.4.refs_0_), channel_id=1, source_target_pairs={{0,64},{32,96},{64,0},{96,32},{1,65},{33,97},{65,1},{97,33},{2,66}... | collective-permute-start | bytes 294920 | tf_op jit(solution)/shard_map/ppermute | solution.py:631
  69.1 11.9 %collective-permute-start.5 = (bf16[96,512]{1,0:T(8,128)(2,1)S(1)}, bf16[96,512]{1,0:T(8,128)(2,1)S(1)}, u32[]{:S(2)}, u32[]{:S(2)}) collective-permute-start(bf16[96,512]{1,0:T(8,128)(2,1)S(1)} %add_all.4.refs_0_), channel_id=1, source_target_pairs={{0,32},{32,64},{64,96},{96,0},{1,33},{33,65},{65,97},{97,1},{2,34}... | collective-permute-start | bytes 294920 | tf_op jit(solution)/shard_map/ppermute | solution.py:631
  74.2 12.0 %all-to-all-start.3 = ((bf16[16,96,128]{2,1,0:T(8,128)(2,1)}), bf16[16,96,128]{2,1,0:T(8,128)(2,1)S(1)}, u32[]{:S(2)}, u32[]{:S(2)}) async-start(bf16[16,96,128]{2,1,0:T(8,128)(2,1)} %sum_spread.3), calls=%async_computation.3 | async-start | bytes 786432 | tf_op jit(solution)/shard_map/all_to_all | solution.py:131
  77.8 8.4 %copy-start = (bf16[1024,384]{1,0:T(8,128)(2,1)S(1)}, bf16[1024,384]{1,0:T(8,128)(2,1)}, u32[]{:S(2)}) copy-start(bf16[1024,384]{1,0:T(8,128)(2,1)} %x_ref.3) | copy-start | bytes 2359300
  87.2 4.0 %collective-permute-start.8 = (bf16[96,384]{1,0:T(8,128)(2,1)S(1)}, bf16[96,384]{1,0:T(8,128)(2,1)S(1)}, u32[]{:S(2)}, u32[]{:S(2)}) collective-permute-start(bf16[96,384]{1,0:T(8,128)(2,1)S(1)} %get-tuple-element.57), channel_id=1, source_target_pairs={{0,16},{16,0},{1,17},{17,1},{2,18},{18,2},{3,19},{19,3},{4,20},{20... | collective-permute-start | bytes 221192 | tf_op jit(solution)/shard_map/ppermute | solution.py:626
  91.2 7.9 %collective-permute-start.12 = (bf16[96,384]{1,0:T(8,128)(2,1)S(1)}, bf16[96,384]{1,0:T(8,128)(2,1)S(1)}, u32[]{:S(2)}, u32[]{:S(2)}) collective-permute-start(bf16[96,384]{1,0:T(8,128)(2,1)S(1)} %add_all.5.refs_0_), channel_id=1, source_target_pairs={{0,96},{32,0},{64,32},{96,64},{1,97},{33,1},{65,33},{97,65},{2,98}... | collective-permute-start | bytes 221192 | tf_op jit(solution)/shard_map/ppermute | solution.py:631
  92.4 6.8 %collective-permute-start.11 = (bf16[96,384]{1,0:T(8,128)(2,1)S(1)}, bf16[96,384]{1,0:T(8,128)(2,1)S(1)}, u32[]{:S(2)}, u32[]{:S(2)}) collective-permute-start(bf16[96,384]{1,0:T(8,128)(2,1)S(1)} %add_all.5.refs_0_), channel_id=1, source_target_pairs={{0,64},{32,96},{64,0},{96,32},{1,65},{33,97},{65,1},{97,33},{2,66}... | collective-permute-start | bytes 221192 | tf_op jit(solution)/shard_map/ppermute | solution.py:631
  93.5 5.7 %collective-permute-start.10 = (bf16[96,384]{1,0:T(8,128)(2,1)S(1)}, bf16[96,384]{1,0:T(8,128)(2,1)S(1)}, u32[]{:S(2)}, u32[]{:S(2)}) collective-permute-start(bf16[96,384]{1,0:T(8,128)(2,1)S(1)} %add_all.5.refs_0_), channel_id=1, source_target_pairs={{0,32},{32,64},{64,96},{96,0},{1,33},{33,65},{65,97},{97,1},{2,34}... | collective-permute-start | bytes 221192 | tf_op jit(solution)/shard_map/ppermute | solution.py:631
  93.6 4.3 %collective-permute-start.9 = (f32[96,512]{1,0:T(8,128)S(1)}, f32[96,512]{1,0:T(8,128)S(1)}, u32[]{:S(2)}, u32[]{:S(2)}) collective-permute-start(f32[96,512]{1,0:T(8,128)S(1)} %add_all.6.own_ref), channel_id=1, source_target_pairs={{0,16},{16,0},{1,17},{17,1},{2,18},{18,2},{3,19},{19,3},{4,20},{20... | collective-permute-start | bytes 589832 | tf_op jit(solution)/shard_map/ppermute | solution.py:626
  99.2 2.1 %collective-permute-start.13 = (f32[96,384]{1,0:T(8,128)S(1)}, f32[96,384]{1,0:T(8,128)S(1)}, u32[]{:S(2)}, u32[]{:S(2)}) collective-permute-start(f32[96,384]{1,0:T(8,128)S(1)} %add_all.7.own_ref), channel_id=1, source_target_pairs={{0,16},{16,0},{1,17},{17,1},{2,18},{18,2},{3,19},{19,3},{4,20},{20... | collective-permute-start | bytes 442376 | tf_op jit(solution)/shard_map/ppermute | solution.py:626

commit v5 on v4

--- a/solution.py
+++ b/solution.py
@@ -13,8 +13,10 @@
 BLOCK = 256
 VMEM_BYTES = 20 * 1024 * 1024
 NEGATIVE = -1e30
-
-CUM, SEG, ENTER, LEAVE, ENTER_ALL, LEAVE_ALL = 0, 4, 8, 12, 16, 20
+UNROLL = 8
+
+CUM, SEG, ENTER, LEAVE, ENTER_ALL, LEAVE_ALL, ENTER_SHUT, LEAVE_SHUT = 0, 4, 8, 12, 16, 20, 24, 25
+ROW_ENTER, ROW_LEAVE = 8, 12
 
 
 def dot_nn(a, b):
@@ -46,6 +48,12 @@
 
 def diagonal_of(pair):
     return diagonal(pair[:, :128], pair[:, 128:])
+
+
+def pair_nt(a, b):
+    return jnp.concatenate(
+        [dot_nt(a[:, :128], b[:, :128]), dot_nt(a[:, 128:], b[:, 128:])], axis=1
+    )
 
 
 def widen(table, lane):
@@ -168,25 +176,38 @@
         here_col = c * CHUNK + lax.broadcasted_iota(jnp.int32, (CHUNK, 1), 0) < live
         head_row = lax.broadcasted_iota(jnp.int32, (8, CHUNK), 0)
         head_lane = lax.broadcasted_iota(jnp.int32, (CHUNK, 8), 1)
-        row_ref[:, span] = jnp.where(here | (head_row != heads), by_row, -1.0)
+        row_ref[0:8, span] = jnp.where(here | (head_row != heads), by_row, -1.0)
+        end_row = by_row[:, CHUNK - 1 : CHUNK]
+        row_seg = by_row[heads : heads + 1]
+        row_ref[ROW_ENTER : ROW_ENTER + heads, span] = jnp.where(
+            (row_seg == 0.0) & here, jnp.exp(by_row[:heads]), 0.0
+        )
+        row_ref[ROW_LEAVE : ROW_LEAVE + heads, span] = jnp.where(
+            (row_seg == end_row[heads : heads + 1]) & here, jnp.exp(end_row[:heads] - by_row[:heads]), 0.0
+        )
         col_ref[span, 0:8] = jnp.where(here_col | (head_lane != heads), by_col, -2.0)
         cum = by_col[:, :heads]
         seg = by_col[:, heads : heads + 1]
         cum_end = by_col[CHUNK - 1 : CHUNK, :heads]
         seg_end = by_col[CHUNK - 1 : CHUNK, heads : heads + 1]
-        enter = jnp.where((seg == 0.0) & here_col, jnp.exp(cum), 0.0)
-        leave = jnp.where((seg == seg_end) & here_col, jnp.exp(cum_end - cum), 0.0)
+        may_enter = (seg == 0.0) & here_col
+        may_leave = (seg == seg_end) & here_col
+        enter = jnp.where(may_enter, jnp.exp(cum), 0.0)
+        leave = jnp.where(may_leave, jnp.exp(cum_end - cum), 0.0)
+        col_ref[span, ENTER_SHUT : ENTER_SHUT + 1] = jnp.where(may_enter, 0.0, NEGATIVE)
+        col_ref[span, LEAVE_SHUT : LEAVE_SHUT + 1] = jnp.where(may_leave, 0.0, NEGATIVE)
         col_ref[span, ENTER : ENTER + heads] = enter
         col_ref[span, LEAVE : LEAVE + heads] = leave
         enters.append(enter)
         leaves.append(leave)
         passes.append(jnp.where(seg_end == 0.0, jnp.exp(cum_end), 0.0))
-        end_row = by_row[:, CHUNK - 1 : CHUNK]
         passing_col = jnp.where(end_row[heads : heads + 1] == 0.0, jnp.exp(end_row[:heads]), 0.0)
         passing_rows_here = jnp.broadcast_to(passing_col, (heads, 128))
         pass_ref[c * heads : (c + 1) * heads, :] = passing_rows_here
         first = (count + c) * heads
         pass_ref[first : first + heads, :] = prefix
+        first = (2 * count + c) * heads
+        pass_ref[first : first + heads, :] = jnp.broadcast_to(end_row[:heads], (heads, 128))
         prefix = prefix * passing_rows_here
     before = jnp.ones((1, heads), F32)
     for c in range(count):
@@ -206,9 +227,9 @@
     return pl.pallas_call(
         decay_kernel,
         out_shape=(
-            jax.ShapeDtypeStruct((8, rows), F32),
+            jax.ShapeDtypeStruct((16, rows), F32),
             jax.ShapeDtypeStruct((rows, 128), F32),
-            jax.ShapeDtypeStruct((2 * count * heads, 128), F32),
+            jax.ShapeDtypeStruct((3 * count * heads, 128), F32),
         ),
         in_specs=[SMEM, VMEM, VMEM],
         out_specs=(VMEM, VMEM, VMEM),
@@ -219,7 +240,7 @@
 
 
 def project_kernel(
-    frozen_ref, low_ref, up_ref, grad_ref, col_ref, pass_ref,
+    frozen_ref, low_ref, up_ref, grad_ref, row_ref, pass_ref,
     moving_ref, before_ref, after_ref, summary_ref, returning, held, sems,
 ):
     chunks = returning.shape[0]
@@ -235,24 +256,23 @@
     states = [jnp.zeros((128, 128), F32)] * heads
     for n, copy in enumerate(copies):
         low = load_pieces(low_ref.at[pl.ds(4 * n, 4)])
+        lifted = [dot_tn(low[i * rank : (i + 1) * rank, :], up_ref[i]) for i in range(3)]
         copy.wait()
         rows = pl.ds(n * BLOCK, BLOCK)
         for i in range(3):
-            lifted = dot_tn(low[i * rank : (i + 1) * rank, :], up_ref[i])
-            moving_ref[i, rows, :] = (held[i, rows, :].astype(F32) + lifted).astype(BF16)
+            moving_ref[i, rows, :] = (held[i, rows, :].astype(F32) + lifted[i]).astype(BF16)
         for c in range(n * BLOCK // CHUNK, (n + 1) * BLOCK // CHUNK):
             rows = pl.ds(c * CHUNK, CHUNK)
-            col = col_ref[rows, :]
             for h in range(heads):
                 span = slice(h * 128, (h + 1) * 128)
                 passing = pass_ref[c * heads + h : c * heads + h + 1, :]
-                leave = col[:, LEAVE + h : LEAVE + h + 1]
-                enter = col[:, ENTER + h : ENTER + h + 1]
-                keyed = (moving_ref[1, rows, span].astype(F32) * leave).astype(BF16)
-                scaled = (moving_ref[0, rows, span].astype(F32) * enter).astype(BF16)
+                leave = row_ref[ROW_LEAVE + h : ROW_LEAVE + h + 1, rows]
+                enter = row_ref[ROW_ENTER + h : ROW_ENTER + h + 1, rows]
+                valued = (moving_ref[2, rows, span].T.astype(F32) * leave).astype(BF16)
+                scaled = (moving_ref[0, rows, span].T.astype(F32) * enter).astype(BF16)
                 before_ref[c, h] = states[h].astype(BF16)
-                states[h] = passing * states[h] + dot_tn(keyed, moving_ref[2, rows, span])
-                returning[c, h] = dot_tn(scaled, grad_ref[rows, span])
+                states[h] = passing * states[h] + dot_nn(valued, moving_ref[1, rows, span])
+                returning[c, h] = dot_nn(scaled, grad_ref[rows, span])
     for h in range(heads):
         back = jnp.zeros((128, 128), F32)
         whole = jnp.ones((1, 128), F32)
@@ -274,7 +294,7 @@
     return jnp.concatenate([first, second, third, jnp.zeros((13, 128), F32)], axis=0).astype(BF16)
 
 
-def project(frozen, low, up, grad, col, passes):
+def project(frozen, low, up, grad, row, passes):
     _, rows, features = frozen.shape
     heads = features // 128
     count = rows // CHUNK
@@ -298,7 +318,7 @@
         compiler_params=params(),
         cost_estimate=cost(4e9, 10e6),
         name="project",
-    )(pltpu.with_memory_space_constraint(frozen, pltpu.HBM), low, up, grad, col, passes)
+    )(pltpu.with_memory_space_constraint(frozen, pltpu.HBM), low, up, grad, row, passes)
 
 
 def passing_of(ref, base):
@@ -350,63 +370,69 @@
     )(meta, own, mate)
 
 
-def inside_kernel(moving_ref, grad_ref, row_ref, col_ref, before_ref, after_ref, part_ref):
+def inside_kernel(moving_ref, grad_ref, row_ref, col_ref, pass_ref, before_ref, after_ref, part_ref):
     features = moving_ref.shape[2]
     heads = features // 128
-    row_i = lax.broadcasted_iota(jnp.int32, (CHUNK, CHUNK), 0)
-    col_i = lax.broadcasted_iota(jnp.int32, (CHUNK, CHUNK), 1)
-
-    @pl.loop(0, moving_ref.shape[1] // CHUNK, unroll=4)
+    square = (CHUNK, CHUNK)
+    row_i = lax.broadcasted_iota(jnp.int32, square, 0)
+    col_i = lax.broadcasted_iota(jnp.int32, square, 1)
+    end_base = pass_ref.shape[0] // 3 * 2
+
+    def paired(make, h):
+        return jnp.concatenate([make(h), make(h + 1)], axis=1)
+
+    @pl.loop(0, moving_ref.shape[1] // CHUNK, unroll=UNROLL)
     def _(c):
         rows = chunk_rows(c)
         col = col_ref[rows, :]
-        row = row_ref[:, rows]
-        allowed = (row_i <= col_i) & (col[:, SEG : SEG + 1] == row[SEG : SEG + 1, :])
-        shut = jnp.where(allowed, 0.0, NEGATIVE)
+        row = row_ref[0:8, rows]
+        same = col[:, SEG : SEG + 1] == row[SEG : SEG + 1, :]
+        shut = jnp.where(same & (row_i <= col_i), 0.0, NEGATIVE)
+        shut_turned = jnp.where(same & (row_i >= col_i), 0.0, NEGATIVE)
+        enter_shut = jnp.broadcast_to(col[:, ENTER_SHUT : ENTER_SHUT + 1], square)
+        leave_shut = jnp.broadcast_to(col[:, LEAVE_SHUT : LEAVE_SHUT + 1], square)
+        sums = [jnp.broadcast_to(col[:, h : h + 1], square) for h in range(heads)]
+        ends = pass_ref[pl.ds(end_base + c * heads, heads), :]
         for h in range(0, heads, 2):
             span = slice(h * 128, (h + 2) * 128)
             q = moving_ref[0, rows, span]
             k = moving_ref[1, rows, span]
             v = moving_ref[2, rows, span]
             g = grad_ref[rows, span]
-            weights = jnp.exp(
-                jnp.concatenate(
-                    [(row[i : i + 1, :] - col[:, i : i + 1]) + shut for i in (h, h + 1)], axis=1
-                )
-            )
+            weights = paired(lambda i: jnp.exp((row[i : i + 1, :] - sums[i]) + shut), h)
+            turned = paired(lambda i: jnp.exp((sums[i] - row[i : i + 1, :]) + shut_turned), h)
+            enter = paired(lambda i: jnp.exp(sums[i] + enter_shut), h)
+            leave = paired(lambda i: jnp.exp((ends[i : i + 1, :] - sums[i]) + leave_shut), h)
             queries = diagonal_of(q)
             cotangents = diagonal_of(g)
             before = diagonal(before_ref[c, h], before_ref[c, h + 1])
             after = diagonal(after_ref[c, h], after_ref[c, h + 1])
-            enter = widen(col, ENTER + h)
-            leave = widen(col, LEAVE + h)
-            a = (dot_nt(k, queries) * weights).astype(BF16)
-            b = (dot_nt(v, cotangents) * weights).astype(BF16)
-            turned = jnp.concatenate([b[:, :128].T, b[:, 128:].T], axis=1)
-            part_ref[0, rows, span] = dot_nn(turned, diagonal_of(k)) + enter * dot_nt(g, before)
+            a = (pair_nt(k, q) * weights).astype(BF16)
+            b = (pair_nt(v, g) * weights).astype(BF16)
+            b_turned = (pair_nt(g, v) * turned).astype(BF16)
+            part_ref[0, rows, span] = dot_nn(b_turned, diagonal_of(k)) + enter * dot_nn(g, before)
             part_ref[1, rows, span] = dot_nn(b, queries) + leave * dot_nt(v, after)
             part_ref[2, rows, span] = dot_nn(a, cotangents) + leave * dot_nn(k, after)
 
 
-def inside(moving, grad, row, col, before, after):
+def inside(moving, grad, row, col, passes, before, after):
     return pl.pallas_call(
         inside_kernel,
         out_shape=jax.ShapeDtypeStruct(moving.shape, F32),
-        in_specs=[VMEM] * 6,
+        in_specs=[VMEM] * 7,
         out_specs=VMEM,
         compiler_params=params(),
         cost_estimate=cost(12e9, 12e6),
         name="inside",
-    )(moving, grad, row, col, before, after)
-
-
-def late_kernel(first_block, moving_ref, row_ref, col_ref, pass_ref, before_ref, state_ref, *refs):
-    attn_ref = refs[-1]
+    )(moving, grad, row, col, passes, before, after)
+
+
+def late_kernel(moving_ref, row_ref, col_ref, pass_ref, before_ref, state_ref, attn_ref):
     features = moving_ref.shape[2]
     heads = features // 128
     inverse = 1.0 / 128.0
-    step = first_block + pl.program_id(0)
-    prefix_base = pass_ref.shape[0] // 2
+    step = pl.program_id(0)
+    prefix_base = pass_ref.shape[0] // 3
     row_i = lax.broadcasted_iota(jnp.int32, (CHUNK, CHUNK), 0)
     col_i = lax.broadcasted_iota(jnp.int32, (CHUNK, CHUNK), 1)
     for n in range(BLOCK // CHUNK):
@@ -431,39 +457,31 @@
             )
             a = (dot_nt(q, diagonal_of(moving_ref[1, rows, span])) * weights).astype(BF16)
             out = dot_nn(a, diagonal_of(moving_ref[2, rows, span]))
-            out = out + widen(col, ENTER + h) * dot_nn(q, diagonal(states[h], states[h + 1]))
+            out = out + widen(col, ENTER + h) * dot_nt(q, diagonal(states[h], states[h + 1]))
             attn_ref[rows, span] = (out * inverse).astype(BF16)
 
 
-def late(moving, row, col, passes, before, state, first_block, block_count, earlier=None):
+def late(moving, row, col, passes, before, state):
     _, rows, features = moving.shape
     heads = features // 128
-    far = pl.BlockSpec(memory_space=pltpu.HBM)
-    return pl.pallas_call(
-        functools.partial(late_kernel, first_block),
+    moving, before = (pltpu.with_memory_space_constraint(a, pltpu.HBM) for a in (moving, before))
+    return pl.pallas_call(
+        late_kernel,
         out_shape=jax.ShapeDtypeStruct((rows, features), BF16),
-        grid=(block_count,),
+        grid=(rows // BLOCK,),
         in_specs=[
-            pl.BlockSpec((3, BLOCK, features), lambda i: (0, first_block + i, 0)),
-            pl.BlockSpec((8, BLOCK), lambda i: (0, first_block + i)),
-            pl.BlockSpec((BLOCK, 128), lambda i: (first_block + i, 0)),
+            pl.BlockSpec((3, BLOCK, features), lambda i: (0, i, 0)),
+            pl.BlockSpec((8, BLOCK), lambda i: (0, i)),
+            pl.BlockSpec((BLOCK, 128), lambda i: (i, 0)),
             pl.BlockSpec(passes.shape, lambda i: (0, 0)),
-            pl.BlockSpec((BLOCK // CHUNK, heads, 128, 128), lambda i: (first_block + i, 0, 0, 0)),
+            pl.BlockSpec((BLOCK // CHUNK, heads, 128, 128), lambda i: (i, 0, 0, 0)),
             pl.BlockSpec(state.shape, lambda i: (0, 0, 0)),
-        ]
-        + ([] if earlier is None else [far]),
-        out_specs=pl.BlockSpec((BLOCK, features), lambda i: (first_block + i, 0)),
-        input_output_aliases={} if earlier is None else {6: 0},
+        ],
+        out_specs=pl.BlockSpec((BLOCK, features), lambda i: (i, 0)),
         compiler_params=params(dimension_semantics=("arbitrary",)),
         cost_estimate=cost(6e9, 6e6),
         name="late",
-    )(
-        pltpu.with_memory_space_constraint(moving, pltpu.HBM),
-        row, col, passes,
-        pltpu.with_memory_space_constraint(before, pltpu.HBM),
-        state,
-        *([] if earlier is None else [earlier]),
-    )
+    )(moving, row, col, passes, before, state)
 
 
 def store_halves(core, total, keep_ref, send_ref):
@@ -515,7 +533,7 @@
             leave = widen(col, LEAVE_ALL + h)
             state = diagonal(state_in[h], state_in[h + 1])
             back = diagonal(back_in[h], back_in[h + 1])
-            query = part_ref[0, rows, span] + enter * dot_nt(g_ref[rows, span], state)
+            query = part_ref[0, rows, span] + enter * dot_nn(g_ref[rows, span], state)
             key = part_ref[1, rows, span] + leave * dot_nt(moving_ref[2, rows, span], back)
             value = part_ref[2, rows, span] + leave * dot_nn(moving_ref[1, rows, span], back)
             for i, result in enumerate((query, key, value)):
@@ -639,29 +657,27 @@
     down = jnp.swapaxes(adapter_down, 1, 2).reshape(3 * rank, inputs.shape[1])
     row, col, passes = decay_tables(meta, log_decay, doc_start)
     low = exchange(sum_spread(exchange(partial_low(inputs, down))))
-    moving, before, after, summary = project(frozen, low, adapter_up, out_grad, col, passes)
+    moving, before, after, summary = project(frozen, low, adapter_up, out_grad, row, passes)
     mate = to_mate(summary)
     messages = [along_y(m, k + 1) for k, m in enumerate(join(meta, summary, mate, chips))]
-    part = inside(moving, out_grad, row, col, before, after)
+    part = inside(moving, out_grad, row, col, passes, before, after)
     grads, low_grad_part, state, up_keep, up_send = finish(
         meta, moving, out_grad, part, col, low, adapter_up, mate, messages
     )
     up_chip = add_all([up_keep, to_mate(up_send)], BF16)
     up_parts = [up_chip] + [along_y(up_chip, k) for k in range(1, chips)]
     pieces, up_chip = lax.optimization_barrier((exchange(low_grad_part), up_chip))
-    half = inputs.shape[0] // BLOCK // 2
-    first_half = late(moving, row, col, passes, before, state, 0, half)
-    low_grad, first_half, *up_parts = lax.optimization_barrier(
-        [exchange(sum_spread(pieces)), first_half] + up_parts
+    attn = late(moving, row, col, passes, before, state)
+    low_grad, attn, *up_parts = lax.optimization_barrier(
+        [exchange(sum_spread(pieces)), attn] + up_parts
     )
     down_keep, down_send = partial_down(meta, inputs, low_grad)
     down_chip = add_all([down_keep, to_mate(down_send)], BF16)
-    down_chip, state, *up_parts = lax.optimization_barrier([down_chip, state] + up_parts)
+    down_chip, *up_parts = lax.optimization_barrier([down_chip] + up_parts)
     down_parts = [down_chip] + [along_y(down_chip, k) for k in range(1, chips)]
     up_half = add_all(up_parts, F32)
     up_total = join_halves(meta, up_half, to_mate(up_half))
-    attn = late(moving, row, col, passes, before, state, half, half, first_half)
-    up_total, attn, *down_parts = lax.optimization_barrier([up_total, attn] + down_parts)
+    up_total, *down_parts = lax.optimization_barrier([up_total] + down_parts)
     down_half = add_all(down_parts, F32)
     down_total = join_halves(meta, down_half, to_mate(down_half))
     down_total = jnp.swapaxes(down_total.reshape(3, rank, inputs.shape[1]), 1, 2)

time: 103 us -> 102 us (level)
  Pallas kernels: 34 us -> 30.2 us
  waiting for transfers between devices: 27.2 us -> 28.9 us
    ppermute x9, waiting for transfers between devices: 0.02 us -> 5.16 us  [along_y(): return lax.ppermute(a, 'y', [(i, (i + k) % count) for i in range(count)])]
    all_to_all x4, waiting for transfers between devices: 23.2 us -> 19.7 us  [exchange(): return lax.all_to_all(pieces, ('z', 'x'), 0, 0)]
    pallas_call x1, Pallas kernels: 5.73 us -> 3.7 us  [project(): pl.pallas_call(project_kernel, out_shape=(jax.ShapeDtypeStruct((3, rows,...]
    ppermute x9, starting transfers between devices: 9.56 us -> 11.2 us  [along_y(): return lax.ppermute(a, 'y', [(i, (i + k) % count) for i in range(count)])]
    pallas_call x1, Pallas kernels: 6.71 us -> 5.36 us  [inside(): pl.pallas_call(inside_kernel, out_shape=jax.ShapeDtypeStruct(moving.shape...]
    ppermute x5, starting transfers between devices: 9.88 us -> 8.79 us  [to_mate(): return lax.ppermute(a, 'core', [(0, 1), (1, 0)])]
    pallas_call x3 -> x2, Pallas kernels: 8.02 us -> 7.56 us  [the longest x1 5.6 us: late(): pl.pallas_call(late_kernel, out_shape=jax.ShapeDtypeStruct((rows, feature...]
  transfers between devices with their start and end apart: 18 -> 18, of which waited for: 8 -> 11; matrix products, arithmetic and copies ran while one was open for 2% -> 2% of each run, Pallas kernels for 16% -> 15%
where the time goes in v5:
time: 102 us; the launch traced here: 101 us
  starting transfers between devices  39.1 us (38%)
  Pallas kernels  30.2 us (30%)
  waiting for transfers between devices  28.9 us (28%)
  local copies, waits for them, and re-layouts  1.28 us (1%)
    all_to_all x4, waiting for transfers between devices, exchange(): return lax.all_to_all(pieces, ('z', 'x'), 0, 0)  19.7 us
    all_to_all x4, starting transfers between devices, exchange(): return lax.all_to_all(pieces, ('z', 'x'), 0, 0)  19.1 us
    ppermute x9, starting transfers between devices, along_y(): return lax.ppermute(a, 'y', [(i, (i + k) % count) for i in range(count)])  11.2 us
    ppermute x5, starting transfers between devices, to_mate(): return lax.ppermute(a, 'core', [(0, 1), (1, 0)])  8.79 us
    pallas_call x1, Pallas kernels, late(): pl.pallas_call(late_kernel, out_shape=jax.ShapeDtypeStruct((rows, feature...  5.6 us
    pallas_call x1, Pallas kernels, inside(): pl.pallas_call(inside_kernel, out_shape=jax.ShapeDtypeStruct(moving.shape...  5.36 us
    ppermute x9, waiting for transfers between devices, along_y(): return lax.ppermute(a, 'y', [(i, (i + k) % count) for i in range(count)])  5.16 us
    pallas_call x1, Pallas kernels, finish(): pl.pallas_call(functools.partial(finish_kernel, chips), out_shape=(jax.Sh...  4.72 us
  transfers between devices with their start and end apart: 18, of which 11 were waited for; matrix products, arithmetic and copies ran while one was open for 2% of the time, Pallas kernels for 15%

profile of v5, /device:TPU:1, one launch (start us, length us, event | category | flops | bytes accessed | tf_op | source)
XLA Modules:
  0.0 101.0 jit_solution(11736584135095164497)
XLA Ops:
  0.7 2.9 %partial_low.1 = bf16[16,96,128]{2,1,0:T(8,128)(2,1)} custom-call(bf16[1024,384]{1,0:T(8,128)(2,1)} %x_ref.3, bf16[192,384]{1,0:T(8,128)(2,1)} %bitcast.13), custom_call_target="tpu_custom_call" | custom-call | tf_op jit(solution)/shard_map/partial_low/pallas_call | solution.py:113
  3.6 8.4 %all-to-all-start = ((bf16[16,96,128]{2,1,0:T(8,128)(2,1)}), bf16[16,96,128]{2,1,0:T(8,128)(2,1)S(1)}, u32[]{:S(2)}, u32[]{:S(2)}) async-start(bf16[16,96,128]{2,1,0:T(8,128)(2,1)} %partial_low.1), calls=%async_computation | async-start | bytes 786432 | tf_op jit(solution)/shard_map/all_to_all | solution.py:139
  12.0 1.2 %dynamic_slice.3 = s32[1]{0:T(128)} dynamic-slice(s32[8]{0:T(128)} %param.15, s32[]{:T(128)S(6)} %select_n.3), dynamic_slice_sizes={1} | dynamic-slice | bytes 12 | tf_op jit(solution)/shard_map/dynamic_slice | solution.py:656
  13.3 0.7 pad_add_fusion.meta_ref
  14.0 7.2 %all-to-all-done.in_ref = bf16[16,96,128]{2,1,0:T(8,128)(2,1)S(1)} async-done(((bf16[16,96,128]{2,1,0:T(8,128)(2,1)}), bf16[16,96,128]{2,1,0:T(8,128)(2,1)S(1)}, u32[]{:S(2)}, u32[]{:S(2)}) %all-to-all-start) | async-done | bytes 393248 | tf_op jit(solution)/shard_map/all_to_all | solution.py:139
  21.2 0.8 sum_spread.2
  22.0 3.6 %all-to-all-start.1 = ((bf16[16,96,128]{2,1,0:T(8,128)(2,1)}), bf16[16,96,128]{2,1,0:T(8,128)(2,1)S(1)}, u32[]{:S(2)}, u32[]{:S(2)}) async-start(bf16[16,96,128]{2,1,0:T(8,128)(2,1)} %sum_spread.2), calls=%async_computation.1 | async-start | bytes 786432 | tf_op jit(solution)/shard_map/all_to_all | solution.py:139
  25.6 0.0 copy-start.1
  25.6 0.0 copy-start.2
  25.6 2.0 %decay_tables.1 = (f32[16,1024]{1,0:T(8,128)S(1)}, f32[1024,128]{1,0:T(8,128)S(1)}, f32[96,128]{1,0:T(8,128)S(1)}) custom-call(s32[3]{0:T(128)S(1)} %pad_add_fusion.meta_ref, bf16[4,1024]{1,0:T(4,128)(2,1)S(1)} %copy-done.3, s32[1,1024]{1,0:T(1,128)S(1)} %bitcast.10), custom_call_target="tpu_custom_call" | custom-call | flops 4000000000 | bytes 1000000 | tf_op jit(solution)/shard_map/decay_tables/pallas_call | solution.py:227
  27.6 6.2 %all-to-all-done.1.low_ref = bf16[16,96,128]{2,1,0:T(8,128)(2,1)S(1)} async-done(((bf16[16,96,128]{2,1,0:T(8,128)(2,1)}), bf16[16,96,128]{2,1,0:T(8,128)(2,1)S(1)}, u32[]{:S(2)}, u32[]{:S(2)}) %all-to-all-start.1) | async-done | bytes 393248 | tf_op jit(solution)/shard_map/all_to_all | solution.py:139
  33.8 3.7 %project.1 = (bf16[3,1024,512]{2,1,0:T(8,128)(2,1)S(1)}, bf16[8,4,128,128]{3,2,1,0:T(8,128)(2,1)S(1)}, bf16[8,4,128,128]{3,2,1,0:T(8,128)(2,1)S(1)}, bf16[1088,128]{1,0:T(8,128)(2,1)S(1)}) custom-call(bf16[3,1024,512]{2,1,0:T(8,128)(2,1)} %frozen_ref.1, bf16[16,96,128]{2,1,0:T(8,128)(2,1)S(1)} %all-to-all-done.1.low_ref, bf16[3,64,512]{2,1,0:T(8,128)(2,1)S(1)} %copy-done.2, ...), custom_call_target="tpu_custom_call" | custom-call | flops 4000000000 | bytes 10000000 | tf_op jit(solution)/shard_map/project/pallas_call | solution.py:303
  37.5 3.1 %collective-permute-start = (bf16[1088,128]{1,0:T(8,128)(2,1)S(1)}, bf16[1088,128]{1,0:T(8,128)(2,1)S(1)}, u32[]{:S(2)}, u32[]{:S(2)}) collective-permute-start(bf16[1088,128]{1,0:T(8,128)(2,1)S(1)} %get-tuple-element.44.own_ref), channel_id=1, source_target_pairs={{0,16},{16,0},{1,17},{17,1},{2,18},{18,2},{3,19},{19,3},{4,20},{20... | collective-permute-start | bytes 835592 | tf_op jit(solution)/shard_map/ppermute | solution.py:644
  40.6 1.2 %collective-permute-done.mate_ref = bf16[1088,128]{1,0:T(8,128)(2,1)S(1)} collective-permute-done((bf16[1088,128]{1,0:T(8,128)(2,1)S(1)}, bf16[1088,128]{1,0:T(8,128)(2,1)S(1)}, u32[]{:S(2)}, u32[]{:S(2)}) %collective-permute-start) | collective-permute-done | bytes 278560 | tf_op jit(solution)/shard_map/ppermute | solution.py:644
  41.8 0.7 join.1
  42.5 1.4 %collective-permute-start.1 = (bf16[576,128]{1,0:T(8,128)(2,1)S(1)}, bf16[576,128]{1,0:T(8,128)(2,1)S(1)}, u32[]{:S(2)}, u32[]{:S(2)}) collective-permute-start(bf16[576,128]{1,0:T(8,128)(2,1)S(1)} %get-tuple-element.45), channel_id=1, source_target_pairs={{0,32},{32,64},{64,96},{96,0},{1,33},{33,65},{65,97},{97,1},{2,34}... | collective-permute-start | bytes 442376 | tf_op jit(solution)/shard_map/ppermute | solution.py:649
  43.9 2.6 %collective-permute-start.2 = (bf16[576,128]{1,0:T(8,128)(2,1)S(1)}, bf16[576,128]{1,0:T(8,128)(2,1)S(1)}, u32[]{:S(2)}, u32[]{:S(2)}) collective-permute-start(bf16[576,128]{1,0:T(8,128)(2,1)S(1)} %get-tuple-element.46), channel_id=1, source_target_pairs={{0,64},{32,96},{64,0},{96,32},{1,65},{33,97},{65,1},{97,33},{2,66}... | collective-permute-start | bytes 442376 | tf_op jit(solution)/shard_map/ppermute | solution.py:649
  46.5 1.1 %collective-permute-start.3 = (bf16[576,128]{1,0:T(8,128)(2,1)S(1)}, bf16[576,128]{1,0:T(8,128)(2,1)S(1)}, u32[]{:S(2)}, u32[]{:S(2)}) collective-permute-start(bf16[576,128]{1,0:T(8,128)(2,1)S(1)} %get-tuple-element.47), channel_id=1, source_target_pairs={{0,96},{32,0},{64,32},{96,64},{1,97},{33,1},{65,33},{97,65},{2,98}... | collective-permute-start | bytes 442376 | tf_op jit(solution)/shard_map/ppermute | solution.py:649
  47.6 5.4 %inside.1.part_ref = f32[3,1024,512]{2,1,0:T(8,128)S(1)} custom-call(bf16[3,1024,512]{2,1,0:T(8,128)(2,1)S(1)} %get-tuple-element.40.moving_ref, bf16[1024,512]{1,0:T(8,128)(2,1)S(1)} %copy-done.1, f32[16,1024]{1,0:T(8,128)S(1)} %get-tuple-element.38.row_ref, f32[1024,128]{1,0:T(8,128)S(1)} %get-tuple-element.41.col_ref, ...), custom_call_target="tpu_custom_call" | custom-call | flops 12000000000 | bytes 12000000 | tf_op jit(solution)/shard_map/inside/pallas_call | solution.py:419
  52.9 0.0 collective-permute-done.1.refs_0_
  52.9 0.3 collective-permute-done.2.refs_1_
  53.2 4.7 %finish.1 = (bf16[3,1024,512]{2,1,0:T(8,128)(2,1)}, bf16[16,96,128]{2,1,0:T(8,128)(2,1)}, bf16[4,128,128]{2,1,0:T(8,128)(2,1)S(1)}, bf16[96,512]{1,0:T(8,128)(2,1)S(1)}, bf16[96,512]{1,0:T(8,128)(2,1)S(1)}) custom-call(s32[3]{0:T(128)S(1)} %pad_add_fusion.meta_ref, bf16[3,1024,512]{2,1,0:T(8,128)(2,1)S(1)} %get-tuple-element.40.moving_ref, ...), custom_call_target="tpu_custom_call" | custom-call | flops 4000000000 | bytes 14000000 | tf_op jit(solution)/shard_map/finish/pallas_call | solution.py:561
  58.0 3.6 %all-to-all-start.2 = ((bf16[16,96,128]{2,1,0:T(8,128)(2,1)}), bf16[16,96,128]{2,1,0:T(8,128)(2,1)S(1)}, u32[]{:S(2)}, u32[]{:S(2)}) async-start(bf16[16,96,128]{2,1,0:T(8,128)(2,1)} %get-tuple-element.48), calls=%async_computation.2 | async-start | bytes 786432 | tf_op jit(solution)/shard_map/all_to_all | solution.py:139
  61.5 1.3 %collective-permute-start.4 = (bf16[96,512]{1,0:T(8,128)(2,1)S(1)}, bf16[96,512]{1,0:T(8,128)(2,1)S(1)}, u32[]{:S(2)}, u32[]{:S(2)}) collective-permute-start(bf16[96,512]{1,0:T(8,128)(2,1)S(1)} %get-tuple-element.50), channel_id=1, source_target_pairs={{0,16},{16,0},{1,17},{17,1},{2,18},{18,2},{3,19},{19,3},{4,20},{20... | collective-permute-start | bytes 294920 | tf_op jit(solution)/shard_map/ppermute | solution.py:644
  62.8 0.9 collective-permute-done.4.refs_1_
  63.8 1.9 %collective-permute-start.7 = (bf16[96,512]{1,0:T(8,128)(2,1)S(1)}, bf16[96,512]{1,0:T(8,128)(2,1)S(1)}, u32[]{:S(2)}, u32[]{:S(2)}) collective-permute-start(bf16[96,512]{1,0:T(8,128)(2,1)S(1)} %add_all.4.refs_0_), channel_id=1, source_target_pairs={{0,96},{32,0},{64,32},{96,64},{1,97},{33,1},{65,33},{97,65},{2,98}... | collective-permute-start | bytes 294920 | tf_op jit(solution)/shard_map/ppermute | solution.py:649
  65.7 0.9 collective-permute-start.6
  66.6 0.4 collective-permute-start.5
  67.0 3.4 %all-to-all-done.2.in_ref = bf16[16,96,128]{2,1,0:T(8,128)(2,1)S(1)} async-done(((bf16[16,96,128]{2,1,0:T(8,128)(2,1)}), bf16[16,96,128]{2,1,0:T(8,128)(2,1)S(1)}, u32[]{:S(2)}, u32[]{:S(2)}) %all-to-all-start.2) | async-done | bytes 393248 | tf_op jit(solution)/shard_map/all_to_all | solution.py:139
  70.4 0.8 sum_spread.3
  71.2 3.6 %all-to-all-start.3 = ((bf16[16,96,128]{2,1,0:T(8,128)(2,1)}), bf16[16,96,128]{2,1,0:T(8,128)(2,1)S(1)}, u32[]{:S(2)}, u32[]{:S(2)}) async-start(bf16[16,96,128]{2,1,0:T(8,128)(2,1)} %sum_spread.3), calls=%async_computation.3 | async-start | bytes 786432 | tf_op jit(solution)/shard_map/all_to_all | solution.py:139
  74.8 0.0 copy-start
  74.8 5.6 %late.1 = bf16[1024,512]{1,0:T(8,128)(2,1)} custom-call(bf16[3,1024,512]{2,1,0:T(8,128)(2,1)} %copy-done.5, f32[16,1024]{1,0:T(8,128)S(1)} %get-tuple-element.38.row_ref, f32[1024,128]{1,0:T(8,128)S(1)} %get-tuple-element.41.col_ref, f32[96,128]{1,0:T(8,128)S(1)} %get-tuple-element.39.pass_ref, bf16[8,4,128,128]{3,2,1,0:T(8,128)(2,1)} %copy-done.6, ...), custom_call_target="tpu_custom_call" | custom-call | flops 6000000000 | bytes 6000000 | tf_op jit(solution)/shard_map/late/pallas_call | solution.py:468
  80.4 2.8 %all-to-all-done.3.grad_ref = bf16[16,96,128]{2,1,0:T(8,128)(2,1)S(1)} async-done(((bf16[16,96,128]{2,1,0:T(8,128)(2,1)}), bf16[16,96,128]{2,1,0:T(8,128)(2,1)S(1)}, u32[]{:S(2)}, u32[]{:S(2)}) %all-to-all-start.3) | async-done | bytes 393248 | tf_op jit(solution)/shard_map/all_to_all | solution.py:139
  83.2 0.9 partial_down.1
  84.2 3.1 %collective-permute-start.8 = (bf16[96,384]{1,0:T(8,128)(2,1)S(1)}, bf16[96,384]{1,0:T(8,128)(2,1)S(1)}, u32[]{:S(2)}, u32[]{:S(2)}) collective-permute-start(bf16[96,384]{1,0:T(8,128)(2,1)S(1)} %get-tuple-element.57), channel_id=1, source_target_pairs={{0,16},{16,0},{1,17},{17,1},{2,18},{18,2},{3,19},{19,3},{4,20},{20... | collective-permute-start | bytes 221192 | tf_op jit(solution)/shard_map/ppermute | solution.py:644
  87.3 0.9 collective-permute-done.8.refs_1_
  88.2 0.1 add_all.6.own_ref
  88.3 0.4 collective-permute-start.9
  88.7 2.1 %collective-permute-start.12 = (bf16[96,384]{1,0:T(8,128)(2,1)S(1)}, bf16[96,384]{1,0:T(8,128)(2,1)S(1)}, u32[]{:S(2)}, u32[]{:S(2)}) collective-permute-start(bf16[96,384]{1,0:T(8,128)(2,1)S(1)} %add_all.5.refs_0_), channel_id=1, source_target_pairs={{0,96},{32,0},{64,32},{96,64},{1,97},{33,1},{65,33},{97,65},{2,98}... | collective-permute-start | bytes 221192 | tf_op jit(solution)/shard_map/ppermute | solution.py:649
  90.8 0.6 collective-permute-start.11
  91.4 0.2 collective-permute-start.10
  91.6 1.3 %join_halves.2 = f32[192,512]{1,0:T(8,128)} custom-call(s32[3]{0:T(128)S(1)} %pad_add_fusion.meta_ref, f32[96,512]{1,0:T(8,128)S(1)} %add_all.6.own_ref, f32[96,512]{1,0:T(8,128)S(1)} %collective-permute-done.9.mate_ref), custom_call_target="tpu_custom_call" | custom-call | tf_op jit(solution)/shard_map/join_halves/pallas_call | solution.py:615
  92.9 2.7 %collective-permute-done.11.refs_2_ = bf16[96,384]{1,0:T(8,128)(2,1)S(1)} collective-permute-done((bf16[96,384]{1,0:T(8,128)(2,1)S(1)}, bf16[96,384]{1,0:T(8,128)(2,1)S(1)}, u32[]{:S(2)}, u32[]{:S(2)}) %collective-permute-start.11) | collective-permute-done | bytes 73760 | tf_op jit(solution)/shard_map/ppermute | solution.py:649
  95.6 2.2 %collective-permute-done.10.refs_1_ = bf16[96,384]{1,0:T(8,128)(2,1)S(1)} collective-permute-done((bf16[96,384]{1,0:T(8,128)(2,1)S(1)}, bf16[96,384]{1,0:T(8,128)(2,1)S(1)}, u32[]{:S(2)}, u32[]{:S(2)}) %collective-permute-start.10) | collective-permute-done | bytes 73760 | tf_op jit(solution)/shard_map/ppermute | solution.py:649
  97.8 0.9 collective-permute-start.13
  98.7 1.0 collective-permute-done.13.mate_ref
  99.7 1.3 %join_halves.3 = f32[192,384]{1,0:T(8,128)} custom-call(s32[3]{0:T(128)S(1)} %pad_add_fusion.meta_ref, f32[96,384]{1,0:T(8,128)S(1)} %add_all.7.own_ref, f32[96,384]{1,0:T(8,128)S(1)} %collective-permute-done.13.mate_ref), custom_call_target="tpu_custom_call" | custom-call | tf_op jit(solution)/shard_map/join_halves/pallas_call | solution.py:615
  (20 shorter events, 0.1 us)
Async XLA Ops:
  0.6 25.0 %copy-start.4 = (s32[1024]{0:T(1024)S(1)}, s32[1024]{0:T(1024)}, u32[]{:S(2)}) copy-start(s32[1024]{0:T(1024)} %param.14) | copy-start | bytes 12292
  0.6 25.0 %copy-start.3 = (bf16[4,1024]{1,0:T(4,128)(2,1)S(1)}, bf16[4,1024]{1,0:T(4,128)(2,1)}, u32[]{:S(2)}) copy-start(bf16[4,1024]{1,0:T(4,128)(2,1)} %decay_ref.1) | copy-start | bytes 24580
  3.6 17.6 %all-to-all-start = ((bf16[16,96,128]{2,1,0:T(8,128)(2,1)}), bf16[16,96,128]{2,1,0:T(8,128)(2,1)S(1)}, u32[]{:S(2)}, u32[]{:S(2)}) async-start(bf16[16,96,128]{2,1,0:T(8,128)(2,1)} %partial_low.1), calls=%async_computation | async-start | bytes 786432 | tf_op jit(solution)/shard_map/all_to_all | solution.py:139
  22.0 11.8 %all-to-all-start.1 = ((bf16[16,96,128]{2,1,0:T(8,128)(2,1)}), bf16[16,96,128]{2,1,0:T(8,128)(2,1)S(1)}, u32[]{:S(2)}, u32[]{:S(2)}) async-start(bf16[16,96,128]{2,1,0:T(8,128)(2,1)} %sum_spread.2), calls=%async_computation.1 | async-start | bytes 786432 | tf_op jit(solution)/shard_map/all_to_all | solution.py:139
  25.6 8.2 %copy-start.1 = (bf16[1024,512]{1,0:T(8,128)(2,1)S(1)}, bf16[1024,512]{1,0:T(8,128)(2,1)}, u32[]{:S(2)}) copy-start(bf16[1024,512]{1,0:T(8,128)(2,1)} %g_ref.1) | copy-start | bytes 3145732
  25.6 8.2 %copy-start.2 = (bf16[3,64,512]{2,1,0:T(8,128)(2,1)S(1)}, bf16[3,64,512]{2,1,0:T(8,128)(2,1)}, u32[]{:S(2)}) copy-start(bf16[3,64,512]{2,1,0:T(8,128)(2,1)} %up_ref.3) | copy-start | bytes 589828
  37.5 15.4 %copy-start.6 = (bf16[8,4,128,128]{3,2,1,0:T(8,128)(2,1)}, bf16[8,4,128,128]{3,2,1,0:T(8,128)(2,1)S(1)}, u32[]{:S(2)}) copy-start(bf16[8,4,128,128]{3,2,1,0:T(8,128)(2,1)S(1)} %get-tuple-element.42.before_ref) | copy-start | bytes 3145732
  37.5 15.7 %copy-start.5 = (bf16[3,1024,512]{2,1,0:T(8,128)(2,1)}, bf16[3,1024,512]{2,1,0:T(8,128)(2,1)S(1)}, u32[]{:S(2)}) copy-start(bf16[3,1024,512]{2,1,0:T(8,128)(2,1)S(1)} %get-tuple-element.40.moving_ref) | copy-start | bytes 9437188
  37.5 4.3 %collective-permute-start = (bf16[1088,128]{1,0:T(8,128)(2,1)S(1)}, bf16[1088,128]{1,0:T(8,128)(2,1)S(1)}, u32[]{:S(2)}, u32[]{:S(2)}) collective-permute-start(bf16[1088,128]{1,0:T(8,128)(2,1)S(1)} %get-tuple-element.44.own_ref), channel_id=1, source_target_pairs={{0,16},{16,0},{1,17},{17,1},{2,18},{18,2},{3,19},{19,3},{4,20},{20... | collective-permute-start | bytes 835592 | tf_op jit(solution)/shard_map/ppermute | solution.py:644
  42.5 10.4 %collective-permute-start.1 = (bf16[576,128]{1,0:T(8,128)(2,1)S(1)}, bf16[576,128]{1,0:T(8,128)(2,1)S(1)}, u32[]{:S(2)}, u32[]{:S(2)}) collective-permute-start(bf16[576,128]{1,0:T(8,128)(2,1)S(1)} %get-tuple-element.45), channel_id=1, source_target_pairs={{0,32},{32,64},{64,96},{96,0},{1,33},{33,65},{65,97},{97,1},{2,34}... | collective-permute-start | bytes 442376 | tf_op jit(solution)/shard_map/ppermute | solution.py:649
  43.9 9.4 %collective-permute-start.2 = (bf16[576,128]{1,0:T(8,128)(2,1)S(1)}, bf16[576,128]{1,0:T(8,128)(2,1)S(1)}, u32[]{:S(2)}, u32[]{:S(2)}) collective-permute-start(bf16[576,128]{1,0:T(8,128)(2,1)S(1)} %get-tuple-element.46), channel_id=1, source_target_pairs={{0,64},{32,96},{64,0},{96,32},{1,65},{33,97},{65,1},{97,33},{2,66}... | collective-permute-start | bytes 442376 | tf_op jit(solution)/shard_map/ppermute | solution.py:649
  46.5 6.8 %collective-permute-start.3 = (bf16[576,128]{1,0:T(8,128)(2,1)S(1)}, bf16[576,128]{1,0:T(8,128)(2,1)S(1)}, u32[]{:S(2)}, u32[]{:S(2)}) collective-permute-start(bf16[576,128]{1,0:T(8,128)(2,1)S(1)} %get-tuple-element.47), channel_id=1, source_target_pairs={{0,96},{32,0},{64,32},{96,64},{1,97},{33,1},{65,33},{97,65},{2,98}... | collective-permute-start | bytes 442376 | tf_op jit(solution)/shard_map/ppermute | solution.py:649
  58.0 12.5 %all-to-all-start.2 = ((bf16[16,96,128]{2,1,0:T(8,128)(2,1)}), bf16[16,96,128]{2,1,0:T(8,128)(2,1)S(1)}, u32[]{:S(2)}, u32[]{:S(2)}) async-start(bf16[16,96,128]{2,1,0:T(8,128)(2,1)} %get-tuple-element.48), calls=%async_computation.2 | async-start | bytes 786432 | tf_op jit(solution)/shard_map/all_to_all | solution.py:139
  61.5 2.2 %collective-permute-start.4 = (bf16[96,512]{1,0:T(8,128)(2,1)S(1)}, bf16[96,512]{1,0:T(8,128)(2,1)S(1)}, u32[]{:S(2)}, u32[]{:S(2)}) collective-permute-start(bf16[96,512]{1,0:T(8,128)(2,1)S(1)} %get-tuple-element.50), channel_id=1, source_target_pairs={{0,16},{16,0},{1,17},{17,1},{2,18},{18,2},{3,19},{19,3},{4,20},{20... | collective-permute-start | bytes 294920 | tf_op jit(solution)/shard_map/ppermute | solution.py:644
  63.8 16.6 %collective-permute-start.7 = (bf16[96,512]{1,0:T(8,128)(2,1)S(1)}, bf16[96,512]{1,0:T(8,128)(2,1)S(1)}, u32[]{:S(2)}, u32[]{:S(2)}) collective-permute-start(bf16[96,512]{1,0:T(8,128)(2,1)S(1)} %add_all.4.refs_0_), channel_id=1, source_target_pairs={{0,96},{32,0},{64,32},{96,64},{1,97},{33,1},{65,33},{97,65},{2,98}... | collective-permute-start | bytes 294920 | tf_op jit(solution)/shard_map/ppermute | solution.py:649
  65.7 14.7 %collective-permute-start.6 = (bf16[96,512]{1,0:T(8,128)(2,1)S(1)}, bf16[96,512]{1,0:T(8,128)(2,1)S(1)}, u32[]{:S(2)}, u32[]{:S(2)}) collective-permute-start(bf16[96,512]{1,0:T(8,128)(2,1)S(1)} %add_all.4.refs_0_), channel_id=1, source_target_pairs={{0,64},{32,96},{64,0},{96,32},{1,65},{33,97},{65,1},{97,33},{2,66}... | collective-permute-start | bytes 294920 | tf_op jit(solution)/shard_map/ppermute | solution.py:649
  66.6 13.8 %collective-permute-start.5 = (bf16[96,512]{1,0:T(8,128)(2,1)S(1)}, bf16[96,512]{1,0:T(8,128)(2,1)S(1)}, u32[]{:S(2)}, u32[]{:S(2)}) collective-permute-start(bf16[96,512]{1,0:T(8,128)(2,1)S(1)} %add_all.4.refs_0_), channel_id=1, source_target_pairs={{0,32},{32,64},{64,96},{96,0},{1,33},{33,65},{65,97},{97,1},{2,34}... | collective-permute-start | bytes 294920 | tf_op jit(solution)/shard_map/ppermute | solution.py:649
  71.2 12.0 %all-to-all-start.3 = ((bf16[16,96,128]{2,1,0:T(8,128)(2,1)}), bf16[16,96,128]{2,1,0:T(8,128)(2,1)S(1)}, u32[]{:S(2)}, u32[]{:S(2)}) async-start(bf16[16,96,128]{2,1,0:T(8,128)(2,1)} %sum_spread.3), calls=%async_computation.3 | async-start | bytes 786432 | tf_op jit(solution)/shard_map/all_to_all | solution.py:139
  74.8 8.5 %copy-start = (bf16[1024,384]{1,0:T(8,128)(2,1)S(1)}, bf16[1024,384]{1,0:T(8,128)(2,1)}, u32[]{:S(2)}) copy-start(bf16[1024,384]{1,0:T(8,128)(2,1)} %x_ref.3) | copy-start | bytes 2359300
  84.2 4.0 %collective-permute-start.8 = (bf16[96,384]{1,0:T(8,128)(2,1)S(1)}, bf16[96,384]{1,0:T(8,128)(2,1)S(1)}, u32[]{:S(2)}, u32[]{:S(2)}) collective-permute-start(bf16[96,384]{1,0:T(8,128)(2,1)S(1)} %get-tuple-element.57), channel_id=1, source_target_pairs={{0,16},{16,0},{1,17},{17,1},{2,18},{18,2},{3,19},{19,3},{4,20},{20... | collective-permute-start | bytes 221192 | tf_op jit(solution)/shard_map/ppermute | solution.py:644
  88.3 3.3 %collective-permute-start.9 = (f32[96,512]{1,0:T(8,128)S(1)}, f32[96,512]{1,0:T(8,128)S(1)}, u32[]{:S(2)}, u32[]{:S(2)}) collective-permute-start(f32[96,512]{1,0:T(8,128)S(1)} %add_all.6.own_ref), channel_id=1, source_target_pairs={{0,16},{16,0},{1,17},{17,1},{2,18},{18,2},{3,19},{19,3},{4,20},{20... | collective-permute-start | bytes 589832 | tf_op jit(solution)/shard_map/ppermute | solution.py:644
  88.7 4.2 %collective-permute-start.12 = (bf16[96,384]{1,0:T(8,128)(2,1)S(1)}, bf16[96,384]{1,0:T(8,128)(2,1)S(1)}, u32[]{:S(2)}, u32[]{:S(2)}) collective-permute-start(bf16[96,384]{1,0:T(8,128)(2,1)S(1)} %add_all.5.refs_0_), channel_id=1, source_target_pairs={{0,96},{32,0},{64,32},{96,64},{1,97},{33,1},{65,33},{97,65},{2,98}... | collective-permute-start | bytes 221192 | tf_op jit(solution)/shard_map/ppermute | solution.py:649
  90.8 4.8 %collective-permute-start.11 = (bf16[96,384]{1,0:T(8,128)(2,1)S(1)}, bf16[96,384]{1,0:T(8,128)(2,1)S(1)}, u32[]{:S(2)}, u32[]{:S(2)}) collective-permute-start(bf16[96,384]{1,0:T(8,128)(2,1)S(1)} %add_all.5.refs_0_), channel_id=1, source_target_pairs={{0,64},{32,96},{64,0},{96,32},{1,65},{33,97},{65,1},{97,33},{2,66}... | collective-permute-start | bytes 221192 | tf_op jit(solution)/shard_map/ppermute | solution.py:649
  91.4 6.3 %collective-permute-start.10 = (bf16[96,384]{1,0:T(8,128)(2,1)S(1)}, bf16[96,384]{1,0:T(8,128)(2,1)S(1)}, u32[]{:S(2)}, u32[]{:S(2)}) collective-permute-start(bf16[96,384]{1,0:T(8,128)(2,1)S(1)} %add_all.5.refs_0_), channel_id=1, source_target_pairs={{0,32},{32,64},{64,96},{96,0},{1,33},{33,65},{65,97},{97,1},{2,34}... | collective-permute-start | bytes 221192 | tf_op jit(solution)/shard_map/ppermute | solution.py:649
  97.8 1.9 %collective-permute-start.13 = (f32[96,384]{1,0:T(8,128)S(1)}, f32[96,384]{1,0:T(8,128)S(1)}, u32[]{:S(2)}, u32[]{:S(2)}) collective-permute-start(f32[96,384]{1,0:T(8,128)S(1)} %add_all.7.own_ref), channel_id=1, source_target_pairs={{0,16},{16,0},{1,17},{17,1},{2,18},{18,2},{3,19},{19,3},{4,20},{20... | collective-permute-start | bytes 442376 | tf_op jit(solution)/shard_map/ppermute | solution.py:644

commit v6 on v5

--- a/solution.py
+++ b/solution.py
@@ -91,11 +91,11 @@
     return pl.BlockSpec((4, width // 2, BLOCK // 2), lambda i: (i, 0, 0))
 
 
-def low_kernel(x_ref, down_ref, out_ref, x_held, down_held, sems):
+def low_kernel(x_ref, down_ref, out_ref, x_held, down_held, out_held, sems, out_sems):
     count = x_ref.shape[0] // BLOCK
     first = pltpu.make_async_copy(down_ref, down_held, sems.at[count])
     first.start()
-    copies = []
+    copies, results = [], []
     for c in range(count):
         rows = pl.ds(c * BLOCK, BLOCK)
         copies.append(pltpu.make_async_copy(x_ref.at[rows], x_held.at[rows], sems.at[c]))
@@ -103,36 +103,47 @@
     first.wait()
     for c in range(count):
         copies[c].wait()
-        part = dot_nt(down_held[...], x_held[c * BLOCK : (c + 1) * BLOCK, :])
-        store_pieces(out_ref.at[pl.ds(4 * c, 4)], part.astype(BF16))
+        part = dot_nt(down_held[...], x_held[c * BLOCK : (c + 1) * BLOCK, :]).astype(BF16)
+        pieces = pl.ds(4 * c, 4)
+        store_pieces(out_held.at[pieces], part)
+        results.append(pltpu.make_async_copy(out_held.at[pieces], out_ref.at[pieces], out_sems.at[c]))
+        results[c].start()
+    for result in results:
+        result.wait()
 
 
 def partial_low(x, down):
     rows, _ = x.shape
     far = pl.BlockSpec(memory_space=pltpu.HBM)
+    shape = piece_shape(rows, down.shape[0])
     return pl.pallas_call(
         low_kernel,
-        out_shape=jax.ShapeDtypeStruct(piece_shape(rows, down.shape[0]), BF16),
+        out_shape=jax.ShapeDtypeStruct(shape, BF16),
         in_specs=[far, far],
-        out_specs=VMEM,
+        out_specs=far,
         scratch_shapes=[
             pltpu.VMEM(x.shape, BF16),
             pltpu.VMEM(down.shape, BF16),
+            pltpu.VMEM(shape, BF16),
             pltpu.SemaphoreType.DMA((rows // BLOCK + 1,)),
+            pltpu.SemaphoreType.DMA((rows // BLOCK,)),
         ],
         compiler_params=params(),
         name="partial_low",
     )(*(pltpu.with_memory_space_constraint(a, pltpu.HBM) for a in (x, down)))
 
 
-def sum_spread_kernel(in_ref, out_ref):
+def sum_spread_kernel(in_ref, out_ref, held, sems):
     count = in_ref.shape[0]
     total = in_ref[0].astype(F32)
     for i in range(1, count):
         total = total + in_ref[i].astype(F32)
-    total = total.astype(BF16)
-    for i in range(count):
-        out_ref[i] = total
+    held[...] = total.astype(BF16)
+    copies = [pltpu.make_async_copy(held, out_ref.at[i], sems.at[i]) for i in range(count)]
+    for copy in copies:
+        copy.start()
+    for copy in copies:
+        copy.wait()
 
 
 def exchange(pieces):
@@ -140,12 +151,15 @@
 
 
 def sum_spread(pieces):
-    count, rows, width = pieces.shape
     return pl.pallas_call(
         sum_spread_kernel,
         out_shape=jax.ShapeDtypeStruct(pieces.shape, BF16),
         in_specs=[VMEM],
-        out_specs=VMEM,
+        out_specs=pl.BlockSpec(memory_space=pltpu.HBM),
+        scratch_shapes=[
+            pltpu.VMEM(pieces.shape[1:], BF16),
+            pltpu.SemaphoreType.DMA((pieces.shape[0],)),
+        ],
         compiler_params=params(),
         name="sum_spread",
     )(pieces)
@@ -252,12 +266,15 @@
     for n in range(frozen_ref.shape[1] // BLOCK):
         rows = pl.ds(n * BLOCK, BLOCK)
         copies.append(pltpu.make_async_copy(frozen_ref.at[:, rows], held.at[:, rows], sems.at[n]))
-        copies[n].start()
+    for copy in copies[:2]:
+        copy.start()
     states = [jnp.zeros((128, 128), F32)] * heads
     for n, copy in enumerate(copies):
         low = load_pieces(low_ref.at[pl.ds(4 * n, 4)])
         lifted = [dot_tn(low[i * rank : (i + 1) * rank, :], up_ref[i]) for i in range(3)]
         copy.wait()
+        if n + 2 < len(copies):
+            copies[n + 2].start()
         rows = pl.ds(n * BLOCK, BLOCK)
         for i in range(3):
             moving_ref[i, rows, :] = (held[i, rows, :].astype(F32) + lifted[i]).astype(BF16)
@@ -427,58 +444,86 @@
     )(moving, grad, row, col, passes, before, after)
 
 
-def late_kernel(moving_ref, row_ref, col_ref, pass_ref, before_ref, state_ref, attn_ref):
+def late_kernel(
+    moving_ref, row_ref, col_ref, pass_ref, before_ref, state_ref, out_ref,
+    held, before_held, attn, sems, before_sems, out_sems,
+):
     features = moving_ref.shape[2]
     heads = features // 128
     inverse = 1.0 / 128.0
-    step = pl.program_id(0)
     prefix_base = pass_ref.shape[0] // 3
-    row_i = lax.broadcasted_iota(jnp.int32, (CHUNK, CHUNK), 0)
-    col_i = lax.broadcasted_iota(jnp.int32, (CHUNK, CHUNK), 1)
-    for n in range(BLOCK // CHUNK):
-        rows = pl.ds(n * CHUNK, CHUNK)
-        col = col_ref[rows, :]
-        row = row_ref[:, rows]
-        allowed = (row_i >= col_i) & (col[:, SEG : SEG + 1] == row[SEG : SEG + 1, :])
-        shut = jnp.where(allowed, 0.0, NEGATIVE)
-        first = prefix_base + (step * (BLOCK // CHUNK) + n) * heads
-        states = []
-        for h in range(heads):
-            prefix = pass_ref[pl.ds(first + h, 1), :]
-            state = before_ref[n, h].astype(F32) + prefix * state_ref[h].astype(F32)
-            states.append(state.astype(BF16))
-        for h in range(0, heads, 2):
-            span = slice(h * 128, (h + 2) * 128)
-            q = moving_ref[0, rows, span]
-            weights = jnp.exp(
-                jnp.concatenate(
-                    [(col[:, i : i + 1] - row[i : i + 1, :]) + shut for i in (h, h + 1)], axis=1
+    square = (CHUNK, CHUNK)
+    row_i = lax.broadcasted_iota(jnp.int32, square, 0)
+    col_i = lax.broadcasted_iota(jnp.int32, square, 1)
+    per_block = BLOCK // CHUNK
+    copies, results = [], []
+    for n in range(moving_ref.shape[1] // BLOCK):
+        rows = pl.ds(n * BLOCK, BLOCK)
+        chunks = pl.ds(n * per_block, per_block)
+        copies.append(pltpu.make_async_copy(moving_ref.at[:, rows], held.at[:, rows], sems.at[n]))
+        copies.append(
+            pltpu.make_async_copy(before_ref.at[chunks], before_held.at[chunks], before_sems.at[n])
+        )
+    for copy in copies[:4]:
+        copy.start()
+    for n in range(moving_ref.shape[1] // BLOCK):
+        copies[2 * n].wait()
+        copies[2 * n + 1].wait()
+        for copy in copies[2 * n + 4 : 2 * n + 6]:
+            copy.start()
+        for c in range(n * per_block, (n + 1) * per_block):
+            rows = pl.ds(c * CHUNK, CHUNK)
+            col = col_ref[rows, :]
+            row = row_ref[0:8, rows]
+            same = col[:, SEG : SEG + 1] == row[SEG : SEG + 1, :]
+            shut = jnp.where(same & (row_i >= col_i), 0.0, NEGATIVE)
+            enter_shut = jnp.broadcast_to(col[:, ENTER_SHUT : ENTER_SHUT + 1], square)
+            for h in range(0, heads, 2):
+                span = slice(h * 128, (h + 2) * 128)
+                q = held[0, rows, span]
+                k = held[1, rows, span]
+                weights, enter, states = [], [], []
+                for i in (h, h + 1):
+                    sums = jnp.broadcast_to(col[:, i : i + 1], square)
+                    weights.append(jnp.exp((sums - row[i : i + 1, :]) + shut))
+                    enter.append(jnp.exp(sums + enter_shut))
+                    first = prefix_base + c * heads + i
+                    prefix = pass_ref[first : first + 1, :]
+                    state = before_held[c, i].astype(F32) + prefix * state_ref[i].astype(F32)
+                    states.append(state.astype(BF16))
+                a = (pair_nt(q, k) * jnp.concatenate(weights, axis=1)).astype(BF16)
+                carried = jnp.concatenate(
+                    [dot_nt(q[:, :128], states[0]), dot_nt(q[:, 128:], states[1])], axis=1
                 )
-            )
-            a = (dot_nt(q, diagonal_of(moving_ref[1, rows, span])) * weights).astype(BF16)
-            out = dot_nn(a, diagonal_of(moving_ref[2, rows, span]))
-            out = out + widen(col, ENTER + h) * dot_nt(q, diagonal(states[h], states[h + 1]))
-            attn_ref[rows, span] = (out * inverse).astype(BF16)
+                out = dot_nn(a, diagonal_of(held[2, rows, span]))
+                out = out + jnp.concatenate(enter, axis=1) * carried
+                attn[rows, span] = (out * inverse).astype(BF16)
+        rows = pl.ds(n * BLOCK, BLOCK)
+        results.append(pltpu.make_async_copy(attn.at[rows], out_ref.at[rows], out_sems.at[n]))
+        results[n].start()
+    for result in results:
+        result.wait()
 
 
 def late(moving, row, col, passes, before, state):
     _, rows, features = moving.shape
-    heads = features // 128
     moving, before = (pltpu.with_memory_space_constraint(a, pltpu.HBM) for a in (moving, before))
+    far = pl.BlockSpec(memory_space=pltpu.HBM)
+    blocks = rows // BLOCK
     return pl.pallas_call(
         late_kernel,
         out_shape=jax.ShapeDtypeStruct((rows, features), BF16),
-        grid=(rows // BLOCK,),
-        in_specs=[
-            pl.BlockSpec((3, BLOCK, features), lambda i: (0, i, 0)),
-            pl.BlockSpec((8, BLOCK), lambda i: (0, i)),
-            pl.BlockSpec((BLOCK, 128), lambda i: (i, 0)),
-            pl.BlockSpec(passes.shape, lambda i: (0, 0)),
-            pl.BlockSpec((BLOCK // CHUNK, heads, 128, 128), lambda i: (i, 0, 0, 0)),
-            pl.BlockSpec(state.shape, lambda i: (0, 0, 0)),
+        in_specs=[far, VMEM, VMEM, VMEM, far, VMEM],
+        out_specs=far,
+        scratch_shapes=[
+            pltpu.VMEM(moving.shape, BF16),
+            pltpu.VMEM(before.shape, BF16),
+            pltpu.VMEM((rows, features), BF16),
+            pltpu.SemaphoreType.DMA((blocks,)),
+            pltpu.SemaphoreType.DMA((blocks,)),
+            pltpu.SemaphoreType.DMA((blocks,)),
         ],
-        out_specs=pl.BlockSpec((BLOCK, features), lambda i: (i, 0)),
-        compiler_params=params(dimension_semantics=("arbitrary",)),
+        compiler_params=params(),
         cost_estimate=cost(6e9, 6e6),
         name="late",
     )(moving, row, col, passes, before, state)
@@ -540,6 +585,8 @@
                 grad_ref[i, rows, span] = (result * inverse).astype(BF16)
         copies.append(pltpu.make_async_copy(grad_ref.at[:, rows], out_ref.at[:, rows], sems.at[n]))
         copies[n].start()
+    for n in range(count):
+        rows = pl.ds(n * BLOCK, BLOCK)
         low_grad = [dot_nt(up_ref[i], grad_ref[i, rows, :]).astype(BF16) for i in range(3)]
         store_pieces(low_grad_ref.at[pl.ds(4 * n, 4)], jnp.concatenate(low_grad, axis=0))
         low = load_pieces(low_ref.at[pl.ds(4 * n, 4)])

time: 102 us -> 101 us (level)
  no operation moved by 1% of the time
where the time goes in v6:
time: 101 us
  starting transfers between devices  39.1 us (39%)
  Pallas kernels  29.6 us (29%)
  waiting for transfers between devices  29.1 us (29%)
  local copies, waits for them, and re-layouts  1.28 us (1%)
    all_to_all x4, waiting for transfers between devices, exchange(): return lax.all_to_all(pieces, ('z', 'x'), 0, 0)  19.9 us
    all_to_all x4, starting transfers between devices, exchange(): return lax.all_to_all(pieces, ('z', 'x'), 0, 0)  19.1 us
    ppermute x9, starting transfers between devices, along_y(): return lax.ppermute(a, 'y', [(i, (i + k) % count) for i in range(count)])  11.2 us
    ppermute x5, starting transfers between devices, to_mate(): return lax.ppermute(a, 'core', [(0, 1), (1, 0)])  8.77 us
    pallas_call x1, Pallas kernels, late(): pl.pallas_call(late_kernel, out_shape=jax.ShapeDtypeStruct((rows, feature...  5.37 us
    pallas_call x1, Pallas kernels, inside(): pl.pallas_call(inside_kernel, out_shape=jax.ShapeDtypeStruct(moving.shape...  5.35 us
    ppermute x9, waiting for transfers between devices, along_y(): return lax.ppermute(a, 'y', [(i, (i + k) % count) for i in range(count)])  5.17 us
    pallas_call x1, Pallas kernels, finish(): pl.pallas_call(functools.partial(finish_kernel, chips), out_shape=(jax.Sh...  4.11 us
  transfers between devices with their start and end apart: 18, of which 11 were waited for; matrix products, arithmetic and copies ran while one was open for 2% of the time, Pallas kernels for 15%

profile of v6, /device:TPU:1, one launch (start us, length us, event | category | flops | bytes accessed | tf_op | source)
XLA Modules:
  0.0 100.6 jit_solution(5944147456411115846)
XLA Ops:
  0.7 2.9 %partial_low.1 = bf16[16,96,128]{2,1,0:T(8,128)(2,1)} custom-call(bf16[1024,384]{1,0:T(8,128)(2,1)} %x_ref.3, bf16[192,384]{1,0:T(8,128)(2,1)} %bitcast.13), custom_call_target="tpu_custom_call" | custom-call | tf_op jit(solution)/shard_map/partial_low/pallas_call | solution.py:119
  3.5 8.4 %all-to-all-start = ((bf16[16,96,128]{2,1,0:T(8,128)(2,1)}), bf16[16,96,128]{2,1,0:T(8,128)(2,1)S(1)}, u32[]{:S(2)}, u32[]{:S(2)}) async-start(bf16[16,96,128]{2,1,0:T(8,128)(2,1)} %partial_low.1), calls=%async_computation | async-start | bytes 786432 | tf_op jit(solution)/shard_map/all_to_all | solution.py:150
  12.0 1.2 %dynamic_slice.3 = s32[1]{0:T(128)} dynamic-slice(s32[8]{0:T(128)} %param.15, s32[]{:T(128)S(6)} %select_n.3), dynamic_slice_sizes={1} | dynamic-slice | bytes 12 | tf_op jit(solution)/shard_map/dynamic_slice | solution.py:703
  13.2 0.7 pad_add_fusion.meta_ref
  13.9 7.2 %all-to-all-done.in_ref = bf16[16,96,128]{2,1,0:T(8,128)(2,1)S(1)} async-done(((bf16[16,96,128]{2,1,0:T(8,128)(2,1)}), bf16[16,96,128]{2,1,0:T(8,128)(2,1)S(1)}, u32[]{:S(2)}, u32[]{:S(2)}) %all-to-all-start) | async-done | bytes 393248 | tf_op jit(solution)/shard_map/all_to_all | solution.py:150
  21.1 0.9 sum_spread.2
  22.1 3.6 %all-to-all-start.1 = ((bf16[16,96,128]{2,1,0:T(8,128)(2,1)}), bf16[16,96,128]{2,1,0:T(8,128)(2,1)S(1)}, u32[]{:S(2)}, u32[]{:S(2)}) async-start(bf16[16,96,128]{2,1,0:T(8,128)(2,1)} %sum_spread.2), calls=%async_computation.1 | async-start | bytes 786432 | tf_op jit(solution)/shard_map/all_to_all | solution.py:150
  25.7 0.0 copy-start.1
  25.7 0.0 copy-start.2
  25.7 2.0 %decay_tables.1 = (f32[16,1024]{1,0:T(8,128)S(1)}, f32[1024,128]{1,0:T(8,128)S(1)}, f32[96,128]{1,0:T(8,128)S(1)}) custom-call(s32[3]{0:T(128)S(1)} %pad_add_fusion.meta_ref, bf16[4,1024]{1,0:T(4,128)(2,1)S(1)} %copy-done.3, s32[1,1024]{1,0:T(1,128)S(1)} %bitcast.10), custom_call_target="tpu_custom_call" | custom-call | flops 4000000000 | bytes 1000000 | tf_op jit(solution)/shard_map/decay_tables/pallas_call | solution.py:241
  27.7 6.2 %all-to-all-done.1.low_ref = bf16[16,96,128]{2,1,0:T(8,128)(2,1)S(1)} async-done(((bf16[16,96,128]{2,1,0:T(8,128)(2,1)}), bf16[16,96,128]{2,1,0:T(8,128)(2,1)S(1)}, u32[]{:S(2)}, u32[]{:S(2)}) %all-to-all-start.1) | async-done | bytes 393248 | tf_op jit(solution)/shard_map/all_to_all | solution.py:150
  33.9 3.7 %project.1 = (bf16[3,1024,512]{2,1,0:T(8,128)(2,1)S(1)}, bf16[8,4,128,128]{3,2,1,0:T(8,128)(2,1)S(1)}, bf16[8,4,128,128]{3,2,1,0:T(8,128)(2,1)S(1)}, bf16[1088,128]{1,0:T(8,128)(2,1)S(1)}) custom-call(bf16[3,1024,512]{2,1,0:T(8,128)(2,1)} %frozen_ref.1, bf16[16,96,128]{2,1,0:T(8,128)(2,1)S(1)} %all-to-all-done.1.low_ref, bf16[3,64,512]{2,1,0:T(8,128)(2,1)S(1)} %copy-done.2, ...), custom_call_target="tpu_custom_call" | custom-call | flops 4000000000 | bytes 10000000 | tf_op jit(solution)/shard_map/project/pallas_call | solution.py:320
  37.6 3.1 %collective-permute-start = (bf16[1088,128]{1,0:T(8,128)(2,1)S(1)}, bf16[1088,128]{1,0:T(8,128)(2,1)S(1)}, u32[]{:S(2)}, u32[]{:S(2)}) collective-permute-start(bf16[1088,128]{1,0:T(8,128)(2,1)S(1)} %get-tuple-element.44.own_ref), channel_id=1, source_target_pairs={{0,16},{16,0},{1,17},{17,1},{2,18},{18,2},{3,19},{19,3},{4,20},{20... | collective-permute-start | bytes 835592 | tf_op jit(solution)/shard_map/ppermute | solution.py:691
  40.7 1.2 %collective-permute-done.mate_ref = bf16[1088,128]{1,0:T(8,128)(2,1)S(1)} collective-permute-done((bf16[1088,128]{1,0:T(8,128)(2,1)S(1)}, bf16[1088,128]{1,0:T(8,128)(2,1)S(1)}, u32[]{:S(2)}, u32[]{:S(2)}) %collective-permute-start) | collective-permute-done | bytes 278560 | tf_op jit(solution)/shard_map/ppermute | solution.py:691
  41.9 0.7 join.1
  42.6 1.4 %collective-permute-start.1 = (bf16[576,128]{1,0:T(8,128)(2,1)S(1)}, bf16[576,128]{1,0:T(8,128)(2,1)S(1)}, u32[]{:S(2)}, u32[]{:S(2)}) collective-permute-start(bf16[576,128]{1,0:T(8,128)(2,1)S(1)} %get-tuple-element.45), channel_id=1, source_target_pairs={{0,32},{32,64},{64,96},{96,0},{1,33},{33,65},{65,97},{97,1},{2,34}... | collective-permute-start | bytes 442376 | tf_op jit(solution)/shard_map/ppermute | solution.py:696
  43.9 2.6 %collective-permute-start.2 = (bf16[576,128]{1,0:T(8,128)(2,1)S(1)}, bf16[576,128]{1,0:T(8,128)(2,1)S(1)}, u32[]{:S(2)}, u32[]{:S(2)}) collective-permute-start(bf16[576,128]{1,0:T(8,128)(2,1)S(1)} %get-tuple-element.46), channel_id=1, source_target_pairs={{0,64},{32,96},{64,0},{96,32},{1,65},{33,97},{65,1},{97,33},{2,66}... | collective-permute-start | bytes 442376 | tf_op jit(solution)/shard_map/ppermute | solution.py:696
  46.6 1.1 %collective-permute-start.3 = (bf16[576,128]{1,0:T(8,128)(2,1)S(1)}, bf16[576,128]{1,0:T(8,128)(2,1)S(1)}, u32[]{:S(2)}, u32[]{:S(2)}) collective-permute-start(bf16[576,128]{1,0:T(8,128)(2,1)S(1)} %get-tuple-element.47), channel_id=1, source_target_pairs={{0,96},{32,0},{64,32},{96,64},{1,97},{33,1},{65,33},{97,65},{2,98}... | collective-permute-start | bytes 442376 | tf_op jit(solution)/shard_map/ppermute | solution.py:696
  47.6 5.4 %inside.1.part_ref = f32[3,1024,512]{2,1,0:T(8,128)S(1)} custom-call(bf16[3,1024,512]{2,1,0:T(8,128)(2,1)S(1)} %get-tuple-element.40.moving_ref, bf16[1024,512]{1,0:T(8,128)(2,1)S(1)} %copy-done.1, f32[16,1024]{1,0:T(8,128)S(1)} %get-tuple-element.38.row_ref, f32[1024,128]{1,0:T(8,128)S(1)} %get-tuple-element.41.col_ref, ...), custom_call_target="tpu_custom_call" | custom-call | flops 12000000000 | bytes 12000000 | tf_op jit(solution)/shard_map/inside/pallas_call | solution.py:436
  53.0 0.3 collective-permute-done.2.refs_1_
  53.3 0.0 collective-permute-done.3.refs_2_
  53.3 4.1 %finish.1 = (bf16[3,1024,512]{2,1,0:T(8,128)(2,1)}, bf16[16,96,128]{2,1,0:T(8,128)(2,1)}, bf16[4,128,128]{2,1,0:T(8,128)(2,1)S(1)}, bf16[96,512]{1,0:T(8,128)(2,1)S(1)}, bf16[96,512]{1,0:T(8,128)(2,1)S(1)}) custom-call(s32[3]{0:T(128)S(1)} %pad_add_fusion.meta_ref, bf16[3,1024,512]{2,1,0:T(8,128)(2,1)S(1)} %get-tuple-element.40.moving_ref, ...), custom_call_target="tpu_custom_call" | custom-call | flops 4000000000 | bytes 14000000 | tf_op jit(solution)/shard_map/finish/pallas_call | solution.py:608
  57.4 3.6 %all-to-all-start.2 = ((bf16[16,96,128]{2,1,0:T(8,128)(2,1)}), bf16[16,96,128]{2,1,0:T(8,128)(2,1)S(1)}, u32[]{:S(2)}, u32[]{:S(2)}) async-start(bf16[16,96,128]{2,1,0:T(8,128)(2,1)} %get-tuple-element.48), calls=%async_computation.2 | async-start | bytes 786432 | tf_op jit(solution)/shard_map/all_to_all | solution.py:150
  61.0 1.3 %collective-permute-start.4 = (bf16[96,512]{1,0:T(8,128)(2,1)S(1)}, bf16[96,512]{1,0:T(8,128)(2,1)S(1)}, u32[]{:S(2)}, u32[]{:S(2)}) collective-permute-start(bf16[96,512]{1,0:T(8,128)(2,1)S(1)} %get-tuple-element.50), channel_id=1, source_target_pairs={{0,16},{16,0},{1,17},{17,1},{2,18},{18,2},{3,19},{19,3},{4,20},{20... | collective-permute-start | bytes 294920 | tf_op jit(solution)/shard_map/ppermute | solution.py:691
  62.3 0.9 collective-permute-done.4.refs_1_
  63.3 1.9 %collective-permute-start.7 = (bf16[96,512]{1,0:T(8,128)(2,1)S(1)}, bf16[96,512]{1,0:T(8,128)(2,1)S(1)}, u32[]{:S(2)}, u32[]{:S(2)}) collective-permute-start(bf16[96,512]{1,0:T(8,128)(2,1)S(1)} %add_all.4.refs_0_), channel_id=1, source_target_pairs={{0,96},{32,0},{64,32},{96,64},{1,97},{33,1},{65,33},{97,65},{2,98}... | collective-permute-start | bytes 294920 | tf_op jit(solution)/shard_map/ppermute | solution.py:696
  65.2 0.9 collective-permute-start.6
  66.1 0.4 collective-permute-start.5
  66.5 3.4 %all-to-all-done.2.in_ref = bf16[16,96,128]{2,1,0:T(8,128)(2,1)S(1)} async-done(((bf16[16,96,128]{2,1,0:T(8,128)(2,1)}), bf16[16,96,128]{2,1,0:T(8,128)(2,1)S(1)}, u32[]{:S(2)}, u32[]{:S(2)}) %all-to-all-start.2) | async-done | bytes 393248 | tf_op jit(solution)/shard_map/all_to_all | solution.py:150
  69.9 0.9 sum_spread.3
  70.8 3.6 %all-to-all-start.3 = ((bf16[16,96,128]{2,1,0:T(8,128)(2,1)}), bf16[16,96,128]{2,1,0:T(8,128)(2,1)S(1)}, u32[]{:S(2)}, u32[]{:S(2)}) async-start(bf16[16,96,128]{2,1,0:T(8,128)(2,1)} %sum_spread.3), calls=%async_computation.3 | async-start | bytes 786432 | tf_op jit(solution)/shard_map/all_to_all | solution.py:150
  74.4 0.0 copy-start
  74.4 5.4 %late.1 = bf16[1024,512]{1,0:T(8,128)(2,1)} custom-call(bf16[3,1024,512]{2,1,0:T(8,128)(2,1)} %copy-done.5, f32[16,1024]{1,0:T(8,128)S(1)} %get-tuple-element.38.row_ref, f32[1024,128]{1,0:T(8,128)S(1)} %get-tuple-element.41.col_ref, f32[96,128]{1,0:T(8,128)S(1)} %get-tuple-element.39.pass_ref, bf16[8,4,128,128]{3,2,1,0:T(8,128)(2,1)} %copy-done.6, ...), custom_call_target="tpu_custom_call" | custom-call | flops 6000000000 | bytes 6000000 | tf_op jit(solution)/shard_map/late/pallas_call | solution.py:513
  79.8 3.0 %all-to-all-done.3.grad_ref = bf16[16,96,128]{2,1,0:T(8,128)(2,1)S(1)} async-done(((bf16[16,96,128]{2,1,0:T(8,128)(2,1)}), bf16[16,96,128]{2,1,0:T(8,128)(2,1)S(1)}, u32[]{:S(2)}, u32[]{:S(2)}) %all-to-all-start.3) | async-done | bytes 393248 | tf_op jit(solution)/shard_map/all_to_all | solution.py:150
  82.9 0.9 partial_down.1
  83.8 3.1 %collective-permute-start.8 = (bf16[96,384]{1,0:T(8,128)(2,1)S(1)}, bf16[96,384]{1,0:T(8,128)(2,1)S(1)}, u32[]{:S(2)}, u32[]{:S(2)}) collective-permute-start(bf16[96,384]{1,0:T(8,128)(2,1)S(1)} %get-tuple-element.57), channel_id=1, source_target_pairs={{0,16},{16,0},{1,17},{17,1},{2,18},{18,2},{3,19},{19,3},{4,20},{20... | collective-permute-start | bytes 221192 | tf_op jit(solution)/shard_map/ppermute | solution.py:691
  86.9 0.9 collective-permute-done.8.refs_1_
  87.8 0.1 add_all.6.own_ref
  87.9 0.4 collective-permute-start.9
  88.3 2.1 %collective-permute-start.12 = (bf16[96,384]{1,0:T(8,128)(2,1)S(1)}, bf16[96,384]{1,0:T(8,128)(2,1)S(1)}, u32[]{:S(2)}, u32[]{:S(2)}) collective-permute-start(bf16[96,384]{1,0:T(8,128)(2,1)S(1)} %add_all.5.refs_0_), channel_id=1, source_target_pairs={{0,96},{32,0},{64,32},{96,64},{1,97},{33,1},{65,33},{97,65},{2,98}... | collective-permute-start | bytes 221192 | tf_op jit(solution)/shard_map/ppermute | solution.py:696
  90.4 0.6 collective-permute-start.11
  91.0 0.2 collective-permute-start.10
  91.2 1.3 %join_halves.2 = f32[192,512]{1,0:T(8,128)} custom-call(s32[3]{0:T(128)S(1)} %pad_add_fusion.meta_ref, f32[96,512]{1,0:T(8,128)S(1)} %add_all.6.own_ref, f32[96,512]{1,0:T(8,128)S(1)} %collective-permute-done.9.mate_ref), custom_call_target="tpu_custom_call" | custom-call | tf_op jit(solution)/shard_map/join_halves/pallas_call | solution.py:662
  92.5 2.7 %collective-permute-done.11.refs_2_ = bf16[96,384]{1,0:T(8,128)(2,1)S(1)} collective-permute-done((bf16[96,384]{1,0:T(8,128)(2,1)S(1)}, bf16[96,384]{1,0:T(8,128)(2,1)S(1)}, u32[]{:S(2)}, u32[]{:S(2)}) %collective-permute-start.11) | collective-permute-done | bytes 73760 | tf_op jit(solution)/shard_map/ppermute | solution.py:696
  95.2 2.2 %collective-permute-done.10.refs_1_ = bf16[96,384]{1,0:T(8,128)(2,1)S(1)} collective-permute-done((bf16[96,384]{1,0:T(8,128)(2,1)S(1)}, bf16[96,384]{1,0:T(8,128)(2,1)S(1)}, u32[]{:S(2)}, u32[]{:S(2)}) %collective-permute-start.10) | collective-permute-done | bytes 73760 | tf_op jit(solution)/shard_map/ppermute | solution.py:696
  97.4 0.9 collective-permute-start.13
  98.3 1.0 %collective-permute-done.13.mate_ref = f32[96,384]{1,0:T(8,128)S(1)} collective-permute-done((f32[96,384]{1,0:T(8,128)S(1)}, f32[96,384]{1,0:T(8,128)S(1)}, u32[]{:S(2)}, u32[]{:S(2)}) %collective-permute-start.13) | collective-permute-done | bytes 147488 | tf_op jit(solution)/shard_map/ppermute | solution.py:691
  99.3 1.3 %join_halves.3 = f32[192,384]{1,0:T(8,128)} custom-call(s32[3]{0:T(128)S(1)} %pad_add_fusion.meta_ref, f32[96,384]{1,0:T(8,128)S(1)} %add_all.7.own_ref, f32[96,384]{1,0:T(8,128)S(1)} %collective-permute-done.13.mate_ref), custom_call_target="tpu_custom_call" | custom-call | tf_op jit(solution)/shard_map/join_halves/pallas_call | solution.py:662
  (20 shorter events, 0.1 us)
Async XLA Ops:
  0.6 25.0 %copy-start.4 = (s32[1024]{0:T(1024)S(1)}, s32[1024]{0:T(1024)}, u32[]{:S(2)}) copy-start(s32[1024]{0:T(1024)} %param.14) | copy-start | bytes 12292
  0.6 25.0 %copy-start.3 = (bf16[4,1024]{1,0:T(4,128)(2,1)S(1)}, bf16[4,1024]{1,0:T(4,128)(2,1)}, u32[]{:S(2)}) copy-start(bf16[4,1024]{1,0:T(4,128)(2,1)} %decay_ref.1) | copy-start | bytes 24580
  3.5 17.6 %all-to-all-start = ((bf16[16,96,128]{2,1,0:T(8,128)(2,1)}), bf16[16,96,128]{2,1,0:T(8,128)(2,1)S(1)}, u32[]{:S(2)}, u32[]{:S(2)}) async-start(bf16[16,96,128]{2,1,0:T(8,128)(2,1)} %partial_low.1), calls=%async_computation | async-start | bytes 786432 | tf_op jit(solution)/shard_map/all_to_all | solution.py:150
  22.1 11.8 %all-to-all-start.1 = ((bf16[16,96,128]{2,1,0:T(8,128)(2,1)}), bf16[16,96,128]{2,1,0:T(8,128)(2,1)S(1)}, u32[]{:S(2)}, u32[]{:S(2)}) async-start(bf16[16,96,128]{2,1,0:T(8,128)(2,1)} %sum_spread.2), calls=%async_computation.1 | async-start | bytes 786432 | tf_op jit(solution)/shard_map/all_to_all | solution.py:150
  25.7 8.2 %copy-start.1 = (bf16[1024,512]{1,0:T(8,128)(2,1)S(1)}, bf16[1024,512]{1,0:T(8,128)(2,1)}, u32[]{:S(2)}) copy-start(bf16[1024,512]{1,0:T(8,128)(2,1)} %g_ref.1) | copy-start | bytes 3145732
  25.7 8.2 %copy-start.2 = (bf16[3,64,512]{2,1,0:T(8,128)(2,1)S(1)}, bf16[3,64,512]{2,1,0:T(8,128)(2,1)}, u32[]{:S(2)}) copy-start(bf16[3,64,512]{2,1,0:T(8,128)(2,1)} %up_ref.3) | copy-start | bytes 589828
  37.6 15.4 %copy-start.6 = (bf16[8,4,128,128]{3,2,1,0:T(8,128)(2,1)}, bf16[8,4,128,128]{3,2,1,0:T(8,128)(2,1)S(1)}, u32[]{:S(2)}) copy-start(bf16[8,4,128,128]{3,2,1,0:T(8,128)(2,1)S(1)} %get-tuple-element.42.before_ref) | copy-start | bytes 3145732
  37.6 15.7 %copy-start.5 = (bf16[3,1024,512]{2,1,0:T(8,128)(2,1)}, bf16[3,1024,512]{2,1,0:T(8,128)(2,1)S(1)}, u32[]{:S(2)}) copy-start(bf16[3,1024,512]{2,1,0:T(8,128)(2,1)S(1)} %get-tuple-element.40.moving_ref) | copy-start | bytes 9437188
  37.6 4.3 %collective-permute-start = (bf16[1088,128]{1,0:T(8,128)(2,1)S(1)}, bf16[1088,128]{1,0:T(8,128)(2,1)S(1)}, u32[]{:S(2)}, u32[]{:S(2)}) collective-permute-start(bf16[1088,128]{1,0:T(8,128)(2,1)S(1)} %get-tuple-element.44.own_ref), channel_id=1, source_target_pairs={{0,16},{16,0},{1,17},{17,1},{2,18},{18,2},{3,19},{19,3},{4,20},{20... | collective-permute-start | bytes 835592 | tf_op jit(solution)/shard_map/ppermute | solution.py:691
  42.6 10.4 %collective-permute-start.1 = (bf16[576,128]{1,0:T(8,128)(2,1)S(1)}, bf16[576,128]{1,0:T(8,128)(2,1)S(1)}, u32[]{:S(2)}, u32[]{:S(2)}) collective-permute-start(bf16[576,128]{1,0:T(8,128)(2,1)S(1)} %get-tuple-element.45), channel_id=1, source_target_pairs={{0,32},{32,64},{64,96},{96,0},{1,33},{33,65},{65,97},{97,1},{2,34}... | collective-permute-start | bytes 442376 | tf_op jit(solution)/shard_map/ppermute | solution.py:696
  43.9 9.4 %collective-permute-start.2 = (bf16[576,128]{1,0:T(8,128)(2,1)S(1)}, bf16[576,128]{1,0:T(8,128)(2,1)S(1)}, u32[]{:S(2)}, u32[]{:S(2)}) collective-permute-start(bf16[576,128]{1,0:T(8,128)(2,1)S(1)} %get-tuple-element.46), channel_id=1, source_target_pairs={{0,64},{32,96},{64,0},{96,32},{1,65},{33,97},{65,1},{97,33},{2,66}... | collective-permute-start | bytes 442376 | tf_op jit(solution)/shard_map/ppermute | solution.py:696
  46.6 6.8 %collective-permute-start.3 = (bf16[576,128]{1,0:T(8,128)(2,1)S(1)}, bf16[576,128]{1,0:T(8,128)(2,1)S(1)}, u32[]{:S(2)}, u32[]{:S(2)}) collective-permute-start(bf16[576,128]{1,0:T(8,128)(2,1)S(1)} %get-tuple-element.47), channel_id=1, source_target_pairs={{0,96},{32,0},{64,32},{96,64},{1,97},{33,1},{65,33},{97,65},{2,98}... | collective-permute-start | bytes 442376 | tf_op jit(solution)/shard_map/ppermute | solution.py:696
  57.4 12.5 %all-to-all-start.2 = ((bf16[16,96,128]{2,1,0:T(8,128)(2,1)}), bf16[16,96,128]{2,1,0:T(8,128)(2,1)S(1)}, u32[]{:S(2)}, u32[]{:S(2)}) async-start(bf16[16,96,128]{2,1,0:T(8,128)(2,1)} %get-tuple-element.48), calls=%async_computation.2 | async-start | bytes 786432 | tf_op jit(solution)/shard_map/all_to_all | solution.py:150
  61.0 2.2 %collective-permute-start.4 = (bf16[96,512]{1,0:T(8,128)(2,1)S(1)}, bf16[96,512]{1,0:T(8,128)(2,1)S(1)}, u32[]{:S(2)}, u32[]{:S(2)}) collective-permute-start(bf16[96,512]{1,0:T(8,128)(2,1)S(1)} %get-tuple-element.50), channel_id=1, source_target_pairs={{0,16},{16,0},{1,17},{17,1},{2,18},{18,2},{3,19},{19,3},{4,20},{20... | collective-permute-start | bytes 294920 | tf_op jit(solution)/shard_map/ppermute | solution.py:691
  63.3 16.5 %collective-permute-start.7 = (bf16[96,512]{1,0:T(8,128)(2,1)S(1)}, bf16[96,512]{1,0:T(8,128)(2,1)S(1)}, u32[]{:S(2)}, u32[]{:S(2)}) collective-permute-start(bf16[96,512]{1,0:T(8,128)(2,1)S(1)} %add_all.4.refs_0_), channel_id=1, source_target_pairs={{0,96},{32,0},{64,32},{96,64},{1,97},{33,1},{65,33},{97,65},{2,98}... | collective-permute-start | bytes 294920 | tf_op jit(solution)/shard_map/ppermute | solution.py:696
  65.2 14.6 %collective-permute-start.6 = (bf16[96,512]{1,0:T(8,128)(2,1)S(1)}, bf16[96,512]{1,0:T(8,128)(2,1)S(1)}, u32[]{:S(2)}, u32[]{:S(2)}) collective-permute-start(bf16[96,512]{1,0:T(8,128)(2,1)S(1)} %add_all.4.refs_0_), channel_id=1, source_target_pairs={{0,64},{32,96},{64,0},{96,32},{1,65},{33,97},{65,1},{97,33},{2,66}... | collective-permute-start | bytes 294920 | tf_op jit(solution)/shard_map/ppermute | solution.py:696
  66.1 13.8 %collective-permute-start.5 = (bf16[96,512]{1,0:T(8,128)(2,1)S(1)}, bf16[96,512]{1,0:T(8,128)(2,1)S(1)}, u32[]{:S(2)}, u32[]{:S(2)}) collective-permute-start(bf16[96,512]{1,0:T(8,128)(2,1)S(1)} %add_all.4.refs_0_), channel_id=1, source_target_pairs={{0,32},{32,64},{64,96},{96,0},{1,33},{33,65},{65,97},{97,1},{2,34}... | collective-permute-start | bytes 294920 | tf_op jit(solution)/shard_map/ppermute | solution.py:696
  70.8 12.0 %all-to-all-start.3 = ((bf16[16,96,128]{2,1,0:T(8,128)(2,1)}), bf16[16,96,128]{2,1,0:T(8,128)(2,1)S(1)}, u32[]{:S(2)}, u32[]{:S(2)}) async-start(bf16[16,96,128]{2,1,0:T(8,128)(2,1)} %sum_spread.3), calls=%async_computation.3 | async-start | bytes 786432 | tf_op jit(solution)/shard_map/all_to_all | solution.py:150
  74.4 8.5 %copy-start = (bf16[1024,384]{1,0:T(8,128)(2,1)S(1)}, bf16[1024,384]{1,0:T(8,128)(2,1)}, u32[]{:S(2)}) copy-start(bf16[1024,384]{1,0:T(8,128)(2,1)} %x_ref.3) | copy-start | bytes 2359300
  83.8 4.0 %collective-permute-start.8 = (bf16[96,384]{1,0:T(8,128)(2,1)S(1)}, bf16[96,384]{1,0:T(8,128)(2,1)S(1)}, u32[]{:S(2)}, u32[]{:S(2)}) collective-permute-start(bf16[96,384]{1,0:T(8,128)(2,1)S(1)} %get-tuple-element.57), channel_id=1, source_target_pairs={{0,16},{16,0},{1,17},{17,1},{2,18},{18,2},{3,19},{19,3},{4,20},{20... | collective-permute-start | bytes 221192 | tf_op jit(solution)/shard_map/ppermute | solution.py:691
  87.9 3.3 %collective-permute-start.9 = (f32[96,512]{1,0:T(8,128)S(1)}, f32[96,512]{1,0:T(8,128)S(1)}, u32[]{:S(2)}, u32[]{:S(2)}) collective-permute-start(f32[96,512]{1,0:T(8,128)S(1)} %add_all.6.own_ref), channel_id=1, source_target_pairs={{0,16},{16,0},{1,17},{17,1},{2,18},{18,2},{3,19},{19,3},{4,20},{20... | collective-permute-start | bytes 589832 | tf_op jit(solution)/shard_map/ppermute | solution.py:691
  88.3 4.2 %collective-permute-start.12 = (bf16[96,384]{1,0:T(8,128)(2,1)S(1)}, bf16[96,384]{1,0:T(8,128)(2,1)S(1)}, u32[]{:S(2)}, u32[]{:S(2)}) collective-permute-start(bf16[96,384]{1,0:T(8,128)(2,1)S(1)} %add_all.5.refs_0_), channel_id=1, source_target_pairs={{0,96},{32,0},{64,32},{96,64},{1,97},{33,1},{65,33},{97,65},{2,98}... | collective-permute-start | bytes 221192 | tf_op jit(solution)/shard_map/ppermute | solution.py:696
  90.4 4.8 %collective-permute-start.11 = (bf16[96,384]{1,0:T(8,128)(2,1)S(1)}, bf16[96,384]{1,0:T(8,128)(2,1)S(1)}, u32[]{:S(2)}, u32[]{:S(2)}) collective-permute-start(bf16[96,384]{1,0:T(8,128)(2,1)S(1)} %add_all.5.refs_0_), channel_id=1, source_target_pairs={{0,64},{32,96},{64,0},{96,32},{1,65},{33,97},{65,1},{97,33},{2,66}... | collective-permute-start | bytes 221192 | tf_op jit(solution)/shard_map/ppermute | solution.py:696
  91.0 6.3 %collective-permute-start.10 = (bf16[96,384]{1,0:T(8,128)(2,1)S(1)}, bf16[96,384]{1,0:T(8,128)(2,1)S(1)}, u32[]{:S(2)}, u32[]{:S(2)}) collective-permute-start(bf16[96,384]{1,0:T(8,128)(2,1)S(1)} %add_all.5.refs_0_), channel_id=1, source_target_pairs={{0,32},{32,64},{64,96},{96,0},{1,33},{33,65},{65,97},{97,1},{2,34}... | collective-permute-start | bytes 221192 | tf_op jit(solution)/shard_map/ppermute | solution.py:696
  97.4 1.9 %collective-permute-start.13 = (f32[96,384]{1,0:T(8,128)S(1)}, f32[96,384]{1,0:T(8,128)S(1)}, u32[]{:S(2)}, u32[]{:S(2)}) collective-permute-start(f32[96,384]{1,0:T(8,128)S(1)} %add_all.7.own_ref), channel_id=1, source_target_pairs={{0,16},{16,0},{1,17},{17,1},{2,18},{18,2},{3,19},{19,3},{4,20},{20... | collective-permute-start | bytes 442376 | tf_op jit(solution)/shard_map/ppermute | solution.py:691

commit v7 on v6

--- a/solution.py
+++ b/solution.py
@@ -133,17 +133,14 @@
     )(*(pltpu.with_memory_space_constraint(a, pltpu.HBM) for a in (x, down)))
 
 
-def sum_spread_kernel(in_ref, out_ref, held, sems):
+def sum_spread_kernel(in_ref, out_ref):
     count = in_ref.shape[0]
     total = in_ref[0].astype(F32)
     for i in range(1, count):
         total = total + in_ref[i].astype(F32)
-    held[...] = total.astype(BF16)
-    copies = [pltpu.make_async_copy(held, out_ref.at[i], sems.at[i]) for i in range(count)]
-    for copy in copies:
-        copy.start()
-    for copy in copies:
-        copy.wait()
+    total = total.astype(BF16)
+    for i in range(count):
+        out_ref[i] = total
 
 
 def exchange(pieces):
@@ -155,11 +152,7 @@
         sum_spread_kernel,
         out_shape=jax.ShapeDtypeStruct(pieces.shape, BF16),
         in_specs=[VMEM],
-        out_specs=pl.BlockSpec(memory_space=pltpu.HBM),
-        scratch_shapes=[
-            pltpu.VMEM(pieces.shape[1:], BF16),
-            pltpu.SemaphoreType.DMA((pieces.shape[0],)),
-        ],
+        out_specs=VMEM,
         compiler_params=params(),
         name="sum_spread",
     )(pieces)
@@ -290,6 +283,7 @@
                 before_ref[c, h] = states[h].astype(BF16)
                 states[h] = passing * states[h] + dot_nn(valued, moving_ref[1, rows, span])
                 returning[c, h] = dot_nn(scaled, grad_ref[rows, span])
+    tails = []
     for h in range(heads):
         back = jnp.zeros((128, 128), F32)
         whole = jnp.ones((1, 128), F32)
@@ -300,7 +294,8 @@
             whole = whole * passing
         summary_ref[h * 128 : (h + 1) * 128, :] = states[h].astype(BF16)
         summary_ref[size + h * 128 : size + (h + 1) * 128, :] = back.astype(BF16)
-        summary_ref[2 * size + 16 * h : 2 * size + 16 * h + 16, :] = passing_rows(whole)
+        tails.append(passing_rows(whole))
+    summary_ref[2 * size : 2 * size + 4 * heads, :] = jnp.concatenate(tails, axis=0).astype(BF16)
 
 
 def passing_rows(row):
@@ -308,14 +303,14 @@
     rest = row - first
     second = rest.astype(BF16).astype(F32)
     third = (rest - second).astype(BF16).astype(F32)
-    return jnp.concatenate([first, second, third, jnp.zeros((13, 128), F32)], axis=0).astype(BF16)
+    return jnp.concatenate([first, second, third, jnp.zeros((1, 128), F32)], axis=0)
 
 
 def project(frozen, low, up, grad, row, passes):
     _, rows, features = frozen.shape
     heads = features // 128
     count = rows // CHUNK
-    summary_rows = 2 * features + 16 * heads
+    summary_rows = 2 * features + 4 * heads
     states = jax.ShapeDtypeStruct((count, heads, 128, 128), BF16)
     return pl.pallas_call(
         project_kernel,
@@ -350,14 +345,15 @@
     y = meta_ref[1]
     core = meta_ref[2]
     total = own_ref.shape[0]
-    heads = total // (2 * 128 + 16)
+    heads = total // (2 * 128 + 4)
     size = heads * 128
     chips = len(out_refs) + 1
     second = core == 1
+    tails = []
     for h in range(heads):
         rows = slice(h * 128, (h + 1) * 128)
         back_rows = slice(size + h * 128, size + (h + 1) * 128)
-        base = 2 * size + 16 * h
+        base = 2 * size + 4 * h
         own_pass = passing_of(own_ref, base)
         mate_pass = passing_of(mate_ref, base)
         own_state = own_ref[rows, :].astype(F32)
@@ -367,16 +363,18 @@
         one = jnp.ones_like(own_pass)
         state = jnp.where(second, own_pass, one) * mate_state + jnp.where(second, one, mate_pass) * own_state
         back = jnp.where(second, one, own_pass) * mate_back + jnp.where(second, mate_pass, one) * own_back
-        tail = passing_rows(own_pass * mate_pass)
+        tails.append(passing_rows(own_pass * mate_pass))
         for k, out_ref in enumerate(out_refs):
             later = y + (k + 1) < chips
             out_ref[rows, :] = jnp.where(later, state, back).astype(BF16)
-            out_ref[size + 16 * h : size + 16 * h + 16, :] = tail
+    tail = jnp.concatenate(tails, axis=0).astype(BF16)
+    for out_ref in out_refs:
+        out_ref[size : size + 4 * heads, :] = tail
 
 
 def join(meta, own, mate, chips):
-    heads = own.shape[0] // (2 * 128 + 16)
-    message = jax.ShapeDtypeStruct((heads * (128 + 16), 128), BF16)
+    heads = own.shape[0] // (2 * 128 + 4)
+    message = jax.ShapeDtypeStruct((heads * (128 + 4), 128), BF16)
     return pl.pallas_call(
         join_kernel,
         out_shape=(message,) * (chips - 1),
@@ -556,14 +554,14 @@
         for k in range(1, chips):
             ref = message_refs[k - 1]
             state = state + jnp.where(k <= y, factor, 0.0) * ref[rows, :].astype(F32)
-            factor = factor * passing_of(ref, size + 16 * h)
+            factor = factor * passing_of(ref, size + 4 * h)
         factor = jnp.ones((1, 128), F32)
         back = jnp.zeros((128, 128), F32)
         for k in reversed(range(1, chips)):
             ref = message_refs[k - 1]
             back = back + jnp.where(k > y, factor, 0.0) * ref[rows, :].astype(F32)
-            factor = factor * passing_of(ref, size + 16 * h)
-        mate_pass = passing_of(mate_ref, 2 * size + 16 * h)
+            factor = factor * passing_of(ref, size + 4 * h)
+        mate_pass = passing_of(mate_ref, 2 * size + 4 * h)
         mate_state = mate_ref[rows, :].astype(F32)
         mate_back = mate_ref[size + h * 128 : size + (h + 1) * 128, :].astype(F32)
         state_in[h] = jnp.where(second, mate_pass * state + mate_state, state).astype(BF16)

time: 101 us -> 101 us (level)
  transfers between devices with their start and end apart: 18 -> 18, of which waited for: 11 -> 10; matrix products, arithmetic and copies ran while one was open for 2% -> 2% of each run, Pallas kernels for 15% -> 15%
where the time goes in v7:
time: 101 us; the launch traced here: 100 us
  starting transfers between devices  38.4 us (38%)
  Pallas kernels  29.7 us (29%)
  waiting for transfers between devices  28.9 us (29%)
  local copies, waits for them, and re-layouts  1.28 us (1%)
    all_to_all x4, waiting for transfers between devices, exchange(): return lax.all_to_all(pieces, ('z', 'x'), 0, 0)  20.2 us
    all_to_all x4, starting transfers between devices, exchange(): return lax.all_to_all(pieces, ('z', 'x'), 0, 0)  19.1 us
    ppermute x9, starting transfers between devices, along_y(): return lax.ppermute(a, 'y', [(i, (i + k) % count) for i in range(count)])  10.4 us
    ppermute x5, starting transfers between devices, to_mate(): return lax.ppermute(a, 'core', [(0, 1), (1, 0)])  8.86 us
    pallas_call x1, Pallas kernels, inside(): pl.pallas_call(inside_kernel, out_shape=jax.ShapeDtypeStruct(moving.shape...  5.46 us
    pallas_call x1, Pallas kernels, late(): pl.pallas_call(late_kernel, out_shape=jax.ShapeDtypeStruct((rows, feature...  5.37 us
    ppermute x9, waiting for transfers between devices, along_y(): return lax.ppermute(a, 'y', [(i, (i + k) % count) for i in range(count)])  4.7 us
    pallas_call x1, Pallas kernels, finish(): pl.pallas_call(functools.partial(finish_kernel, chips), out_shape=(jax.Sh...  4.27 us
  transfers between devices with their start and end apart: 18, of which 10 were waited for; matrix products, arithmetic and copies ran while one was open for 2% of the time, Pallas kernels for 15%

profile of v7, /device:TPU:1, one launch (start us, length us, event | category | flops | bytes accessed | tf_op | source)
XLA Modules:
  0.0 100.0 jit_solution(15486652740779420545)
XLA Ops:
  0.7 2.9 %partial_low.1 = bf16[16,96,128]{2,1,0:T(8,128)(2,1)} custom-call(bf16[1024,384]{1,0:T(8,128)(2,1)} %x_ref.3, bf16[192,384]{1,0:T(8,128)(2,1)} %bitcast.13), custom_call_target="tpu_custom_call" | custom-call | tf_op jit(solution)/shard_map/partial_low/pallas_call | solution.py:119
  3.5 8.4 %all-to-all-start = ((bf16[16,96,128]{2,1,0:T(8,128)(2,1)}), bf16[16,96,128]{2,1,0:T(8,128)(2,1)S(1)}, u32[]{:S(2)}, u32[]{:S(2)}) async-start(bf16[16,96,128]{2,1,0:T(8,128)(2,1)} %partial_low.1), calls=%async_computation | async-start | bytes 786432 | tf_op jit(solution)/shard_map/all_to_all | solution.py:147
  12.0 1.2 %dynamic_slice.3 = s32[1]{0:T(128)} dynamic-slice(s32[8]{0:T(128)} %param.15, s32[]{:T(128)S(6)} %select_n.3), dynamic_slice_sizes={1} | dynamic-slice | bytes 12 | tf_op jit(solution)/shard_map/dynamic_slice | solution.py:701
  13.2 0.7 pad_add_fusion.meta_ref
  13.9 7.2 %all-to-all-done.in_ref = bf16[16,96,128]{2,1,0:T(8,128)(2,1)S(1)} async-done(((bf16[16,96,128]{2,1,0:T(8,128)(2,1)}), bf16[16,96,128]{2,1,0:T(8,128)(2,1)S(1)}, u32[]{:S(2)}, u32[]{:S(2)}) %all-to-all-start) | async-done | bytes 393248 | tf_op jit(solution)/shard_map/all_to_all | solution.py:147
  21.1 0.8 sum_spread.2
  22.0 3.6 %all-to-all-start.1 = ((bf16[16,96,128]{2,1,0:T(8,128)(2,1)}), bf16[16,96,128]{2,1,0:T(8,128)(2,1)S(1)}, u32[]{:S(2)}, u32[]{:S(2)}) async-start(bf16[16,96,128]{2,1,0:T(8,128)(2,1)} %sum_spread.2), calls=%async_computation.1 | async-start | bytes 786432 | tf_op jit(solution)/shard_map/all_to_all | solution.py:147
  25.5 0.0 copy-start.1
  25.5 0.0 copy-start.2
  25.6 2.0 %decay_tables.1 = (f32[16,1024]{1,0:T(8,128)S(1)}, f32[1024,128]{1,0:T(8,128)S(1)}, f32[96,128]{1,0:T(8,128)S(1)}) custom-call(s32[3]{0:T(128)S(1)} %pad_add_fusion.meta_ref, bf16[4,1024]{1,0:T(4,128)(2,1)S(1)} %copy-done.3, s32[1,1024]{1,0:T(1,128)S(1)} %bitcast.10), custom_call_target="tpu_custom_call" | custom-call | flops 4000000000 | bytes 1000000 | tf_op jit(solution)/shard_map/decay_tables/pallas_call | solution.py:234
  27.5 6.2 %all-to-all-done.1.low_ref = bf16[16,96,128]{2,1,0:T(8,128)(2,1)S(1)} async-done(((bf16[16,96,128]{2,1,0:T(8,128)(2,1)}), bf16[16,96,128]{2,1,0:T(8,128)(2,1)S(1)}, u32[]{:S(2)}, u32[]{:S(2)}) %all-to-all-start.1) | async-done | bytes 393248 | tf_op jit(solution)/shard_map/all_to_all | solution.py:147
  33.8 3.8 %project.1 = (bf16[3,1024,512]{2,1,0:T(8,128)(2,1)S(1)}, bf16[8,4,128,128]{3,2,1,0:T(8,128)(2,1)S(1)}, bf16[8,4,128,128]{3,2,1,0:T(8,128)(2,1)S(1)}, bf16[1040,128]{1,0:T(8,128)(2,1)S(1)}) custom-call(bf16[3,1024,512]{2,1,0:T(8,128)(2,1)} %frozen_ref.1, bf16[16,96,128]{2,1,0:T(8,128)(2,1)S(1)} %all-to-all-done.1.low_ref, bf16[3,64,512]{2,1,0:T(8,128)(2,1)S(1)} %copy-done.2, ...), custom_call_target="tpu_custom_call" | custom-call | flops 4000000000 | bytes 10000000 | tf_op jit(solution)/shard_map/project/pallas_call | solution.py:315
  37.6 3.1 %collective-permute-start = (bf16[1040,128]{1,0:T(8,128)(2,1)S(1)}, bf16[1040,128]{1,0:T(8,128)(2,1)S(1)}, u32[]{:S(2)}, u32[]{:S(2)}) collective-permute-start(bf16[1040,128]{1,0:T(8,128)(2,1)S(1)} %get-tuple-element.44.own_ref), channel_id=1, source_target_pairs={{0,16},{16,0},{1,17},{17,1},{2,18},{18,2},{3,19},{19,3},{4,20},{20... | collective-permute-start | bytes 798728 | tf_op jit(solution)/shard_map/ppermute | solution.py:689
  40.7 1.2 %collective-permute-done.mate_ref = bf16[1040,128]{1,0:T(8,128)(2,1)S(1)} collective-permute-done((bf16[1040,128]{1,0:T(8,128)(2,1)S(1)}, bf16[1040,128]{1,0:T(8,128)(2,1)S(1)}, u32[]{:S(2)}, u32[]{:S(2)}) %collective-permute-start) | collective-permute-done | bytes 266272 | tf_op jit(solution)/shard_map/ppermute | solution.py:689
  41.8 0.7 join.1
  42.5 1.4 %collective-permute-start.1 = (bf16[528,128]{1,0:T(8,128)(2,1)S(1)}, bf16[528,128]{1,0:T(8,128)(2,1)S(1)}, u32[]{:S(2)}, u32[]{:S(2)}) collective-permute-start(bf16[528,128]{1,0:T(8,128)(2,1)S(1)} %get-tuple-element.45), channel_id=1, source_target_pairs={{0,32},{32,64},{64,96},{96,0},{1,33},{33,65},{65,97},{97,1},{2,34}... | collective-permute-start | bytes 405512 | tf_op jit(solution)/shard_map/ppermute | solution.py:694
  43.9 2.6 %collective-permute-start.2 = (bf16[528,128]{1,0:T(8,128)(2,1)S(1)}, bf16[528,128]{1,0:T(8,128)(2,1)S(1)}, u32[]{:S(2)}, u32[]{:S(2)}) collective-permute-start(bf16[528,128]{1,0:T(8,128)(2,1)S(1)} %get-tuple-element.46), channel_id=1, source_target_pairs={{0,64},{32,96},{64,0},{96,32},{1,65},{33,97},{65,1},{97,33},{2,66}... | collective-permute-start | bytes 405512 | tf_op jit(solution)/shard_map/ppermute | solution.py:694
  46.5 1.1 %collective-permute-start.3 = (bf16[528,128]{1,0:T(8,128)(2,1)S(1)}, bf16[528,128]{1,0:T(8,128)(2,1)S(1)}, u32[]{:S(2)}, u32[]{:S(2)}) collective-permute-start(bf16[528,128]{1,0:T(8,128)(2,1)S(1)} %get-tuple-element.47), channel_id=1, source_target_pairs={{0,96},{32,0},{64,32},{96,64},{1,97},{33,1},{65,33},{97,65},{2,98}... | collective-permute-start | bytes 405512 | tf_op jit(solution)/shard_map/ppermute | solution.py:694
  47.6 5.5 %inside.1.part_ref = f32[3,1024,512]{2,1,0:T(8,128)S(1)} custom-call(bf16[3,1024,512]{2,1,0:T(8,128)(2,1)S(1)} %get-tuple-element.40.moving_ref, bf16[1024,512]{1,0:T(8,128)(2,1)S(1)} %copy-done.1, f32[16,1024]{1,0:T(8,128)S(1)} %get-tuple-element.38.row_ref, f32[1024,128]{1,0:T(8,128)S(1)} %get-tuple-element.41.col_ref, ...), custom_call_target="tpu_custom_call" | custom-call | flops 12000000000 | bytes 12000000 | tf_op jit(solution)/shard_map/inside/pallas_call | solution.py:434
  53.1 0.0 collective-permute-done.3.refs_2_
  53.1 4.3 %finish.1 = (bf16[3,1024,512]{2,1,0:T(8,128)(2,1)}, bf16[16,96,128]{2,1,0:T(8,128)(2,1)}, bf16[4,128,128]{2,1,0:T(8,128)(2,1)S(1)}, bf16[96,512]{1,0:T(8,128)(2,1)S(1)}, bf16[96,512]{1,0:T(8,128)(2,1)S(1)}) custom-call(s32[3]{0:T(128)S(1)} %pad_add_fusion.meta_ref, bf16[3,1024,512]{2,1,0:T(8,128)(2,1)S(1)} %get-tuple-element.40.moving_ref, ...), custom_call_target="tpu_custom_call" | custom-call | flops 4000000000 | bytes 14000000 | tf_op jit(solution)/shard_map/finish/pallas_call | solution.py:606
  57.4 3.6 %all-to-all-start.2 = ((bf16[16,96,128]{2,1,0:T(8,128)(2,1)}), bf16[16,96,128]{2,1,0:T(8,128)(2,1)S(1)}, u32[]{:S(2)}, u32[]{:S(2)}) async-start(bf16[16,96,128]{2,1,0:T(8,128)(2,1)} %get-tuple-element.48), calls=%async_computation.2 | async-start | bytes 786432 | tf_op jit(solution)/shard_map/all_to_all | solution.py:147
  61.0 1.3 %collective-permute-start.4 = (bf16[96,512]{1,0:T(8,128)(2,1)S(1)}, bf16[96,512]{1,0:T(8,128)(2,1)S(1)}, u32[]{:S(2)}, u32[]{:S(2)}) collective-permute-start(bf16[96,512]{1,0:T(8,128)(2,1)S(1)} %get-tuple-element.50), channel_id=1, source_target_pairs={{0,16},{16,0},{1,17},{17,1},{2,18},{18,2},{3,19},{19,3},{4,20},{20... | collective-permute-start | bytes 294920 | tf_op jit(solution)/shard_map/ppermute | solution.py:689
  62.3 0.9 collective-permute-done.4.refs_1_
  63.2 1.6 %collective-permute-start.7 = (bf16[96,512]{1,0:T(8,128)(2,1)S(1)}, bf16[96,512]{1,0:T(8,128)(2,1)S(1)}, u32[]{:S(2)}, u32[]{:S(2)}) collective-permute-start(bf16[96,512]{1,0:T(8,128)(2,1)S(1)} %add_all.4.refs_0_), channel_id=1, source_target_pairs={{0,96},{32,0},{64,32},{96,64},{1,97},{33,1},{65,33},{97,65},{2,98}... | collective-permute-start | bytes 294920 | tf_op jit(solution)/shard_map/ppermute | solution.py:694
  64.8 0.9 collective-permute-start.6
  65.7 0.4 collective-permute-start.5
  66.1 3.7 %all-to-all-done.2.in_ref = bf16[16,96,128]{2,1,0:T(8,128)(2,1)S(1)} async-done(((bf16[16,96,128]{2,1,0:T(8,128)(2,1)}), bf16[16,96,128]{2,1,0:T(8,128)(2,1)S(1)}, u32[]{:S(2)}, u32[]{:S(2)}) %all-to-all-start.2) | async-done | bytes 393248 | tf_op jit(solution)/shard_map/all_to_all | solution.py:147
  69.8 0.8 sum_spread.3
  70.7 3.6 %all-to-all-start.3 = ((bf16[16,96,128]{2,1,0:T(8,128)(2,1)}), bf16[16,96,128]{2,1,0:T(8,128)(2,1)S(1)}, u32[]{:S(2)}, u32[]{:S(2)}) async-start(bf16[16,96,128]{2,1,0:T(8,128)(2,1)} %sum_spread.3), calls=%async_computation.3 | async-start | bytes 786432 | tf_op jit(solution)/shard_map/all_to_all | solution.py:147
  74.2 0.0 copy-start
  74.2 5.4 %late.1 = bf16[1024,512]{1,0:T(8,128)(2,1)} custom-call(bf16[3,1024,512]{2,1,0:T(8,128)(2,1)} %copy-done.5, f32[16,1024]{1,0:T(8,128)S(1)} %get-tuple-element.38.row_ref, f32[1024,128]{1,0:T(8,128)S(1)} %get-tuple-element.41.col_ref, f32[96,128]{1,0:T(8,128)S(1)} %get-tuple-element.39.pass_ref, bf16[8,4,128,128]{3,2,1,0:T(8,128)(2,1)} %copy-done.6, ...), custom_call_target="tpu_custom_call" | custom-call | flops 6000000000 | bytes 6000000 | tf_op jit(solution)/shard_map/late/pallas_call | solution.py:511
  79.6 0.0 collective-permute-done.6.refs_2_
  79.6 3.0 %all-to-all-done.3.grad_ref = bf16[16,96,128]{2,1,0:T(8,128)(2,1)S(1)} async-done(((bf16[16,96,128]{2,1,0:T(8,128)(2,1)}), bf16[16,96,128]{2,1,0:T(8,128)(2,1)S(1)}, u32[]{:S(2)}, u32[]{:S(2)}) %all-to-all-start.3) | async-done | bytes 393248 | tf_op jit(solution)/shard_map/all_to_all | solution.py:147
  82.7 0.9 partial_down.1
  83.6 3.1 %collective-permute-start.8 = (bf16[96,384]{1,0:T(8,128)(2,1)S(1)}, bf16[96,384]{1,0:T(8,128)(2,1)S(1)}, u32[]{:S(2)}, u32[]{:S(2)}) collective-permute-start(bf16[96,384]{1,0:T(8,128)(2,1)S(1)} %get-tuple-element.57), channel_id=1, source_target_pairs={{0,16},{16,0},{1,17},{17,1},{2,18},{18,2},{3,19},{19,3},{4,20},{20... | collective-permute-start | bytes 221192 | tf_op jit(solution)/shard_map/ppermute | solution.py:689
  86.7 0.9 collective-permute-done.8.refs_1_
  87.6 0.1 add_all.6.own_ref
  87.7 0.4 collective-permute-start.9
  88.1 1.6 %collective-permute-start.12 = (bf16[96,384]{1,0:T(8,128)(2,1)S(1)}, bf16[96,384]{1,0:T(8,128)(2,1)S(1)}, u32[]{:S(2)}, u32[]{:S(2)}) collective-permute-start(bf16[96,384]{1,0:T(8,128)(2,1)S(1)} %add_all.5.refs_0_), channel_id=1, source_target_pairs={{0,96},{32,0},{64,32},{96,64},{1,97},{33,1},{65,33},{97,65},{2,98}... | collective-permute-start | bytes 221192 | tf_op jit(solution)/shard_map/ppermute | solution.py:694
  89.8 0.7 collective-permute-start.11
  90.5 0.2 collective-permute-start.10
  90.7 1.3 %join_halves.2 = f32[192,512]{1,0:T(8,128)} custom-call(s32[3]{0:T(128)S(1)} %pad_add_fusion.meta_ref, f32[96,512]{1,0:T(8,128)S(1)} %add_all.6.own_ref, f32[96,512]{1,0:T(8,128)S(1)} %collective-permute-done.9.mate_ref), custom_call_target="tpu_custom_call" | custom-call | tf_op jit(solution)/shard_map/join_halves/pallas_call | solution.py:660
  92.0 2.5 %collective-permute-done.11.refs_2_ = bf16[96,384]{1,0:T(8,128)(2,1)S(1)} collective-permute-done((bf16[96,384]{1,0:T(8,128)(2,1)S(1)}, bf16[96,384]{1,0:T(8,128)(2,1)S(1)}, u32[]{:S(2)}, u32[]{:S(2)}) %collective-permute-start.11) | collective-permute-done | bytes 73760 | tf_op jit(solution)/shard_map/ppermute | solution.py:694
  94.5 2.2 %collective-permute-done.10.refs_1_ = bf16[96,384]{1,0:T(8,128)(2,1)S(1)} collective-permute-done((bf16[96,384]{1,0:T(8,128)(2,1)S(1)}, bf16[96,384]{1,0:T(8,128)(2,1)S(1)}, u32[]{:S(2)}, u32[]{:S(2)}) %collective-permute-start.10) | collective-permute-done | bytes 73760 | tf_op jit(solution)/shard_map/ppermute | solution.py:694
  96.7 1.0 collective-permute-start.13
  97.7 1.0 %collective-permute-done.13.mate_ref = f32[96,384]{1,0:T(8,128)S(1)} collective-permute-done((f32[96,384]{1,0:T(8,128)S(1)}, f32[96,384]{1,0:T(8,128)S(1)}, u32[]{:S(2)}, u32[]{:S(2)}) %collective-permute-start.13) | collective-permute-done | bytes 147488 | tf_op jit(solution)/shard_map/ppermute | solution.py:689
  98.7 1.3 %join_halves.3 = f32[192,384]{1,0:T(8,128)} custom-call(s32[3]{0:T(128)S(1)} %pad_add_fusion.meta_ref, f32[96,384]{1,0:T(8,128)S(1)} %add_all.7.own_ref, f32[96,384]{1,0:T(8,128)S(1)} %collective-permute-done.13.mate_ref), custom_call_target="tpu_custom_call" | custom-call | tf_op jit(solution)/shard_map/join_halves/pallas_call | solution.py:660
  (20 shorter events, 0.1 us)
Async XLA Ops:
  0.6 24.9 %copy-start.4 = (s32[1024]{0:T(1024)S(1)}, s32[1024]{0:T(1024)}, u32[]{:S(2)}) copy-start(s32[1024]{0:T(1024)} %param.14) | copy-start | bytes 12292
  0.6 24.9 %copy-start.3 = (bf16[4,1024]{1,0:T(4,128)(2,1)S(1)}, bf16[4,1024]{1,0:T(4,128)(2,1)}, u32[]{:S(2)}) copy-start(bf16[4,1024]{1,0:T(4,128)(2,1)} %decay_ref.1) | copy-start | bytes 24580
  3.5 17.6 %all-to-all-start = ((bf16[16,96,128]{2,1,0:T(8,128)(2,1)}), bf16[16,96,128]{2,1,0:T(8,128)(2,1)S(1)}, u32[]{:S(2)}, u32[]{:S(2)}) async-start(bf16[16,96,128]{2,1,0:T(8,128)(2,1)} %partial_low.1), calls=%async_computation | async-start | bytes 786432 | tf_op jit(solution)/shard_map/all_to_all | solution.py:147
  22.0 11.8 %all-to-all-start.1 = ((bf16[16,96,128]{2,1,0:T(8,128)(2,1)}), bf16[16,96,128]{2,1,0:T(8,128)(2,1)S(1)}, u32[]{:S(2)}, u32[]{:S(2)}) async-start(bf16[16,96,128]{2,1,0:T(8,128)(2,1)} %sum_spread.2), calls=%async_computation.1 | async-start | bytes 786432 | tf_op jit(solution)/shard_map/all_to_all | solution.py:147
  25.5 8.2 %copy-start.1 = (bf16[1024,512]{1,0:T(8,128)(2,1)S(1)}, bf16[1024,512]{1,0:T(8,128)(2,1)}, u32[]{:S(2)}) copy-start(bf16[1024,512]{1,0:T(8,128)(2,1)} %g_ref.1) | copy-start | bytes 3145732
  25.5 8.2 %copy-start.2 = (bf16[3,64,512]{2,1,0:T(8,128)(2,1)S(1)}, bf16[3,64,512]{2,1,0:T(8,128)(2,1)}, u32[]{:S(2)}) copy-start(bf16[3,64,512]{2,1,0:T(8,128)(2,1)} %up_ref.3) | copy-start | bytes 589828
  37.6 15.5 %copy-start.6 = (bf16[8,4,128,128]{3,2,1,0:T(8,128)(2,1)}, bf16[8,4,128,128]{3,2,1,0:T(8,128)(2,1)S(1)}, u32[]{:S(2)}) copy-start(bf16[8,4,128,128]{3,2,1,0:T(8,128)(2,1)S(1)} %get-tuple-element.42.before_ref) | copy-start | bytes 3145732
  37.6 15.5 %copy-start.5 = (bf16[3,1024,512]{2,1,0:T(8,128)(2,1)}, bf16[3,1024,512]{2,1,0:T(8,128)(2,1)S(1)}, u32[]{:S(2)}) copy-start(bf16[3,1024,512]{2,1,0:T(8,128)(2,1)S(1)} %get-tuple-element.40.moving_ref) | copy-start | bytes 9437188
  37.6 4.2 %collective-permute-start = (bf16[1040,128]{1,0:T(8,128)(2,1)S(1)}, bf16[1040,128]{1,0:T(8,128)(2,1)S(1)}, u32[]{:S(2)}, u32[]{:S(2)}) collective-permute-start(bf16[1040,128]{1,0:T(8,128)(2,1)S(1)} %get-tuple-element.44.own_ref), channel_id=1, source_target_pairs={{0,16},{16,0},{1,17},{17,1},{2,18},{18,2},{3,19},{19,3},{4,20},{20... | collective-permute-start | bytes 798728 | tf_op jit(solution)/shard_map/ppermute | solution.py:689
  42.5 10.5 %collective-permute-start.1 = (bf16[528,128]{1,0:T(8,128)(2,1)S(1)}, bf16[528,128]{1,0:T(8,128)(2,1)S(1)}, u32[]{:S(2)}, u32[]{:S(2)}) collective-permute-start(bf16[528,128]{1,0:T(8,128)(2,1)S(1)} %get-tuple-element.45), channel_id=1, source_target_pairs={{0,32},{32,64},{64,96},{96,0},{1,33},{33,65},{65,97},{97,1},{2,34}... | collective-permute-start | bytes 405512 | tf_op jit(solution)/shard_map/ppermute | solution.py:694
  43.9 9.2 %collective-permute-start.2 = (bf16[528,128]{1,0:T(8,128)(2,1)S(1)}, bf16[528,128]{1,0:T(8,128)(2,1)S(1)}, u32[]{:S(2)}, u32[]{:S(2)}) collective-permute-start(bf16[528,128]{1,0:T(8,128)(2,1)S(1)} %get-tuple-element.46), channel_id=1, source_target_pairs={{0,64},{32,96},{64,0},{96,32},{1,65},{33,97},{65,1},{97,33},{2,66}... | collective-permute-start | bytes 405512 | tf_op jit(solution)/shard_map/ppermute | solution.py:694
  46.5 6.6 %collective-permute-start.3 = (bf16[528,128]{1,0:T(8,128)(2,1)S(1)}, bf16[528,128]{1,0:T(8,128)(2,1)S(1)}, u32[]{:S(2)}, u32[]{:S(2)}) collective-permute-start(bf16[528,128]{1,0:T(8,128)(2,1)S(1)} %get-tuple-element.47), channel_id=1, source_target_pairs={{0,96},{32,0},{64,32},{96,64},{1,97},{33,1},{65,33},{97,65},{2,98}... | collective-permute-start | bytes 405512 | tf_op jit(solution)/shard_map/ppermute | solution.py:694
  57.4 12.4 %all-to-all-start.2 = ((bf16[16,96,128]{2,1,0:T(8,128)(2,1)}), bf16[16,96,128]{2,1,0:T(8,128)(2,1)S(1)}, u32[]{:S(2)}, u32[]{:S(2)}) async-start(bf16[16,96,128]{2,1,0:T(8,128)(2,1)} %get-tuple-element.48), calls=%async_computation.2 | async-start | bytes 786432 | tf_op jit(solution)/shard_map/all_to_all | solution.py:147
  61.0 2.2 %collective-permute-start.4 = (bf16[96,512]{1,0:T(8,128)(2,1)S(1)}, bf16[96,512]{1,0:T(8,128)(2,1)S(1)}, u32[]{:S(2)}, u32[]{:S(2)}) collective-permute-start(bf16[96,512]{1,0:T(8,128)(2,1)S(1)} %get-tuple-element.50), channel_id=1, source_target_pairs={{0,16},{16,0},{1,17},{17,1},{2,18},{18,2},{3,19},{19,3},{4,20},{20... | collective-permute-start | bytes 294920 | tf_op jit(solution)/shard_map/ppermute | solution.py:689
  63.2 16.4 %collective-permute-start.7 = (bf16[96,512]{1,0:T(8,128)(2,1)S(1)}, bf16[96,512]{1,0:T(8,128)(2,1)S(1)}, u32[]{:S(2)}, u32[]{:S(2)}) collective-permute-start(bf16[96,512]{1,0:T(8,128)(2,1)S(1)} %add_all.4.refs_0_), channel_id=1, source_target_pairs={{0,96},{32,0},{64,32},{96,64},{1,97},{33,1},{65,33},{97,65},{2,98}... | collective-permute-start | bytes 294920 | tf_op jit(solution)/shard_map/ppermute | solution.py:694
  64.8 14.8 %collective-permute-start.6 = (bf16[96,512]{1,0:T(8,128)(2,1)S(1)}, bf16[96,512]{1,0:T(8,128)(2,1)S(1)}, u32[]{:S(2)}, u32[]{:S(2)}) collective-permute-start(bf16[96,512]{1,0:T(8,128)(2,1)S(1)} %add_all.4.refs_0_), channel_id=1, source_target_pairs={{0,64},{32,96},{64,0},{96,32},{1,65},{33,97},{65,1},{97,33},{2,66}... | collective-permute-start | bytes 294920 | tf_op jit(solution)/shard_map/ppermute | solution.py:694
  65.7 14.0 %collective-permute-start.5 = (bf16[96,512]{1,0:T(8,128)(2,1)S(1)}, bf16[96,512]{1,0:T(8,128)(2,1)S(1)}, u32[]{:S(2)}, u32[]{:S(2)}) collective-permute-start(bf16[96,512]{1,0:T(8,128)(2,1)S(1)} %add_all.4.refs_0_), channel_id=1, source_target_pairs={{0,32},{32,64},{64,96},{96,0},{1,33},{33,65},{65,97},{97,1},{2,34}... | collective-permute-start | bytes 294920 | tf_op jit(solution)/shard_map/ppermute | solution.py:694
  70.7 12.0 %all-to-all-start.3 = ((bf16[16,96,128]{2,1,0:T(8,128)(2,1)}), bf16[16,96,128]{2,1,0:T(8,128)(2,1)S(1)}, u32[]{:S(2)}, u32[]{:S(2)}) async-start(bf16[16,96,128]{2,1,0:T(8,128)(2,1)} %sum_spread.3), calls=%async_computation.3 | async-start | bytes 786432 | tf_op jit(solution)/shard_map/all_to_all | solution.py:147
  74.2 8.4 %copy-start = (bf16[1024,384]{1,0:T(8,128)(2,1)S(1)}, bf16[1024,384]{1,0:T(8,128)(2,1)}, u32[]{:S(2)}) copy-start(bf16[1024,384]{1,0:T(8,128)(2,1)} %x_ref.3) | copy-start | bytes 2359300
  83.6 4.0 %collective-permute-start.8 = (bf16[96,384]{1,0:T(8,128)(2,1)S(1)}, bf16[96,384]{1,0:T(8,128)(2,1)S(1)}, u32[]{:S(2)}, u32[]{:S(2)}) collective-permute-start(bf16[96,384]{1,0:T(8,128)(2,1)S(1)} %get-tuple-element.57), channel_id=1, source_target_pairs={{0,16},{16,0},{1,17},{17,1},{2,18},{18,2},{3,19},{19,3},{4,20},{20... | collective-permute-start | bytes 221192 | tf_op jit(solution)/shard_map/ppermute | solution.py:689
  87.7 3.0 %collective-permute-start.9 = (f32[96,512]{1,0:T(8,128)S(1)}, f32[96,512]{1,0:T(8,128)S(1)}, u32[]{:S(2)}, u32[]{:S(2)}) collective-permute-start(f32[96,512]{1,0:T(8,128)S(1)} %add_all.6.own_ref), channel_id=1, source_target_pairs={{0,16},{16,0},{1,17},{17,1},{2,18},{18,2},{3,19},{19,3},{4,20},{20... | collective-permute-start | bytes 589832 | tf_op jit(solution)/shard_map/ppermute | solution.py:689
  88.1 3.8 %collective-permute-start.12 = (bf16[96,384]{1,0:T(8,128)(2,1)S(1)}, bf16[96,384]{1,0:T(8,128)(2,1)S(1)}, u32[]{:S(2)}, u32[]{:S(2)}) collective-permute-start(bf16[96,384]{1,0:T(8,128)(2,1)S(1)} %add_all.5.refs_0_), channel_id=1, source_target_pairs={{0,96},{32,0},{64,32},{96,64},{1,97},{33,1},{65,33},{97,65},{2,98}... | collective-permute-start | bytes 221192 | tf_op jit(solution)/shard_map/ppermute | solution.py:694
  89.8 4.7 %collective-permute-start.11 = (bf16[96,384]{1,0:T(8,128)(2,1)S(1)}, bf16[96,384]{1,0:T(8,128)(2,1)S(1)}, u32[]{:S(2)}, u32[]{:S(2)}) collective-permute-start(bf16[96,384]{1,0:T(8,128)(2,1)S(1)} %add_all.5.refs_0_), channel_id=1, source_target_pairs={{0,64},{32,96},{64,0},{96,32},{1,65},{33,97},{65,1},{97,33},{2,66}... | collective-permute-start | bytes 221192 | tf_op jit(solution)/shard_map/ppermute | solution.py:694
  90.5 6.2 %collective-permute-start.10 = (bf16[96,384]{1,0:T(8,128)(2,1)S(1)}, bf16[96,384]{1,0:T(8,128)(2,1)S(1)}, u32[]{:S(2)}, u32[]{:S(2)}) collective-permute-start(bf16[96,384]{1,0:T(8,128)(2,1)S(1)} %add_all.5.refs_0_), channel_id=1, source_target_pairs={{0,32},{32,64},{64,96},{96,0},{1,33},{33,65},{65,97},{97,1},{2,34}... | collective-permute-start | bytes 221192 | tf_op jit(solution)/shard_map/ppermute | solution.py:694
  96.7 2.0 %collective-permute-start.13 = (f32[96,384]{1,0:T(8,128)S(1)}, f32[96,384]{1,0:T(8,128)S(1)}, u32[]{:S(2)}, u32[]{:S(2)}) collective-permute-start(f32[96,384]{1,0:T(8,128)S(1)} %add_all.7.own_ref), channel_id=1, source_target_pairs={{0,16},{16,0},{1,17},{17,1},{2,18},{18,2},{3,19},{19,3},{4,20},{20... | collective-permute-start | bytes 442376 | tf_op jit(solution)/shard_map/ppermute | solution.py:689

commit v8 on v7

--- a/solution.py
+++ b/solution.py
@@ -581,8 +581,11 @@
             value = part_ref[2, rows, span] + leave * dot_nn(moving_ref[1, rows, span], back)
             for i, result in enumerate((query, key, value)):
                 grad_ref[i, rows, span] = (result * inverse).astype(BF16)
-        copies.append(pltpu.make_async_copy(grad_ref.at[:, rows], out_ref.at[:, rows], sems.at[n]))
-        copies[n].start()
+            part = (slice(None), rows, pl.ds(h * 128, 256))
+            copies.append(
+                pltpu.make_async_copy(grad_ref.at[part], out_ref.at[part], sems.at[n * heads // 2 + h // 2])
+            )
+            copies[-1].start()
     for n in range(count):
         rows = pl.ds(n * BLOCK, BLOCK)
         low_grad = [dot_nt(up_ref[i], grad_ref[i, rows, :]).astype(BF16) for i in range(3)]
@@ -618,7 +621,7 @@
             pltpu.VMEM((heads, 128, 128), BF16),
             pltpu.VMEM(moving.shape, BF16),
             pltpu.VMEM((width, features), F32),
-            pltpu.SemaphoreType.DMA((rows // BLOCK,)),
+            pltpu.SemaphoreType.DMA((rows // BLOCK * heads // 2,)),
         ],
         compiler_params=params(),
         cost_estimate=cost(4e9, 14e6),

time: 101 us -> 102 us (level)
  Pallas kernels: 29.7 us -> 31.1 us
    pallas_call x1, Pallas kernels: 4.27 us -> 5.66 us  [finish(): pl.pallas_call(functools.partial(finish_kernel, chips), out_shape=(jax.Sh...]
where the time goes in v8:
time: 102 us; the launch traced here: 101 us
  starting transfers between devices  38.6 us (38%)
  Pallas kernels  31.1 us (30%)
  waiting for transfers between devices  28.7 us (28%)
  local copies, waits for them, and re-layouts  1.28 us (1%)
    all_to_all x4, waiting for transfers between devices, exchange(): return lax.all_to_all(pieces, ('z', 'x'), 0, 0)  20 us
    all_to_all x4, starting transfers between devices, exchange(): return lax.all_to_all(pieces, ('z', 'x'), 0, 0)  19.3 us
    ppermute x9, starting transfers between devices, along_y(): return lax.ppermute(a, 'y', [(i, (i + k) % count) for i in range(count)])  10.4 us
    ppermute x5, starting transfers between devices, to_mate(): return lax.ppermute(a, 'core', [(0, 1), (1, 0)])  8.86 us
    pallas_call x1, Pallas kernels, finish(): pl.pallas_call(functools.partial(finish_kernel, chips), out_shape=(jax.Sh...  5.66 us
    pallas_call x1, Pallas kernels, inside(): pl.pallas_call(inside_kernel, out_shape=jax.ShapeDtypeStruct(moving.shape...  5.46 us
    pallas_call x1, Pallas kernels, late(): pl.pallas_call(late_kernel, out_shape=jax.ShapeDtypeStruct((rows, feature...  5.38 us
    ppermute x9, waiting for transfers between devices, along_y(): return lax.ppermute(a, 'y', [(i, (i + k) % count) for i in range(count)])  4.7 us
  transfers between devices with their start and end apart: 18, of which 10 were waited for; matrix products, arithmetic and copies ran while one was open for 2% of the time, Pallas kernels for 15%

profile of v8, /device:TPU:1, one launch (start us, length us, event | category | flops | bytes accessed | tf_op | source)
XLA Modules:
  0.0 101.3 jit_solution(4253918805940399760)
XLA Ops:
  0.7 2.9 %partial_low.1 = bf16[16,96,128]{2,1,0:T(8,128)(2,1)} custom-call(bf16[1024,384]{1,0:T(8,128)(2,1)} %x_ref.3, bf16[192,384]{1,0:T(8,128)(2,1)} %bitcast.13), custom_call_target="tpu_custom_call" | custom-call | tf_op jit(solution)/shard_map/partial_low/pallas_call | solution.py:119
  3.5 8.4 %all-to-all-start = ((bf16[16,96,128]{2,1,0:T(8,128)(2,1)}), bf16[16,96,128]{2,1,0:T(8,128)(2,1)S(1)}, u32[]{:S(2)}, u32[]{:S(2)}) async-start(bf16[16,96,128]{2,1,0:T(8,128)(2,1)} %partial_low.1), calls=%async_computation | async-start | bytes 786432 | tf_op jit(solution)/shard_map/all_to_all | solution.py:147
  12.0 1.2 %dynamic_slice.3 = s32[1]{0:T(128)} dynamic-slice(s32[8]{0:T(128)} %param.15, s32[]{:T(128)S(6)} %select_n.3), dynamic_slice_sizes={1} | dynamic-slice | bytes 12 | tf_op jit(solution)/shard_map/dynamic_slice | solution.py:704
  13.2 0.7 pad_add_fusion.meta_ref
  13.9 7.2 %all-to-all-done.in_ref = bf16[16,96,128]{2,1,0:T(8,128)(2,1)S(1)} async-done(((bf16[16,96,128]{2,1,0:T(8,128)(2,1)}), bf16[16,96,128]{2,1,0:T(8,128)(2,1)S(1)}, u32[]{:S(2)}, u32[]{:S(2)}) %all-to-all-start) | async-done | bytes 393248 | tf_op jit(solution)/shard_map/all_to_all | solution.py:147
  21.1 0.8 sum_spread.2
  22.0 3.6 %all-to-all-start.1 = ((bf16[16,96,128]{2,1,0:T(8,128)(2,1)}), bf16[16,96,128]{2,1,0:T(8,128)(2,1)S(1)}, u32[]{:S(2)}, u32[]{:S(2)}) async-start(bf16[16,96,128]{2,1,0:T(8,128)(2,1)} %sum_spread.2), calls=%async_computation.1 | async-start | bytes 786432 | tf_op jit(solution)/shard_map/all_to_all | solution.py:147
  25.5 0.0 copy-start.1
  25.5 0.0 copy-start.2
  25.6 2.0 %decay_tables.1 = (f32[16,1024]{1,0:T(8,128)S(1)}, f32[1024,128]{1,0:T(8,128)S(1)}, f32[96,128]{1,0:T(8,128)S(1)}) custom-call(s32[3]{0:T(128)S(1)} %pad_add_fusion.meta_ref, bf16[4,1024]{1,0:T(4,128)(2,1)S(1)} %copy-done.3, s32[1,1024]{1,0:T(1,128)S(1)} %bitcast.10), custom_call_target="tpu_custom_call" | custom-call | flops 4000000000 | bytes 1000000 | tf_op jit(solution)/shard_map/decay_tables/pallas_call | solution.py:234
  27.5 6.2 %all-to-all-done.1.low_ref = bf16[16,96,128]{2,1,0:T(8,128)(2,1)S(1)} async-done(((bf16[16,96,128]{2,1,0:T(8,128)(2,1)}), bf16[16,96,128]{2,1,0:T(8,128)(2,1)S(1)}, u32[]{:S(2)}, u32[]{:S(2)}) %all-to-all-start.1) | async-done | bytes 393248 | tf_op jit(solution)/shard_map/all_to_all | solution.py:147
  33.8 3.8 %project.1 = (bf16[3,1024,512]{2,1,0:T(8,128)(2,1)S(1)}, bf16[8,4,128,128]{3,2,1,0:T(8,128)(2,1)S(1)}, bf16[8,4,128,128]{3,2,1,0:T(8,128)(2,1)S(1)}, bf16[1040,128]{1,0:T(8,128)(2,1)S(1)}) custom-call(bf16[3,1024,512]{2,1,0:T(8,128)(2,1)} %frozen_ref.1, bf16[16,96,128]{2,1,0:T(8,128)(2,1)S(1)} %all-to-all-done.1.low_ref, bf16[3,64,512]{2,1,0:T(8,128)(2,1)S(1)} %copy-done.2, ...), custom_call_target="tpu_custom_call" | custom-call | flops 4000000000 | bytes 10000000 | tf_op jit(solution)/shard_map/project/pallas_call | solution.py:315
  37.6 3.1 %collective-permute-start = (bf16[1040,128]{1,0:T(8,128)(2,1)S(1)}, bf16[1040,128]{1,0:T(8,128)(2,1)S(1)}, u32[]{:S(2)}, u32[]{:S(2)}) collective-permute-start(bf16[1040,128]{1,0:T(8,128)(2,1)S(1)} %get-tuple-element.44.own_ref), channel_id=1, source_target_pairs={{0,16},{16,0},{1,17},{17,1},{2,18},{18,2},{3,19},{19,3},{4,20},{20... | collective-permute-start | bytes 798728 | tf_op jit(solution)/shard_map/ppermute | solution.py:692
  40.7 1.2 %collective-permute-done.mate_ref = bf16[1040,128]{1,0:T(8,128)(2,1)S(1)} collective-permute-done((bf16[1040,128]{1,0:T(8,128)(2,1)S(1)}, bf16[1040,128]{1,0:T(8,128)(2,1)S(1)}, u32[]{:S(2)}, u32[]{:S(2)}) %collective-permute-start) | collective-permute-done | bytes 266272 | tf_op jit(solution)/shard_map/ppermute | solution.py:692
  41.8 0.7 join.1
  42.5 1.4 %collective-permute-start.1 = (bf16[528,128]{1,0:T(8,128)(2,1)S(1)}, bf16[528,128]{1,0:T(8,128)(2,1)S(1)}, u32[]{:S(2)}, u32[]{:S(2)}) collective-permute-start(bf16[528,128]{1,0:T(8,128)(2,1)S(1)} %get-tuple-element.45), channel_id=1, source_target_pairs={{0,32},{32,64},{64,96},{96,0},{1,33},{33,65},{65,97},{97,1},{2,34}... | collective-permute-start | bytes 405512 | tf_op jit(solution)/shard_map/ppermute | solution.py:697
  43.9 2.6 %collective-permute-start.2 = (bf16[528,128]{1,0:T(8,128)(2,1)S(1)}, bf16[528,128]{1,0:T(8,128)(2,1)S(1)}, u32[]{:S(2)}, u32[]{:S(2)}) collective-permute-start(bf16[528,128]{1,0:T(8,128)(2,1)S(1)} %get-tuple-element.46), channel_id=1, source_target_pairs={{0,64},{32,96},{64,0},{96,32},{1,65},{33,97},{65,1},{97,33},{2,66}... | collective-permute-start | bytes 405512 | tf_op jit(solution)/shard_map/ppermute | solution.py:697
  46.5 1.1 %collective-permute-start.3 = (bf16[528,128]{1,0:T(8,128)(2,1)S(1)}, bf16[528,128]{1,0:T(8,128)(2,1)S(1)}, u32[]{:S(2)}, u32[]{:S(2)}) collective-permute-start(bf16[528,128]{1,0:T(8,128)(2,1)S(1)} %get-tuple-element.47), channel_id=1, source_target_pairs={{0,96},{32,0},{64,32},{96,64},{1,97},{33,1},{65,33},{97,65},{2,98}... | collective-permute-start | bytes 405512 | tf_op jit(solution)/shard_map/ppermute | solution.py:697
  47.6 5.5 %inside.1.part_ref = f32[3,1024,512]{2,1,0:T(8,128)S(1)} custom-call(bf16[3,1024,512]{2,1,0:T(8,128)(2,1)S(1)} %get-tuple-element.40.moving_ref, bf16[1024,512]{1,0:T(8,128)(2,1)S(1)} %copy-done.1, f32[16,1024]{1,0:T(8,128)S(1)} %get-tuple-element.38.row_ref, f32[1024,128]{1,0:T(8,128)S(1)} %get-tuple-element.41.col_ref, ...), custom_call_target="tpu_custom_call" | custom-call | flops 12000000000 | bytes 12000000 | tf_op jit(solution)/shard_map/inside/pallas_call | solution.py:434
  53.1 0.0 collective-permute-done.3.refs_2_
  53.1 5.7 %finish.1 = (bf16[3,1024,512]{2,1,0:T(8,128)(2,1)}, bf16[16,96,128]{2,1,0:T(8,128)(2,1)}, bf16[4,128,128]{2,1,0:T(8,128)(2,1)S(1)}, bf16[96,512]{1,0:T(8,128)(2,1)S(1)}, bf16[96,512]{1,0:T(8,128)(2,1)S(1)}) custom-call(s32[3]{0:T(128)S(1)} %pad_add_fusion.meta_ref, bf16[3,1024,512]{2,1,0:T(8,128)(2,1)S(1)} %get-tuple-element.40.moving_ref, ...), custom_call_target="tpu_custom_call" | custom-call | flops 4000000000 | bytes 14000000 | tf_op jit(solution)/shard_map/finish/pallas_call | solution.py:609
  58.8 3.6 %all-to-all-start.2 = ((bf16[16,96,128]{2,1,0:T(8,128)(2,1)}), bf16[16,96,128]{2,1,0:T(8,128)(2,1)S(1)}, u32[]{:S(2)}, u32[]{:S(2)}) async-start(bf16[16,96,128]{2,1,0:T(8,128)(2,1)} %get-tuple-element.48), calls=%async_computation.2 | async-start | bytes 786432 | tf_op jit(solution)/shard_map/all_to_all | solution.py:147
  62.4 1.3 %collective-permute-start.4 = (bf16[96,512]{1,0:T(8,128)(2,1)S(1)}, bf16[96,512]{1,0:T(8,128)(2,1)S(1)}, u32[]{:S(2)}, u32[]{:S(2)}) collective-permute-start(bf16[96,512]{1,0:T(8,128)(2,1)S(1)} %get-tuple-element.50), channel_id=1, source_target_pairs={{0,16},{16,0},{1,17},{17,1},{2,18},{18,2},{3,19},{19,3},{4,20},{20... | collective-permute-start | bytes 294920 | tf_op jit(solution)/shard_map/ppermute | solution.py:692
  63.6 0.9 collective-permute-done.4.refs_1_
  64.6 1.6 %collective-permute-start.7 = (bf16[96,512]{1,0:T(8,128)(2,1)S(1)}, bf16[96,512]{1,0:T(8,128)(2,1)S(1)}, u32[]{:S(2)}, u32[]{:S(2)}) collective-permute-start(bf16[96,512]{1,0:T(8,128)(2,1)S(1)} %add_all.4.refs_0_), channel_id=1, source_target_pairs={{0,96},{32,0},{64,32},{96,64},{1,97},{33,1},{65,33},{97,65},{2,98}... | collective-permute-start | bytes 294920 | tf_op jit(solution)/shard_map/ppermute | solution.py:697
  66.2 0.9 collective-permute-start.6
  67.1 0.4 collective-permute-start.5
  67.5 3.7 %all-to-all-done.2.in_ref = bf16[16,96,128]{2,1,0:T(8,128)(2,1)S(1)} async-done(((bf16[16,96,128]{2,1,0:T(8,128)(2,1)}), bf16[16,96,128]{2,1,0:T(8,128)(2,1)S(1)}, u32[]{:S(2)}, u32[]{:S(2)}) %all-to-all-start.2) | async-done | bytes 393248 | tf_op jit(solution)/shard_map/all_to_all | solution.py:147
  71.2 0.8 sum_spread.3
  72.0 3.8 %all-to-all-start.3 = ((bf16[16,96,128]{2,1,0:T(8,128)(2,1)}), bf16[16,96,128]{2,1,0:T(8,128)(2,1)S(1)}, u32[]{:S(2)}, u32[]{:S(2)}) async-start(bf16[16,96,128]{2,1,0:T(8,128)(2,1)} %sum_spread.3), calls=%async_computation.3 | async-start | bytes 786432 | tf_op jit(solution)/shard_map/all_to_all | solution.py:147
  75.8 0.0 copy-start
  75.8 5.4 %late.1 = bf16[1024,512]{1,0:T(8,128)(2,1)} custom-call(bf16[3,1024,512]{2,1,0:T(8,128)(2,1)} %copy-done.5, f32[16,1024]{1,0:T(8,128)S(1)} %get-tuple-element.38.row_ref, f32[1024,128]{1,0:T(8,128)S(1)} %get-tuple-element.41.col_ref, f32[96,128]{1,0:T(8,128)S(1)} %get-tuple-element.39.pass_ref, bf16[8,4,128,128]{3,2,1,0:T(8,128)(2,1)} %copy-done.6, ...), custom_call_target="tpu_custom_call" | custom-call | flops 6000000000 | bytes 6000000 | tf_op jit(solution)/shard_map/late/pallas_call | solution.py:511
  81.2 0.0 collective-permute-done.7.refs_3_
  81.2 2.8 %all-to-all-done.3.grad_ref = bf16[16,96,128]{2,1,0:T(8,128)(2,1)S(1)} async-done(((bf16[16,96,128]{2,1,0:T(8,128)(2,1)}), bf16[16,96,128]{2,1,0:T(8,128)(2,1)S(1)}, u32[]{:S(2)}, u32[]{:S(2)}) %all-to-all-start.3) | async-done | bytes 393248 | tf_op jit(solution)/shard_map/all_to_all | solution.py:147
  84.0 0.9 partial_down.1
  85.0 3.1 %collective-permute-start.8 = (bf16[96,384]{1,0:T(8,128)(2,1)S(1)}, bf16[96,384]{1,0:T(8,128)(2,1)S(1)}, u32[]{:S(2)}, u32[]{:S(2)}) collective-permute-start(bf16[96,384]{1,0:T(8,128)(2,1)S(1)} %get-tuple-element.57), channel_id=1, source_target_pairs={{0,16},{16,0},{1,17},{17,1},{2,18},{18,2},{3,19},{19,3},{4,20},{20... | collective-permute-start | bytes 221192 | tf_op jit(solution)/shard_map/ppermute | solution.py:692
  88.1 0.9 collective-permute-done.8.refs_1_
  89.0 0.1 add_all.6.own_ref
  89.1 0.4 collective-permute-start.9
  89.5 1.6 %collective-permute-start.12 = (bf16[96,384]{1,0:T(8,128)(2,1)S(1)}, bf16[96,384]{1,0:T(8,128)(2,1)S(1)}, u32[]{:S(2)}, u32[]{:S(2)}) collective-permute-start(bf16[96,384]{1,0:T(8,128)(2,1)S(1)} %add_all.5.refs_0_), channel_id=1, source_target_pairs={{0,96},{32,0},{64,32},{96,64},{1,97},{33,1},{65,33},{97,65},{2,98}... | collective-permute-start | bytes 221192 | tf_op jit(solution)/shard_map/ppermute | solution.py:697
  91.2 0.7 collective-permute-start.11
  91.9 0.2 collective-permute-start.10
  92.0 1.3 %join_halves.2 = f32[192,512]{1,0:T(8,128)} custom-call(s32[3]{0:T(128)S(1)} %pad_add_fusion.meta_ref, f32[96,512]{1,0:T(8,128)S(1)} %add_all.6.own_ref, f32[96,512]{1,0:T(8,128)S(1)} %collective-permute-done.9.mate_ref), custom_call_target="tpu_custom_call" | custom-call | tf_op jit(solution)/shard_map/join_halves/pallas_call | solution.py:663
  93.4 2.5 %collective-permute-done.11.refs_2_ = bf16[96,384]{1,0:T(8,128)(2,1)S(1)} collective-permute-done((bf16[96,384]{1,0:T(8,128)(2,1)S(1)}, bf16[96,384]{1,0:T(8,128)(2,1)S(1)}, u32[]{:S(2)}, u32[]{:S(2)}) %collective-permute-start.11) | collective-permute-done | bytes 73760 | tf_op jit(solution)/shard_map/ppermute | solution.py:697
  95.9 2.2 %collective-permute-done.10.refs_1_ = bf16[96,384]{1,0:T(8,128)(2,1)S(1)} collective-permute-done((bf16[96,384]{1,0:T(8,128)(2,1)S(1)}, bf16[96,384]{1,0:T(8,128)(2,1)S(1)}, u32[]{:S(2)}, u32[]{:S(2)}) %collective-permute-start.10) | collective-permute-done | bytes 73760 | tf_op jit(solution)/shard_map/ppermute | solution.py:697
  98.1 1.0 collective-permute-start.13
  99.0 1.0 collective-permute-done.13.mate_ref
  100.1 1.3 %join_halves.3 = f32[192,384]{1,0:T(8,128)} custom-call(s32[3]{0:T(128)S(1)} %pad_add_fusion.meta_ref, f32[96,384]{1,0:T(8,128)S(1)} %add_all.7.own_ref, f32[96,384]{1,0:T(8,128)S(1)} %collective-permute-done.13.mate_ref), custom_call_target="tpu_custom_call" | custom-call | tf_op jit(solution)/shard_map/join_halves/pallas_call | solution.py:663
  (20 shorter events, 0.1 us)
Async XLA Ops:
  0.6 24.9 %copy-start.4 = (s32[1024]{0:T(1024)S(1)}, s32[1024]{0:T(1024)}, u32[]{:S(2)}) copy-start(s32[1024]{0:T(1024)} %param.14) | copy-start | bytes 12292
  0.6 24.9 %copy-start.3 = (bf16[4,1024]{1,0:T(4,128)(2,1)S(1)}, bf16[4,1024]{1,0:T(4,128)(2,1)}, u32[]{:S(2)}) copy-start(bf16[4,1024]{1,0:T(4,128)(2,1)} %decay_ref.1) | copy-start | bytes 24580
  3.5 17.6 %all-to-all-start = ((bf16[16,96,128]{2,1,0:T(8,128)(2,1)}), bf16[16,96,128]{2,1,0:T(8,128)(2,1)S(1)}, u32[]{:S(2)}, u32[]{:S(2)}) async-start(bf16[16,96,128]{2,1,0:T(8,128)(2,1)} %partial_low.1), calls=%async_computation | async-start | bytes 786432 | tf_op jit(solution)/shard_map/all_to_all | solution.py:147
  22.0 11.8 %all-to-all-start.1 = ((bf16[16,96,128]{2,1,0:T(8,128)(2,1)}), bf16[16,96,128]{2,1,0:T(8,128)(2,1)S(1)}, u32[]{:S(2)}, u32[]{:S(2)}) async-start(bf16[16,96,128]{2,1,0:T(8,128)(2,1)} %sum_spread.2), calls=%async_computation.1 | async-start | bytes 786432 | tf_op jit(solution)/shard_map/all_to_all | solution.py:147
  25.5 8.2 %copy-start.1 = (bf16[1024,512]{1,0:T(8,128)(2,1)S(1)}, bf16[1024,512]{1,0:T(8,128)(2,1)}, u32[]{:S(2)}) copy-start(bf16[1024,512]{1,0:T(8,128)(2,1)} %g_ref.1) | copy-start | bytes 3145732
  25.5 8.2 %copy-start.2 = (bf16[3,64,512]{2,1,0:T(8,128)(2,1)S(1)}, bf16[3,64,512]{2,1,0:T(8,128)(2,1)}, u32[]{:S(2)}) copy-start(bf16[3,64,512]{2,1,0:T(8,128)(2,1)} %up_ref.3) | copy-start | bytes 589828
  37.6 15.5 %copy-start.6 = (bf16[8,4,128,128]{3,2,1,0:T(8,128)(2,1)}, bf16[8,4,128,128]{3,2,1,0:T(8,128)(2,1)S(1)}, u32[]{:S(2)}) copy-start(bf16[8,4,128,128]{3,2,1,0:T(8,128)(2,1)S(1)} %get-tuple-element.42.before_ref) | copy-start | bytes 3145732
  37.6 15.5 %copy-start.5 = (bf16[3,1024,512]{2,1,0:T(8,128)(2,1)}, bf16[3,1024,512]{2,1,0:T(8,128)(2,1)S(1)}, u32[]{:S(2)}) copy-start(bf16[3,1024,512]{2,1,0:T(8,128)(2,1)S(1)} %get-tuple-element.40.moving_ref) | copy-start | bytes 9437188
  37.6 4.2 %collective-permute-start = (bf16[1040,128]{1,0:T(8,128)(2,1)S(1)}, bf16[1040,128]{1,0:T(8,128)(2,1)S(1)}, u32[]{:S(2)}, u32[]{:S(2)}) collective-permute-start(bf16[1040,128]{1,0:T(8,128)(2,1)S(1)} %get-tuple-element.44.own_ref), channel_id=1, source_target_pairs={{0,16},{16,0},{1,17},{17,1},{2,18},{18,2},{3,19},{19,3},{4,20},{20... | collective-permute-start | bytes 798728 | tf_op jit(solution)/shard_map/ppermute | solution.py:692
  42.5 10.5 %collective-permute-start.1 = (bf16[528,128]{1,0:T(8,128)(2,1)S(1)}, bf16[528,128]{1,0:T(8,128)(2,1)S(1)}, u32[]{:S(2)}, u32[]{:S(2)}) collective-permute-start(bf16[528,128]{1,0:T(8,128)(2,1)S(1)} %get-tuple-element.45), channel_id=1, source_target_pairs={{0,32},{32,64},{64,96},{96,0},{1,33},{33,65},{65,97},{97,1},{2,34}... | collective-permute-start | bytes 405512 | tf_op jit(solution)/shard_map/ppermute | solution.py:697
  43.9 9.2 %collective-permute-start.2 = (bf16[528,128]{1,0:T(8,128)(2,1)S(1)}, bf16[528,128]{1,0:T(8,128)(2,1)S(1)}, u32[]{:S(2)}, u32[]{:S(2)}) collective-permute-start(bf16[528,128]{1,0:T(8,128)(2,1)S(1)} %get-tuple-element.46), channel_id=1, source_target_pairs={{0,64},{32,96},{64,0},{96,32},{1,65},{33,97},{65,1},{97,33},{2,66}... | collective-permute-start | bytes 405512 | tf_op jit(solution)/shard_map/ppermute | solution.py:697
  46.5 6.6 %collective-permute-start.3 = (bf16[528,128]{1,0:T(8,128)(2,1)S(1)}, bf16[528,128]{1,0:T(8,128)(2,1)S(1)}, u32[]{:S(2)}, u32[]{:S(2)}) collective-permute-start(bf16[528,128]{1,0:T(8,128)(2,1)S(1)} %get-tuple-element.47), channel_id=1, source_target_pairs={{0,96},{32,0},{64,32},{96,64},{1,97},{33,1},{65,33},{97,65},{2,98}... | collective-permute-start | bytes 405512 | tf_op jit(solution)/shard_map/ppermute | solution.py:697
  58.8 12.4 %all-to-all-start.2 = ((bf16[16,96,128]{2,1,0:T(8,128)(2,1)}), bf16[16,96,128]{2,1,0:T(8,128)(2,1)S(1)}, u32[]{:S(2)}, u32[]{:S(2)}) async-start(bf16[16,96,128]{2,1,0:T(8,128)(2,1)} %get-tuple-element.48), calls=%async_computation.2 | async-start | bytes 786432 | tf_op jit(solution)/shard_map/all_to_all | solution.py:147
  62.4 2.2 %collective-permute-start.4 = (bf16[96,512]{1,0:T(8,128)(2,1)S(1)}, bf16[96,512]{1,0:T(8,128)(2,1)S(1)}, u32[]{:S(2)}, u32[]{:S(2)}) collective-permute-start(bf16[96,512]{1,0:T(8,128)(2,1)S(1)} %get-tuple-element.50), channel_id=1, source_target_pairs={{0,16},{16,0},{1,17},{17,1},{2,18},{18,2},{3,19},{19,3},{4,20},{20... | collective-permute-start | bytes 294920 | tf_op jit(solution)/shard_map/ppermute | solution.py:692
  64.6 16.6 %collective-permute-start.7 = (bf16[96,512]{1,0:T(8,128)(2,1)S(1)}, bf16[96,512]{1,0:T(8,128)(2,1)S(1)}, u32[]{:S(2)}, u32[]{:S(2)}) collective-permute-start(bf16[96,512]{1,0:T(8,128)(2,1)S(1)} %add_all.4.refs_0_), channel_id=1, source_target_pairs={{0,96},{32,0},{64,32},{96,64},{1,97},{33,1},{65,33},{97,65},{2,98}... | collective-permute-start | bytes 294920 | tf_op jit(solution)/shard_map/ppermute | solution.py:697
  66.2 15.0 %collective-permute-start.6 = (bf16[96,512]{1,0:T(8,128)(2,1)S(1)}, bf16[96,512]{1,0:T(8,128)(2,1)S(1)}, u32[]{:S(2)}, u32[]{:S(2)}) collective-permute-start(bf16[96,512]{1,0:T(8,128)(2,1)S(1)} %add_all.4.refs_0_), channel_id=1, source_target_pairs={{0,64},{32,96},{64,0},{96,32},{1,65},{33,97},{65,1},{97,33},{2,66}... | collective-permute-start | bytes 294920 | tf_op jit(solution)/shard_map/ppermute | solution.py:697
  67.1 14.2 %collective-permute-start.5 = (bf16[96,512]{1,0:T(8,128)(2,1)S(1)}, bf16[96,512]{1,0:T(8,128)(2,1)S(1)}, u32[]{:S(2)}, u32[]{:S(2)}) collective-permute-start(bf16[96,512]{1,0:T(8,128)(2,1)S(1)} %add_all.4.refs_0_), channel_id=1, source_target_pairs={{0,32},{32,64},{64,96},{96,0},{1,33},{33,65},{65,97},{97,1},{2,34}... | collective-permute-start | bytes 294920 | tf_op jit(solution)/shard_map/ppermute | solution.py:697
  72.0 12.0 %all-to-all-start.3 = ((bf16[16,96,128]{2,1,0:T(8,128)(2,1)}), bf16[16,96,128]{2,1,0:T(8,128)(2,1)S(1)}, u32[]{:S(2)}, u32[]{:S(2)}) async-start(bf16[16,96,128]{2,1,0:T(8,128)(2,1)} %sum_spread.3), calls=%async_computation.3 | async-start | bytes 786432 | tf_op jit(solution)/shard_map/all_to_all | solution.py:147
  75.8 8.2 %copy-start = (bf16[1024,384]{1,0:T(8,128)(2,1)S(1)}, bf16[1024,384]{1,0:T(8,128)(2,1)}, u32[]{:S(2)}) copy-start(bf16[1024,384]{1,0:T(8,128)(2,1)} %x_ref.3) | copy-start | bytes 2359300
  85.0 4.0 %collective-permute-start.8 = (bf16[96,384]{1,0:T(8,128)(2,1)S(1)}, bf16[96,384]{1,0:T(8,128)(2,1)S(1)}, u32[]{:S(2)}, u32[]{:S(2)}) collective-permute-start(bf16[96,384]{1,0:T(8,128)(2,1)S(1)} %get-tuple-element.57), channel_id=1, source_target_pairs={{0,16},{16,0},{1,17},{17,1},{2,18},{18,2},{3,19},{19,3},{4,20},{20... | collective-permute-start | bytes 221192 | tf_op jit(solution)/shard_map/ppermute | solution.py:692
  89.1 3.0 %collective-permute-start.9 = (f32[96,512]{1,0:T(8,128)S(1)}, f32[96,512]{1,0:T(8,128)S(1)}, u32[]{:S(2)}, u32[]{:S(2)}) collective-permute-start(f32[96,512]{1,0:T(8,128)S(1)} %add_all.6.own_ref), channel_id=1, source_target_pairs={{0,16},{16,0},{1,17},{17,1},{2,18},{18,2},{3,19},{19,3},{4,20},{20... | collective-permute-start | bytes 589832 | tf_op jit(solution)/shard_map/ppermute | solution.py:692
  89.5 3.8 %collective-permute-start.12 = (bf16[96,384]{1,0:T(8,128)(2,1)S(1)}, bf16[96,384]{1,0:T(8,128)(2,1)S(1)}, u32[]{:S(2)}, u32[]{:S(2)}) collective-permute-start(bf16[96,384]{1,0:T(8,128)(2,1)S(1)} %add_all.5.refs_0_), channel_id=1, source_target_pairs={{0,96},{32,0},{64,32},{96,64},{1,97},{33,1},{65,33},{97,65},{2,98}... | collective-permute-start | bytes 221192 | tf_op jit(solution)/shard_map/ppermute | solution.py:697
  91.2 4.7 %collective-permute-start.11 = (bf16[96,384]{1,0:T(8,128)(2,1)S(1)}, bf16[96,384]{1,0:T(8,128)(2,1)S(1)}, u32[]{:S(2)}, u32[]{:S(2)}) collective-permute-start(bf16[96,384]{1,0:T(8,128)(2,1)S(1)} %add_all.5.refs_0_), channel_id=1, source_target_pairs={{0,64},{32,96},{64,0},{96,32},{1,65},{33,97},{65,1},{97,33},{2,66}... | collective-permute-start | bytes 221192 | tf_op jit(solution)/shard_map/ppermute | solution.py:697
  91.9 6.2 %collective-permute-start.10 = (bf16[96,384]{1,0:T(8,128)(2,1)S(1)}, bf16[96,384]{1,0:T(8,128)(2,1)S(1)}, u32[]{:S(2)}, u32[]{:S(2)}) collective-permute-start(bf16[96,384]{1,0:T(8,128)(2,1)S(1)} %add_all.5.refs_0_), channel_id=1, source_target_pairs={{0,32},{32,64},{64,96},{96,0},{1,33},{33,65},{65,97},{97,1},{2,34}... | collective-permute-start | bytes 221192 | tf_op jit(solution)/shard_map/ppermute | solution.py:697
  98.1 2.0 %collective-permute-start.13 = (f32[96,384]{1,0:T(8,128)S(1)}, f32[96,384]{1,0:T(8,128)S(1)}, u32[]{:S(2)}, u32[]{:S(2)}) collective-permute-start(f32[96,384]{1,0:T(8,128)S(1)} %add_all.7.own_ref), channel_id=1, source_target_pairs={{0,16},{16,0},{1,17},{17,1},{2,18},{18,2},{3,19},{19,3},{4,20},{20... | collective-permute-start | bytes 442376 | tf_op jit(solution)/shard_map/ppermute | solution.py:692
